TPU v7x, 32 devices: a whole 2x2x4 slice. The times are simulated.
32 devices in a mesh: bucket: 4 (over y, x), dp: 8 (over z, core).
Axes of the slice: x: 2, y: 2, z: 4, core: 2. Of those that a mesh axis runs over, the one named last changes fastest.
Arguments:
- tokens: bfloat16 [32768, 384], P(('bucket', 'dp')), may hold values from -6 to 6
- cotangent: bfloat16 [32768, 384], P(('bucket', 'dp')), may hold values from -6 to 6
- segment_ids: int32 [32768], P(('bucket', 'dp')), may hold values from 0 to 6, as said below
- keep_mask: int32 [32768], P(('bucket', 'dp')), may hold values from 0 to 1, as said below
- bucket_patches: int32 [4], replicated, may hold values from 64 to 576
- master: float32 [1771776], P(('bucket', 'dp')), may hold values from -3 to 3
- first_moment: float32 [1771776], P(('bucket', 'dp')), may hold values from -90.50967 to 90.50967
- second_moment: float32 [1771776], P(('bucket', 'dp')), may hold values from 3.2768 to 68.8128, as said below
Outputs:
- block_output: bfloat16 [32768, 384], P(('bucket', 'dp'))
- input_grad: float32 [32768, 384], P(('bucket', 'dp'))
- new_first: float32 [1771776], P(('bucket', 'dp'))
- new_second: float32 [1771776], P(('bucket', 'dp'))
- new_master: float32 [1771776], P(('bucket', 'dp'))
- norms: float32 [2, 10], replicated
- trust: float32 [10], replicated
Inputs may be any that keep to these rules, and one draw needn't show every extreme that they name: `segment_ids`: within each sequence (aligned blocks of 1024 rows) ids start at 0 and never fall; in buckets 0 to 1 no id occurs in both halves of a sequence. `keep_mask`: the first row of every sequence (aligned blocks of 1024 rows) is 1. `second_moment`: no entry is zero.
All inputs are finite; a program needn't handle non-finite values.
Results may differ from a plain program's by a relative error of at most 0.0085.
The roundings to bfloat16 on the way count: a program that leaves them out, or rounds other values in their place, can miss the bound.
Values may be sent and summed in bfloat16 or wider, within the bound.
No kernel may reach another device: no remote copies, remote signals or barrier semaphores. Data moves between devices by JAX's collectives and lax.ppermute only.
A program may use at most 128 MiB of HBM per device.

v0:
```python
import jax
import jax.numpy as jnp
from jax import lax
from jax.sharding import PartitionSpec as P

D = 384
HEADS = 6
HD = 64
FF = 1536
SEQ = 1024
STEP = 10
MATS = 10
HALF = 512


norm_epsilon = 1e-06
adam_epsilon = 1e-06
beta_one = 0.9
beta_two = 0.999
learn_rate = 0.5
weight_decay = 0.01
masked_score = -1e30


def layer_norm(values):
    average = jnp.mean(values, axis=-1, keepdims=True)
    centered = values - average
    variance = jnp.mean(centered * centered, axis=-1, keepdims=True)
    return centered * lax.rsqrt(variance + norm_epsilon)


def tensor_bounds():
    matrix_end = 4 * D * D + 2 * D * FF
    return [0, 3 * D * D, 4 * D * D, 4 * D * D + D * FF, matrix_end] + [
        matrix_end + (j + 1) * D for j in range(6)
    ]


def tensor_ids(index):
    owners = jnp.zeros(index.shape, jnp.int32)
    for bound in tensor_bounds()[1:-1]:
        owners = owners + (index >= bound).astype(jnp.int32)
    return owners


def split_params(flat_params):
    bounds = tensor_bounds()
    pieces = [flat_params[bounds[j] : bounds[j + 1]] for j in range(len(bounds) - 1)]
    return (
        pieces[0].reshape(D, 3 * D),
        pieces[1].reshape(D, D),
        pieces[2].reshape(D, FF),
        pieces[3].reshape(FF, D),
        pieces[4:],
    )


def gelu_exact(values):
    return jax.nn.gelu(values, approximate=False)


def query_key_norm(query_raw, key_raw, query_gain, key_gain):
    return (layer_norm(query_raw) * query_gain, layer_norm(key_raw) * key_gain)


def block_scores(queries, key_rows, row_segment, col_segment, col_kept, row_place, col_place):
    raw_scores = jnp.einsum(
        "qhd,khd->hqk", queries, key_rows, preferred_element_type=jnp.float32
    ) * queries.shape[-1] ** (-0.5)
    allowed = (row_segment[:, None] == col_segment[None, :]) & (
        (col_kept[None, :] == 1) | (row_place[:, None] == col_place[None, :])
    )
    return jnp.where(allowed[None], raw_scores, masked_score)


def group_forward(queries, key_rows, values, segment, kept):
    length = key_rows.shape[0]
    places = jnp.arange(length, dtype=jnp.int32)

    def one_block(offset):
        query_block = lax.dynamic_slice_in_dim(queries, offset, HALF, 0)
        row_segment = lax.dynamic_slice_in_dim(segment, offset, HALF, 0)
        row_place = lax.dynamic_slice_in_dim(places, offset, HALF, 0)
        scores = block_scores(query_block, key_rows, row_segment, segment, kept, row_place, places)
        highest = jnp.max(scores, axis=-1, keepdims=True)
        expo_rows = jnp.exp(scores - highest)
        totals = jnp.sum(expo_rows, axis=-1, keepdims=True)
        attention = (expo_rows / totals).astype(jnp.bfloat16)
        attended = jnp.einsum("hqk,khd->qhd", attention, values, preferred_element_type=jnp.float32)
        return (attended, (highest + jnp.log(totals))[..., 0])

    offsets = jnp.arange(length // HALF, dtype=jnp.int32) * HALF
    attended, log_totals = lax.map(one_block, offsets)
    return (attended.reshape(queries.shape), log_totals)


def group_backward(queries, key_rows, values, segment, kept, grad_attended, log_totals):
    length = key_rows.shape[0]
    places = jnp.arange(length, dtype=jnp.int32)
    scale_factor = queries.shape[-1] ** (-0.5)

    def one_block(carry, operands):
        offset, block_totals = operands
        grad_keys, grad_values = carry
        query_block = lax.dynamic_slice_in_dim(queries, offset, HALF, 0)
        grad_block = lax.dynamic_slice_in_dim(grad_attended, offset, HALF, 0)
        row_segment = lax.dynamic_slice_in_dim(segment, offset, HALF, 0)
        row_place = lax.dynamic_slice_in_dim(places, offset, HALF, 0)
        scores = block_scores(query_block, key_rows, row_segment, segment, kept, row_place, places)
        attention = jnp.exp(scores - block_totals[..., None])
        attention_low = attention.astype(jnp.bfloat16)
        grad_attention = jnp.einsum(
            "qhd,khd->hqk", grad_block, values, preferred_element_type=jnp.float32
        )
        inner_sum = jnp.sum(attention * grad_attention, axis=-1, keepdims=True)
        grad_scores = (attention * (grad_attention - inner_sum)).astype(jnp.bfloat16)
        grad_query = (
            jnp.einsum("hqk,khd->qhd", grad_scores, key_rows, preferred_element_type=jnp.float32)
            * scale_factor
        )
        grad_keys = (
            grad_keys
            + jnp.einsum(
                "hqk,qhd->khd", grad_scores, query_block, preferred_element_type=jnp.float32
            )
            * scale_factor
        )
        grad_values = grad_values + jnp.einsum(
            "hqk,qhd->khd", attention_low, grad_block, preferred_element_type=jnp.float32
        )
        return ((grad_keys, grad_values), grad_query)

    offsets = jnp.arange(length // HALF, dtype=jnp.int32) * HALF
    zeros_start = jnp.zeros(key_rows.shape, jnp.float32)
    (grad_keys, grad_values), grad_queries = lax.scan(
        one_block, (zeros_start, zeros_start), (offsets, log_totals)
    )
    return (grad_queries.reshape(queries.shape), grad_keys, grad_values)


def forward_whole(operands):
    return group_forward(*operands)


def backward_whole(operands):
    return group_backward(*operands)


def pair_forward(operands):
    return forward_whole(operands)


def pair_backward(operands):
    return backward_whole(operands)


def to_pairs(matrix):
    return matrix.reshape(matrix.shape[0], matrix.shape[1] // 2, 2, matrix.shape[2]).transpose(
        1, 0, 2, 3
    )


def from_pairs(matrix):
    return matrix.transpose(1, 0, 2, 3).reshape(
        matrix.shape[1], 2 * matrix.shape[0], matrix.shape[3]
    )


def sequence_forward(operands):
    queries, key_rows, values, segment, kept = operands

    def per_pair(triple):
        return pair_forward((triple[0], triple[1], triple[2], segment, kept))

    attended, log_totals = lax.map(
        per_pair, (to_pairs(queries), to_pairs(key_rows), to_pairs(values))
    )
    return (from_pairs(attended), log_totals)


def sequence_backward(operands):
    queries, key_rows, values, segment, kept, grad_attended, log_totals = operands

    def per_pair(bundle):
        return pair_backward((bundle[0], bundle[1], bundle[2], segment, kept, bundle[3], bundle[4]))

    gradients = lax.map(
        per_pair,
        (
            to_pairs(queries),
            to_pairs(key_rows),
            to_pairs(values),
            to_pairs(grad_attended),
            log_totals,
        ),
    )
    return tuple((from_pairs(gradient) for gradient in gradients))


def affine_norm(values, gain, shift):
    return layer_norm(values) * gain + shift


def local(
    tokens, cotangent, segment_ids, keep_mask, bucket_patches, master, first_moment, second_moment
):
    shard_size = master.shape[0]
    row_count = tokens.shape[0]
    sequences = row_count // SEQ
    flat_index = lax.axis_index(("bucket", "dp")) * shard_size + jnp.arange(
        shard_size, dtype=jnp.int32
    )
    owners = tensor_ids(flat_index)
    ownership = (owners[:, None] == jnp.arange(MATS, dtype=jnp.int32)[None, :]).astype(jnp.float32)
    weight_sq_local = jnp.sum((master * master)[:, None] * ownership, axis=0)
    gathered = lax.all_gather(master.astype(jnp.bfloat16), ("bucket", "dp"), axis=0, tiled=True)
    project_weight, output_weight, up_weight, down_weight, gain_rows = split_params(gathered)
    first_gain, first_shift, query_gain, key_gain, second_gain, second_shift = [
        piece.astype(jnp.float32) for piece in gain_rows
    ]
    query_gain = query_gain.reshape(HEADS, HD)
    key_gain = key_gain.reshape(HEADS, HD)
    bucket_hot = (
        jnp.arange(bucket_patches.shape[0], dtype=jnp.int32) == lax.axis_index("bucket")
    ).astype(jnp.float32)
    keep_float = keep_mask.astype(jnp.float32)
    kept_local = bucket_hot * jnp.sum(keep_float)
    kept_all = lax.psum(kept_local, ("bucket", "dp"))
    token_float = tokens.astype(jnp.float32)
    normed, first_back = jax.vjp(affine_norm, token_float, first_gain, first_shift)
    normed_low = normed.astype(jnp.bfloat16)
    project = jnp.dot(normed_low, project_weight, preferred_element_type=jnp.float32)
    project_view = project.reshape(row_count, 3, HEADS, HD)
    (queries, key_rows), norm_back = jax.vjp(
        query_key_norm, project_view[:, 0], project_view[:, 1], query_gain, key_gain
    )
    queries_low = queries.astype(jnp.bfloat16).reshape(sequences, SEQ, HEADS, HD)
    keys_low = key_rows.astype(jnp.bfloat16).reshape(sequences, SEQ, HEADS, HD)
    values_low = project_view[:, 2].astype(jnp.bfloat16).reshape(sequences, SEQ, HEADS, HD)
    segment_rows = segment_ids.reshape(sequences, SEQ)
    kept_rows = keep_mask.reshape(sequences, SEQ)
    attended, log_totals = lax.map(
        sequence_forward, (queries_low, keys_low, values_low, segment_rows, kept_rows)
    )
    attended_low = attended.reshape(row_count, D).astype(jnp.bfloat16)
    middle = token_float + jnp.dot(attended_low, output_weight, preferred_element_type=jnp.float32)
    normed_two, second_back = jax.vjp(affine_norm, middle, second_gain, second_shift)
    normed_two_low = normed_two.astype(jnp.bfloat16)
    hidden_pre = jnp.dot(normed_two_low, up_weight, preferred_element_type=jnp.float32)
    hidden, gelu_back = jax.vjp(gelu_exact, hidden_pre)
    hidden_low = hidden.astype(jnp.bfloat16)
    output = middle + jnp.dot(hidden_low, down_weight, preferred_element_type=jnp.float32)
    block_output = output.astype(jnp.bfloat16)
    patches = bucket_patches.astype(jnp.float32)
    own_patches = jnp.sum(patches * bucket_hot)
    own_kept = jnp.sum(kept_all * bucket_hot)
    bucket_rows = row_count * lax.axis_size("dp")
    bucket_scale = patches.shape[0] * own_patches / jnp.sum(patches) * bucket_rows / own_kept
    seed_grad = cotangent.astype(jnp.float32) * (keep_float * bucket_scale)[:, None]
    seed_low = seed_grad.astype(jnp.bfloat16)
    grad_down = jnp.einsum("tf,td->fd", hidden_low, seed_low, preferred_element_type=jnp.float32)
    (grad_hidden_pre,) = gelu_back(
        jnp.einsum("td,fd->tf", seed_low, down_weight, preferred_element_type=jnp.float32)
    )
    grad_pre_low = grad_hidden_pre.astype(jnp.bfloat16)
    grad_up = jnp.einsum(
        "td,tf->df", normed_two_low, grad_pre_low, preferred_element_type=jnp.float32
    )
    grad_middle_norm, grad_second_gain, grad_second_shift = second_back(
        jnp.einsum("tf,df->td", grad_pre_low, up_weight, preferred_element_type=jnp.float32)
    )
    grad_middle = seed_grad + grad_middle_norm
    grad_middle_low = grad_middle.astype(jnp.bfloat16)
    grad_output_w = jnp.einsum(
        "ti,tj->ij", attended_low, grad_middle_low, preferred_element_type=jnp.float32
    )
    grad_attended = jnp.einsum(
        "tj,ij->ti", grad_middle_low, output_weight, preferred_element_type=jnp.float32
    ).astype(jnp.bfloat16)
    grad_queries, grad_keys, grad_values = lax.map(
        sequence_backward,
        (
            queries_low,
            keys_low,
            values_low,
            segment_rows,
            kept_rows,
            grad_attended.reshape(sequences, SEQ, HEADS, HD),
            log_totals,
        ),
    )
    grad_query_raw, grad_key_raw, grad_query_gain, grad_key_gain = norm_back(
        (grad_queries.reshape(row_count, HEADS, HD), grad_keys.reshape(row_count, HEADS, HD))
    )
    grad_project = (
        jnp.stack([grad_query_raw, grad_key_raw, grad_values.reshape(row_count, HEADS, HD)], axis=1)
        .reshape(row_count, 3 * D)
        .astype(jnp.bfloat16)
    )
    grad_project_w = jnp.einsum(
        "ti,tj->ij", normed_low, grad_project, preferred_element_type=jnp.float32
    )
    grad_token_norm, grad_first_gain, grad_first_shift = first_back(
        jnp.einsum("tj,ij->ti", grad_project, project_weight, preferred_element_type=jnp.float32)
    )
    input_grad = grad_middle + grad_token_norm
    grad_flat = jnp.concatenate(
        [
            grad_project_w.reshape(-1),
            grad_output_w.reshape(-1),
            grad_up.reshape(-1),
            grad_down.reshape(-1),
            grad_first_gain,
            grad_first_shift,
            grad_query_gain.reshape(-1),
            grad_key_gain.reshape(-1),
            grad_second_gain,
            grad_second_shift,
        ]
    )
    grads = lax.psum_scatter(grad_flat, ("bucket", "dp"), scatter_dimension=0, tiled=True)
    first_new = beta_one * first_moment + (1.0 - beta_one) * grads
    second_new = beta_two * second_moment + (1.0 - beta_two) * grads * grads
    first_hat = first_new / (1.0 - beta_one**STEP)
    second_hat = second_new / (1.0 - beta_two**STEP)
    decay_rows = jnp.where(owners < 4, weight_decay, 0.0)
    update = first_hat / (jnp.sqrt(second_hat) + adam_epsilon) + decay_rows * master
    update_sq_local = jnp.sum((update * update)[:, None] * ownership, axis=0)
    weight_sq, update_sq = lax.psum((weight_sq_local, update_sq_local), ("bucket", "dp"))
    trust = jnp.sqrt(weight_sq) / (jnp.sqrt(update_sq) + adam_epsilon)
    trust_rows = jnp.sum(ownership * trust[None, :], axis=1)
    new_master = master - learn_rate * trust_rows * update
    norms = jnp.stack([jnp.sqrt(weight_sq), jnp.sqrt(update_sq)])
    return (block_output, input_grad, first_new, second_new, new_master, norms, trust)


def solution(mesh):
    placed = (
        P(("bucket", "dp"), None),
        P(("bucket", "dp"), None),
        P(("bucket", "dp")),
        P(("bucket", "dp")),
        P(),
        P(("bucket", "dp")),
        P(("bucket", "dp")),
        P(("bucket", "dp")),
    )
    return jax.shard_map(
        local,
        mesh=mesh,
        in_specs=placed,
        out_specs=(
            P(("bucket", "dp"), None),
            P(("bucket", "dp"), None),
            P(("bucket", "dp")),
            P(("bucket", "dp")),
            P(("bucket", "dp")),
            P(),
            P(),
        ),
        check_vma=False,
    )
```

profile of v0, /device:TPU:0, one launch (start us, length us, event | category | flops | bytes accessed | tf_op | source)
XLA Modules:
  0.0 623.0 jit_solution(5818625127306661249)
XLA Ops:
  14.4 42.3 %psum.21 = f32[4]{0:T(128)S(1)} all-reduce(f32[4]{0:T(128)S(1)} %fusion.91), channel_id=1, replica_groups=mesh['bucket'=4,'dp'=8] {'bucket','dp'}, use_global_device_ids=true, to_apply=%region_17.18 | all-reduce | flops 4 | bytes 32 | tf_op jit(solution)/shard_map/psum | solution.py:228
  64.6 90.9 %all-reduce.6.cloned.1.call-done = bf16[1771776]{0:T(1024)(128)(2,1)} async-done(((bf16[1771776]{0:T(1024)(128)(2,1)}), bf16[1771776]{0:T(1024)(128)(2,1)}) %all-reduce.6.cloned.1.call-update) | async-done | bytes 3543568
  165.0 2.9 multiply_reduce_fusion.4
  168.9 2.8 fusion.103
  171.7 3.1 slice.113
  179.2 50.5 %while.82 = (s32[]{:T(128)}, bf16[3,1024,2,64]{1,3,2,0:T(8,128)(2,1)}, f32[3,2,2,512]{3,2,1,0:T(2,128)S(1)}, bf16[3,1024,2,64]{1,3,2,0:T(8,128)(2,1)S(1)}, bf16[...) while((s32[]{:T(128)}, ...), condition=%wide.region_11.12_spmd.clone, body=%wide.region_6.11_spmd.sunk.clone | while | flops 283115520 | bytes 18823636 | solution.py:175
  180.5 14.2 %while.81 = (s32[]{:T(128)}, bf16[2,512,2,64]{1,3,2,0:T(8,128)(2,1)S(1)}, f32[2,2,512]{2,1,0:T(2,128)S(1)}, s32[2]{0:T(128)S(1)}, s32[1024]{0:T(1024)S(1)}, /*in...) while((s32[]{:T(128)}, ...), condition=%wide.region_10.10_spmd.clone, body=%wide.region_7.9_spmd.clone.sunk | while | flops 283115520 | bytes 15657159 | solution.py:93
  197.2 14.2 %while.81 = (s32[]{:T(128)}, bf16[2,512,2,64]{1,3,2,0:T(8,128)(2,1)S(1)}, f32[2,2,512]{2,1,0:T(2,128)S(1)}, s32[2]{0:T(128)S(1)}, s32[1024]{0:T(1024)S(1)}, /*in...) while((s32[]{:T(128)}, ...), condition=%wide.region_10.10_spmd.clone, body=%wide.region_7.9_spmd.clone.sunk | while | flops 283115520 | bytes 15657159 | solution.py:93
  214.0 14.2 %while.81 = (s32[]{:T(128)}, bf16[2,512,2,64]{1,3,2,0:T(8,128)(2,1)S(1)}, f32[2,2,512]{2,1,0:T(2,128)S(1)}, s32[2]{0:T(128)S(1)}, s32[1024]{0:T(1024)S(1)}, /*in...) while((s32[]{:T(128)}, ...), condition=%wide.region_10.10_spmd.clone, body=%wide.region_7.9_spmd.clone.sunk | while | flops 283115520 | bytes 15657159 | solution.py:93
  232.9 16.7 %multiply_convert_fusion.1 = (bf16[1024,1536]{1,0:T(8,128)(2,1)}, f32[1024,1536]{1,0:T(8,128)S(1)}, f32[1024,1536]{1,0:T(8,128)S(1)}) fusion(bf16[384,1536]{1,0:T(8,128)(2,1)S(1)} %copy-done.36, f32[1024,384]{0,1:T(8,128)S(1)} %get-tuple-element.711, f32[384]{0:T(512)S(1)} %copy-done.85, f32[384]{0:T(512)S(1)} %copy-done.81, f32[1024]{0:T(1024)S(1)} %fusion.90, ...), kind=kOutput, calls=%fused_computation.63 | convolution fusion | flops 1312161792 | bytes 18492416 | tf_op jit(solution)/shard_map/dot_general | solution.py:249
  249.6 3.7 add_convert_fusion
  253.3 3.6 fusion.107
  257.0 3.0 fusion.98
  260.0 3.0 copy.191
  263.0 2.5 multiply_reduce_fusion.1
  271.2 82.5 %while.84 = (s32[]{:T(128)}, f32[3,1024,2,64]{1,3,2,0:T(8,128)}, f32[3,1024,2,64]{1,3,2,0:T(8,128)}, bf16[3,1024,2,64]{1,3,2,0:T(8,128)(2,1)}, f32[3,2,2,512]{3,...) while((s32[]{:T(128)}, f32[3,1024,2,64]{1,3,2,0:T(8,128)}, ...), condition=%wide.region_25.26_spmd.clone, body=%wide.region_21.25_spmd.sunk.clone | while | flops 689635328 | bytes 55126684 | solution.py:187
  273.9 21.0 %while.83 = (s32[]{:T(128)}, f32[1024,2,64]{0,2,1:T(8,128)S(1)}, f32[1024,2,64]{0,2,1:T(8,128)}, f32[2,512,2,64]{1,3,2,0:T(8,128)S(1)}, s32[2]{0:T(128)S(1)}, /*...) while((s32[]{:T(128)}, f32[1024,2,64]{0,2,1:T(8,128)S(1)}, ...), condition=%wide.region_24.24_spmd.clone.clone, body=%wide.region_22.23_spmd.clone.clone.sunk | while | flops 689635328 | bytes 41474348 | solution.py:135
  301.2 21.0 %while.83 = (s32[]{:T(128)}, f32[1024,2,64]{0,2,1:T(8,128)S(1)}, f32[1024,2,64]{0,2,1:T(8,128)}, f32[2,512,2,64]{1,3,2,0:T(8,128)S(1)}, s32[2]{0:T(128)S(1)}, /*...) while((s32[]{:T(128)}, f32[1024,2,64]{0,2,1:T(8,128)S(1)}, ...), condition=%wide.region_24.24_spmd.clone.clone, body=%wide.region_22.23_spmd.clone.clone.sunk | while | flops 689635328 | bytes 41474348 | solution.py:135
  328.5 21.0 %while.83 = (s32[]{:T(128)}, f32[1024,2,64]{0,2,1:T(8,128)S(1)}, f32[1024,2,64]{0,2,1:T(8,128)}, f32[2,512,2,64]{1,3,2,0:T(8,128)S(1)}, s32[2]{0:T(128)S(1)}, /*...) while((s32[]{:T(128)}, f32[1024,2,64]{0,2,1:T(8,128)S(1)}, ...), condition=%wide.region_24.24_spmd.clone.clone, body=%wide.region_22.23_spmd.clone.clone.sunk | while | flops 689635328 | bytes 41474348 | solution.py:135
  353.8 3.9 fusion.63
  363.8 3.2 fusion.54
  368.2 2.7 fusion.106
  370.9 2.6 fusion.95
  373.5 3.3 fusion.75
  376.8 3.2 reshape.620
  380.1 3.2 reshape.619
  384.3 2.8 reshape.617
  406.9 4.5 add_convert_fusion.1
  413.9 3.3 add_add_fusion.6
  417.3 3.2 copy.201
  420.4 149.9 %all-reduce.8.cloned.1.call-done = f32[1771776]{0:T(1024)} async-done(((f32[1771776]{0:T(1024)}), f32[1771776]{0:T(1024)}) %all-reduce.8.cloned.1.call-update) | async-done | bytes 7087120
  573.2 39.9 %all-reduce.2 = (f32[10]{0:T(128)S(1)}, f32[10]{0:T(128)S(1)}) all-reduce(f32[10]{0:T(128)S(1)} %get-tuple-element.584, f32[10]{0:T(128)S(1)} %get-tuple-element.583), channel_id=1, replica_groups=mesh['bucket'=4,'dp'=8] {'bucket','dp'}, use_global_device_ids=true, to_apply=%region_42.43 | all-reduce | flops 20 | bytes 160 | tf_op jit(solution)/shard_map/psum | solution.py:329
  (505 shorter events, 180.5 us)
Async XLA Ops:
  7.2 148.4 %all-reduce.6.cloned.1.call-start = ((), (), s32[]{:S(2)}) async-start(), calls=%async_computation | async-start | bytes 7090176
  13.1 45.1 %copy-start.43 = (bf16[1024,384]{1,0:T(8,128)(2,1)S(1)}, bf16[1024,384]{1,0:T(8,128)(2,1)}, u32[]{:S(2)}) copy-start(bf16[1024,384]{1,0:T(8,128)(2,1)} %param.17) | copy-start | bytes 2359300
  13.1 557.3 %all-reduce.8.cloned.1.call-start = ((), (), s32[]{:S(2)}) async-start(), calls=%async_computation.1 | async-start | bytes 14180352
  58.2 102.2 %copy-start = (bf16[1024,384]{0,1:T(8,128)(2,1)}, bf16[1024,384]{0,1:T(8,128)(2,1)S(1)}, u32[]{:S(2)}) copy-start(bf16[1024,384]{0,1:T(8,128)(2,1)S(1)} %copy.185) | copy-start | bytes 2359300
  59.5 99.0 %copy-start.22 = (bf16[3,1024,2,64]{1,3,2,0:T(8,128)(2,1)}, bf16[3,1024,2,64]{1,3,2,0:T(8,128)(2,1)S(1)}, u32[]{:S(2)}) copy-start(bf16[3,1024,2,64]{1,3,2,0:T(8,128)(2,1)S(1)} %fusion.104) | copy-start | bytes 2359300
  63.8 96.6 %copy-start.63 = (f32[1024]{0:T(1024)}, f32[1024]{0:T(1024)S(1)}, u32[]{:S(2)}) copy-start(f32[1024]{0:T(1024)S(1)} %broadcast_multiply_fusion.3) | copy-start | bytes 12292
  64.0 96.4 %copy-start.68 = (f32[1024]{0:T(1024)}, f32[1024]{0:T(1024)S(1)}, u32[]{:S(2)}) copy-start(f32[1024]{0:T(1024)S(1)} %fusion.51) | copy-start | bytes 12292
  64.6 95.8 %copy-start.72 = (f32[1024]{0:T(1024)}, f32[1024]{0:T(1024)S(1)}, u32[]{:S(2)}) copy-start(f32[1024]{0:T(1024)S(1)} %fusion.89) | copy-start | bytes 12292
  157.0 21.8 %copy-start.78 = (f32[3,2,64]{2,1,0:T(2,128)}, f32[3,2,64]{2,1,0:T(2,128)S(1)}, u32[]{:S(2)}) copy-start(f32[3,2,64]{2,1,0:T(2,128)S(1)} %reshape.624) | copy-start | bytes 4612
  157.8 19.3 %copy-start.79 = (f32[3,2,64]{2,1,0:T(2,128)}, f32[3,2,64]{2,1,0:T(2,128)S(1)}, u32[]{:S(2)}) copy-start(f32[3,2,64]{2,1,0:T(2,128)S(1)} %reshape.623) | copy-start | bytes 4612
  164.9 13.9 %copy-start.14 = (f32[1024,1,6,64]{0,3,2,1:T(8,128)}, f32[1024,1,6,64]{0,3,2,1:T(8,128)S(1)}, u32[]{:S(2)}) copy-start(f32[1024,1,6,64]{0,3,2,1:T(8,128)S(1)} %get-tuple-element.690) | copy-start | bytes 4718596
  165.0 13.9 %copy-start.50 = (f32[1024,3,2]{0,2,1:T(2,128)}, f32[1024,3,2]{0,2,1:T(2,128)S(1)}, u32[]{:S(2)}) copy-start(f32[1024,3,2]{0,2,1:T(2,128)S(1)} %div.128) | copy-start | bytes 73732
  165.0 12.1 %copy-start.52 = (f32[1024,3,2]{0,2,1:T(2,128)}, f32[1024,3,2]{0,2,1:T(2,128)S(1)}, u32[]{:S(2)}) copy-start(f32[1024,3,2]{0,2,1:T(2,128)S(1)} %div.125) | copy-start | bytes 73732
  168.0 8.9 %copy-start.44 = (f32[1024,6]{0,1:T(8,128)}, f32[1024,6]{0,1:T(8,128)S(1)}, u32[]{:S(2)}) copy-start(f32[1024,6]{0,1:T(8,128)S(1)} %get-tuple-element.571) | copy-start | bytes 73732
  168.0 9.0 %copy-start.46 = (f32[1024,6]{0,1:T(8,128)}, f32[1024,6]{0,1:T(8,128)S(1)}, u32[]{:S(2)}) copy-start(f32[1024,6]{0,1:T(8,128)S(1)} %get-tuple-element.572) | copy-start | bytes 73732
  179.2 51.4 %copy-start.1 = (bf16[1024,384]{0,1:T(8,128)(2,1)S(1)}, bf16[1024,384]{0,1:T(8,128)(2,1)}, u32[]{:S(2)}) copy-start(bf16[1024,384]{0,1:T(8,128)(2,1)} %copy-done) | copy-start | bytes 2359300
  232.6 33.0 %copy-start.5 = (f32[1024,384]{0,1:T(8,128)}, f32[1024,384]{0,1:T(8,128)S(1)}, u32[]{:S(2)}) copy-start(f32[1024,384]{0,1:T(8,128)S(1)} %get-tuple-element.711) | copy-start | bytes 4718596
  232.8 16.7 %copy-start.25 = (bf16[1024,384]{0,1:T(8,128)(2,1)S(1)}, bf16[1024,384]{0,1:T(8,128)(2,1)}, u32[]{:S(2)}) copy-start(bf16[1024,384]{0,1:T(8,128)(2,1)} %copy.190) | copy-start | bytes 2359300
  232.9 16.7 %copy-start.35 = (bf16[1536,384]{1,0:T(8,128)(2,1)S(1)}, bf16[1536,384]{1,0:T(8,128)(2,1)}, u32[]{:S(2)}) copy-start(bf16[1536,384]{1,0:T(8,128)(2,1)} %slice.113) | copy-start | bytes 3538948
  232.9 16.7 %copy-start.70 = (f32[1024]{0:T(1024)S(1)}, f32[1024]{0:T(1024)}, u32[]{:S(2)}) copy-start(f32[1024]{0:T(1024)} %convert_multiply_fusion.1) | copy-start | bytes 12292
  271.2 82.5 %copy-start.40 = (f32[1024,6]{0,1:T(8,128)S(1)}, f32[1024,6]{0,1:T(8,128)}, u32[]{:S(2)}) copy-start(f32[1024,6]{0,1:T(8,128)} %copy-done.39) | copy-start | bytes 73732
  271.2 82.5 %copy-start.42 = (f32[1024,6]{0,1:T(8,128)S(1)}, f32[1024,6]{0,1:T(8,128)}, u32[]{:S(2)}) copy-start(f32[1024,6]{0,1:T(8,128)} %copy-done.41) | copy-start | bytes 73732
  271.2 82.5 %copy-start.65 = (f32[6,64]{1,0:T(8,128)S(1)}, f32[6,64]{1,0:T(8,128)}, u32[]{:S(2)}) copy-start(f32[6,64]{1,0:T(8,128)} %reshape.626) | copy-start | bytes 4612
  271.2 82.5 %copy-start.66 = (f32[6,64]{1,0:T(8,128)S(1)}, f32[6,64]{1,0:T(8,128)}, u32[]{:S(2)}) copy-start(f32[6,64]{1,0:T(8,128)} %reshape.625) | copy-start | bytes 4612
  396.2 6.8 %copy-start.82 = (f32[384]{0:T(512)S(1)}, f32[384]{0:T(512)}, u32[]{:S(2)}) copy-start(f32[384]{0:T(512)} %get-tuple-element.579) | copy-start | bytes 4612
  396.2 8.1 %copy-start.86 = (f32[384]{0:T(512)S(1)}, f32[384]{0:T(512)}, u32[]{:S(2)}) copy-start(f32[384]{0:T(512)} %get-tuple-element.715) | copy-start | bytes 4612
  406.9 7.0 %copy-start.75 = (f32[1024]{0:T(1024)S(1)}, f32[1024]{0:T(1024)}, u32[]{:S(2)}) copy-start(f32[1024]{0:T(1024)} %copy-done.74) | copy-start | bytes 12292
  417.3 153.1 %copy-start.34 = (f32[55368]{0:T(1024)S(1)}, f32[55368]{0:T(1024)}, u32[]{:S(2)}) copy-start(f32[55368]{0:T(1024)} %param.21) | copy-start | bytes 664420
  417.3 153.1 %copy-start.48 = (f32[55368]{0:T(1024)S(1)}, f32[55368]{0:T(1024)}, u32[]{:S(2)}) copy-start(f32[55368]{0:T(1024)} %param.23) | copy-start | bytes 664420
  417.3 153.1 %copy-start.49 = (f32[55368]{0:T(1024)S(1)}, f32[55368]{0:T(1024)}, u32[]{:S(2)}) copy-start(f32[55368]{0:T(1024)} %param.22) | copy-start | bytes 664420
  571.7 44.2 %copy-start.37 = (f32[55368]{0:T(1024)}, f32[55368]{0:T(1024)S(1)}, u32[]{:S(2)}) copy-start(f32[55368]{0:T(1024)S(1)} %get-tuple-element.674) | copy-start | bytes 664420
  571.8 44.2 %copy-start.38 = (f32[55368]{0:T(1024)}, f32[55368]{0:T(1024)S(1)}, u32[]{:S(2)}) copy-start(f32[55368]{0:T(1024)S(1)} %get-tuple-element.675) | copy-start | bytes 664420
  (76 other events, 200.6 us)
Sparse Core Ops, SparseCore 0:
  13.6 141.8 all-reduce.5
  405.7 164.6 all-reduce.7
where the time goes:
time: 632 us; the launch traced here: 623 us
  waiting for transfers between devices  241 us (38%)
  local copies, waits for them, and re-layouts  100 us (16%)
  matrix products  95.2 us (15%)
  blocking collectives  82.2 us (13%)
  other arithmetic  62.6 us (10%)
  loops' own time  24.6 us (4%)
  between operations  17.5 us (3%)
    unnamed x4, waiting for transfers between devices  241 us
    psum x1, blocking collectives, local(): kept_all = lax.psum(kept_local, ('bucket', 'dp'))  42.3 us
    psum x1, blocking collectives, local(): lax.psum((weight_sq_local, update_sq_local), ('bucket', 'dp'))  39.9 us
    unnamed x188, local copies, waits for them, and re-layouts  32.2 us
    dot_general x1, matrix products, local(): jnp.dot(normed_two_low, up_weight, preferred_element_type=jnp.float32)  16.7 us
    dynamic_update_slice x18, local copies, waits for them, and re-layouts, sequence_forward(): lax.map(per_pair, (to_pairs(queries), to_pairs(key_rows), to_pairs(values)))  13.7 us
  transfers between devices with their start and end apart: 2, of which 2 were waited for; matrix products, arithmetic and copies ran while one was open for 3% of the time, Pallas kernels for 0%

commit v1 on v0

v1 whole, which is shorter than its diff:
```python
import functools
import math

import jax
import jax.numpy as jnp
from jax import lax
from jax.experimental import pallas as pl
from jax.experimental.pallas import tpu as pltpu
from jax.sharding import PartitionSpec as P

D = 384
HEADS = 6
HD = 64
FF = 1536
SEQ = 1024
STEP = 10
MATS = 10
LANES = 128
PAIRS = HEADS // 2
TILE = 256
TILES = SEQ // TILE

norm_epsilon = 1e-06
adam_epsilon = 1e-06
beta_one = 0.9
beta_two = 0.999
learn_rate = 0.5
weight_decay = 0.01
masked_score = -1e30

MATRIX_END = 4 * D * D + 2 * D * FF
BOUNDS = [0, 3 * D * D, 4 * D * D, 4 * D * D + D * FF, MATRIX_END] + [
    MATRIX_END + (j + 1) * D for j in range(6)
]
PARAMS = BOUNDS[-1]
ROW_OUT = BOUNDS[1] // LANES
ROW_UP = BOUNDS[2] // LANES
ROW_DOWN = BOUNDS[3] // LANES
ROW_VEC = BOUNDS[4] // LANES
VEC_ROWS = 6 * D // LANES
ROWS_ALL = PARAMS // LANES

score_scale = HD ** (-0.5) * math.log2(math.e)
grad_scale = HD ** (-0.5)

BF = jnp.bfloat16
F32 = jnp.float32
VMEM = pl.BlockSpec(memory_space=pltpu.VMEM)
SMEM = pl.BlockSpec(memory_space=pltpu.SMEM)
ANY = pl.BlockSpec(memory_space=pl.ANY)


def params(limit=56):
    return pltpu.CompilerParams(vmem_limit_bytes=limit * 1024 * 1024)


def round_up(value, step):
    return -(-value // step) * step


class Plan:
    def __init__(self, mesh_shape, shard):
        self.nb = mesh_shape["bucket"]
        self.nd = mesh_shape["dp"]
        self.n = self.nb * self.nd
        self.shard = shard
        self.start = [k * shard // LANES for k in range(self.n)]
        self.rows = [
            -(-((k + 1) * shard) // LANES) - self.start[k] for k in range(self.n)
        ]
        self.win = round_up(max(self.rows) + 1, 16)
        self.tail = round_up(self.win + VEC_ROWS, 16)
        self.quarter_row = self.nd * shard // LANES

    def device(self):
        return lax.axis_index("bucket") * self.nd + lax.axis_index("dp")


def nn(a, b):
    return lax.dot_general(a, b, (((1,), (0,)), ((), ())), preferred_element_type=F32)


def nt(a, b):
    return lax.dot_general(a, b, (((1,), (1,)), ((), ())), preferred_element_type=F32)


def split_low(x):
    high = x.astype(BF)
    return high, (x - high.astype(F32)).astype(BF)


def rows_at(step):
    return pl.ds(pl.multiple_of(step * TILE, TILE), TILE)


def norm_parts(values):
    average = jnp.mean(values, axis=-1, keepdims=True)
    centered = values - average
    variance = jnp.mean(centered * centered, axis=-1, keepdims=True)
    rstd = lax.rsqrt(variance + norm_epsilon)
    return centered * rstd, rstd


def norm_back(hat, rstd, grad):
    mean_grad = jnp.mean(grad, axis=-1, keepdims=True)
    mean_both = jnp.mean(grad * hat, axis=-1, keepdims=True)
    return rstd * (grad - mean_grad - hat * mean_both)


def head_mean_matrix():
    row = lax.broadcasted_iota(jnp.int32, (D, D), 0)
    col = lax.broadcasted_iota(jnp.int32, (D, D), 1)
    return jnp.where(row // HD == col // HD, 1.0 / HD, 0.0).astype(BF)


def head_mean(x, matrix):
    high, rest = split_low(x)
    return nn(high, matrix) + nn(rest, matrix)


def prepare_kernel(plan, master_ref, keep_ref, out_ref):
    me = plan.device()
    offset = lax.rem(me * plan.shard, LANES)
    values = master_ref[...]
    turned = pltpu.roll(values, offset, 1)
    below = pltpu.roll(turned, 1, 0)
    lane = lax.broadcasted_iota(jnp.int32, values.shape, 1)
    row = lax.broadcasted_iota(jnp.int32, values.shape, 0)
    count = jnp.sum(keep_ref[...].astype(F32), axis=1, keepdims=True)
    high = jnp.floor(count * (1.0 / 32.0))
    parts = jnp.where(lane == 0, high, jnp.where(lane == 1, count - 32.0 * high, 0.0))
    window = jnp.where(lane < offset, below, turned)
    out_ref[...] = jnp.where(row == plan.win - 1, parts, window).astype(BF)


def prepare(plan, master_rows, keep_row):
    return pl.pallas_call(
        functools.partial(prepare_kernel, plan),
        out_shape=jax.ShapeDtypeStruct((plan.win, LANES), BF),
        in_specs=[VMEM, VMEM],
        out_specs=VMEM,
        compiler_params=params(),
    )(master_rows, keep_row)


def assemble_kernel(
    plan, own_ref, other_ref, wq_ref, wo_ref, wu_ref, wd_ref, vec_ref, kept_ref, held, flat, sems
):
    me = plan.device()
    copies = [
        pltpu.make_async_copy(own_ref, held.at[0], sems.at[0]),
        pltpu.make_async_copy(other_ref, held.at[1], sems.at[1]),
    ]
    for copy in copies:
        copy.start()
    for copy in copies:
        copy.wait()
    for k in range(plan.n):
        rel = jnp.bitwise_xor(me, k)
        window = held[jnp.bitwise_and(rel, 1), jnp.right_shift(rel, 1)].astype(F32)
        first, count = plan.start[k], plan.rows[k]
        if k > 0:
            before = flat[first : first + 1, :]
        flat[first : first + count, :] = window[:count]
        if k > 0 and (k * plan.shard) % LANES:
            flat[first : first + 1, :] = before + window[:1]

    def columns(target, base, height, width):
        stride = width // LANES
        for j in range(stride):
            target[:, j * LANES : (j + 1) * LANES] = flat[
                pl.ds(base + j, height, stride=stride), :
            ].astype(BF)

    columns(wq_ref, 0, D, 3 * D)
    columns(wo_ref, ROW_OUT, D, D)
    columns(wu_ref, ROW_UP, D, FF)
    columns(wd_ref, ROW_DOWN, FF, D)
    for t in range(6):
        for j in range(D // LANES):
            vec_ref[t : t + 1, j * LANES : (j + 1) * LANES] = flat[
                ROW_VEC + 3 * t + j : ROW_VEC + 3 * t + j + 1, :
            ]
    total = jnp.zeros((1, LANES), F32)
    for j in range(plan.nd):
        total = total + held[j & 1, j >> 1, plan.win - 16 : plan.win, :].astype(F32)[15:16]
    count = 32.0 * total[:, 0:1] + total[:, 1:2]
    kept_ref[...] = jnp.broadcast_to(count, (8, LANES))


def assemble(plan, own, other):
    return pl.pallas_call(
        functools.partial(assemble_kernel, plan),
        out_shape=(
            jax.ShapeDtypeStruct((D, 3 * D), BF),
            jax.ShapeDtypeStruct((D, D), BF),
            jax.ShapeDtypeStruct((D, FF), BF),
            jax.ShapeDtypeStruct((FF, D), BF),
            jax.ShapeDtypeStruct((8, D), F32),
            jax.ShapeDtypeStruct((8, LANES), F32),
        ),
        in_specs=[ANY, ANY],
        out_specs=(VMEM,) * 6,
        scratch_shapes=[
            pltpu.VMEM((2, plan.n // 2, plan.win, LANES), BF),
            pltpu.VMEM((round_up(ROWS_ALL, 8), LANES), F32),
            pltpu.SemaphoreType.DMA((2,)),
        ],
        compiler_params=params(),
    )(own, other)


def overlap(seg_ref, ti, tj):
    first_i, last_i = seg_ref[ti * TILE], seg_ref[ti * TILE + TILE - 1]
    first_j, last_j = seg_ref[tj * TILE], seg_ref[tj * TILE + TILE - 1]
    return jnp.logical_and(first_j <= last_i, first_i <= last_j)


def tile_bias(ti, tj, row_seg, key_seg):
    key_place = lax.broadcasted_iota(jnp.int32, (TILE, TILE), 0) + tj * TILE
    row_place = lax.broadcasted_iota(jnp.int32, (TILE, TILE), 1) + ti * TILE
    seen = jnp.logical_or(
        key_seg == row_seg, jnp.logical_and(key_place == row_place, key_place >= 0)
    )
    return jnp.where(seen, 0.0, masked_score)


def to_column(row):
    return jnp.transpose(jnp.broadcast_to(row, (LANES, row.shape[1])))


def stack_heads(pair):
    lane = lax.broadcasted_iota(jnp.int32, pair.shape, 1)
    zero = jnp.zeros_like(pair)
    return jnp.concatenate(
        [jnp.where(lane < HD, pair, zero), jnp.where(lane >= HD, pair, zero)], axis=0
    )


def forward_kernel(
    plan,
    tokens_ref,
    wq_ref,
    vec_ref,
    seg_smem,
    seg_ref,
    keep_ref,
    q_ref,
    k_ref,
    v_ref,
    raw_ref,
    o_ref,
    ot_ref,
    lse_ref,
    kab,
    vt,
    ot,
    sums,
    segk,
    expo,
):
    matrix = head_mean_matrix()
    gain1, shift1 = vec_ref[0:1, :], vec_ref[1:2, :]
    gain_q, gain_k = vec_ref[2:3, :], vec_ref[3:4, :]
    seg_row = seg_ref[...].astype(F32)
    segk[...] = to_column(jnp.where(keep_ref[...] == 1, seg_row, -1.0))

    def project(step, carry):
        at = rows_at(step)
        hat, _ = norm_parts(tokens_ref[at, :].astype(F32))
        low = (hat * gain1 + shift1).astype(BF)
        raw = nn(low, wq_ref[...])
        raw_ref[at, :] = raw[:, : 2 * D]

        def head_norm(x, gain):
            centered = x - head_mean(x, matrix)
            rstd = lax.rsqrt(head_mean(centered * centered, matrix) + norm_epsilon)
            return (centered * rstd * gain).astype(BF)

        queries = head_norm(raw[:, :D], gain_q)
        keys = head_norm(raw[:, D : 2 * D], gain_k)
        values = raw[:, 2 * D :].astype(BF)
        q_ref[at, :] = queries
        k_ref[at, :] = keys
        v_ref[at, :] = values
        for hp in range(PAIRS):
            kab[hp, step] = stack_heads(keys[:, hp * LANES : (hp + 1) * LANES])
        vt[step] = jnp.transpose(values.astype(F32)).astype(BF)
        return carry

    lax.fori_loop(0, TILES, project, 0)

    def query_tile(ti, carry):
        ot[...] = jnp.zeros_like(ot)
        sums[...] = jnp.zeros_like(sums)
        row_seg = seg_ref[:, pl.ds(pl.multiple_of(ti * TILE, TILE), TILE)].astype(F32)

        def score_tile(tj, inner):
            @pl.when(overlap(seg_smem, ti, tj))
            def _():
                column = segk[rows_at(tj), :]
                bias = tile_bias(ti, tj, row_seg, jnp.concatenate([column, column], axis=1))
                for hp in range(PAIRS):
                    queries = q_ref[rows_at(ti), hp * LANES : (hp + 1) * LANES]
                    scores = nt(kab[hp, tj], queries)
                    for side in range(2):
                        head = 2 * hp + side
                        value = jnp.exp2(
                            scores[side * TILE : (side + 1) * TILE] * score_scale + bias
                        )
                        expo[tj, head] = value
                        sums[head : head + 1, :] += jnp.sum(value, axis=0, keepdims=True)

            return inner

        lax.fori_loop(0, TILES, score_tile, 0)
        lse_ref[ti] = jnp.log2(sums[...])
        sums[...] = 1.0 / sums[...]

        def value_tile(tj, inner):
            @pl.when(overlap(seg_smem, ti, tj))
            def _():
                for head in range(HEADS):
                    prob = (expo[tj, head] * sums[head : head + 1, :]).astype(BF)
                    ot[head * HD : (head + 1) * HD, :] += nn(
                        vt[tj, head * HD : (head + 1) * HD, :], prob
                    )

            return inner

        lax.fori_loop(0, TILES, value_tile, 0)
        attended = ot[...]
        ot_ref[ti] = attended.astype(BF)
        o_ref[rows_at(ti), :] = jnp.transpose(attended).astype(BF)
        return carry

    lax.fori_loop(0, TILES, query_tile, 0)


def forward(plan, tokens, wq, vec, seg, seg_row, keep_row):
    rows = tokens.shape[0]
    return pl.pallas_call(
        functools.partial(forward_kernel, plan),
        out_shape=(
            jax.ShapeDtypeStruct((rows, D), BF),
            jax.ShapeDtypeStruct((rows, D), BF),
            jax.ShapeDtypeStruct((rows, D), BF),
            jax.ShapeDtypeStruct((rows, 2 * D), F32),
            jax.ShapeDtypeStruct((rows, D), BF),
            jax.ShapeDtypeStruct((TILES, D, TILE), BF),
            jax.ShapeDtypeStruct((TILES, 8, TILE), F32),
        ),
        in_specs=[VMEM, VMEM, VMEM, SMEM, VMEM, VMEM],
        out_specs=(VMEM,) * 7,
        scratch_shapes=[
            pltpu.VMEM((PAIRS, TILES, 2 * TILE, LANES), BF),
            pltpu.VMEM((TILES, D, TILE), BF),
            pltpu.VMEM((D, TILE), F32),
            pltpu.VMEM((8, TILE), F32),
            pltpu.VMEM((SEQ, LANES), F32),
            pltpu.VMEM((TILES, HEADS, TILE, TILE), F32),
        ],
        compiler_params=params(),
    )(tokens, wq, vec, seg, seg_row, keep_row)


def middle_kernel(
    plan,
    tokens_ref,
    cot_ref,
    o_ref,
    ot_ref,
    wo_ref,
    wu_ref,
    wd_ref,
    vec_ref,
    keep_ref,
    kept_ref,
    patches_ref,
    out_ref,
    dh1_ref,
    do_ref,
    near_ref,
    far_ref,
    tail_ref,
    gvec_ref,
    keepc,
    gout,
    gup,
    gdownt,
    flat,
):
    me = plan.device()
    bucket = lax.axis_index("bucket")
    gain2, shift2 = vec_ref[4:5, :], vec_ref[5:6, :]
    own = patches_ref[bucket].astype(F32)
    total = patches_ref[0].astype(F32)
    for b in range(1, plan.nb):
        total = total + patches_ref[b].astype(F32)
    ones = jnp.ones((1, LANES), F32)
    scale = (plan.nb * own) * ones / (total * ones) * float(SEQ * plan.nd) / kept_ref[0:1, :]
    keepc[...] = to_column(keep_ref[...].astype(F32)) * scale
    gout[...] = jnp.zeros_like(gout)
    gup[...] = jnp.zeros_like(gup)
    gdownt[...] = jnp.zeros_like(gdownt)
    gvec_ref[...] = jnp.zeros_like(gvec_ref)

    def chunk(step, carry):
        at = rows_at(step)
        middle = tokens_ref[at, :].astype(F32) + nn(o_ref[at, :], wo_ref[...])
        hat, rstd = norm_parts(middle)
        low = (hat * gain2 + shift2).astype(BF)
        u = nn(low, wu_ref[...])
        phi = 0.5 + 0.5 * lax.erf(u * math.sqrt(0.5))
        hidden = (u * phi).astype(BF)
        out_ref[at, :] = (middle + nn(hidden, wd_ref[...])).astype(BF)
        weights = keepc[at, :]
        seed = cot_ref[at, :].astype(F32) * jnp.concatenate([weights] * (D // LANES), axis=1)
        seed_low = seed.astype(BF)
        slope = phi + u * (jnp.exp(-0.5 * u * u) * (1.0 / math.sqrt(2.0 * math.pi)))
        du = (nt(seed_low, wd_ref[...]) * slope).astype(BF)
        gdownt[...] += nn(jnp.transpose(seed).astype(BF), hidden)
        gup[...] += nn(jnp.transpose(low.astype(F32)).astype(BF), du)
        da2 = nt(du, wu_ref[...])
        gvec_ref[0:1, :] += jnp.sum(da2 * hat, axis=0, keepdims=True)
        gvec_ref[1:2, :] += jnp.sum(da2, axis=0, keepdims=True)
        dh1 = seed + norm_back(hat, rstd, da2 * gain2)
        dh1_ref[at, :] = dh1
        dh1_low = dh1.astype(BF)
        gout[...] += nn(ot_ref[step], dh1_low)
        do_ref[at, :] = nt(dh1_low, wo_ref[...]).astype(BF)
        return carry

    lax.fori_loop(0, o_ref.shape[0] // TILE, chunk, 0)

    base = ROW_OUT
    for j in range(D // LANES):
        flat[pl.ds(j, D, stride=D // LANES), :] = gout[:, j * LANES : (j + 1) * LANES]
    for j in range(FF // LANES):
        flat[pl.ds(ROW_UP - base + j, D, stride=FF // LANES), :] = gup[
            :, j * LANES : (j + 1) * LANES
        ]
    for j in range(D // LANES):
        flat[pl.ds(ROW_DOWN - base + j, FF, stride=D // LANES), :] = jnp.transpose(
            gdownt[j * LANES : (j + 1) * LANES, :]
        )
    tail_ref[...] = flat[0:8, :]
    side = jnp.bitwise_and(me, 1)
    dp = lax.axis_index("dp")
    for k in range(plan.nd, plan.n):
        first = plan.start[k] - base
        relb = jnp.bitwise_xor(bucket, k // plan.nd)
        reld = jnp.right_shift(jnp.bitwise_xor(dp, k % plan.nd), 1)
        window = flat[first : first + plan.win, :].astype(BF)

        @pl.when(side == k % 2)
        def _():
            near_ref[relb, reld] = window

        @pl.when(side != k % 2)
        def _():
            far_ref[relb, reld] = window


def middle_part(plan, tokens, cot, o, ot, wo, wu, wd, vec, keep_row, kept, patches):
    rows = tokens.shape[0]
    windows = jax.ShapeDtypeStruct((plan.nb, plan.nd // 2, plan.win, LANES), BF)
    return pl.pallas_call(
        functools.partial(middle_kernel, plan),
        out_shape=(
            jax.ShapeDtypeStruct((rows, D), BF),
            jax.ShapeDtypeStruct((rows, D), F32),
            jax.ShapeDtypeStruct((rows, D), BF),
            windows,
            windows,
            jax.ShapeDtypeStruct((8, LANES), F32),
            jax.ShapeDtypeStruct((8, D), F32),
        ),
        in_specs=[VMEM] * 10 + [SMEM],
        out_specs=(VMEM,) * 7,
        scratch_shapes=[
            pltpu.VMEM((rows, LANES), F32),
            pltpu.VMEM((D, D), F32),
            pltpu.VMEM((D, FF), F32),
            pltpu.VMEM((D, FF), F32),
            pltpu.VMEM((round_up(plan.start[-1] + plan.win - ROW_OUT, 8), LANES), F32),
        ],
        compiler_params=params(),
    )(tokens, cot, o, ot, wo, wu, wd, vec, keep_row, kept, patches)


def backward_kernel(
    plan,
    tokens_ref,
    wq_ref,
    vec_ref,
    seg_smem,
    seg_ref,
    keep_ref,
    q_ref,
    k_ref,
    v_ref,
    raw_ref,
    o_ref,
    lse_ref,
    do_ref,
    dh1_ref,
    tail_ref,
    gvec_ref,
    grad_ref,
    near_ref,
    far_ref,
    kab,
    vab,
    qab,
    dab,
    kt,
    dqt,
    dk,
    dv,
    inner_sums,
    segk,
    gq,
    gains,
    flat,
):
    matrix = head_mean_matrix()
    gain1, shift1 = vec_ref[0:1, :], vec_ref[1:2, :]
    gain_q, gain_k = vec_ref[2:3, :], vec_ref[3:4, :]
    seg_row = seg_ref[...].astype(F32)
    segk[...] = to_column(jnp.where(keep_ref[...] == 1, seg_row, -1.0))
    head_row = lax.broadcasted_iota(jnp.int32, (8, D), 0)
    head_lane = lax.broadcasted_iota(jnp.int32, (8, D), 1)
    hot = jnp.where(head_lane // HD == head_row, 1.0, 0.0).astype(BF)
    dqt[...] = jnp.zeros_like(dqt)
    dk[...] = jnp.zeros_like(dk)
    dv[...] = jnp.zeros_like(dv)
    gq[...] = jnp.zeros_like(gq)
    gains[...] = jnp.zeros_like(gains)

    def stack(step, carry):
        at = rows_at(step)
        keys = k_ref[at, :]
        grads = do_ref[at, :]
        for hp in range(PAIRS):
            lanes = slice(hp * LANES, (hp + 1) * LANES)
            kab[hp, step] = stack_heads(keys[:, lanes])
            vab[hp, step] = stack_heads(v_ref[at, lanes])
            qab[hp, step] = stack_heads(q_ref[at, lanes])
            dab[hp, step] = stack_heads(grads[:, lanes])
        kt[step] = jnp.transpose(keys.astype(F32)).astype(BF)
        high, rest = split_low(grads.astype(F32) * o_ref[at, :].astype(F32))
        inner_sums[step] = nt(hot, high) + nt(hot, rest)
        return carry

    lax.fori_loop(0, TILES, stack, 0)

    def query_tile(ti, carry):
        row_seg = seg_ref[:, pl.ds(pl.multiple_of(ti * TILE, TILE), TILE)].astype(F32)

        def key_tile(tj, inner):
            @pl.when(overlap(seg_smem, ti, tj))
            def _():
                column = segk[rows_at(tj), :]
                bias = tile_bias(ti, tj, row_seg, jnp.concatenate([column, column], axis=1))
                for hp in range(PAIRS):
                    lanes = slice(hp * LANES, (hp + 1) * LANES)
                    scores = nt(kab[hp, tj], q_ref[rows_at(ti), lanes])
                    grads = nt(vab[hp, tj], do_ref[rows_at(ti), lanes])
                    probs, dscores = [], []
                    for side in range(2):
                        head = 2 * hp + side
                        part = slice(side * TILE, (side + 1) * TILE)
                        prob = jnp.exp2(
                            scores[part] * score_scale + (bias - lse_ref[ti, head : head + 1, :])
                        )
                        dscore = prob * (grads[part] - inner_sums[ti, head : head + 1, :])
                        dscore = dscore.astype(BF)
                        probs.append(prob.astype(BF))
                        dscores.append(dscore)
                        dqt[ti, head * HD : (head + 1) * HD, :] += nn(
                            kt[tj, head * HD : (head + 1) * HD, :], dscore
                        )
                    dv[hp, tj] += nn(jnp.concatenate(probs, axis=1), dab[hp, ti])
                    dk[hp, tj] += nn(jnp.concatenate(dscores, axis=1), qab[hp, ti])

            return inner

        lax.fori_loop(0, TILES, key_tile, 0)
        return carry

    lax.fori_loop(0, TILES, query_tile, 0)

    def finish(step, carry):
        at = rows_at(step)

        def head_norm_back(raw, gain, grad, place):
            centered = raw - head_mean(raw, matrix)
            rstd = lax.rsqrt(head_mean(centered * centered, matrix) + norm_epsilon)
            hat = centered * rstd
            gains[place : place + 1, :] += jnp.sum(grad * hat, axis=0, keepdims=True)
            scaled = grad * gain
            return rstd * (
                scaled - head_mean(scaled, matrix) - hat * head_mean(scaled * hat, matrix)
            )

        grad_q = jnp.transpose(dqt[step]) * grad_scale
        grad_k = jnp.concatenate([dk[hp, step] for hp in range(PAIRS)], axis=1) * grad_scale
        grad_v = jnp.concatenate([dv[hp, step] for hp in range(PAIRS)], axis=1)
        low_q = head_norm_back(raw_ref[at, :D], gain_q, grad_q, 2).astype(BF)
        low_k = head_norm_back(raw_ref[at, D:], gain_k, grad_k, 3).astype(BF)
        low = jnp.concatenate([low_q, low_k, grad_v.astype(BF)], axis=1)
        hat, rstd = norm_parts(tokens_ref[at, :].astype(F32))
        normed = hat * gain1 + shift1
        gq[...] += nn(jnp.transpose(normed).astype(BF), low)
        da1 = nt(low, wq_ref[...])
        gains[0:1, :] += jnp.sum(da1 * hat, axis=0, keepdims=True)
        gains[1:2, :] += jnp.sum(da1, axis=0, keepdims=True)
        grad_ref[at, :] = dh1_ref[at, :] + norm_back(hat, rstd, da1 * gain1)
        return carry

    lax.fori_loop(0, TILES, finish, 0)
    gains[4:6, :] = gvec_ref[0:2, :]

    for j in range(3 * D // LANES):
        flat[pl.ds(j, D, stride=3 * D // LANES), :] = gq[:, j * LANES : (j + 1) * LANES]
    flat[ROW_OUT : ROW_OUT + 8, :] = tail_ref[...]
    side = jnp.bitwise_and(lax.axis_index("dp"), 1)
    dp = lax.axis_index("dp")
    rest = jnp.zeros((plan.tail - plan.win, LANES), BF)
    vector_rows = []
    for t in range(6):
        for j in range(D // LANES):
            vector_rows.append(gains[t : t + 1, j * LANES : (j + 1) * LANES])
    vector_rows.append(jnp.zeros((plan.tail - plan.win - VEC_ROWS, LANES), F32))
    vectors = jnp.concatenate(vector_rows, axis=0).astype(BF)
    for k in range(plan.nd):
        first = plan.start[k]
        reld = jnp.right_shift(jnp.bitwise_xor(dp, k), 1)
        window = flat[first : first + plan.win, :].astype(BF)
        extra = vectors if k == plan.nd - 1 else rest

        @pl.when(side == k % 2)
        def _():
            near_ref[reld, : plan.win] = window
            near_ref[reld, plan.win :] = extra

        @pl.when(side != k % 2)
        def _():
            far_ref[reld, : plan.win] = window
            far_ref[reld, plan.win :] = extra


def backward(plan, tokens, wq, vec, seg, seg_row, keep_row, q, k, v, raw, o, lse, do, dh1, tail, gvec):
    rows = tokens.shape[0]
    windows = jax.ShapeDtypeStruct((plan.nd // 2, plan.tail, LANES), BF)
    stacked = pltpu.VMEM((PAIRS, TILES, 2 * TILE, LANES), BF)
    return pl.pallas_call(
        functools.partial(backward_kernel, plan),
        out_shape=(jax.ShapeDtypeStruct((rows, D), F32), windows, windows),
        in_specs=[VMEM, VMEM, VMEM, SMEM] + [VMEM] * 12,
        out_specs=(VMEM,) * 3,
        scratch_shapes=[
            stacked,
            stacked,
            stacked,
            stacked,
            pltpu.VMEM((TILES, D, TILE), BF),
            pltpu.VMEM((TILES, D, TILE), F32),
            pltpu.VMEM((PAIRS, TILES, TILE, LANES), F32),
            pltpu.VMEM((PAIRS, TILES, TILE, LANES), F32),
            pltpu.VMEM((TILES, 8, TILE), F32),
            pltpu.VMEM((SEQ, LANES), F32),
            pltpu.VMEM((D, 3 * D), F32),
            pltpu.VMEM((8, D), F32),
            pltpu.VMEM((round_up(plan.start[plan.nd - 1] + plan.win, 8), LANES), F32),
        ],
        compiler_params=params(),
    )(tokens, wq, vec, seg, seg_row, keep_row, q, k, v, raw, o, lse, do, dh1, tail, gvec)


def flat_place(plan, shape):
    row = lax.broadcasted_iota(jnp.int32, shape, 0)
    lane = lax.broadcasted_iota(jnp.int32, shape, 1)
    place = row * LANES + lane
    return place, plan.device() * plan.shard + place


def update_kernel(
    plan,
    rest_ref,
    first_ref,
    master_ref,
    moment_ref,
    second_ref,
    new_moment_ref,
    new_second_ref,
    update_ref,
    sums_ref,
    window,
):
    bucket = lax.axis_index("bucket")
    dp = lax.axis_index("dp")
    window[...] = jnp.where(bucket == 0, first_ref[: plan.win, :], rest_ref[...])
    place_vec = ROW_VEC - plan.start[-1]

    @pl.when(jnp.logical_and(bucket == plan.nb - 1, dp == plan.nd - 1))
    def _():
        window[place_vec : place_vec + VEC_ROWS, :] = first_ref[plan.win : plan.win + VEC_ROWS, :]

    offset = lax.rem(plan.device() * plan.shard, LANES)
    back = lax.rem(LANES - offset, LANES)
    turned = pltpu.roll(window[...], back, 1)
    above = pltpu.roll(turned, plan.win - 1, 0)
    lane = lax.broadcasted_iota(jnp.int32, turned.shape, 1)
    place, index = flat_place(plan, turned.shape)
    inside = place < plan.shard
    grad = jnp.where(inside, jnp.where(lane + offset < LANES, turned, above), 0.0)
    master = master_ref[...]
    moment = beta_one * moment_ref[...] + (1.0 - beta_one) * grad
    second = beta_two * second_ref[...] + (1.0 - beta_two) * grad * grad
    first_hat = moment / (1.0 - beta_one**STEP)
    second_hat = second / (1.0 - beta_two**STEP)
    decay = jnp.where(index < BOUNDS[4], weight_decay, 0.0)
    update = first_hat / (jnp.sqrt(second_hat) + adam_epsilon) + decay * master
    update = jnp.where(inside, update, 0.0)
    new_moment_ref[...] = moment
    new_second_ref[...] = second
    update_ref[...] = update
    master_sq = jnp.where(inside, master * master, 0.0)
    update_sq = update * update
    lanes = lax.broadcasted_iota(jnp.int32, (1, LANES), 1)
    rows = []
    for squares in (master_sq, update_sq):
        row = jnp.zeros((1, LANES), F32)
        for t in range(MATS):
            mine = jnp.logical_and(index >= BOUNDS[t], index < BOUNDS[t + 1])
            part = jnp.sum(jnp.where(mine, squares, 0.0), axis=0, keepdims=True)
            row = jnp.where(lanes == t, jnp.sum(part, axis=1, keepdims=True), row)
        rows.append(row)
    rows.append(jnp.zeros((6, LANES), F32))
    sums_ref[...] = jnp.concatenate(rows, axis=0)


def update_part(plan, rest, first, master_rows, moment_rows, second_rows):
    rows = jax.ShapeDtypeStruct((plan.win, LANES), F32)
    return pl.pallas_call(
        functools.partial(update_kernel, plan),
        out_shape=(rows, rows, rows, jax.ShapeDtypeStruct((8, LANES), F32)),
        in_specs=[VMEM] * 5,
        out_specs=(VMEM,) * 4,
        scratch_shapes=[pltpu.VMEM((plan.win, LANES), F32)],
        compiler_params=params(),
    )(rest, first, master_rows, moment_rows, second_rows)


def apply_kernel(plan, sums_ref, master_ref, update_ref, new_ref, norms_ref):
    roots = jnp.sqrt(sums_ref[...])
    trust = roots[0:1, :] / (roots[1:2, :] + adam_epsilon)
    norms_ref[...] = jnp.concatenate([roots[0:2, :], trust, roots[0:5, :]], axis=0)
    master = master_ref[...]
    _, index = flat_place(plan, master.shape)
    factor = jnp.broadcast_to(trust[:, 0:1], (1, LANES))
    factors = jnp.broadcast_to(factor, master.shape)
    for t in range(1, MATS):
        factor = jnp.broadcast_to(trust[:, t : t + 1], (1, LANES))
        factors = jnp.where(index >= BOUNDS[t], factor, factors)
    new_ref[...] = master - learn_rate * factors * update_ref[...]


def apply_part(plan, sums, master_rows, update_rows):
    return pl.pallas_call(
        functools.partial(apply_kernel, plan),
        out_shape=(
            jax.ShapeDtypeStruct((plan.win, LANES), F32),
            jax.ShapeDtypeStruct((8, LANES), F32),
        ),
        in_specs=[VMEM] * 3,
        out_specs=(VMEM,) * 2,
        compiler_params=params(),
    )(sums, master_rows, update_rows)


def groups_of(size, skip=0):
    bits = list(range(skip, size.bit_length() - 1))
    return [bits[i : i + 2] for i in range(0, len(bits), 2)]


def masks_of(bits):
    masks = [1 << bits[0]]
    if len(bits) == 2:
        masks += [1 << bits[1], (1 << bits[0]) | (1 << bits[1])]
    return masks


def swap(x, axis, size, mask, targets=None):
    pairs = [(i, i ^ mask) for i in range(size)]
    if targets is not None:
        pairs = [pair for pair in pairs if pair[1] in targets]
    return lax.ppermute(x, axis, pairs)


def tree_sum(parts):
    if len(parts) == 4:
        return (parts[0] + parts[1]) + (parts[2] + parts[3])
    return parts[0] + parts[1]


def gather_windows(plan, window):
    held = window[None]
    for bits in groups_of(plan.nd, 1):
        held = jnp.concatenate(
            [held] + [swap(held, "dp", plan.nd, mask) for mask in masks_of(bits)], axis=0
        )
    for bits in groups_of(plan.nb):
        held = jnp.concatenate(
            [held] + [swap(held, "bucket", plan.nb, mask) for mask in masks_of(bits)], axis=0
        )
    return held, swap(held, "dp", plan.nd, 1)


def scatter_dp(plan, held):
    for bits in reversed(groups_of(plan.nd, 1)):
        size = 1 << len(bits)
        step = held.shape[0] // size
        parts = [held[i * step : (i + 1) * step] for i in range(size)]
        got = [parts[0].astype(F32)]
        for i, mask in zip(range(1, size), masks_of(bits)):
            got.append(swap(parts[i].astype(BF), "dp", plan.nd, mask).astype(F32))
        held = tree_sum(got)
    return held[0]


def scatter_rest(plan, near, far):
    got = swap(far, "dp", plan.nd, 1)
    held = [near[i].astype(F32) + got[i].astype(F32) for i in range(plan.nb)]
    targets = set(range(1, plan.nb))
    (bits,) = groups_of(plan.nb)
    parts = [held[0]]
    for i, mask in zip(range(1, plan.nb), masks_of(bits)):
        parts.append(
            swap(held[i].astype(BF), "bucket", plan.nb, mask, targets).astype(F32)
        )
    return scatter_dp(plan, tree_sum(parts))


def scatter_first(plan, near, far):
    got = swap(far, "dp", plan.nd, 1)
    own = scatter_dp(plan, near.astype(F32) + got.astype(F32))
    (bits,) = groups_of(plan.nb)
    low = own.astype(BF)
    parts = [own] + [
        swap(low, "bucket", plan.nb, mask).astype(F32) for mask in masks_of(bits)
    ]
    return tree_sum(parts)


def sum_all(plan, x):
    x = x + swap(x, "dp", plan.nd, 1)
    for axis, size, skip in (("dp", plan.nd, 1), ("bucket", plan.nb, 0)):
        for bits in groups_of(size, skip):
            x = tree_sum([x] + [swap(x, axis, size, mask) for mask in masks_of(bits)])
    return x


def local(
    plan, tokens, cotangent, segment_ids, keep_mask, bucket_patches, master, first_moment, second_moment
):
    def as_rows(flat):
        return jnp.pad(flat, (0, plan.win * LANES - plan.shard)).reshape(plan.win, LANES)

    def as_flat(rows):
        return rows.reshape(-1)[: plan.shard]

    master_rows = as_rows(master)
    seg_row = segment_ids.reshape(1, SEQ)
    keep_row = keep_mask.reshape(1, SEQ)
    own, other = gather_windows(plan, prepare(plan, master_rows, keep_row))
    wq, wo, wu, wd, vec, kept = assemble(plan, own, other)
    q, k, v, raw, o, ot, lse = forward(plan, tokens, wq, vec, segment_ids, seg_row, keep_row)
    block_output, dh1, do, near, far, tail, gvec = middle_part(
        plan, tokens, cotangent, o, ot, wo, wu, wd, vec, keep_row, kept, bucket_patches
    )
    rest = scatter_rest(plan, near, far)
    input_grad, near_first, far_first = backward(
        plan, tokens, wq, vec, segment_ids, seg_row, keep_row, q, k, v, raw, o, lse, do, dh1, tail, gvec
    )
    first = scatter_first(plan, near_first, far_first)
    moment_rows, second_rows, update_rows, sums = update_part(
        plan, rest, first, master_rows, as_rows(first_moment), as_rows(second_moment)
    )
    new_master, norms = apply_part(plan, sum_all(plan, sums), master_rows, update_rows)
    return (
        block_output,
        input_grad,
        as_flat(moment_rows),
        as_flat(second_rows),
        as_flat(new_master),
        norms[0:2, :MATS],
        norms[2, :MATS],
    )


def solution(mesh):
    shards = mesh.shape["bucket"] * mesh.shape["dp"]
    plan = Plan(mesh.shape, PARAMS // shards)
    both = ("bucket", "dp")
    return jax.shard_map(
        functools.partial(local, plan),
        mesh=mesh,
        in_specs=(P(both, None), P(both, None), P(both), P(both), P(), P(both), P(both), P(both)),
        out_specs=(P(both, None), P(both, None), P(both), P(both), P(both), P(), P()),
        check_vma=False,
    )
```

time: 632 us -> 200 us (0.32)
  waiting for transfers between devices: 241 us -> 56 us
  matrix products: 95.2 us -> 0 us
  local copies, waits for them, and re-layouts: 100 us -> 12.2 us
  Pallas kernels: 0 us -> 82.6 us
  blocking collectives: 82.2 us -> 0 us
  other arithmetic: 62.6 us -> 5.68 us
  starting transfers between devices: 0.08 us -> 39.7 us
  loops' own time: 24.6 us -> 0 us
  between operations: 17.5 us -> 0.81 us
    unnamed x4 -> x0, waiting for transfers between devices: 241 us -> none
    dot_general x54 -> x0, matrix products: 95.2 us -> none  [the longest x1 16.7 us: local(): jnp.dot(normed_two_low, up_weight, preferred_element_type=jnp.float32)]
    pallas_call x0 -> x7, Pallas kernels: none -> 82.6 us  [the longest x1 31.5 us: backward(): pl.pallas_call(functools.partial(backward_kernel, plan), out_shape=(jax.S...]
    psum x2 -> x0, blocking collectives: 82.2 us -> none  [the longest x1 42.3 us: local(): kept_all = lax.psum(kept_local, ('bucket', 'dp'))]
    ppermute x0 -> x28, waiting for transfers between devices: none -> 56 us  [swap(): return lax.ppermute(x, axis, pairs)]
    ppermute x0 -> x28, starting transfers between devices: none -> 39.7 us  [swap(): return lax.ppermute(x, axis, pairs)]
    unnamed x188 -> x16, local copies, waits for them, and re-layouts: 32.2 us -> 2.33 us
    reduce_sum x23 -> x0, other arithmetic: 29 us -> none  [the longest x6 6.97 us: one_block(): totals = jnp.sum(expo_rows, axis=-1, keepdims=True)]
  transfers between devices with their start and end apart: 2 -> 28, of which waited for: 2 -> 13; matrix products, arithmetic and copies ran while one was open for 3% -> 4% of each run, Pallas kernels for 0% -> 16%
where the time goes in v1:
time: 200 us; the launch traced here: 197 us
  Pallas kernels  82.6 us (41%)
  waiting for transfers between devices  56 us (28%)
  starting transfers between devices  39.7 us (20%)
  local copies, waits for them, and re-layouts  12.2 us (6%)
  other arithmetic  5.68 us (3%)
    ppermute x28, waiting for transfers between devices, swap(): return lax.ppermute(x, axis, pairs)  56 us
    ppermute x28, starting transfers between devices, swap(): return lax.ppermute(x, axis, pairs)  39.7 us
    pallas_call x1, Pallas kernels, backward(): pl.pallas_call(functools.partial(backward_kernel, plan), out_shape=(jax.S...  31.5 us
    pallas_call x1, Pallas kernels, middle_part(): pl.pallas_call(functools.partial(middle_kernel, plan), out_shape=(jax.Sha...  21.3 us
    pallas_call x1, Pallas kernels, forward(): pl.pallas_call(functools.partial(forward_kernel, plan), out_shape=(jax.Sh...  18.3 us
    slice x3, local copies, waits for them, and re-layouts, as_flat(): return rows.reshape(-1)[:plan.shard]  4.91 us
    pallas_call x1, Pallas kernels, assemble(): pl.pallas_call(functools.partial(assemble_kernel, plan), out_shape=(jax.S...  4.77 us
  transfers between devices with their start and end apart: 28, of which 13 were waited for; matrix products, arithmetic and copies ran while one was open for 4% of the time, Pallas kernels for 16%

profile of v1, /device:TPU:0, one launch (start us, length us, event | category | flops | bytes accessed | tf_op | source)
XLA Modules:
  0.0 197.1 jit_solution(14435747464362244412)
XLA Ops:
  0.6 1.7 pad_bitcast_fusion.2.master_ref
  2.3 1.7 shard_map.135
  4.0 3.0 %collective-permute-start = (bf16[1,448,128]{2,1,0:T(8,128)(2,1)}, bf16[1,448,128]{2,1,0:T(8,128)(2,1)S(1)}, u32[]{:S(2)}, u32[]{:S(2)}) collective-permute-start(bf16[1,448,128]{2,1,0:T(8,128)(2,1)} %bitcast.34), channel_id=1, source_target_pairs={{0,2},{1,3},{2,0},{3,1},{4,6},{5,7},{6,4},{7,5},{8,10},{9,11},{10,... | collective-permute-start | bytes 344072 | tf_op jit(solution)/shard_map/ppermute | solution.py:800
  7.0 2.6 %collective-permute-start.1 = (bf16[1,448,128]{2,1,0:T(8,128)(2,1)}, bf16[1,448,128]{2,1,0:T(8,128)(2,1)S(1)}, u32[]{:S(2)}, u32[]{:S(2)}) collective-permute-start(bf16[1,448,128]{2,1,0:T(8,128)(2,1)} %bitcast.35), channel_id=1, source_target_pairs={{0,4},{1,5},{2,6},{3,7},{4,0},{5,1},{6,2},{7,3},{8,12},{9,13},{10,... | collective-permute-start | bytes 344072 | tf_op jit(solution)/shard_map/ppermute | solution.py:800
  10.4 8.5 %collective-permute-done.1 = bf16[1,448,128]{2,1,0:T(8,128)(2,1)S(1)} collective-permute-done((bf16[1,448,128]{2,1,0:T(8,128)(2,1)}, bf16[1,448,128]{2,1,0:T(8,128)(2,1)S(1)}, u32[]{:S(2)}, u32[]{:S(2)}) %collective-permute-start.1) | collective-permute-done | bytes 114720 | tf_op jit(solution)/shard_map/ppermute | solution.py:800
  19.9 1.6 collective-permute-start.3
  22.4 1.5 collective-permute-start.4
  24.4 9.0 %collective-permute-done.3 = bf16[4,448,128]{2,1,0:T(8,128)(2,1)S(1)} collective-permute-done((bf16[4,448,128]{2,1,0:T(8,128)(2,1)S(1)}, bf16[4,448,128]{2,1,0:T(8,128)(2,1)S(1)}, u32[]{:S(2)}, u32[]{:S(2)}) %collective-permute-start.3) | collective-permute-done | bytes 458784 | tf_op jit(solution)/shard_map/ppermute | solution.py:800
  33.5 8.4 %collective-permute-done.4 = bf16[4,448,128]{2,1,0:T(8,128)(2,1)S(1)} collective-permute-done((bf16[4,448,128]{2,1,0:T(8,128)(2,1)S(1)}, bf16[4,448,128]{2,1,0:T(8,128)(2,1)S(1)}, u32[]{:S(2)}, u32[]{:S(2)}) %collective-permute-start.4) | collective-permute-done | bytes 458784 | tf_op jit(solution)/shard_map/ppermute | solution.py:800
  42.1 3.8 %collective-permute-done.6.other_ref = bf16[16,448,128]{2,1,0:T(8,128)(2,1)S(1)} collective-permute-done((bf16[16,448,128]{2,1,0:T(8,128)(2,1)S(1)}, bf16[16,448,128]{2,1,0:T(8,128)(2,1)S(1)}, u32[]{:S(2)}, u32[]{:S(2)}) %collective-permute-start.6) | collective-permute-done | bytes 1835040 | tf_op jit(solution)/shard_map/ppermute | solution.py:800
  47.1 4.8 %shard_map.136 = (bf16[384,1152]{1,0:T(8,128)(2,1)}, bf16[384,384]{1,0:T(8,128)(2,1)}, bf16[384,1536]{1,0:T(8,128)(2,1)}, bf16[1536,384]{1,0:T(8,128)(2,1)}, f32[8,384]{1,0:T(8,128)}, /*index=5*/f32[8,128]{1,0:T(8,128)}) custom-call(bf16[16,448,128]{2,1,0:T(8,128)(2,1)} %copy-done, bf16[16,448,128]{2,1,0:T(8,128)(2,1)} %copy-done.2), custom_call_target="tpu_custom_call" | custom-call | tf_op jit(solution)/shard_map/pallas_call | solution.py:192
  51.9 18.3 %shard_map.137 = (bf16[1024,384]{1,0:T(8,128)(2,1)}, bf16[1024,384]{1,0:T(8,128)(2,1)}, bf16[1024,384]{1,0:T(8,128)(2,1)}, f32[1024,768]{1,0:T(8,128)}, bf16[102...) custom-call(bf16[1024,384]{1,0:T(8,128)(2,1)} %tokens_ref.5, ...), custom_call_target="tpu_custom_call" | custom-call | tf_op jit(solution)/shard_map/pallas_call | solution.py:342
  70.2 21.3 %shard_map.138 = (bf16[1024,384]{1,0:T(8,128)(2,1)}, f32[1024,384]{1,0:T(8,128)}, bf16[1024,384]{1,0:T(8,128)(2,1)}, bf16[4,4,448,128]{3,2,1,0:T(8,128)(2,1)}, b...) custom-call(bf16[1024,384]{1,0:T(8,128)(2,1)} %tokens_ref.5, bf16[1024,384]{1,0:T(8,128)(2,1)} %cot_ref.1, ...), custom_call_target="tpu_custom_call" | custom-call | tf_op jit(solution)/shard_map/pallas_call | solution.py:468
  91.6 31.5 %shard_map.139 = (f32[1024,384]{1,0:T(8,128)}, bf16[4,480,128]{2,1,0:T(8,128)(2,1)}, bf16[4,480,128]{2,1,0:T(8,128)(2,1)}) custom-call(bf16[1024,384]{1,0:T(8,128)(2,1)} %tokens_ref.5, bf16[384,1152]{1,0:T(8,128)(2,1)} %get-tuple-element.36.wq_ref, f32[8,384]{1,0:T(8,128)} %get-tuple-element.37.vec_ref, s32[1024]{0:T(1024)} %seg_smem.3, s32[1,1024]{1,0:T(1,128)} %bitcast.42, ...), custom_call_target="tpu_custom_call" | custom-call | tf_op jit(solution)/shard_map/pallas_call | solution.py:658
  123.5 1.7 collective-permute-done.14
  126.4 2.9 %collective-permute-start.15 = (bf16[1,480,128]{2,1,0:T(8,128)(2,1)S(1)}, bf16[1,480,128]{2,1,0:T(8,128)(2,1)S(1)}, u32[]{:S(2)}, u32[]{:S(2)}) collective-permute-start(bf16[1,480,128]{2,1,0:T(8,128)(2,1)S(1)} %get-tuple-element.72), channel_id=1, source_target_pairs={{0,2},{1,3},{2,0},{3,1},{4,6},{5,7},{6,4},{7,5},{8,10},{9,11},{10,... | collective-permute-start | bytes 368648 | tf_op jit(solution)/shard_map/ppermute | solution.py:800
  131.0 5.3 %collective-permute-start.8 = (bf16[4,448,128]{2,1,0:T(8,128)(2,1)S(1)}, bf16[4,448,128]{2,1,0:T(8,128)(2,1)S(1)}, u32[]{:S(2)}, u32[]{:S(2)}) collective-permute-start(bf16[4,448,128]{2,1,0:T(8,128)(2,1)S(1)} %get-tuple-element.67), channel_id=1, source_target_pairs={{0,8},{16,24},{24,16},{1,9},{17,25},{25,17},{2,10},{18,26},{26,18}... | collective-permute-start | bytes 1376264 | tf_op jit(solution)/shard_map/ppermute | solution.py:800
  138.9 1.5 collective-permute-start.17
  141.2 7.4 %collective-permute-done.16 = bf16[1,480,128]{2,1,0:T(8,128)(2,1)S(1)} collective-permute-done((bf16[1,480,128]{2,1,0:T(8,128)(2,1)S(1)}, bf16[1,480,128]{2,1,0:T(8,128)(2,1)S(1)}, u32[]{:S(2)}, u32[]{:S(2)}) %collective-permute-start.16) | collective-permute-done | bytes 122912 | tf_op jit(solution)/shard_map/ppermute | solution.py:800
  150.8 1.5 collective-permute-start.20
  152.3 3.9 %collective-permute-done.9 = bf16[4,448,128]{2,1,0:T(8,128)(2,1)S(1)} collective-permute-done((bf16[4,448,128]{2,1,0:T(8,128)(2,1)S(1)}, bf16[4,448,128]{2,1,0:T(8,128)(2,1)S(1)}, u32[]{:S(2)}, u32[]{:S(2)}) %collective-permute-start.9) | collective-permute-done | bytes 458784 | tf_op jit(solution)/shard_map/ppermute | solution.py:800
  156.6 3.3 %collective-permute-start.12 = (bf16[1,448,128]{2,1,0:T(8,128)(2,1)S(1)}, bf16[1,448,128]{2,1,0:T(8,128)(2,1)S(1)}, u32[]{:S(2)}, u32[]{:S(2)}) collective-permute-start(bf16[1,448,128]{2,1,0:T(8,128)(2,1)S(1)} %get-tuple-element.77), channel_id=1, source_target_pairs={{0,4},{1,5},{2,6},{3,7},{4,0},{5,1},{6,2},{7,3},{8,12},{9,13},{10,... | collective-permute-start | bytes 344072 | tf_op jit(solution)/shard_map/ppermute | solution.py:800
  163.0 5.8 %collective-permute-done.12 = bf16[1,448,128]{2,1,0:T(8,128)(2,1)S(1)} collective-permute-done((bf16[1,448,128]{2,1,0:T(8,128)(2,1)S(1)}, bf16[1,448,128]{2,1,0:T(8,128)(2,1)S(1)}, u32[]{:S(2)}, u32[]{:S(2)}) %collective-permute-start.12) | collective-permute-done | bytes 114720 | tf_op jit(solution)/shard_map/ppermute | solution.py:800
  169.6 3.1 %shard_map.140 = (f32[448,128]{1,0:T(8,128)}, f32[448,128]{1,0:T(8,128)}, f32[448,128]{1,0:T(8,128)}, f32[8,128]{1,0:T(8,128)}) custom-call(f32[448,128]{1,0:T(8,128)} %fusion.7.rest_ref, f32[480,128]{1,0:T(8,128)} %add_add_fusion.first_ref, f32[448,128]{1,0:T(8,128)} %pad_bitcast_fusion.2.master_ref, f32[448,128]{1,0:T(8,128)} %get-tuple-element.79.moment_ref, ...), custom_call_target="tpu_custom_call" | custom-call | tf_op jit(solution)/shard_map/pallas_call | solution.py:747
  174.7 1.9 collective-permute-start.22
  179.1 2.0 collective-permute-done.23
  181.1 2.0 %collective-permute-done.24 = f32[8,128]{1,0:T(8,128)S(1)} collective-permute-done((f32[8,128]{1,0:T(8,128)S(1)}, f32[8,128]{1,0:T(8,128)S(1)}, u32[]{:S(2)}, u32[]{:S(2)}) %collective-permute-start.24) | collective-permute-done | bytes 4128 | tf_op jit(solution)/shard_map/ppermute | solution.py:800
  183.1 2.5 %collective-permute-start.26 = (f32[8,128]{1,0:T(8,128)S(1)}, f32[8,128]{1,0:T(8,128)S(1)}, u32[]{:S(2)}, u32[]{:S(2)}) collective-permute-start(f32[8,128]{1,0:T(8,128)S(1)} %add_add_fusion.2), channel_id=1, source_target_pairs={{0,16},{8,24},{16,0},{24,8},{1,17},{9,25},{17,1},{25,9},{2,18},{10... | collective-permute-start | bytes 12296 | tf_op jit(solution)/shard_map/ppermute | solution.py:800
  187.1 1.6 slice.102
  188.7 1.6 slice.103
  191.0 2.1 %shard_map.141 = (f32[448,128]{1,0:T(8,128)}, f32[8,128]{1,0:T(8,128)}) custom-call(f32[8,128]{1,0:T(8,128)} %add_add_fusion.1.sums_ref, f32[448,128]{1,0:T(8,128)} %pad_bitcast_fusion.2.master_ref, f32[448,128]{1,0:T(8,128)} %get-tuple-element.62.update_ref), custom_call_target="tpu_custom_call" | custom-call | tf_op jit(solution)/shard_map/pallas_call | solution.py:772
  195.5 1.6 slice.104
  (67 shorter events, 26.8 us)
Async XLA Ops:
  4.0 6.4 %collective-permute-start = (bf16[1,448,128]{2,1,0:T(8,128)(2,1)}, bf16[1,448,128]{2,1,0:T(8,128)(2,1)S(1)}, u32[]{:S(2)}, u32[]{:S(2)}) collective-permute-start(bf16[1,448,128]{2,1,0:T(8,128)(2,1)} %bitcast.34), channel_id=1, source_target_pairs={{0,2},{1,3},{2,0},{3,1},{4,6},{5,7},{6,4},{7,5},{8,10},{9,11},{10,... | collective-permute-start | bytes 344072 | tf_op jit(solution)/shard_map/ppermute | solution.py:800
  7.0 11.9 %collective-permute-start.1 = (bf16[1,448,128]{2,1,0:T(8,128)(2,1)}, bf16[1,448,128]{2,1,0:T(8,128)(2,1)S(1)}, u32[]{:S(2)}, u32[]{:S(2)}) collective-permute-start(bf16[1,448,128]{2,1,0:T(8,128)(2,1)} %bitcast.35), channel_id=1, source_target_pairs={{0,4},{1,5},{2,6},{3,7},{4,0},{5,1},{6,2},{7,3},{8,12},{9,13},{10,... | collective-permute-start | bytes 344072 | tf_op jit(solution)/shard_map/ppermute | solution.py:800
  9.6 9.3 %collective-permute-start.2 = (bf16[1,448,128]{2,1,0:T(8,128)(2,1)}, bf16[1,448,128]{2,1,0:T(8,128)(2,1)S(1)}, u32[]{:S(2)}, u32[]{:S(2)}) collective-permute-start(bf16[1,448,128]{2,1,0:T(8,128)(2,1)} %bitcast.36), channel_id=1, source_target_pairs={{0,6},{1,7},{2,4},{3,5},{4,2},{5,3},{6,0},{7,1},{8,14},{9,15},{10,... | collective-permute-start | bytes 344072 | tf_op jit(solution)/shard_map/ppermute | solution.py:800
  19.9 13.5 %collective-permute-start.3 = (bf16[4,448,128]{2,1,0:T(8,128)(2,1)S(1)}, bf16[4,448,128]{2,1,0:T(8,128)(2,1)S(1)}, u32[]{:S(2)}, u32[]{:S(2)}) collective-permute-start(bf16[4,448,128]{2,1,0:T(8,128)(2,1)S(1)} %pad_maximum_fusion), channel_id=1, source_target_pairs={{0,8},{8,0},{16,24},{24,16},{1,9},{9,1},{17,25},{25,17},{2,10},{10... | collective-permute-start | bytes 1376264 | tf_op jit(solution)/shard_map/ppermute | solution.py:800
  22.4 19.5 %collective-permute-start.4 = (bf16[4,448,128]{2,1,0:T(8,128)(2,1)S(1)}, bf16[4,448,128]{2,1,0:T(8,128)(2,1)S(1)}, u32[]{:S(2)}, u32[]{:S(2)}) collective-permute-start(bf16[4,448,128]{2,1,0:T(8,128)(2,1)S(1)} %pad_maximum_fusion), channel_id=1, source_target_pairs={{0,16},{8,24},{16,0},{24,8},{1,17},{9,25},{17,1},{25,9},{2,18},{10... | collective-permute-start | bytes 1376264 | tf_op jit(solution)/shard_map/ppermute | solution.py:800
  23.9 18.1 %collective-permute-start.5 = (bf16[4,448,128]{2,1,0:T(8,128)(2,1)S(1)}, bf16[4,448,128]{2,1,0:T(8,128)(2,1)S(1)}, u32[]{:S(2)}, u32[]{:S(2)}) collective-permute-start(bf16[4,448,128]{2,1,0:T(8,128)(2,1)S(1)} %pad_maximum_fusion), channel_id=1, source_target_pairs={{0,24},{8,16},{16,8},{24,0},{1,25},{9,17},{17,9},{25,1},{2,26},{10... | collective-permute-start | bytes 1376264 | tf_op jit(solution)/shard_map/ppermute | solution.py:800
  42.0 3.9 %copy-start = (bf16[16,448,128]{2,1,0:T(8,128)(2,1)}, bf16[16,448,128]{2,1,0:T(8,128)(2,1)S(1)}, u32[]{:S(2)}) copy-start(bf16[16,448,128]{2,1,0:T(8,128)(2,1)S(1)} %constant_dynamic-update-slice_fusion.own_ref) | copy-start | bytes 5505028
  42.0 3.9 %collective-permute-start.6 = (bf16[16,448,128]{2,1,0:T(8,128)(2,1)S(1)}, bf16[16,448,128]{2,1,0:T(8,128)(2,1)S(1)}, u32[]{:S(2)}, u32[]{:S(2)}) collective-permute-start(bf16[16,448,128]{2,1,0:T(8,128)(2,1)S(1)} %constant_dynamic-update-slice_fusion.own_ref), channel_id=1, source_target_pairs={{0,1},{1,0},{2,3},{3,2},{4,5},{5,4},{6,7},{7,6},{8,9},{9,8},{10,11... | collective-permute-start | bytes 5505032 | tf_op jit(solution)/shard_map/ppermute | solution.py:800
  91.4 37.8 %collective-permute-start.7 = (bf16[4,4,448,128]{3,2,1,0:T(8,128)(2,1)}, bf16[4,4,448,128]{3,2,1,0:T(8,128)(2,1)S(1)}, u32[]{:S(2)}, u32[]{:S(2)}) collective-permute-start(bf16[4,4,448,128]{3,2,1,0:T(8,128)(2,1)} %get-tuple-element.56), channel_id=1, source_target_pairs={{0,1},{1,0},{2,3},{3,2},{4,5},{5,4},{6,7},{7,6},{8,9},{9,8},{10,11... | collective-permute-start | bytes 5505032 | tf_op jit(solution)/shard_map/ppermute | solution.py:800
  123.1 6.2 %copy-start.1 = (bf16[4,4,448,128]{3,2,1,0:T(8,128)(2,1)S(1)}, bf16[4,4,448,128]{3,2,1,0:T(8,128)(2,1)}, u32[]{:S(2)}) copy-start(bf16[4,4,448,128]{3,2,1,0:T(8,128)(2,1)} %get-tuple-element.55) | copy-start | bytes 5505028
  123.1 2.1 %collective-permute-start.14 = (bf16[4,480,128]{2,1,0:T(8,128)(2,1)}, bf16[4,480,128]{2,1,0:T(8,128)(2,1)S(1)}, u32[]{:S(2)}, u32[]{:S(2)}) collective-permute-start(bf16[4,480,128]{2,1,0:T(8,128)(2,1)} %get-tuple-element.58), channel_id=1, source_target_pairs={{0,1},{1,0},{2,3},{3,2},{4,5},{5,4},{6,7},{7,6},{8,9},{9,8},{10,11... | collective-permute-start | bytes 1474568 | tf_op jit(solution)/shard_map/ppermute | solution.py:800
  126.4 12.5 %collective-permute-start.15 = (bf16[1,480,128]{2,1,0:T(8,128)(2,1)S(1)}, bf16[1,480,128]{2,1,0:T(8,128)(2,1)S(1)}, u32[]{:S(2)}, u32[]{:S(2)}) collective-permute-start(bf16[1,480,128]{2,1,0:T(8,128)(2,1)S(1)} %get-tuple-element.72), channel_id=1, source_target_pairs={{0,2},{1,3},{2,0},{3,1},{4,6},{5,7},{6,4},{7,5},{8,10},{9,11},{10,... | collective-permute-start | bytes 368648 | tf_op jit(solution)/shard_map/ppermute | solution.py:800
  129.3 11.1 %copy-start.3 = (f32[55368]{0:T(1024)S(1)}, f32[55368]{0:T(1024)}, u32[]{:S(2)}) copy-start(f32[55368]{0:T(1024)} %param.15) | copy-start | bytes 664420
  129.3 11.1 %copy-start.4 = (f32[55368]{0:T(1024)S(1)}, f32[55368]{0:T(1024)}, u32[]{:S(2)}) copy-start(f32[55368]{0:T(1024)} %param.14) | copy-start | bytes 664420
  129.7 21.1 %collective-permute-start.10 = (bf16[4,448,128]{2,1,0:T(8,128)(2,1)S(1)}, bf16[4,448,128]{2,1,0:T(8,128)(2,1)S(1)}, u32[]{:S(2)}, u32[]{:S(2)}) collective-permute-start(bf16[4,448,128]{2,1,0:T(8,128)(2,1)S(1)} %get-tuple-element.68), channel_id=1, source_target_pairs={{0,24},{8,16},{16,8},{1,25},{9,17},{17,9},{2,26},{10,18},{18,10},{... | collective-permute-start | bytes 1376264 | tf_op jit(solution)/shard_map/ppermute | solution.py:800
  131.0 21.3 %collective-permute-start.8 = (bf16[4,448,128]{2,1,0:T(8,128)(2,1)S(1)}, bf16[4,448,128]{2,1,0:T(8,128)(2,1)S(1)}, u32[]{:S(2)}, u32[]{:S(2)}) collective-permute-start(bf16[4,448,128]{2,1,0:T(8,128)(2,1)S(1)} %get-tuple-element.67), channel_id=1, source_target_pairs={{0,8},{16,24},{24,16},{1,9},{17,25},{25,17},{2,10},{18,26},{26,18}... | collective-permute-start | bytes 1376264 | tf_op jit(solution)/shard_map/ppermute | solution.py:800
  136.3 19.8 %collective-permute-start.9 = (bf16[4,448,128]{2,1,0:T(8,128)(2,1)S(1)}, bf16[4,448,128]{2,1,0:T(8,128)(2,1)S(1)}, u32[]{:S(2)}, u32[]{:S(2)}) collective-permute-start(bf16[4,448,128]{2,1,0:T(8,128)(2,1)S(1)} %get-tuple-element.69), channel_id=1, source_target_pairs={{0,16},{8,24},{24,8},{1,17},{9,25},{25,9},{2,18},{10,26},{26,10},{... | collective-permute-start | bytes 1376264 | tf_op jit(solution)/shard_map/ppermute | solution.py:800
  137.7 11.0 %collective-permute-start.16 = (bf16[1,480,128]{2,1,0:T(8,128)(2,1)S(1)}, bf16[1,480,128]{2,1,0:T(8,128)(2,1)S(1)}, u32[]{:S(2)}, u32[]{:S(2)}) collective-permute-start(bf16[1,480,128]{2,1,0:T(8,128)(2,1)S(1)} %get-tuple-element.74), channel_id=1, source_target_pairs={{0,4},{1,5},{2,6},{3,7},{4,0},{5,1},{6,2},{7,3},{8,12},{9,13},{10,... | collective-permute-start | bytes 368648 | tf_op jit(solution)/shard_map/ppermute | solution.py:800
  138.9 9.8 %collective-permute-start.17 = (bf16[1,480,128]{2,1,0:T(8,128)(2,1)S(1)}, bf16[1,480,128]{2,1,0:T(8,128)(2,1)S(1)}, u32[]{:S(2)}, u32[]{:S(2)}) collective-permute-start(bf16[1,480,128]{2,1,0:T(8,128)(2,1)S(1)} %get-tuple-element.73), channel_id=1, source_target_pairs={{0,6},{1,7},{2,4},{3,5},{4,2},{5,3},{6,0},{7,1},{8,14},{9,15},{10,... | collective-permute-start | bytes 368648 | tf_op jit(solution)/shard_map/ppermute | solution.py:800
  148.7 11.2 %collective-permute-start.18 = (bf16[480,128]{1,0:T(8,128)(2,1)S(1)}, bf16[480,128]{1,0:T(8,128)(2,1)S(1)}, u32[]{:S(2)}, u32[]{:S(2)}) collective-permute-start(bf16[480,128]{1,0:T(8,128)(2,1)S(1)} %fusion.8), channel_id=1, source_target_pairs={{0,8},{8,0},{16,24},{24,16},{1,9},{9,1},{17,25},{25,17},{2,10},{10... | collective-permute-start | bytes 368648 | tf_op jit(solution)/shard_map/ppermute | solution.py:800
  149.9 11.0 %collective-permute-start.19 = (bf16[480,128]{1,0:T(8,128)(2,1)S(1)}, bf16[480,128]{1,0:T(8,128)(2,1)S(1)}, u32[]{:S(2)}, u32[]{:S(2)}) collective-permute-start(bf16[480,128]{1,0:T(8,128)(2,1)S(1)} %fusion.8), channel_id=1, source_target_pairs={{0,16},{8,24},{16,0},{24,8},{1,17},{9,25},{17,1},{25,9},{2,18},{10... | collective-permute-start | bytes 368648 | tf_op jit(solution)/shard_map/ppermute | solution.py:800
  150.8 10.2 %collective-permute-start.20 = (bf16[480,128]{1,0:T(8,128)(2,1)S(1)}, bf16[480,128]{1,0:T(8,128)(2,1)S(1)}, u32[]{:S(2)}, u32[]{:S(2)}) collective-permute-start(bf16[480,128]{1,0:T(8,128)(2,1)S(1)} %fusion.8), channel_id=1, source_target_pairs={{0,24},{8,16},{16,8},{24,0},{1,25},{9,17},{17,9},{25,1},{2,26},{10... | collective-permute-start | bytes 368648 | tf_op jit(solution)/shard_map/ppermute | solution.py:800
  156.5 6.5 %collective-permute-start.11 = (bf16[1,448,128]{2,1,0:T(8,128)(2,1)S(1)}, bf16[1,448,128]{2,1,0:T(8,128)(2,1)S(1)}, u32[]{:S(2)}, u32[]{:S(2)}) collective-permute-start(bf16[1,448,128]{2,1,0:T(8,128)(2,1)S(1)} %get-tuple-element.75), channel_id=1, source_target_pairs={{0,2},{1,3},{2,0},{3,1},{4,6},{5,7},{6,4},{7,5},{8,10},{9,11},{10,... | collective-permute-start | bytes 344072 | tf_op jit(solution)/shard_map/ppermute | solution.py:800
  156.6 12.3 %collective-permute-start.12 = (bf16[1,448,128]{2,1,0:T(8,128)(2,1)S(1)}, bf16[1,448,128]{2,1,0:T(8,128)(2,1)S(1)}, u32[]{:S(2)}, u32[]{:S(2)}) collective-permute-start(bf16[1,448,128]{2,1,0:T(8,128)(2,1)S(1)} %get-tuple-element.77), channel_id=1, source_target_pairs={{0,4},{1,5},{2,6},{3,7},{4,0},{5,1},{6,2},{7,3},{8,12},{9,13},{10,... | collective-permute-start | bytes 344072 | tf_op jit(solution)/shard_map/ppermute | solution.py:800
  159.9 8.9 %collective-permute-start.13 = (bf16[1,448,128]{2,1,0:T(8,128)(2,1)S(1)}, bf16[1,448,128]{2,1,0:T(8,128)(2,1)S(1)}, u32[]{:S(2)}, u32[]{:S(2)}) collective-permute-start(bf16[1,448,128]{2,1,0:T(8,128)(2,1)S(1)} %get-tuple-element.76), channel_id=1, source_target_pairs={{0,6},{1,7},{2,4},{3,5},{4,2},{5,3},{6,0},{7,1},{8,14},{9,15},{10,... | collective-permute-start | bytes 344072 | tf_op jit(solution)/shard_map/ppermute | solution.py:800
  172.7 1.4 collective-permute-start.21
  174.7 4.4 %collective-permute-start.22 = (f32[8,128]{1,0:T(8,128)S(1)}, f32[8,128]{1,0:T(8,128)S(1)}, u32[]{:S(2)}, u32[]{:S(2)}) collective-permute-start(f32[8,128]{1,0:T(8,128)S(1)} %add.102), channel_id=1, source_target_pairs={{0,2},{1,3},{2,0},{3,1},{4,6},{5,7},{6,4},{7,5},{8,10},{9,11},{10,... | collective-permute-start | bytes 12296 | tf_op jit(solution)/shard_map/ppermute | solution.py:800
  176.6 4.5 %collective-permute-start.23 = (f32[8,128]{1,0:T(8,128)S(1)}, f32[8,128]{1,0:T(8,128)S(1)}, u32[]{:S(2)}, u32[]{:S(2)}) collective-permute-start(f32[8,128]{1,0:T(8,128)S(1)} %add.102), channel_id=1, source_target_pairs={{0,4},{1,5},{2,6},{3,7},{4,0},{5,1},{6,2},{7,3},{8,12},{9,13},{10,... | collective-permute-start | bytes 12296 | tf_op jit(solution)/shard_map/ppermute | solution.py:800
  177.7 5.4 %collective-permute-start.24 = (f32[8,128]{1,0:T(8,128)S(1)}, f32[8,128]{1,0:T(8,128)S(1)}, u32[]{:S(2)}, u32[]{:S(2)}) collective-permute-start(f32[8,128]{1,0:T(8,128)S(1)} %add.102), channel_id=1, source_target_pairs={{0,6},{1,7},{2,4},{3,5},{4,2},{5,3},{6,0},{7,1},{8,14},{9,15},{10,... | collective-permute-start | bytes 12296 | tf_op jit(solution)/shard_map/ppermute | solution.py:800
  183.1 7.2 %collective-permute-start.25 = (f32[8,128]{1,0:T(8,128)S(1)}, f32[8,128]{1,0:T(8,128)S(1)}, u32[]{:S(2)}, u32[]{:S(2)}) collective-permute-start(f32[8,128]{1,0:T(8,128)S(1)} %add_add_fusion.2), channel_id=1, source_target_pairs={{0,8},{8,0},{16,24},{24,16},{1,9},{9,1},{17,25},{25,17},{2,10},{10... | collective-permute-start | bytes 12296 | tf_op jit(solution)/shard_map/ppermute | solution.py:800
  183.1 7.2 %collective-permute-start.26 = (f32[8,128]{1,0:T(8,128)S(1)}, f32[8,128]{1,0:T(8,128)S(1)}, u32[]{:S(2)}, u32[]{:S(2)}) collective-permute-start(f32[8,128]{1,0:T(8,128)S(1)} %add_add_fusion.2), channel_id=1, source_target_pairs={{0,16},{8,24},{16,0},{24,8},{1,17},{9,25},{17,1},{25,9},{2,18},{10... | collective-permute-start | bytes 12296 | tf_op jit(solution)/shard_map/ppermute | solution.py:800
  185.7 4.7 %collective-permute-start.27 = (f32[8,128]{1,0:T(8,128)S(1)}, f32[8,128]{1,0:T(8,128)S(1)}, u32[]{:S(2)}, u32[]{:S(2)}) collective-permute-start(f32[8,128]{1,0:T(8,128)S(1)} %add_add_fusion.2), channel_id=1, source_target_pairs={{0,24},{8,16},{16,8},{24,0},{1,25},{9,17},{17,9},{25,1},{2,26},{10... | collective-permute-start | bytes 12296 | tf_op jit(solution)/shard_map/ppermute | solution.py:800
  (1 other events, 1.2 us)

commit v2 on v1

v2 whole, which is shorter than its diff:
```python
import functools
import math

import jax
import jax.numpy as jnp
from jax import lax
from jax.experimental import pallas as pl
from jax.experimental.pallas import tpu as pltpu
from jax.sharding import PartitionSpec as P

D = 384
HEADS = 6
HD = 64
FF = 1536
SEQ = 1024
STEP = 10
MATS = 10
LANES = 128
PAIRS = HEADS // 2
TILE = 256
TILES = SEQ // TILE
BLOCKS = SEQ // LANES

norm_epsilon = 1e-06
adam_epsilon = 1e-06
beta_one = 0.9
beta_two = 0.999
learn_rate = 0.5
weight_decay = 0.01
masked_score = -1e30

MATRIX_END = 4 * D * D + 2 * D * FF
BOUNDS = [0, 3 * D * D, 4 * D * D, 4 * D * D + D * FF, MATRIX_END] + [
    MATRIX_END + (j + 1) * D for j in range(6)
]
PARAMS = BOUNDS[-1]
ROW_OUT = BOUNDS[1] // LANES
ROW_UP = BOUNDS[2] // LANES
ROW_DOWN = BOUNDS[3] // LANES
ROW_VEC = BOUNDS[4] // LANES
VEC_ROWS = 6 * D // LANES
ROWS_ALL = PARAMS // LANES

score_scale = HD ** (-0.5) * math.log2(math.e)
grad_scale = HD ** (-0.5)

BF = jnp.bfloat16
F32 = jnp.float32
VMEM = pl.BlockSpec(memory_space=pltpu.VMEM)
SMEM = pl.BlockSpec(memory_space=pltpu.SMEM)


QUICK = pl.CostEstimate(flops=1000, bytes_accessed=1000, transcendentals=0)


def params(limit):
    return pltpu.CompilerParams(vmem_limit_bytes=limit * 1024 * 1024)


def round_up(value, step):
    return -(-value // step) * step


class Plan:
    def __init__(self, mesh_shape, shard):
        self.nb = mesh_shape["bucket"]
        self.nd = mesh_shape["dp"]
        self.n = self.nb * self.nd
        self.shard = shard
        self.start = [k * shard // LANES for k in range(self.n)]
        self.rows = [
            -(-((k + 1) * shard) // LANES) - self.start[k] for k in range(self.n)
        ]
        self.win = round_up(max(self.rows) + 1, 16)
        self.tail = round_up(self.win + VEC_ROWS, 16)
        self.vec_place = ROW_VEC - self.start[-1]
        self.vec_from = self.vec_place // 16 * 16
        self.kept_row = 2 * self.win - self.vec_from
        self.early = self.kept_row + 16

    def device(self):
        return lax.axis_index("bucket") * self.nd + lax.axis_index("dp")


def nn(a, b):
    return lax.dot_general(a, b, (((1,), (0,)), ((), ())), preferred_element_type=F32)


def nt(a, b):
    return lax.dot_general(a, b, (((1,), (1,)), ((), ())), preferred_element_type=F32)


def split_low(x):
    high = x.astype(BF)
    return high, (x - high.astype(F32)).astype(BF)


def rows_at(step):
    return pl.ds(pl.multiple_of(step * TILE, TILE), TILE)


def norm_parts(values):
    average = jnp.mean(values, axis=-1, keepdims=True)
    centered = values - average
    variance = jnp.mean(centered * centered, axis=-1, keepdims=True)
    rstd = lax.rsqrt(variance + norm_epsilon)
    return centered * rstd, rstd


def norm_back(hat, rstd, grad):
    mean_grad = jnp.mean(grad, axis=-1, keepdims=True)
    mean_both = jnp.mean(grad * hat, axis=-1, keepdims=True)
    return rstd * (grad - mean_grad - hat * mean_both)


def head_mean_matrix():
    row = lax.broadcasted_iota(jnp.int32, (TILE, TILE), 0)
    col = lax.broadcasted_iota(jnp.int32, (TILE, TILE), 1)
    return jnp.where(row // HD == col // HD, 1.0 / HD, 0.0).astype(BF)


def head_mean_low(low, matrix):
    rest = D - TILE
    return jnp.concatenate(
        [nn(low[:, :TILE], matrix), nn(low[:, TILE:], matrix[:rest, :rest])], axis=1
    )


def head_mean(x, matrix):
    high, rest = split_low(x)
    return head_mean_low(high, matrix) + head_mean_low(rest, matrix)


def prepare_kernel(plan, master_ref, keep_ref, out_ref):
    me = plan.device()
    offset = lax.rem(me * plan.shard, LANES)
    values = master_ref[...]
    turned = pltpu.roll(values, offset, 1)
    below = pltpu.roll(turned, 1, 0)
    lane = lax.broadcasted_iota(jnp.int32, values.shape, 1)
    row = lax.broadcasted_iota(jnp.int32, values.shape, 0)
    count = jnp.sum(keep_ref[...].astype(F32), axis=1, keepdims=True)
    high = jnp.floor(count * (1.0 / 32.0))
    parts = jnp.where(lane == 0, high, jnp.where(lane == 1, count - 32.0 * high, 0.0))
    window = jnp.where(lane < offset, below, turned)
    out_ref[...] = jnp.where(row == plan.win - 1, parts, window).astype(BF)


def prepare(plan, master_rows, keep_row):
    return pl.pallas_call(
        functools.partial(prepare_kernel, plan),
        out_shape=jax.ShapeDtypeStruct((plan.win, LANES), BF),
        in_specs=[VMEM, VMEM],
        out_specs=VMEM,
        compiler_params=params(8),
    )(master_rows, keep_row)


def held_window(own_ref, other_ref, rel, at):
    place = jnp.right_shift(rel, 1)
    return jnp.where(
        jnp.bitwise_and(rel, 1) == 0,
        own_ref[place, at].astype(F32),
        other_ref[place, at].astype(F32),
    )


def lay_windows(plan, owners, rel_of, own_ref, other_ref, flat, base):
    for k in owners:
        window = held_window(own_ref, other_ref, rel_of(k), slice(0, plan.win))
        first, count = plan.start[k] - base, plan.rows[k]
        shared = k > 0 and (k * plan.shard) % LANES
        if shared:
            before = flat[first : first + 1, :]
        flat[first : first + count, :] = window[:count]
        if shared:
            flat[first : first + 1, :] = before + window[:1]


def take_matrix(target, flat, base, height, width):
    stride = width // LANES
    for j in range(stride):
        target[:, j * LANES : (j + 1) * LANES] = flat[pl.ds(base + j, height, stride=stride), :].astype(BF)


def put_matrix(flat, base, source, height, width):
    stride = width // LANES
    for j in range(stride):
        flat[pl.ds(base + j, height, stride=stride), :] = source[:, j * LANES : (j + 1) * LANES]


def key_chunks(seg_ref, ti):
    first_i, last_i = seg_ref[ti * TILE], seg_ref[ti * TILE + TILE - 1]
    low, high = jnp.int32(0), jnp.int32(0)
    for b in range(BLOCKS):
        low += (seg_ref[b * LANES + LANES - 1] < first_i).astype(jnp.int32)
        high += (seg_ref[b * LANES] <= last_i).astype(jnp.int32)
    count = jnp.right_shift(high - low + 1, 1)
    return jnp.minimum(low, BLOCKS - 2 * count), count


def tile_bias(ti, block, row_seg, key_seg):
    key_place = lax.broadcasted_iota(jnp.int32, (TILE, TILE), 0) + block * LANES
    row_place = lax.broadcasted_iota(jnp.int32, (TILE, TILE), 1) + ti * TILE
    return jnp.where(
        jnp.logical_or(key_seg == row_seg, key_place == row_place), 0.0, masked_score
    )


def keys_at(block):
    return pl.ds(pl.multiple_of(block * LANES, LANES), TILE)


def side_rows(stacked, side):
    return jnp.concatenate(
        [stacked[side * LANES : (side + 1) * LANES], stacked[(2 + side) * LANES : (3 + side) * LANES]],
        axis=0,
    )


def to_column(row):
    return jnp.transpose(jnp.broadcast_to(row, (LANES, row.shape[1])))


def block_heads(pair):
    lane = lax.broadcasted_iota(jnp.int32, pair.shape, 1)
    zero = jnp.zeros_like(pair)
    sides = [jnp.where(lane < HD, pair, zero), jnp.where(lane >= HD, pair, zero)]
    return [side[b * LANES : (b + 1) * LANES] for b in range(2) for side in sides]


def put_blocks(ref, hp, step, pair):
    for i, part in enumerate(block_heads(pair)):
        ref[hp, 2 * step + i // 2, i % 2] = part


def two_blocks(ref, hp, block):
    return ref[hp, pl.ds(block, 2)].reshape(4 * LANES, LANES)


def stack_heads(pair):
    lane = lax.broadcasted_iota(jnp.int32, pair.shape, 1)
    zero = jnp.zeros_like(pair)
    return jnp.concatenate(
        [jnp.where(lane < HD, pair, zero), jnp.where(lane >= HD, pair, zero)], axis=0
    )


def project_kernel(
    plan,
    own_ref,
    other_ref,
    tokens_ref,
    wq_ref,
    vec_ref,
    head_ref,
    kept_ref,
    q_ref,
    k_ref,
    v_ref,
    hat_ref,
    rstd_ref,
    flat,
):
    dp = lax.axis_index("dp")
    lay_windows(plan, range(plan.nd), lambda k: jnp.bitwise_xor(dp, k), own_ref, other_ref, flat, 0)
    take_matrix(wq_ref, flat, 0, D, 3 * D)
    head_ref[...] = flat[ROW_OUT : ROW_OUT + 8, :]
    rel = jnp.bitwise_xor(dp, plan.nd - 1)
    late = held_window(own_ref, other_ref, rel, slice(plan.win, plan.kept_row))
    kept = jnp.zeros((1, LANES), F32)
    for j in range(plan.nd):
        half = other_ref if j & 1 else own_ref
        kept = kept + half[j >> 1, plan.kept_row :].astype(F32)[15:16]
    kept_ref[...] = jnp.broadcast_to(32.0 * kept[:, 0:1] + kept[:, 1:2], kept_ref.shape)
    for t in range(6):
        for j in range(D // LANES):
            at = plan.vec_place - plan.vec_from + 3 * t + j
            vec_ref[t : t + 1, j * LANES : (j + 1) * LANES] = late[at : at + 1]
    matrix = head_mean_matrix()
    gain1, shift1 = vec_ref[0:1, :], vec_ref[1:2, :]
    gain_q, gain_k = vec_ref[2:3, :], vec_ref[3:4, :]

    def project(step, carry):
        at = rows_at(step)
        hat, _ = norm_parts(tokens_ref[at, :].astype(F32))
        low = (hat * gain1 + shift1).astype(BF)
        raw = nn(low, wq_ref[...])

        def head_norm(low_out, part, gain):
            lanes = slice(part * D, (part + 1) * D)
            x = raw[:, lanes]
            centered = x - head_mean(x, matrix)
            rstd = lax.rsqrt(head_mean(centered * centered, matrix) + norm_epsilon)
            normed = centered * rstd
            hat_ref[at, lanes] = normed
            rstd_ref[at, lanes] = rstd
            low_out[at, :] = (normed * gain).astype(BF)

        head_norm(q_ref, 0, gain_q)
        head_norm(k_ref, 1, gain_k)
        v_ref[at, :] = raw[:, 2 * D :].astype(BF)
        return carry

    lax.fori_loop(0, TILES, project, 0)


def project_part(plan, own, other, tokens):
    rows = tokens.shape[0]
    low = jax.ShapeDtypeStruct((rows, D), BF)
    return pl.pallas_call(
        functools.partial(project_kernel, plan),
        out_shape=(
            jax.ShapeDtypeStruct((D, 3 * D), BF),
            jax.ShapeDtypeStruct((8, D), F32),
            jax.ShapeDtypeStruct((8, LANES), F32),
            jax.ShapeDtypeStruct((8, LANES), F32),
            low,
            low,
            low,
            jax.ShapeDtypeStruct((rows, 2 * D), F32),
            jax.ShapeDtypeStruct((rows, 2 * D), F32),
        ),
        in_specs=[VMEM] * 3,
        out_specs=(VMEM,) * 9,
        scratch_shapes=[
            pltpu.VMEM((round_up(plan.start[plan.nd - 1] + plan.win, 8), LANES), F32),
        ],
        compiler_params=params(24),
        cost_estimate=QUICK,
    )(own, other, tokens)


def forward_kernel(
    plan,
    seg_smem,
    seg_ref,
    keep_ref,
    q_ref,
    k_ref,
    v_ref,
    o_ref,
    ot_ref,
    lse_ref,
    kab,
    vt,
    ot,
    sums,
    segk,
    expo,
):
    seg_row = seg_ref[...].astype(F32)
    segk[...] = to_column(jnp.where(keep_ref[...] == 1, seg_row, -1.0))

    def stack(step, carry):
        at = rows_at(step)
        for hp in range(PAIRS):
            put_blocks(kab, hp, step, k_ref[at, hp * LANES : (hp + 1) * LANES])
        vt[:, at] = jnp.transpose(v_ref[at, :].astype(F32)).astype(BF)
        return carry

    lax.fori_loop(0, TILES, stack, 0)

    def query_tile(ti, carry):
        ot[...] = jnp.zeros_like(ot)
        sums[...] = jnp.zeros_like(sums)
        row_seg = seg_ref[:, rows_at(ti)].astype(F32)
        first, count = key_chunks(seg_smem, ti)

        def score_chunk(c, inner):
            block = first + 2 * c
            column = segk[keys_at(block), :]
            bias = tile_bias(ti, block, row_seg, jnp.concatenate([column, column], axis=1))
            for hp in range(PAIRS):
                queries = q_ref[rows_at(ti), hp * LANES : (hp + 1) * LANES]
                scores = nt(two_blocks(kab, hp, block), queries)
                for side in range(2):
                    head = 2 * hp + side
                    value = jnp.exp2(side_rows(scores, side) * score_scale + bias)
                    expo[c, head] = value
                    sums[head : head + 1, :] += jnp.sum(value, axis=0, keepdims=True)
            return inner

        lax.fori_loop(0, count, score_chunk, 0)
        lse_ref[ti] = jnp.log2(sums[...])
        sums[...] = 1.0 / sums[...]

        def value_chunk(c, inner):
            keys = keys_at(first + 2 * c)
            for head in range(HEADS):
                prob = (expo[c, head] * sums[head : head + 1, :]).astype(BF)
                at = slice(head * HD, (head + 1) * HD)
                ot[at, :] += nn(vt[at, keys], prob)
            return inner

        lax.fori_loop(0, count, value_chunk, 0)
        attended = ot[...]
        ot_ref[ti] = attended.astype(BF)
        o_ref[rows_at(ti), :] = jnp.transpose(attended).astype(BF)
        return carry

    lax.fori_loop(0, TILES, query_tile, 0)


def forward(plan, seg, seg_row, keep_row, q, k, v):
    rows = q.shape[0]
    return pl.pallas_call(
        functools.partial(forward_kernel, plan),
        out_shape=(
            jax.ShapeDtypeStruct((rows, D), BF),
            jax.ShapeDtypeStruct((TILES, D, TILE), BF),
            jax.ShapeDtypeStruct((TILES, 8, TILE), F32),
        ),
        in_specs=[SMEM] + [VMEM] * 5,
        out_specs=(VMEM,) * 3,
        scratch_shapes=[
            pltpu.VMEM((PAIRS, BLOCKS, 2, LANES, LANES), BF),
            pltpu.VMEM((D, SEQ), BF),
            pltpu.VMEM((D, TILE), F32),
            pltpu.VMEM((8, TILE), F32),
            pltpu.VMEM((SEQ, LANES), F32),
            pltpu.VMEM((TILES, HEADS, TILE, TILE), F32),
        ],
        compiler_params=params(24),
        cost_estimate=QUICK,
    )(seg, seg_row, keep_row, q, k, v)


erfc_step = 0.3275911 * math.sqrt(0.5)
erfc_terms = [0.254829592, -0.284496736, 1.421413741, -1.453152027, 1.061405429]


def normal_parts(u):
    expo = jnp.exp2(u * u * (-0.5 * math.log2(math.e)))
    t = 1.0 / (1.0 + erfc_step * jnp.abs(u))
    poly = 0.5 * erfc_terms[4]
    for term in reversed(erfc_terms[:4]):
        poly = poly * t + 0.5 * term
    below = poly * t * expo
    return jnp.where(u > 0.0, 1.0 - below, below), expo * (1.0 / math.sqrt(2.0 * math.pi))


def middle_kernel(
    plan,
    tokens_ref,
    cot_ref,
    o_ref,
    ot_ref,
    own_ref,
    other_ref,
    head_ref,
    kept_ref,
    vec_ref,
    keep_ref,
    patches_ref,
    out_ref,
    dh1_ref,
    do_ref,
    near_ref,
    far_ref,
    tail_ref,
    gvec_ref,
    keepc,
    gout,
    gup,
    gdownt,
    flat,
    wo_ref,
    wu_ref,
    wd_ref,
):
    bucket = lax.axis_index("bucket")
    base = ROW_OUT
    flat[0:8, :] = head_ref[...]
    dp = lax.axis_index("dp")
    lay_windows(
        plan,
        range(plan.nd, plan.n),
        lambda k: (k // plan.nd - 1) * plan.nd + jnp.bitwise_xor(dp, k % plan.nd),
        own_ref,
        other_ref,
        flat,
        base,
    )
    take_matrix(wo_ref, flat, 0, D, D)
    take_matrix(wu_ref, flat, ROW_UP - base, D, FF)
    take_matrix(wd_ref, flat, ROW_DOWN - base, FF, D)
    gain2, shift2 = vec_ref[4:5, :], vec_ref[5:6, :]
    own = patches_ref[bucket].astype(F32)
    total = patches_ref[0].astype(F32)
    for b in range(1, plan.nb):
        total = total + patches_ref[b].astype(F32)
    ones = jnp.ones((1, LANES), F32)
    scale = (plan.nb * own) * ones / (total * ones) * float(SEQ * plan.nd) / kept_ref[0:1, :]
    keepc[...] = to_column(keep_ref[...].astype(F32)) * scale
    gout[...] = jnp.zeros_like(gout)
    gup[...] = jnp.zeros_like(gup)
    gdownt[...] = jnp.zeros_like(gdownt)
    gvec_ref[...] = jnp.zeros_like(gvec_ref)

    def chunk(step, carry):
        at = rows_at(step)
        middle = tokens_ref[at, :].astype(F32) + nn(o_ref[at, :], wo_ref[...])
        hat, rstd = norm_parts(middle)
        low = (hat * gain2 + shift2).astype(BF)
        u = nn(low, wu_ref[...])
        phi, bell = normal_parts(u)
        hidden = (u * phi).astype(BF)
        out_ref[at, :] = (middle + nn(hidden, wd_ref[...])).astype(BF)
        weights = keepc[at, :]
        seed = cot_ref[at, :].astype(F32) * jnp.concatenate([weights] * (D // LANES), axis=1)
        seed_low = seed.astype(BF)
        du = (nt(seed_low, wd_ref[...]) * (phi + u * bell)).astype(BF)
        gdownt[...] += nn(jnp.transpose(seed).astype(BF), hidden)
        gup[...] += nn(jnp.transpose(low.astype(F32)).astype(BF), du)
        da2 = nt(du, wu_ref[...])
        gvec_ref[0:1, :] += jnp.sum(da2 * hat, axis=0, keepdims=True)
        gvec_ref[1:2, :] += jnp.sum(da2, axis=0, keepdims=True)
        dh1 = seed + norm_back(hat, rstd, da2 * gain2)
        dh1_ref[at, :] = dh1
        dh1_low = dh1.astype(BF)
        gout[...] += nn(ot_ref[step], dh1_low)
        do_ref[at, :] = nt(dh1_low, wo_ref[...]).astype(BF)
        return carry

    lax.fori_loop(0, o_ref.shape[0] // TILE, chunk, 0)

    put_matrix(flat, 0, gout, D, D)
    put_matrix(flat, ROW_UP - base, gup, D, FF)
    for j in range(D // LANES):
        flat[pl.ds(ROW_DOWN - base + j, FF, stride=D // LANES), :] = jnp.transpose(
            gdownt[j * LANES : (j + 1) * LANES, :]
        )
    tail_ref[...] = flat[0:8, :]
    side = jnp.bitwise_and(dp, 1)
    for k in range(plan.nd, plan.n):
        first = plan.start[k] - base
        quarter = k // plan.nd - 1
        reld = jnp.right_shift(jnp.bitwise_xor(dp, k % plan.nd), 1)
        window = flat[first : first + plan.win, :].astype(BF)

        @pl.when(side == k % 2)
        def _():
            near_ref[quarter, reld] = window

        @pl.when(side != k % 2)
        def _():
            far_ref[quarter, reld] = window


def middle_part(plan, tokens, cot, o, ot, own, other, head, kept, vec, keep_row, patches):
    rows = tokens.shape[0]
    windows = jax.ShapeDtypeStruct((plan.nb - 1, plan.nd // 2, plan.win, LANES), BF)
    return pl.pallas_call(
        functools.partial(middle_kernel, plan),
        out_shape=(
            jax.ShapeDtypeStruct((rows, D), BF),
            jax.ShapeDtypeStruct((rows, D), F32),
            jax.ShapeDtypeStruct((rows, D), BF),
            windows,
            windows,
            jax.ShapeDtypeStruct((8, LANES), F32),
            jax.ShapeDtypeStruct((8, D), F32),
        ),
        in_specs=[VMEM] * 10 + [SMEM],
        out_specs=(VMEM,) * 7,
        scratch_shapes=[
            pltpu.VMEM((rows, LANES), F32),
            pltpu.VMEM((D, D), F32),
            pltpu.VMEM((D, FF), F32),
            pltpu.VMEM((D, FF), F32),
            pltpu.VMEM((round_up(plan.start[-1] + plan.win - ROW_OUT, 8), LANES), F32),
            pltpu.VMEM((D, D), BF),
            pltpu.VMEM((D, FF), BF),
            pltpu.VMEM((FF, D), BF),
        ],
        compiler_params=params(30),
        cost_estimate=QUICK,
    )(tokens, cot, o, ot, own, other, head, kept, vec, keep_row, patches)


def backward_kernel(
    plan,
    vec_ref,
    seg_smem,
    seg_ref,
    keep_ref,
    lse_ref,
    q_ref,
    k_ref,
    v_ref,
    o_ref,
    do_ref,
    hat_ref,
    rstd_ref,
    token_ref,
    low_ref,
    gains_ref,
    kab,
    vab,
    qab,
    dab,
    kt,
    dqt,
    dk,
    dv,
    inner_sums,
    segk,
):
    matrix = head_mean_matrix()
    seg_row = seg_ref[...].astype(F32)
    segk[...] = to_column(jnp.where(keep_ref[...] == 1, seg_row, -1.0))
    head_row = lax.broadcasted_iota(jnp.int32, (8, D), 0)
    head_lane = lax.broadcasted_iota(jnp.int32, (8, D), 1)
    hot = jnp.where(head_lane // HD == head_row, 1.0, 0.0).astype(BF)
    dqt[...] = jnp.zeros_like(dqt)
    dk[...] = jnp.zeros_like(dk)
    dv[...] = jnp.zeros_like(dv)
    gains_ref[...] = jnp.zeros_like(gains_ref)

    def stack(step, carry):
        at = rows_at(step)
        keys = k_ref[at, :]
        grads = do_ref[at, :]
        for hp in range(PAIRS):
            lanes = slice(hp * LANES, (hp + 1) * LANES)
            put_blocks(kab, hp, step, keys[:, lanes])
            put_blocks(vab, hp, step, v_ref[at, lanes])
            qab[hp, step] = stack_heads(q_ref[at, lanes])
            dab[hp, step] = stack_heads(grads[:, lanes])
        kt[:, at] = jnp.transpose(keys.astype(F32)).astype(BF)
        high, rest = split_low(grads.astype(F32) * o_ref[at, :].astype(F32))
        inner_sums[step] = nt(hot, high) + nt(hot, rest)
        return carry

    lax.fori_loop(0, TILES, stack, 0)

    def query_tile(ti, carry):
        row_seg = seg_ref[:, rows_at(ti)].astype(F32)
        first, count = key_chunks(seg_smem, ti)

        def key_chunk(c, inner):
            block = first + 2 * c
            keys = keys_at(block)
            column = segk[keys, :]
            bias = tile_bias(ti, block, row_seg, jnp.concatenate([column, column], axis=1))
            for hp in range(PAIRS):
                lanes = slice(hp * LANES, (hp + 1) * LANES)
                scores = nt(two_blocks(kab, hp, block), q_ref[rows_at(ti), lanes])
                grads = nt(two_blocks(vab, hp, block), do_ref[rows_at(ti), lanes])
                probs, dscores = [], []
                for side in range(2):
                    head = 2 * hp + side
                    prob = jnp.exp2(
                        side_rows(scores, side) * score_scale
                        + (bias - lse_ref[ti, head : head + 1, :])
                    )
                    dscore = prob * (side_rows(grads, side) - inner_sums[ti, head : head + 1, :])
                    dscore = dscore.astype(BF)
                    probs.append(prob.astype(BF))
                    dscores.append(dscore)
                    at = slice(head * HD, (head + 1) * HD)
                    dqt[ti, at, :] += nn(kt[at, keys], dscore)
                dv[hp, keys] += nn(jnp.concatenate(probs, axis=1), dab[hp, ti])
                dk[hp, keys] += nn(jnp.concatenate(dscores, axis=1), qab[hp, ti])
            return inner

        lax.fori_loop(0, count, key_chunk, 0)
        return carry

    lax.fori_loop(0, TILES, query_tile, 0)

    def finish(step, carry):
        at = rows_at(step)

        def head_norm_back(part, gain, grad):
            lanes = slice(part * D, (part + 1) * D)
            hat = hat_ref[at, lanes]
            both = grad * hat
            gains_ref[part : part + 1, :] += jnp.sum(both, axis=0, keepdims=True)
            scaled = grad * gain
            mean_grad = head_mean_low(scaled.astype(BF), matrix)
            mean_both = head_mean_low((both * gain).astype(BF), matrix)
            back = rstd_ref[at, lanes] * (scaled - mean_grad - hat * mean_both)
            low_ref[at, lanes] = back.astype(BF)

        grad_k = jnp.concatenate([dk[hp, at] for hp in range(PAIRS)], axis=1) * grad_scale
        grad_v = jnp.concatenate([dv[hp, at] for hp in range(PAIRS)], axis=1)
        head_norm_back(0, vec_ref[2:3, :], jnp.transpose(dqt[step]) * grad_scale)
        head_norm_back(1, vec_ref[3:4, :], grad_k)
        low_ref[at, 2 * D :] = grad_v.astype(BF)
        return carry

    lax.fori_loop(0, TILES, finish, 0)


def backward(plan, vec, seg, seg_row, keep_row, lse, q, k, v, o, do, hat, rstd, token):
    rows = q.shape[0]
    stacked = pltpu.VMEM((PAIRS, TILES, 2 * TILE, LANES), BF)
    blocked = pltpu.VMEM((PAIRS, BLOCKS, 2, LANES, LANES), BF)
    return pl.pallas_call(
        functools.partial(backward_kernel, plan),
        out_shape=(
            jax.ShapeDtypeStruct((rows, 3 * D), BF),
            jax.ShapeDtypeStruct((8, D), F32),
        ),
        in_specs=[VMEM, SMEM] + [VMEM] * 11,
        out_specs=(VMEM, VMEM),
        scratch_shapes=[
            blocked,
            blocked,
            stacked,
            stacked,
            pltpu.VMEM((D, SEQ), BF),
            pltpu.VMEM((TILES, D, TILE), F32),
            pltpu.VMEM((PAIRS, SEQ, LANES), F32),
            pltpu.VMEM((PAIRS, SEQ, LANES), F32),
            pltpu.VMEM((TILES, 8, TILE), F32),
            pltpu.VMEM((SEQ, LANES), F32),
        ],
        compiler_params=params(32),
        cost_estimate=QUICK,
    )(vec, seg, seg_row, keep_row, lse, q, k, v, o, do, hat, rstd, token)


def finish_kernel(
    plan,
    tokens_ref,
    wq_ref,
    vec_ref,
    dh1_ref,
    tail_ref,
    gvec_ref,
    low_ref,
    gqk_ref,
    grad_ref,
    near_ref,
    far0_ref,
    far1_ref,
    gq,
    gains,
    flat,
):
    gain1, shift1 = vec_ref[0:1, :], vec_ref[1:2, :]
    gq[...] = jnp.zeros_like(gq)
    gains[...] = jnp.zeros_like(gains)

    def finish(step, carry):
        at = rows_at(step)
        low = low_ref[at, :]
        hat, rstd = norm_parts(tokens_ref[at, :].astype(F32))
        normed = hat * gain1 + shift1
        gq[...] += nn(jnp.transpose(normed).astype(BF), low)
        da1 = nt(low, wq_ref[...])
        gains[0:1, :] += jnp.sum(da1 * hat, axis=0, keepdims=True)
        gains[1:2, :] += jnp.sum(da1, axis=0, keepdims=True)
        grad_ref[at, :] = dh1_ref[at, :] + norm_back(hat, rstd, da1 * gain1)
        return carry

    lax.fori_loop(0, TILES, finish, 0)
    gains[2:4, :] = gqk_ref[0:2, :]
    gains[4:6, :] = gvec_ref[0:2, :]
    put_matrix(flat, 0, gq, D, 3 * D)
    flat[ROW_OUT : ROW_OUT + 8, :] = tail_ref[...]
    dp = lax.axis_index("dp")
    side = jnp.bitwise_and(dp, 1)
    rest = jnp.zeros((plan.tail - plan.win, LANES), BF)
    vector_rows = []
    for t in range(6):
        for j in range(D // LANES):
            vector_rows.append(gains[t : t + 1, j * LANES : (j + 1) * LANES])
    vector_rows.append(jnp.zeros((plan.tail - plan.win - VEC_ROWS, LANES), F32))
    vectors = jnp.concatenate(vector_rows, axis=0).astype(BF)
    for k in range(plan.nd):
        first = plan.start[k]
        reld = jnp.right_shift(jnp.bitwise_xor(dp, k), 1)
        window = flat[first : first + plan.win, :].astype(BF)
        window = jnp.concatenate([window, vectors if k == plan.nd - 1 else rest], axis=0)

        @pl.when(side == k % 2)
        def _():
            near_ref[reld] = window

        @pl.when(side != k % 2)
        def _():
            far0_ref[reld] = window[: plan.tail // 2]
            far1_ref[reld] = window[plan.tail // 2 :]


def finish_part(plan, tokens, wq, vec, dh1, tail, gvec, low, gains):
    rows = tokens.shape[0]
    windows = jax.ShapeDtypeStruct((plan.nd // 2, plan.tail, LANES), BF)
    halves = jax.ShapeDtypeStruct((plan.nd // 2, plan.tail // 2, LANES), BF)
    return pl.pallas_call(
        functools.partial(finish_kernel, plan),
        out_shape=(jax.ShapeDtypeStruct((rows, D), F32), windows, halves, halves),
        in_specs=[VMEM] * 8,
        out_specs=(VMEM,) * 4,
        scratch_shapes=[
            pltpu.VMEM((D, 3 * D), F32),
            pltpu.VMEM((8, D), F32),
            pltpu.VMEM((round_up(plan.start[plan.nd - 1] + plan.win, 8), LANES), F32),
        ],
        compiler_params=params(28),
        cost_estimate=QUICK,
    )(tokens, wq, vec, dh1, tail, gvec, low, gains)


def flat_place(plan, shape):
    row = lax.broadcasted_iota(jnp.int32, shape, 0)
    lane = lax.broadcasted_iota(jnp.int32, shape, 1)
    place = row * LANES + lane
    return place, plan.device() * plan.shard + place


def update_kernel(
    plan,
    own_ref,
    got0_ref,
    got1_ref,
    got2_ref,
    master_ref,
    moment_ref,
    second_ref,
    new_moment_ref,
    new_second_ref,
    update_ref,
    sums_ref,
    window,
):
    bucket = lax.axis_index("bucket")
    dp = lax.axis_index("dp")
    total = tree_sum([ref[...].astype(F32) for ref in (own_ref, got0_ref, got1_ref, got2_ref)])
    window[...] = jnp.where(bucket == 0, total[plan.win : 2 * plan.win], total[: plan.win])

    @pl.when(jnp.logical_and(bucket == plan.nb - 1, dp == plan.nd - 1))
    def _():
        window[plan.vec_place : plan.vec_place + VEC_ROWS, :] = total[
            2 * plan.win : 2 * plan.win + VEC_ROWS
        ]

    offset = lax.rem(plan.device() * plan.shard, LANES)
    back = lax.rem(LANES - offset, LANES)
    turned = pltpu.roll(window[...], back, 1)
    above = pltpu.roll(turned, plan.win - 1, 0)
    lane = lax.broadcasted_iota(jnp.int32, turned.shape, 1)
    place, index = flat_place(plan, turned.shape)
    inside = place < plan.shard
    grad = jnp.where(inside, jnp.where(lane + offset < LANES, turned, above), 0.0)
    master = master_ref[...]
    moment = beta_one * moment_ref[...] + (1.0 - beta_one) * grad
    second = beta_two * second_ref[...] + (1.0 - beta_two) * grad * grad
    first_hat = moment / (1.0 - beta_one**STEP)
    second_hat = second / (1.0 - beta_two**STEP)
    decay = jnp.where(index < BOUNDS[4], weight_decay, 0.0)
    update = first_hat / (jnp.sqrt(second_hat) + adam_epsilon) + decay * master
    update = jnp.where(inside, update, 0.0)
    new_moment_ref[...] = moment
    new_second_ref[...] = second
    update_ref[...] = update
    master_sq = jnp.where(inside, master * master, 0.0)
    update_sq = update * update
    lanes = lax.broadcasted_iota(jnp.int32, (1, LANES), 1)
    rows = []
    for squares in (master_sq, update_sq):
        row = jnp.zeros((1, LANES), F32)
        for t in range(MATS):
            mine = jnp.logical_and(index >= BOUNDS[t], index < BOUNDS[t + 1])
            part = jnp.sum(jnp.where(mine, squares, 0.0), axis=0, keepdims=True)
            row = jnp.where(lanes == t, jnp.sum(part, axis=1, keepdims=True), row)
        rows.append(row)
    rows.append(jnp.zeros((6, LANES), F32))
    sums_ref[...] = jnp.concatenate(rows, axis=0)


def update_part(plan, parts, master_rows, moment_rows, second_rows):
    rows = jax.ShapeDtypeStruct((plan.win, LANES), F32)
    return pl.pallas_call(
        functools.partial(update_kernel, plan),
        out_shape=(rows, rows, rows, jax.ShapeDtypeStruct((8, LANES), F32)),
        in_specs=[VMEM] * 7,
        out_specs=(VMEM,) * 4,
        scratch_shapes=[pltpu.VMEM((plan.win, LANES), F32)],
        compiler_params=params(12),
    )(*parts, master_rows, moment_rows, second_rows)


def apply_kernel(plan, *refs):
    *sums_refs, master_ref, update_ref, new_ref, norms_ref, trust_ref = refs
    roots = jnp.sqrt(tree_sum([ref[...] for ref in sums_refs]))
    trust = roots[0:1, :] / (roots[1:2, :] + adam_epsilon)
    norms_ref[...] = roots[0:2, :MATS]
    trust_ref[...] = trust[:, :MATS]
    master = master_ref[...]
    _, index = flat_place(plan, master.shape)
    factors = jnp.broadcast_to(trust[:, 0:1], master.shape)
    for t in range(1, MATS):
        factors = jnp.where(index >= BOUNDS[t], trust[:, t : t + 1], factors)
    new_ref[...] = master - learn_rate * factors * update_ref[...]


def apply_part(plan, sums, master_rows, update_rows):
    return pl.pallas_call(
        functools.partial(apply_kernel, plan),
        out_shape=(
            jax.ShapeDtypeStruct((plan.win, LANES), F32),
            jax.ShapeDtypeStruct((2, MATS), F32),
            jax.ShapeDtypeStruct((1, MATS), F32),
        ),
        in_specs=[VMEM] * (len(sums) + 2),
        out_specs=(VMEM,) * 3,
        compiler_params=params(8),
    )(*sums, master_rows, update_rows)


def lay_column_kernel(*refs):
    for i, part in enumerate(refs[:-1]):
        refs[-1][i] = part[...]


def lay_column(parts):
    return pl.pallas_call(
        lay_column_kernel,
        out_shape=jax.ShapeDtypeStruct((len(parts), *parts[0].shape), parts[0].dtype),
        in_specs=[VMEM] * len(parts),
        out_specs=VMEM,
        compiler_params=params(4),
    )(*parts)


def choose_kernel(plan, *refs):
    columns, (early_ref, late_ref) = refs[:-2], refs[-2:]
    step = columns[0].shape[0]
    bucket = lax.axis_index("bucket")
    early_ref[:, plan.kept_row :] = columns[0][:, plan.win - 16 :]
    for i, part in enumerate(columns):
        owner = jnp.bitwise_xor(bucket, i)

        @pl.when(owner == 0)
        def _():
            early_ref[:, : plan.win] = part[...]

        @pl.when(owner == plan.nb - 1)
        def _():
            early_ref[:, plan.win : plan.kept_row] = part[:, plan.vec_from :]

        @pl.when(owner > 0)
        def _():
            late_ref[pl.ds((owner - 1) * step, step)] = part[...]


def choose(plan, columns):
    step = columns[0].shape[0]
    return pl.pallas_call(
        functools.partial(choose_kernel, plan),
        out_shape=(
            jax.ShapeDtypeStruct((step, plan.early, LANES), BF),
            jax.ShapeDtypeStruct(((plan.nb - 1) * step, plan.win, LANES), BF),
        ),
        in_specs=[VMEM] * len(columns),
        out_specs=(VMEM, VMEM),
        compiler_params=params(8),
    )(*columns)


def add_parts_kernel(halves, *refs):
    refs = list(refs)
    parts = [[refs.pop(0) for _ in range(count)] for count in halves]
    for i, out in enumerate(refs[1:-1]):
        step = out.shape[-3]
        at = slice(i * step, (i + 1) * step)
        at = (slice(None), at) if len(out.shape) == 4 else at
        values = [
            jnp.concatenate([half[at].astype(F32) for half in part], axis=-2) for part in parts
        ]
        out[...] = tree_sum(values).astype(out.dtype)
    refs[-1][...] = jnp.zeros_like(refs[-1])


def add_parts(parts, pieces, token):
    *lead, total, height, width = parts[0].shape
    parts = [part if isinstance(part, list) else [part] for part in parts]
    halves = [len(part) for part in parts]
    parts = [half for part in parts for half in part]
    return pl.pallas_call(
        functools.partial(add_parts_kernel, halves),
        out_shape=tuple(
            jax.ShapeDtypeStruct((*lead, total // pieces, height, width), BF if i else F32)
            for i in range(pieces)
        )
        + (jax.ShapeDtypeStruct((8, LANES), F32),),
        in_specs=[VMEM] * (len(parts) + 1),
        out_specs=(VMEM,) * (pieces + 1),
        compiler_params=params(14),
    )(*parts, token)


def blend_kernel(plan, count, *refs):
    rest = refs[0]
    parts, outs = refs[1 : 1 + count], refs[1 + count :]
    bucket = lax.axis_index("bucket")
    first = tree_sum([part[...].astype(F32) for part in parts])
    for i, out in enumerate(outs):
        quarter = jnp.maximum(jnp.bitwise_xor(bucket, i) - 1, 0)
        out[: plan.win] = rest[quarter].astype(out.dtype)
        out[plan.win :] = first.astype(out.dtype)


def blend(plan, rest, parts):
    height = plan.win + plan.tail
    return pl.pallas_call(
        functools.partial(blend_kernel, plan, len(parts)),
        out_shape=tuple(
            jax.ShapeDtypeStruct((height, LANES), BF if i else F32) for i in range(plan.nb)
        ),
        in_specs=[VMEM] * (1 + len(parts)),
        out_specs=(VMEM,) * plan.nb,
        compiler_params=params(8),
    )(rest, *parts)


def add_rows_kernel(*refs):
    refs[-1][...] = tree_sum([ref[...] for ref in refs[:-1]])


def add_rows(parts):
    return pl.pallas_call(
        add_rows_kernel,
        out_shape=jax.ShapeDtypeStruct(parts[0].shape, F32),
        in_specs=[VMEM] * len(parts),
        out_specs=VMEM,
        compiler_params=params(4),
    )(*parts)


def groups_of(size, skip=0):
    bits = list(range(skip, size.bit_length() - 1))
    return [bits[i : i + 2] for i in range(0, len(bits), 2)]


def masks_of(bits):
    masks = [1 << bits[0]]
    if len(bits) == 2:
        masks += [1 << bits[1], (1 << bits[0]) | (1 << bits[1])]
    return masks


def swap(x, axis, size, mask):
    return lax.ppermute(x, axis, [(i, i ^ mask) for i in range(size)])


def tree_sum(parts):
    if len(parts) == 4:
        return (parts[0] + parts[1]) + (parts[2] + parts[3])
    return parts[0] + parts[1]


def with_partners(x, axis, size, bits):
    return [x] + [swap(x, axis, size, mask) for mask in masks_of(bits)]


def gather_windows(plan, window):
    first, *more = groups_of(plan.nd, 1)
    column = lay_column(with_partners(window, "dp", plan.nd, first))
    for bits in more:
        column = jnp.concatenate(with_partners(column, "dp", plan.nd, bits), axis=0)
    (bits,) = groups_of(plan.nb)
    early, late = choose(plan, with_partners(column, "bucket", plan.nb, bits))
    return (early, swap(early, "dp", plan.nd, 1)), (late, swap(late, "dp", plan.nd, 1))


def scatter_dp(plan, pieces):
    *more, last = groups_of(plan.nd, 1)
    got = [pieces[0]] + [
        swap(piece, "dp", plan.nd, mask) for piece, mask in zip(pieces[1:], masks_of(last))
    ]
    for bits in reversed(more):
        held = tree_sum([x.astype(F32) for x in got])
        size = 1 << len(bits)
        step = held.shape[-3] // size
        parts = [held[..., i * step : (i + 1) * step, :, :] for i in range(size)]
        got = [parts[0]] + [
            swap(part.astype(BF), "dp", plan.nd, mask)
            for part, mask in zip(parts[1:], masks_of(bits))
        ]
    return [x.reshape(*x.shape[:-3], *x.shape[-2:]) for x in got]


def sum_all(plan, x):
    x = [x, swap(x, "dp", plan.nd, 1)]
    for bits in groups_of(plan.nd, 1):
        x = with_partners(add_rows(x), "dp", plan.nd, bits)
    (bits,) = groups_of(plan.nb)
    return with_partners(add_rows(x), "bucket", plan.nb, bits)


def local(
    plan, tokens, cotangent, segment_ids, keep_mask, bucket_patches, master, first_moment, second_moment
):
    def as_rows(flat):
        return jnp.pad(flat, (0, plan.win * LANES - plan.shard)).reshape(plan.win, LANES)

    def as_flat(rows):
        return rows.reshape(-1)[: plan.shard]

    master_rows = as_rows(master)
    seg_row = segment_ids.reshape(1, SEQ)
    keep_row = keep_mask.reshape(1, SEQ)
    count = 1 << len(groups_of(plan.nd, 1)[-1])
    (b_bits,) = groups_of(plan.nb)

    early, late = gather_windows(plan, prepare(plan, master_rows, keep_row))
    wq, vec, head, kept, q, k, v, hat, rstd = project_part(plan, *early, tokens)
    o, ot, lse = forward(plan, segment_ids, seg_row, keep_row, q, k, v)
    block_output, dh1, do, near, far, tail, gvec = middle_part(
        plan, tokens, cotangent, o, ot, *late, head, kept, vec, keep_row, bucket_patches
    )
    *pieces, token = add_parts([near, swap(far, "dp", plan.nd, 1)], count, gvec)
    rest = scatter_dp(plan, pieces)
    low, gains = backward(
        plan, vec, segment_ids, seg_row, keep_row, lse, q, k, v, o, do, hat, rstd, token
    )
    input_grad, near, *far = finish_part(plan, tokens, wq, vec, dh1, tail, gvec, low, gains)
    rest, token = add_parts(rest, 1, gains)
    *pieces, _ = add_parts([near, [swap(half, "dp", plan.nd, 1) for half in far]], count, token)
    first = scatter_dp(plan, pieces)
    mine, *sent = blend(plan, rest, first)
    parts = [mine] + [
        swap(x, "bucket", plan.nb, mask) for x, mask in zip(sent, masks_of(b_bits))
    ]
    moment_rows, second_rows, update_rows, sums = update_part(
        plan, parts, master_rows, as_rows(first_moment), as_rows(second_moment)
    )
    new_master, norms, trust = apply_part(plan, sum_all(plan, sums), master_rows, update_rows)
    return (
        block_output,
        input_grad,
        as_flat(moment_rows),
        as_flat(second_rows),
        as_flat(new_master),
        norms,
        trust.reshape(MATS),
    )


def solution(mesh):
    shards = mesh.shape["bucket"] * mesh.shape["dp"]
    plan = Plan(mesh.shape, PARAMS // shards)
    both = ("bucket", "dp")
    return jax.shard_map(
        functools.partial(local, plan),
        mesh=mesh,
        in_specs=(P(both, None), P(both, None), P(both), P(both), P(), P(both), P(both), P(both)),
        out_specs=(P(both, None), P(both, None), P(both), P(both), P(both), P(), P()),
        check_vma=False,
    )
```

time: 200 us -> 161 us (0.81); the launches traced: 197 us -> 162 us
  Pallas kernels: 82.6 us -> 56.4 us
  local copies, waits for them, and re-layouts: 12.2 us -> 3.89 us
  other arithmetic: 5.68 us -> 0 us
  starting transfers between devices: 39.7 us -> 42.5 us
  waiting for transfers between devices: 56 us -> 58 us
    pallas_call x1, Pallas kernels: 31.5 us -> 13.7 us  [backward(): pl.pallas_call(functools.partial(backward_kernel, plan), out_shape=(jax.S...]
    pallas_call x1, Pallas kernels: 18.3 us -> 6.4 us  [forward(): pl.pallas_call(functools.partial(forward_kernel, plan), out_shape=(jax.Sh...]
    pallas_call x1 -> x10, Pallas kernels: 4.77 us -> 13.3 us  [the longest x1 6.29 us: finish_part(): pl.pallas_call(functools.partial(finish_kernel, plan), out_shape=(jax.Sha...]
    add x5 -> x0, other arithmetic: 3.25 us -> none  [the longest x3 1.4 us: tree_sum(): return parts[0] + parts[1] + (parts[2] + parts[3])]
    slice x3, local copies, waits for them, and re-layouts: 4.91 us -> 2.1 us  [as_flat(): return rows.reshape(-1)[:plan.shard]]
    ppermute x28 -> x27, starting transfers between devices: 39.7 us -> 42.5 us  [swap(): return lax.ppermute(x, axis, [(i, i ^ mask) for i in range(size)])]
    ppermute x28 -> x27, waiting for transfers between devices: 56 us -> 58 us  [swap(): return lax.ppermute(x, axis, [(i, i ^ mask) for i in range(size)])]
  transfers between devices with their start and end apart: 28 -> 27, of which waited for: 13 -> 16; matrix products, arithmetic and copies ran while one was open for 4% -> 1% of each run, Pallas kernels for 16% -> 20%
where the time goes in v2:
time: 161 us; the launch traced here: 162 us
  waiting for transfers between devices  58 us (36%)
  Pallas kernels  56.4 us (35%)
  starting transfers between devices  42.5 us (26%)
  local copies, waits for them, and re-layouts  3.89 us (2%)
    ppermute x27, waiting for transfers between devices, swap(): return lax.ppermute(x, axis, [(i, i ^ mask) for i in range(size)])  58 us
    ppermute x27, starting transfers between devices, swap(): return lax.ppermute(x, axis, [(i, i ^ mask) for i in range(size)])  42.5 us
    pallas_call x1, Pallas kernels, middle_part(): pl.pallas_call(functools.partial(middle_kernel, plan), out_shape=(jax.Sha...  20.8 us
    pallas_call x1, Pallas kernels, backward(): pl.pallas_call(functools.partial(backward_kernel, plan), out_shape=(jax.S...  13.7 us
    pallas_call x1, Pallas kernels, forward(): pl.pallas_call(functools.partial(forward_kernel, plan), out_shape=(jax.Sh...  6.4 us
    pallas_call x1, Pallas kernels, finish_part(): pl.pallas_call(functools.partial(finish_kernel, plan), out_shape=(jax.Sha...  6.29 us
    pallas_call x1, Pallas kernels, project_part(): pl.pallas_call(functools.partial(project_kernel, plan), out_shape=(jax.Sh...  5.56 us
  transfers between devices with their start and end apart: 27, of which 16 were waited for; matrix products, arithmetic and copies ran while one was open for 1% of the time, Pallas kernels for 20%

profile of v2, /device:TPU:0, one launch (start us, length us, event | category | flops | bytes accessed | tf_op | source)
XLA Modules:
  0.0 161.7 jit_solution(2248668954606463375)
XLA Ops:
  2.5 3.1 %collective-permute-start = (bf16[448,128]{1,0:T(8,128)(2,1)S(1)}, bf16[448,128]{1,0:T(8,128)(2,1)S(1)}, u32[]{:S(2)}, u32[]{:S(2)}) collective-permute-start(bf16[448,128]{1,0:T(8,128)(2,1)S(1)} %shard_map.135.refs_0_), channel_id=1, source_target_pairs={{0,2},{1,3},{2,0},{3,1},{4,6},{5,7},{6,4},{7,5},{8,10},{9,11},{10,... | collective-permute-start | bytes 344072 | tf_op jit(solution)/shard_map/ppermute | solution.py:1049
  5.6 2.6 %collective-permute-start.1 = (bf16[448,128]{1,0:T(8,128)(2,1)S(1)}, bf16[448,128]{1,0:T(8,128)(2,1)S(1)}, u32[]{:S(2)}, u32[]{:S(2)}) collective-permute-start(bf16[448,128]{1,0:T(8,128)(2,1)S(1)} %shard_map.135.refs_0_), channel_id=1, source_target_pairs={{0,4},{1,5},{2,6},{3,7},{4,0},{5,1},{6,2},{7,3},{8,12},{9,13},{10,... | collective-permute-start | bytes 344072 | tf_op jit(solution)/shard_map/ppermute | solution.py:1049
  8.7 8.5 %collective-permute-done.1.refs_2_ = bf16[448,128]{1,0:T(8,128)(2,1)S(1)} collective-permute-done((bf16[448,128]{1,0:T(8,128)(2,1)S(1)}, bf16[448,128]{1,0:T(8,128)(2,1)S(1)}, u32[]{:S(2)}, u32[]{:S(2)}) %collective-permute-start.1) | collective-permute-done | bytes 114720 | tf_op jit(solution)/shard_map/ppermute | solution.py:1049
  17.3 1.6 collective-permute-start.3
  18.9 1.5 collective-permute-start.4
  20.9 10.0 %collective-permute-done.3.refs_1_ = bf16[4,448,128]{2,1,0:T(8,128)(2,1)S(1)} collective-permute-done((bf16[4,448,128]{2,1,0:T(8,128)(2,1)S(1)}, bf16[4,448,128]{2,1,0:T(8,128)(2,1)S(1)}, u32[]{:S(2)}, u32[]{:S(2)}) %collective-permute-start.3) | collective-permute-done | bytes 458784 | tf_op jit(solution)/shard_map/ppermute | solution.py:1049
  30.9 7.6 %collective-permute-done.4.refs_2_ = bf16[4,448,128]{2,1,0:T(8,128)(2,1)S(1)} collective-permute-done((bf16[4,448,128]{2,1,0:T(8,128)(2,1)S(1)}, bf16[4,448,128]{2,1,0:T(8,128)(2,1)S(1)}, u32[]{:S(2)}, u32[]{:S(2)}) %collective-permute-start.4) | collective-permute-done | bytes 458784 | tf_op jit(solution)/shard_map/ppermute | solution.py:1049
  39.2 3.4 %collective-permute-done.6.other_ref = bf16[4,512,128]{2,1,0:T(8,128)(2,1)S(1)} collective-permute-done((bf16[4,512,128]{2,1,0:T(8,128)(2,1)S(1)}, bf16[4,512,128]{2,1,0:T(8,128)(2,1)S(1)}, u32[]{:S(2)}, u32[]{:S(2)}) %collective-permute-start.6) | collective-permute-done | bytes 524320 | tf_op jit(solution)/shard_map/ppermute | solution.py:1049
  42.6 5.6 %shard_map.138 = (bf16[384,1152]{1,0:T(8,128)(2,1)S(1)}, f32[8,384]{1,0:T(8,128)S(1)}, f32[8,128]{1,0:T(8,128)S(1)}, f32[8,128]{1,0:T(8,128)S(1)}, bf16[1024,384...) custom-call(bf16[4,512,128]{2,1,0:T(8,128)(2,1)S(1)} %get-tuple-elem, ...), custom_call_target="tpu_custom_call" | custom-call | flops 1000 | bytes 1000 | tf_op jit(solution)/shard_map/pallas_call | solution.py:311
  48.2 6.4 %shard_map.139 = (bf16[1024,384]{1,0:T(8,128)(2,1)S(1)}, bf16[4,384,256]{2,1,0:T(8,128)(2,1)S(1)}, f32[4,8,256]{2,1,0:T(8,128)S(1)}) custom-call(s32[1024]{0:T(1024)S(1)} %copy-done.2, s32[1,1024]{1,0:T(1,128)S(1)} %bitcast.34, s32[1,1024]{1,0:T(1,128)S(1)} %bitcast.37, bf16[1024,384]{1,0:T(8,128)(2,1)S(1)} %get-tuple-element.57.q_ref, ...), custom_call_target="tpu_custom_call" | custom-call | flops 1000 | bytes 1000 | tf_op jit(solution)/shard_map/pallas_call | solution.py:407
  54.6 20.8 %shard_map.140 = (bf16[1024,384]{1,0:T(8,128)(2,1)}, f32[1024,384]{1,0:T(8,128)S(1)}, bf16[1024,384]{1,0:T(8,128)(2,1)S(1)}, bf16[3,4,448,128]{3,2,1,0:T(8,128)(...) custom-call(bf16[1024,384]{1,0:T(8,128)(2,1)S(1)} %copy-done, ...), custom_call_target="tpu_custom_call" | custom-call | flops 1000 | bytes 1000 | tf_op jit(solution)/shard_map/pallas_call | solution.py:554
  75.4 1.5 collective-permute-start.8
  76.9 2.8 %collective-permute-done.8.refs_1_ = bf16[3,4,448,128]{3,2,1,0:T(8,128)(2,1)S(1)} collective-permute-done((bf16[3,4,448,128]{3,2,1,0:T(8,128)(2,1)S(1)}, bf16[3,4,448,128]{3,2,1,0:T(8,128)(2,1)S(1)}, u32[]{:S(2)}, u32[]{:S(2)}) %collective-permute-start.8) | collective-permute-done | bytes 1376288 | tf_op jit(solution)/shard_map/ppermute | solution.py:1049
  80.0 3.1 %collective-permute-start.9 = (bf16[3,1,448,128]{3,2,0,1:T(8,128)(2,1)S(1)}, bf16[3,1,448,128]{3,2,0,1:T(8,128)(2,1)S(1)}, u32[]{:S(2)}, u32[]{:S(2)}) collective-permute-start(bf16[3,1,448,128]{3,2,0,1:T(8,128)(2,1)S(1)} %bitcast.42), channel_id=1, source_target_pairs={{0,2},{1,3},{2,0},{3,1},{4,6},{5,7},{6,4},{7,5},{8,10},{9,11},{10,... | collective-permute-start | bytes 1032200 | tf_op jit(solution)/shard_map/ppermute | solution.py:1049
  84.1 1.4 collective-permute-start.11
  85.5 13.7 %shard_map.142 = (bf16[1024,1152]{1,0:T(8,128)(2,1)S(1)}, f32[8,384]{1,0:T(8,128)S(1)}) custom-call(f32[8,384]{1,0:T(8,128)S(1)} %get-tuple-element.65.vec_ref, s32[1024]{0:T(1024)S(1)} %copy-done.2, s32[1,1024]{1,0:T(1,128)S(1)} %bitcast.35, s32[1,1024]{1,0:T(1,128)S(1)} %bitcast.39, f32[4,8,256]{2,1,0:T(8,128)S(1)} %get-tuple-element.71.lse_ref, ...), custom_call_target="tpu_custom_call" | custom-call | flops 1000 | bytes 1000 | tf_op jit(solution)/shard_map/pallas_call | solution.py:701
  99.2 6.3 %shard_map.143 = (f32[1024,384]{1,0:T(8,128)}, bf16[4,480,128]{2,1,0:T(8,128)(2,1)S(1)}, bf16[4,240,128]{2,1,0:T(8,128)(2,1)S(1)}, bf16[4,240,128]{2,1,0:T(8,128)(2,1)S(1)}) custom-call(bf16[1024,384]{1,0:T(8,128)(2,1)S(1)} %copy-done, bf16[384,1152]{1,0:T(8,128)(2,1)S(1)} %get-tuple-element.67.wq_ref, f32[8,384]{1,0:T(8,128)S(1)} %get-tuple-element.65.vec_ref, ...), custom_call_target="tpu_custom_call" | custom-call | flops 1000 | bytes 1000 | tf_op jit(solution)/shard_map/pallas_call | solution.py:794
  105.5 2.4 %collective-permute-start.12 = (bf16[4,240,128]{2,1,0:T(8,128)(2,1)S(1)}, bf16[4,240,128]{2,1,0:T(8,128)(2,1)S(1)}, u32[]{:S(2)}, u32[]{:S(2)}) collective-permute-start(bf16[4,240,128]{2,1,0:T(8,128)(2,1)S(1)} %get-tuple-element.87), channel_id=1, source_target_pairs={{0,1},{1,0},{2,3},{3,2},{4,5},{5,4},{6,7},{7,6},{8,9},{9,8},{10,11... | collective-permute-start | bytes 737288 | tf_op jit(solution)/shard_map/ppermute | solution.py:1049
  108.0 1.6 collective-permute-done.10
  110.5 6.9 %collective-permute-start.14 = (bf16[1,480,128]{2,1,0:T(8,128)(2,1)S(1)}, bf16[1,480,128]{2,1,0:T(8,128)(2,1)S(1)}, u32[]{:S(2)}, u32[]{:S(2)}) collective-permute-start(bf16[1,480,128]{2,1,0:T(8,128)(2,1)S(1)} %get-tuple-element.91), channel_id=1, source_target_pairs={{0,2},{1,3},{2,0},{3,1},{4,6},{5,7},{6,4},{7,5},{8,10},{9,11},{10,... | collective-permute-start | bytes 368648 | tf_op jit(solution)/shard_map/ppermute | solution.py:1049
  118.4 1.5 collective-permute-start.16
  119.8 1.6 collective-permute-done.14
  121.4 7.4 %collective-permute-done.15 = bf16[1,480,128]{2,1,0:T(8,128)(2,1)S(1)} collective-permute-done((bf16[1,480,128]{2,1,0:T(8,128)(2,1)S(1)}, bf16[1,480,128]{2,1,0:T(8,128)(2,1)S(1)}, u32[]{:S(2)}, u32[]{:S(2)}) %collective-permute-start.15) | collective-permute-done | bytes 122912 | tf_op jit(solution)/shard_map/ppermute | solution.py:1049
  130.0 2.3 %collective-permute-start.18 = (bf16[928,128]{1,0:T(8,128)(2,1)S(1)}, bf16[928,128]{1,0:T(8,128)(2,1)S(1)}, u32[]{:S(2)}, u32[]{:S(2)}) collective-permute-start(bf16[928,128]{1,0:T(8,128)(2,1)S(1)} %get-tuple-element.96), channel_id=1, source_target_pairs={{0,16},{8,24},{16,0},{24,8},{1,17},{9,25},{17,1},{25,9},{2,18},{10... | collective-permute-start | bytes 712712 | tf_op jit(solution)/shard_map/ppermute | solution.py:1049
  133.7 3.7 %collective-permute-done.17.got0_ref = bf16[928,128]{1,0:T(8,128)(2,1)S(1)} collective-permute-done((bf16[928,128]{1,0:T(8,128)(2,1)S(1)}, bf16[928,128]{1,0:T(8,128)(2,1)S(1)}, u32[]{:S(2)}, u32[]{:S(2)}) %collective-permute-start.17) | collective-permute-done | bytes 237600 | tf_op jit(solution)/shard_map/ppermute | solution.py:1049
  137.4 3.0 %collective-permute-done.18.got1_ref = bf16[928,128]{1,0:T(8,128)(2,1)S(1)} collective-permute-done((bf16[928,128]{1,0:T(8,128)(2,1)S(1)}, bf16[928,128]{1,0:T(8,128)(2,1)S(1)}, u32[]{:S(2)}, u32[]{:S(2)}) %collective-permute-start.18) | collective-permute-done | bytes 237600 | tf_op jit(solution)/shard_map/ppermute | solution.py:1049
  140.4 1.8 %collective-permute-done.19.got2_ref = bf16[928,128]{1,0:T(8,128)(2,1)S(1)} collective-permute-done((bf16[928,128]{1,0:T(8,128)(2,1)S(1)}, bf16[928,128]{1,0:T(8,128)(2,1)S(1)}, u32[]{:S(2)}, u32[]{:S(2)}) %collective-permute-start.19) | collective-permute-done | bytes 237600 | tf_op jit(solution)/shard_map/ppermute | solution.py:1049
  144.6 3.2 %collective-permute-start.21 = (f32[8,128]{1,0:T(8,128)S(1)}, f32[8,128]{1,0:T(8,128)S(1)}, u32[]{:S(2)}, u32[]{:S(2)}) collective-permute-start(f32[8,128]{1,0:T(8,128)S(1)} %shard_map.148.refs_0_), channel_id=1, source_target_pairs={{0,2},{1,3},{2,0},{3,1},{4,6},{5,7},{6,4},{7,5},{8,10},{9,11},{10,... | collective-permute-start | bytes 12296 | tf_op jit(solution)/shard_map/ppermute | solution.py:1049
  147.8 2.4 %collective-permute-start.23 = (f32[8,128]{1,0:T(8,128)S(1)}, f32[8,128]{1,0:T(8,128)S(1)}, u32[]{:S(2)}, u32[]{:S(2)}) collective-permute-start(f32[8,128]{1,0:T(8,128)S(1)} %shard_map.148.refs_0_), channel_id=1, source_target_pairs={{0,6},{1,7},{2,4},{3,5},{4,2},{5,3},{6,0},{7,1},{8,14},{9,15},{10,... | collective-permute-start | bytes 12296 | tf_op jit(solution)/shard_map/ppermute | solution.py:1049
  150.2 2.1 %collective-permute-done.22.refs_2_ = f32[8,128]{1,0:T(8,128)S(1)} collective-permute-done((f32[8,128]{1,0:T(8,128)S(1)}, f32[8,128]{1,0:T(8,128)S(1)}, u32[]{:S(2)}, u32[]{:S(2)}) %collective-permute-start.22) | collective-permute-done | bytes 4128 | tf_op jit(solution)/shard_map/ppermute | solution.py:1049
  153.8 1.7 %collective-permute-start.25 = (f32[8,128]{1,0:T(8,128)S(1)}, f32[8,128]{1,0:T(8,128)S(1)}, u32[]{:S(2)}, u32[]{:S(2)}) collective-permute-start(f32[8,128]{1,0:T(8,128)S(1)} %shard_map.149.refs_0_), channel_id=1, source_target_pairs={{0,16},{8,24},{16,0},{24,8},{1,17},{9,25},{17,1},{25,9},{2,18},{10... | collective-permute-start | bytes 12296 | tf_op jit(solution)/shard_map/ppermute | solution.py:1049
  158.1 1.9 %collective-permute-done.26.refs_3_ = f32[8,128]{1,0:T(8,128)S(1)} collective-permute-done((f32[8,128]{1,0:T(8,128)S(1)}, f32[8,128]{1,0:T(8,128)S(1)}, u32[]{:S(2)}, u32[]{:S(2)}) %collective-permute-start.26) | collective-permute-done | bytes 4128 | tf_op jit(solution)/shard_map/ppermute | solution.py:1049
  (59 shorter events, 17.6 us)
Async XLA Ops:
  1.6 41.0 %copy-start = (bf16[1024,384]{1,0:T(8,128)(2,1)S(1)}, bf16[1024,384]{1,0:T(8,128)(2,1)}, u32[]{:S(2)}) copy-start(bf16[1024,384]{1,0:T(8,128)(2,1)} %tokens_ref.5) | copy-start | bytes 2359300
  2.5 6.2 %collective-permute-start = (bf16[448,128]{1,0:T(8,128)(2,1)S(1)}, bf16[448,128]{1,0:T(8,128)(2,1)S(1)}, u32[]{:S(2)}, u32[]{:S(2)}) collective-permute-start(bf16[448,128]{1,0:T(8,128)(2,1)S(1)} %shard_map.135.refs_0_), channel_id=1, source_target_pairs={{0,2},{1,3},{2,0},{3,1},{4,6},{5,7},{6,4},{7,5},{8,10},{9,11},{10,... | collective-permute-start | bytes 344072 | tf_op jit(solution)/shard_map/ppermute | solution.py:1049
  5.6 11.7 %collective-permute-start.1 = (bf16[448,128]{1,0:T(8,128)(2,1)S(1)}, bf16[448,128]{1,0:T(8,128)(2,1)S(1)}, u32[]{:S(2)}, u32[]{:S(2)}) collective-permute-start(bf16[448,128]{1,0:T(8,128)(2,1)S(1)} %shard_map.135.refs_0_), channel_id=1, source_target_pairs={{0,4},{1,5},{2,6},{3,7},{4,0},{5,1},{6,2},{7,3},{8,12},{9,13},{10,... | collective-permute-start | bytes 344072 | tf_op jit(solution)/shard_map/ppermute | solution.py:1049
  8.2 9.1 %collective-permute-start.2 = (bf16[448,128]{1,0:T(8,128)(2,1)S(1)}, bf16[448,128]{1,0:T(8,128)(2,1)S(1)}, u32[]{:S(2)}, u32[]{:S(2)}) collective-permute-start(bf16[448,128]{1,0:T(8,128)(2,1)S(1)} %shard_map.135.refs_0_), channel_id=1, source_target_pairs={{0,6},{1,7},{2,4},{3,5},{4,2},{5,3},{6,0},{7,1},{8,14},{9,15},{10,... | collective-permute-start | bytes 344072 | tf_op jit(solution)/shard_map/ppermute | solution.py:1049
  17.3 30.8 %copy-start.2 = (s32[1024]{0:T(1024)S(1)}, s32[1024]{0:T(1024)}, u32[]{:S(2)}) copy-start(s32[1024]{0:T(1024)} %seg_smem.3) | copy-start | bytes 12292
  17.3 30.8 %copy-start.4 = (s32[1024]{0:T(1024)S(1)}, s32[1024]{0:T(1024)}, u32[]{:S(2)}) copy-start(s32[1024]{0:T(1024)} %param.11) | copy-start | bytes 12292
  17.3 13.5 %collective-permute-start.3 = (bf16[4,448,128]{2,1,0:T(8,128)(2,1)S(1)}, bf16[4,448,128]{2,1,0:T(8,128)(2,1)S(1)}, u32[]{:S(2)}, u32[]{:S(2)}) collective-permute-start(bf16[4,448,128]{2,1,0:T(8,128)(2,1)S(1)} %shard_map.136.refs_0_), channel_id=1, source_target_pairs={{0,8},{8,0},{16,24},{24,16},{1,9},{9,1},{17,25},{25,17},{2,10},{10... | collective-permute-start | bytes 1376264 | tf_op jit(solution)/shard_map/ppermute | solution.py:1049
  18.9 19.5 %collective-permute-start.4 = (bf16[4,448,128]{2,1,0:T(8,128)(2,1)S(1)}, bf16[4,448,128]{2,1,0:T(8,128)(2,1)S(1)}, u32[]{:S(2)}, u32[]{:S(2)}) collective-permute-start(bf16[4,448,128]{2,1,0:T(8,128)(2,1)S(1)} %shard_map.136.refs_0_), channel_id=1, source_target_pairs={{0,16},{8,24},{16,0},{24,8},{1,17},{9,25},{17,1},{25,9},{2,18},{10... | collective-permute-start | bytes 1376264 | tf_op jit(solution)/shard_map/ppermute | solution.py:1049
  20.4 18.0 %collective-permute-start.5 = (bf16[4,448,128]{2,1,0:T(8,128)(2,1)S(1)}, bf16[4,448,128]{2,1,0:T(8,128)(2,1)S(1)}, u32[]{:S(2)}, u32[]{:S(2)}) collective-permute-start(bf16[4,448,128]{2,1,0:T(8,128)(2,1)S(1)} %shard_map.136.refs_0_), channel_id=1, source_target_pairs={{0,24},{8,16},{16,8},{24,0},{1,25},{9,17},{17,9},{25,1},{2,26},{10... | collective-permute-start | bytes 1376264 | tf_op jit(solution)/shard_map/ppermute | solution.py:1049
  38.6 16.0 %collective-permute-start.7 = (bf16[12,448,128]{2,1,0:T(8,128)(2,1)S(1)}, bf16[12,448,128]{2,1,0:T(8,128)(2,1)S(1)}, u32[]{:S(2)}, u32[]{:S(2)}) collective-permute-start(bf16[12,448,128]{2,1,0:T(8,128)(2,1)S(1)} %get-tuple-element.62.own_ref), channel_id=1, source_target_pairs={{0,1},{1,0},{2,3},{3,2},{4,5},{5,4},{6,7},{7,6},{8,9},{9,8},{10,11... | collective-permute-start | bytes 4128776 | tf_op jit(solution)/shard_map/ppermute | solution.py:1049
  38.7 3.9 %collective-permute-start.6 = (bf16[4,512,128]{2,1,0:T(8,128)(2,1)S(1)}, bf16[4,512,128]{2,1,0:T(8,128)(2,1)S(1)}, u32[]{:S(2)}, u32[]{:S(2)}) collective-permute-start(bf16[4,512,128]{2,1,0:T(8,128)(2,1)S(1)} %get-tuple-element.56.own_ref), channel_id=1, source_target_pairs={{0,1},{1,0},{2,3},{3,2},{4,5},{5,4},{6,7},{7,6},{8,9},{9,8},{10,11... | collective-permute-start | bytes 1572872 | tf_op jit(solution)/shard_map/ppermute | solution.py:1049
  75.4 4.2 %collective-permute-start.8 = (bf16[3,4,448,128]{3,2,1,0:T(8,128)(2,1)S(1)}, bf16[3,4,448,128]{3,2,1,0:T(8,128)(2,1)S(1)}, u32[]{:S(2)}, u32[]{:S(2)}) collective-permute-start(bf16[3,4,448,128]{3,2,1,0:T(8,128)(2,1)S(1)} %get-tuple-element.76), channel_id=1, source_target_pairs={{0,1},{1,0},{2,3},{3,2},{4,5},{5,4},{6,7},{7,6},{8,9},{9,8},{10,11... | collective-permute-start | bytes 4128776 | tf_op jit(solution)/shard_map/ppermute | solution.py:1049
  80.0 28.0 %collective-permute-start.9 = (bf16[3,1,448,128]{3,2,0,1:T(8,128)(2,1)S(1)}, bf16[3,1,448,128]{3,2,0,1:T(8,128)(2,1)S(1)}, u32[]{:S(2)}, u32[]{:S(2)}) collective-permute-start(bf16[3,1,448,128]{3,2,0,1:T(8,128)(2,1)S(1)} %bitcast.42), channel_id=1, source_target_pairs={{0,2},{1,3},{2,0},{3,1},{4,6},{5,7},{6,4},{7,5},{8,10},{9,11},{10,... | collective-permute-start | bytes 1032200 | tf_op jit(solution)/shard_map/ppermute | solution.py:1049
  83.0 26.6 %collective-permute-start.10 = (bf16[3,1,448,128]{3,2,0,1:T(8,128)(2,1)S(1)}, bf16[3,1,448,128]{3,2,0,1:T(8,128)(2,1)S(1)}, u32[]{:S(2)}, u32[]{:S(2)}) collective-permute-start(bf16[3,1,448,128]{3,2,0,1:T(8,128)(2,1)S(1)} %bitcast.41), channel_id=1, source_target_pairs={{0,4},{1,5},{2,6},{3,7},{4,0},{5,1},{6,2},{7,3},{8,12},{9,13},{10,... | collective-permute-start | bytes 1032200 | tf_op jit(solution)/shard_map/ppermute | solution.py:1049
  84.1 25.5 %collective-permute-start.11 = (bf16[3,1,448,128]{3,2,0,1:T(8,128)(2,1)S(1)}, bf16[3,1,448,128]{3,2,0,1:T(8,128)(2,1)S(1)}, u32[]{:S(2)}, u32[]{:S(2)}) collective-permute-start(bf16[3,1,448,128]{3,2,0,1:T(8,128)(2,1)S(1)} %bitcast.40), channel_id=1, source_target_pairs={{0,6},{1,7},{2,4},{3,5},{4,2},{5,3},{6,0},{7,1},{8,14},{9,15},{10,... | collective-permute-start | bytes 1032200 | tf_op jit(solution)/shard_map/ppermute | solution.py:1049
  105.5 4.3 %collective-permute-start.12 = (bf16[4,240,128]{2,1,0:T(8,128)(2,1)S(1)}, bf16[4,240,128]{2,1,0:T(8,128)(2,1)S(1)}, u32[]{:S(2)}, u32[]{:S(2)}) collective-permute-start(bf16[4,240,128]{2,1,0:T(8,128)(2,1)S(1)} %get-tuple-element.87), channel_id=1, source_target_pairs={{0,1},{1,0},{2,3},{3,2},{4,5},{5,4},{6,7},{7,6},{8,9},{9,8},{10,11... | collective-permute-start | bytes 737288 | tf_op jit(solution)/shard_map/ppermute | solution.py:1049
  108.0 1.8 %collective-permute-start.13 = (bf16[4,240,128]{2,1,0:T(8,128)(2,1)S(1)}, bf16[4,240,128]{2,1,0:T(8,128)(2,1)S(1)}, u32[]{:S(2)}, u32[]{:S(2)}) collective-permute-start(bf16[4,240,128]{2,1,0:T(8,128)(2,1)S(1)} %get-tuple-element.88), channel_id=1, source_target_pairs={{0,1},{1,0},{2,3},{3,2},{4,5},{5,4},{6,7},{7,6},{8,9},{9,8},{10,11... | collective-permute-start | bytes 737288 | tf_op jit(solution)/shard_map/ppermute | solution.py:1049
  109.8 23.9 %copy-start.6 = (f32[55368]{0:T(1024)S(1)}, f32[55368]{0:T(1024)}, u32[]{:S(2)}) copy-start(f32[55368]{0:T(1024)} %param.15) | copy-start | bytes 664420
  109.8 23.9 %copy-start.7 = (f32[55368]{0:T(1024)S(1)}, f32[55368]{0:T(1024)}, u32[]{:S(2)}) copy-start(f32[55368]{0:T(1024)} %param.14) | copy-start | bytes 664420
  110.5 10.9 %collective-permute-start.14 = (bf16[1,480,128]{2,1,0:T(8,128)(2,1)S(1)}, bf16[1,480,128]{2,1,0:T(8,128)(2,1)S(1)}, u32[]{:S(2)}, u32[]{:S(2)}) collective-permute-start(bf16[1,480,128]{2,1,0:T(8,128)(2,1)S(1)} %get-tuple-element.91), channel_id=1, source_target_pairs={{0,2},{1,3},{2,0},{3,1},{4,6},{5,7},{6,4},{7,5},{8,10},{9,11},{10,... | collective-permute-start | bytes 368648 | tf_op jit(solution)/shard_map/ppermute | solution.py:1049
  117.3 11.5 %collective-permute-start.15 = (bf16[1,480,128]{2,1,0:T(8,128)(2,1)S(1)}, bf16[1,480,128]{2,1,0:T(8,128)(2,1)S(1)}, u32[]{:S(2)}, u32[]{:S(2)}) collective-permute-start(bf16[1,480,128]{2,1,0:T(8,128)(2,1)S(1)} %get-tuple-element.92), channel_id=1, source_target_pairs={{0,4},{1,5},{2,6},{3,7},{4,0},{5,1},{6,2},{7,3},{8,12},{9,13},{10,... | collective-permute-start | bytes 368648 | tf_op jit(solution)/shard_map/ppermute | solution.py:1049
  118.4 10.5 %collective-permute-start.16 = (bf16[1,480,128]{2,1,0:T(8,128)(2,1)S(1)}, bf16[1,480,128]{2,1,0:T(8,128)(2,1)S(1)}, u32[]{:S(2)}, u32[]{:S(2)}) collective-permute-start(bf16[1,480,128]{2,1,0:T(8,128)(2,1)S(1)} %get-tuple-element.93), channel_id=1, source_target_pairs={{0,6},{1,7},{2,4},{3,5},{4,2},{5,3},{6,0},{7,1},{8,14},{9,15},{10,... | collective-permute-start | bytes 368648 | tf_op jit(solution)/shard_map/ppermute | solution.py:1049
  129.0 8.5 %collective-permute-start.17 = (bf16[928,128]{1,0:T(8,128)(2,1)S(1)}, bf16[928,128]{1,0:T(8,128)(2,1)S(1)}, u32[]{:S(2)}, u32[]{:S(2)}) collective-permute-start(bf16[928,128]{1,0:T(8,128)(2,1)S(1)} %get-tuple-element.95), channel_id=1, source_target_pairs={{0,8},{8,0},{16,24},{24,16},{1,9},{9,1},{17,25},{25,17},{2,10},{10... | collective-permute-start | bytes 712712 | tf_op jit(solution)/shard_map/ppermute | solution.py:1049
  130.0 10.4 %collective-permute-start.18 = (bf16[928,128]{1,0:T(8,128)(2,1)S(1)}, bf16[928,128]{1,0:T(8,128)(2,1)S(1)}, u32[]{:S(2)}, u32[]{:S(2)}) collective-permute-start(bf16[928,128]{1,0:T(8,128)(2,1)S(1)} %get-tuple-element.96), channel_id=1, source_target_pairs={{0,16},{8,24},{16,0},{24,8},{1,17},{9,25},{17,1},{25,9},{2,18},{10... | collective-permute-start | bytes 712712 | tf_op jit(solution)/shard_map/ppermute | solution.py:1049
  132.3 9.9 %collective-permute-start.19 = (bf16[928,128]{1,0:T(8,128)(2,1)S(1)}, bf16[928,128]{1,0:T(8,128)(2,1)S(1)}, u32[]{:S(2)}, u32[]{:S(2)}) collective-permute-start(bf16[928,128]{1,0:T(8,128)(2,1)S(1)} %get-tuple-element.97), channel_id=1, source_target_pairs={{0,24},{8,16},{16,8},{24,0},{1,25},{9,17},{17,9},{25,1},{2,26},{10... | collective-permute-start | bytes 712712 | tf_op jit(solution)/shard_map/ppermute | solution.py:1049
  143.4 1.2 collective-permute-start.20
  144.6 5.6 %collective-permute-start.21 = (f32[8,128]{1,0:T(8,128)S(1)}, f32[8,128]{1,0:T(8,128)S(1)}, u32[]{:S(2)}, u32[]{:S(2)}) collective-permute-start(f32[8,128]{1,0:T(8,128)S(1)} %shard_map.148.refs_0_), channel_id=1, source_target_pairs={{0,2},{1,3},{2,0},{3,1},{4,6},{5,7},{6,4},{7,5},{8,10},{9,11},{10,... | collective-permute-start | bytes 12296 | tf_op jit(solution)/shard_map/ppermute | solution.py:1049
  147.8 4.5 %collective-permute-start.22 = (f32[8,128]{1,0:T(8,128)S(1)}, f32[8,128]{1,0:T(8,128)S(1)}, u32[]{:S(2)}, u32[]{:S(2)}) collective-permute-start(f32[8,128]{1,0:T(8,128)S(1)} %shard_map.148.refs_0_), channel_id=1, source_target_pairs={{0,4},{1,5},{2,6},{3,7},{4,0},{5,1},{6,2},{7,3},{8,12},{9,13},{10,... | collective-permute-start | bytes 12296 | tf_op jit(solution)/shard_map/ppermute | solution.py:1049
  147.8 5.4 %collective-permute-start.23 = (f32[8,128]{1,0:T(8,128)S(1)}, f32[8,128]{1,0:T(8,128)S(1)}, u32[]{:S(2)}, u32[]{:S(2)}) collective-permute-start(f32[8,128]{1,0:T(8,128)S(1)} %shard_map.148.refs_0_), channel_id=1, source_target_pairs={{0,6},{1,7},{2,4},{3,5},{4,2},{5,3},{6,0},{7,1},{8,14},{9,15},{10,... | collective-permute-start | bytes 12296 | tf_op jit(solution)/shard_map/ppermute | solution.py:1049
  153.2 4.9 %collective-permute-start.24 = (f32[8,128]{1,0:T(8,128)S(1)}, f32[8,128]{1,0:T(8,128)S(1)}, u32[]{:S(2)}, u32[]{:S(2)}) collective-permute-start(f32[8,128]{1,0:T(8,128)S(1)} %shard_map.149.refs_0_), channel_id=1, source_target_pairs={{0,8},{8,0},{16,24},{24,16},{1,9},{9,1},{17,25},{25,17},{2,10},{10... | collective-permute-start | bytes 12296 | tf_op jit(solution)/shard_map/ppermute | solution.py:1049
  153.8 4.3 %collective-permute-start.25 = (f32[8,128]{1,0:T(8,128)S(1)}, f32[8,128]{1,0:T(8,128)S(1)}, u32[]{:S(2)}, u32[]{:S(2)}) collective-permute-start(f32[8,128]{1,0:T(8,128)S(1)} %shard_map.149.refs_0_), channel_id=1, source_target_pairs={{0,16},{8,24},{16,0},{24,8},{1,17},{9,25},{17,1},{25,9},{2,18},{10... | collective-permute-start | bytes 12296 | tf_op jit(solution)/shard_map/ppermute | solution.py:1049
  155.6 4.5 %collective-permute-start.26 = (f32[8,128]{1,0:T(8,128)S(1)}, f32[8,128]{1,0:T(8,128)S(1)}, u32[]{:S(2)}, u32[]{:S(2)}) collective-permute-start(f32[8,128]{1,0:T(8,128)S(1)} %shard_map.149.refs_0_), channel_id=1, source_target_pairs={{0,24},{8,16},{16,8},{24,0},{1,25},{9,17},{17,9},{25,1},{2,26},{10... | collective-permute-start | bytes 12296 | tf_op jit(solution)/shard_map/ppermute | solution.py:1049
  (3 other events, 13.7 us)

commit v3 on v2

--- a/solution.py
+++ b/solution.py
@@ -20,6 +20,8 @@
 TILE = 256
 TILES = SEQ // TILE
 BLOCKS = SEQ // LANES
+MIDDLE_BLOCK = 512
+FAR_PARTS = 3
 
 norm_epsilon = 1e-06
 adam_epsilon = 1e-06
@@ -72,7 +74,7 @@
             -(-((k + 1) * shard) // LANES) - self.start[k] for k in range(self.n)
         ]
         self.win = round_up(max(self.rows) + 1, 16)
-        self.tail = round_up(self.win + VEC_ROWS, 16)
+        self.tail = round_up(self.win + VEC_ROWS, 16 * FAR_PARTS)
         self.vec_place = ROW_VEC - self.start[-1]
         self.vec_from = self.vec_place // 16 * 16
         self.kept_row = 2 * self.win - self.vec_from
@@ -96,6 +98,8 @@
 
 
 def rows_at(step):
+    if isinstance(step, int):
+        return slice(step * TILE, (step + 1) * TILE)
     return pl.ds(pl.multiple_of(step * TILE, TILE), TILE)
 
 
@@ -165,9 +169,11 @@
     )
 
 
-def lay_windows(plan, owners, rel_of, own_ref, other_ref, flat, base):
+def lay_windows(plan, owners, refs_of, flat, base):
+    dp = lax.axis_index("dp")
     for k in owners:
-        window = held_window(own_ref, other_ref, rel_of(k), slice(0, plan.win))
+        own_ref, other_ref = refs_of(k)
+        window = held_window(own_ref, other_ref, jnp.bitwise_xor(dp, k % plan.nd), slice(0, plan.win))
         first, count = plan.start[k] - base, plan.rows[k]
         shared = k > 0 and (k * plan.shard) % LANES
         if shared:
@@ -263,7 +269,7 @@
     flat,
 ):
     dp = lax.axis_index("dp")
-    lay_windows(plan, range(plan.nd), lambda k: jnp.bitwise_xor(dp, k), own_ref, other_ref, flat, 0)
+    lay_windows(plan, range(plan.nd), lambda k: (own_ref, other_ref), flat, 0)
     take_matrix(wq_ref, flat, 0, D, 3 * D)
     head_ref[...] = flat[ROW_OUT : ROW_OUT + 8, :]
     rel = jnp.bitwise_xor(dp, plan.nd - 1)
@@ -281,28 +287,22 @@
     gain1, shift1 = vec_ref[0:1, :], vec_ref[1:2, :]
     gain_q, gain_k = vec_ref[2:3, :], vec_ref[3:4, :]
 
-    def project(step, carry):
-        at = rows_at(step)
-        hat, _ = norm_parts(tokens_ref[at, :].astype(F32))
-        low = (hat * gain1 + shift1).astype(BF)
-        raw = nn(low, wq_ref[...])
-
-        def head_norm(low_out, part, gain):
-            lanes = slice(part * D, (part + 1) * D)
-            x = raw[:, lanes]
-            centered = x - head_mean(x, matrix)
-            rstd = lax.rsqrt(head_mean(centered * centered, matrix) + norm_epsilon)
-            normed = centered * rstd
-            hat_ref[at, lanes] = normed
-            rstd_ref[at, lanes] = rstd
-            low_out[at, :] = (normed * gain).astype(BF)
-
-        head_norm(q_ref, 0, gain_q)
-        head_norm(k_ref, 1, gain_k)
-        v_ref[at, :] = raw[:, 2 * D :].astype(BF)
-        return carry
-
-    lax.fori_loop(0, TILES, project, 0)
+    hat, _ = norm_parts(tokens_ref[...].astype(F32))
+    raw = nn((hat * gain1 + shift1).astype(BF), wq_ref[...])
+
+    def head_norm(low_out, part, gain):
+        lanes = slice(part * D, (part + 1) * D)
+        x = raw[:, lanes]
+        centered = x - head_mean(x, matrix)
+        rstd = lax.rsqrt(head_mean(centered * centered, matrix) + norm_epsilon)
+        normed = centered * rstd
+        hat_ref[:, lanes] = normed
+        rstd_ref[:, lanes] = rstd
+        low_out[...] = (normed * gain).astype(BF)
+
+    head_norm(q_ref, 0, gain_q)
+    head_norm(k_ref, 1, gain_k)
+    v_ref[...] = raw[:, 2 * D :].astype(BF)
 
 
 def project_part(plan, own, other, tokens):
@@ -352,14 +352,11 @@
     seg_row = seg_ref[...].astype(F32)
     segk[...] = to_column(jnp.where(keep_ref[...] == 1, seg_row, -1.0))
 
-    def stack(step, carry):
+    for step in range(TILES):
         at = rows_at(step)
         for hp in range(PAIRS):
             put_blocks(kab, hp, step, k_ref[at, hp * LANES : (hp + 1) * LANES])
         vt[:, at] = jnp.transpose(v_ref[at, :].astype(F32)).astype(BF)
-        return carry
-
-    lax.fori_loop(0, TILES, stack, 0)
 
     def query_tile(ti, carry):
         ot[...] = jnp.zeros_like(ot)
@@ -440,14 +437,18 @@
     return jnp.where(u > 0.0, 1.0 - below, below), expo * (1.0 / math.sqrt(2.0 * math.pi))
 
 
-def middle_kernel(
+def middle_kernel(plan, *refs):
+    late_refs, rest = refs[: 2 * plan.nb - 2], refs[2 * plan.nb - 2 :]
+    middle_body(plan, late_refs, *rest)
+
+
+def middle_body(
     plan,
+    late_refs,
     tokens_ref,
     cot_ref,
     o_ref,
     ot_ref,
-    own_ref,
-    other_ref,
     head_ref,
     kept_ref,
     vec_ref,
@@ -461,9 +462,8 @@
     tail_ref,
     gvec_ref,
     keepc,
-    gout,
-    gup,
-    gdownt,
+    hid,
+    dus,
     flat,
     wo_ref,
     wu_ref,
@@ -473,12 +473,11 @@
     base = ROW_OUT
     flat[0:8, :] = head_ref[...]
     dp = lax.axis_index("dp")
+    owns, others = late_refs[: plan.nb - 1], late_refs[plan.nb - 1 :]
     lay_windows(
         plan,
         range(plan.nd, plan.n),
-        lambda k: (k // plan.nd - 1) * plan.nd + jnp.bitwise_xor(dp, k % plan.nd),
-        own_ref,
-        other_ref,
+        lambda k: (owns[k // plan.nd - 1], others[k // plan.nd - 1]),
         flat,
         base,
     )
@@ -493,44 +492,44 @@
     ones = jnp.ones((1, LANES), F32)
     scale = (plan.nb * own) * ones / (total * ones) * float(SEQ * plan.nd) / kept_ref[0:1, :]
     keepc[...] = to_column(keep_ref[...].astype(F32)) * scale
-    gout[...] = jnp.zeros_like(gout)
-    gup[...] = jnp.zeros_like(gup)
-    gdownt[...] = jnp.zeros_like(gdownt)
     gvec_ref[...] = jnp.zeros_like(gvec_ref)
 
-    def chunk(step, carry):
-        at = rows_at(step)
-        middle = tokens_ref[at, :].astype(F32) + nn(o_ref[at, :], wo_ref[...])
-        hat, rstd = norm_parts(middle)
-        low = (hat * gain2 + shift2).astype(BF)
-        u = nn(low, wu_ref[...])
+    middle = tokens_ref[...].astype(F32) + nn(o_ref[...], wo_ref[...])
+    hat, rstd = norm_parts(middle)
+    low = (hat * gain2 + shift2).astype(BF)
+    weights = keepc[...]
+    seed = cot_ref[...].astype(F32) * jnp.concatenate([weights] * (D // LANES), axis=1)
+    seed_low = seed.astype(BF)
+    for first in range(0, FF, MIDDLE_BLOCK):
+        cols = slice(first, first + MIDDLE_BLOCK)
+        u = nn(low, wu_ref[:, cols])
         phi, bell = normal_parts(u)
-        hidden = (u * phi).astype(BF)
-        out_ref[at, :] = (middle + nn(hidden, wd_ref[...])).astype(BF)
-        weights = keepc[at, :]
-        seed = cot_ref[at, :].astype(F32) * jnp.concatenate([weights] * (D // LANES), axis=1)
-        seed_low = seed.astype(BF)
-        du = (nt(seed_low, wd_ref[...]) * (phi + u * bell)).astype(BF)
-        gdownt[...] += nn(jnp.transpose(seed).astype(BF), hidden)
-        gup[...] += nn(jnp.transpose(low.astype(F32)).astype(BF), du)
-        da2 = nt(du, wu_ref[...])
-        gvec_ref[0:1, :] += jnp.sum(da2 * hat, axis=0, keepdims=True)
-        gvec_ref[1:2, :] += jnp.sum(da2, axis=0, keepdims=True)
-        dh1 = seed + norm_back(hat, rstd, da2 * gain2)
-        dh1_ref[at, :] = dh1
-        dh1_low = dh1.astype(BF)
-        gout[...] += nn(ot_ref[step], dh1_low)
-        do_ref[at, :] = nt(dh1_low, wo_ref[...]).astype(BF)
-        return carry
-
-    lax.fori_loop(0, o_ref.shape[0] // TILE, chunk, 0)
-
+        hid[:, cols] = (u * phi).astype(BF)
+        dus[:, cols] = (nt(seed_low, wd_ref[cols, :]) * (phi + u * bell)).astype(BF)
+    out_ref[...] = (middle + nn(hid[...], wd_ref[...])).astype(BF)
+    seedt = jnp.transpose(seed).astype(BF)
+    lowt = jnp.transpose(low.astype(F32)).astype(BF)
+    da2 = nt(dus[...], wu_ref[...])
+    gvec_ref[0:1, :] = jnp.sum(da2 * hat, axis=0, keepdims=True)
+    gvec_ref[1:2, :] = jnp.sum(da2, axis=0, keepdims=True)
+    dh1 = seed + norm_back(hat, rstd, da2 * gain2)
+    dh1_ref[...] = dh1
+    dh1_low = dh1.astype(BF)
+    gout = nn(jnp.concatenate([ot_ref[t] for t in range(TILES)], axis=1), dh1_low)
+    do_ref[...] = nt(dh1_low, wo_ref[...]).astype(BF)
     put_matrix(flat, 0, gout, D, D)
-    put_matrix(flat, ROW_UP - base, gup, D, FF)
-    for j in range(D // LANES):
-        flat[pl.ds(ROW_DOWN - base + j, FF, stride=D // LANES), :] = jnp.transpose(
-            gdownt[j * LANES : (j + 1) * LANES, :]
-        )
+    block = 2 * TILE
+    for i in range(FF // block):
+        part = nn(lowt, dus[:, i * block : (i + 1) * block])
+        for j in range(block // LANES):
+            flat[pl.ds(ROW_UP - base + i * (block // LANES) + j, D, stride=FF // LANES), :] = part[
+                :, j * LANES : (j + 1) * LANES
+            ]
+        part = jnp.transpose(nn(seedt, hid[:, i * block : (i + 1) * block]))
+        for j in range(D // LANES):
+            flat[
+                pl.ds(ROW_DOWN - base + i * block * (D // LANES) + j, block, stride=D // LANES), :
+            ] = part[:, j * LANES : (j + 1) * LANES]
     tail_ref[...] = flat[0:8, :]
     side = jnp.bitwise_and(dp, 1)
     for k in range(plan.nd, plan.n):
@@ -548,7 +547,7 @@
             far_ref[quarter, reld] = window
 
 
-def middle_part(plan, tokens, cot, o, ot, own, other, head, kept, vec, keep_row, patches):
+def middle_part(plan, late, tokens, cot, o, ot, head, kept, vec, keep_row, patches):
     rows = tokens.shape[0]
     windows = jax.ShapeDtypeStruct((plan.nb - 1, plan.nd // 2, plan.win, LANES), BF)
     return pl.pallas_call(
@@ -562,21 +561,20 @@
             jax.ShapeDtypeStruct((8, LANES), F32),
             jax.ShapeDtypeStruct((8, D), F32),
         ),
-        in_specs=[VMEM] * 10 + [SMEM],
+        in_specs=[VMEM] * (len(late) + 8) + [SMEM],
         out_specs=(VMEM,) * 7,
         scratch_shapes=[
             pltpu.VMEM((rows, LANES), F32),
-            pltpu.VMEM((D, D), F32),
-            pltpu.VMEM((D, FF), F32),
-            pltpu.VMEM((D, FF), F32),
+            pltpu.VMEM((rows, FF), BF),
+            pltpu.VMEM((rows, FF), BF),
             pltpu.VMEM((round_up(plan.start[-1] + plan.win - ROW_OUT, 8), LANES), F32),
             pltpu.VMEM((D, D), BF),
             pltpu.VMEM((D, FF), BF),
             pltpu.VMEM((FF, D), BF),
         ],
-        compiler_params=params(30),
+        compiler_params=params(36),
         cost_estimate=QUICK,
-    )(tokens, cot, o, ot, own, other, head, kept, vec, keep_row, patches)
+    )(*late, tokens, cot, o, ot, head, kept, vec, keep_row, patches)
 
 
 def backward_kernel(
@@ -618,7 +616,7 @@
     dv[...] = jnp.zeros_like(dv)
     gains_ref[...] = jnp.zeros_like(gains_ref)
 
-    def stack(step, carry):
+    for step in range(TILES):
         at = rows_at(step)
         keys = k_ref[at, :]
         grads = do_ref[at, :]
@@ -631,9 +629,6 @@
         kt[:, at] = jnp.transpose(keys.astype(F32)).astype(BF)
         high, rest = split_low(grads.astype(F32) * o_ref[at, :].astype(F32))
         inner_sums[step] = nt(hot, high) + nt(hot, rest)
-        return carry
-
-    lax.fori_loop(0, TILES, stack, 0)
 
     def query_tile(ti, carry):
         row_seg = seg_ref[:, rows_at(ti)].astype(F32)
@@ -728,39 +723,30 @@
     tokens_ref,
     wq_ref,
     vec_ref,
-    dh1_ref,
     tail_ref,
     gvec_ref,
     low_ref,
     gqk_ref,
-    grad_ref,
+    da1_ref,
     near_ref,
-    far0_ref,
-    far1_ref,
-    gq,
-    gains,
-    flat,
+    *refs,
 ):
-    gain1, shift1 = vec_ref[0:1, :], vec_ref[1:2, :]
-    gq[...] = jnp.zeros_like(gq)
+    *far_refs, gains, flat = refs
+    hat, _ = norm_parts(tokens_ref[...].astype(F32))
+    normed = jnp.transpose(hat * vec_ref[0:1, :] + vec_ref[1:2, :]).astype(BF)
+    for i in range(3):
+        part = nn(normed, low_ref[:, i * D : (i + 1) * D])
+        for j in range(D // LANES):
+            flat[pl.ds(i * (D // LANES) + j, D, stride=3 * D // LANES), :] = part[
+                :, j * LANES : (j + 1) * LANES
+            ]
+    da1 = nt(low_ref[...], wq_ref[...])
+    da1_ref[...] = da1
     gains[...] = jnp.zeros_like(gains)
-
-    def finish(step, carry):
-        at = rows_at(step)
-        low = low_ref[at, :]
-        hat, rstd = norm_parts(tokens_ref[at, :].astype(F32))
-        normed = hat * gain1 + shift1
-        gq[...] += nn(jnp.transpose(normed).astype(BF), low)
-        da1 = nt(low, wq_ref[...])
-        gains[0:1, :] += jnp.sum(da1 * hat, axis=0, keepdims=True)
-        gains[1:2, :] += jnp.sum(da1, axis=0, keepdims=True)
-        grad_ref[at, :] = dh1_ref[at, :] + norm_back(hat, rstd, da1 * gain1)
-        return carry
-
-    lax.fori_loop(0, TILES, finish, 0)
+    gains[0:1, :] = jnp.sum(da1 * hat, axis=0, keepdims=True)
+    gains[1:2, :] = jnp.sum(da1, axis=0, keepdims=True)
     gains[2:4, :] = gqk_ref[0:2, :]
     gains[4:6, :] = gvec_ref[0:2, :]
-    put_matrix(flat, 0, gq, D, 3 * D)
     flat[ROW_OUT : ROW_OUT + 8, :] = tail_ref[...]
     dp = lax.axis_index("dp")
     side = jnp.bitwise_and(dp, 1)
@@ -783,27 +769,47 @@
 
         @pl.when(side != k % 2)
         def _():
-            far0_ref[reld] = window[: plan.tail // 2]
-            far1_ref[reld] = window[plan.tail // 2 :]
-
-
-def finish_part(plan, tokens, wq, vec, dh1, tail, gvec, low, gains):
+            height = plan.tail // FAR_PARTS
+            for i, far_ref in enumerate(far_refs):
+                far_ref[reld] = window[i * height : (i + 1) * height]
+
+
+def finish_part(plan, tokens, wq, vec, tail, gvec, low, gains):
     rows = tokens.shape[0]
     windows = jax.ShapeDtypeStruct((plan.nd // 2, plan.tail, LANES), BF)
-    halves = jax.ShapeDtypeStruct((plan.nd // 2, plan.tail // 2, LANES), BF)
+    part = jax.ShapeDtypeStruct((plan.nd // 2, plan.tail // FAR_PARTS, LANES), BF)
     return pl.pallas_call(
         functools.partial(finish_kernel, plan),
-        out_shape=(jax.ShapeDtypeStruct((rows, D), F32), windows, halves, halves),
-        in_specs=[VMEM] * 8,
-        out_specs=(VMEM,) * 4,
+        out_shape=(jax.ShapeDtypeStruct((rows, D), F32), windows) + (part,) * FAR_PARTS,
+        in_specs=[VMEM] * 7,
+        out_specs=(VMEM,) * (2 + FAR_PARTS),
         scratch_shapes=[
-            pltpu.VMEM((D, 3 * D), F32),
             pltpu.VMEM((8, D), F32),
             pltpu.VMEM((round_up(plan.start[plan.nd - 1] + plan.win, 8), LANES), F32),
         ],
         compiler_params=params(28),
         cost_estimate=QUICK,
-    )(tokens, wq, vec, dh1, tail, gvec, low, gains)
+    )(tokens, wq, vec, tail, gvec, low, gains)
+
+
+def input_kernel(tokens_ref, vec_ref, da1_ref, dh1_ref, grad_ref, token_ref):
+    hat, rstd = norm_parts(tokens_ref[...].astype(F32))
+    grad_ref[...] = dh1_ref[...] + norm_back(hat, rstd, da1_ref[...] * vec_ref[0:1, :])
+    token_ref[...] = jnp.zeros_like(token_ref)
+
+
+def input_part(tokens, vec, da1, dh1):
+    return pl.pallas_call(
+        input_kernel,
+        out_shape=(
+            jax.ShapeDtypeStruct(dh1.shape, F32),
+            jax.ShapeDtypeStruct((8, LANES), F32),
+        ),
+        in_specs=[VMEM] * 4,
+        out_specs=(VMEM, VMEM),
+        compiler_params=params(16),
+        cost_estimate=QUICK,
+    )(tokens, vec, da1, dh1)
 
 
 def flat_place(plan, shape):
@@ -831,12 +837,12 @@
     bucket = lax.axis_index("bucket")
     dp = lax.axis_index("dp")
     total = tree_sum([ref[...].astype(F32) for ref in (own_ref, got0_ref, got1_ref, got2_ref)])
-    window[...] = jnp.where(bucket == 0, total[plan.win : 2 * plan.win], total[: plan.win])
+    window[...] = total[: plan.win]
 
     @pl.when(jnp.logical_and(bucket == plan.nb - 1, dp == plan.nd - 1))
     def _():
         window[plan.vec_place : plan.vec_place + VEC_ROWS, :] = total[
-            2 * plan.win : 2 * plan.win + VEC_ROWS
+            plan.win : plan.win + VEC_ROWS
         ]
 
     offset = lax.rem(plan.device() * plan.shard, LANES)
@@ -929,8 +935,7 @@
 
 
 def choose_kernel(plan, *refs):
-    columns, (early_ref, late_ref) = refs[:-2], refs[-2:]
-    step = columns[0].shape[0]
+    columns, early_ref, late_refs = refs[: plan.nb], refs[plan.nb], refs[plan.nb + 1 :]
     bucket = lax.axis_index("bucket")
     early_ref[:, plan.kept_row :] = columns[0][:, plan.win - 16 :]
     for i, part in enumerate(columns):
@@ -944,9 +949,11 @@
         def _():
             early_ref[:, plan.win : plan.kept_row] = part[:, plan.vec_from :]
 
-        @pl.when(owner > 0)
-        def _():
-            late_ref[pl.ds((owner - 1) * step, step)] = part[...]
+        for quarter, late_ref in enumerate(late_refs):
+
+            @pl.when(owner == quarter + 1)
+            def _():
+                late_ref[...] = part[...]
 
 
 def choose(plan, columns):
@@ -955,10 +962,10 @@
         functools.partial(choose_kernel, plan),
         out_shape=(
             jax.ShapeDtypeStruct((step, plan.early, LANES), BF),
-            jax.ShapeDtypeStruct(((plan.nb - 1) * step, plan.win, LANES), BF),
-        ),
+        )
+        + (jax.ShapeDtypeStruct(columns[0].shape, BF),) * (plan.nb - 1),
         in_specs=[VMEM] * len(columns),
-        out_specs=(VMEM, VMEM),
+        out_specs=(VMEM,) * plan.nb,
         compiler_params=params(8),
     )(*columns)
 
@@ -995,28 +1002,30 @@
     )(*parts, token)
 
 
-def blend_kernel(plan, count, *refs):
-    rest = refs[0]
-    parts, outs = refs[1 : 1 + count], refs[1 + count :]
+def blend_kernel(plan, late_count, *refs):
+    late, parts, outs = refs[:late_count], refs[late_count + 1 : -plan.nb], refs[-plan.nb :]
     bucket = lax.axis_index("bucket")
     first = tree_sum([part[...].astype(F32) for part in parts])
     for i, out in enumerate(outs):
-        quarter = jnp.maximum(jnp.bitwise_xor(bucket, i) - 1, 0)
-        out[: plan.win] = rest[quarter].astype(out.dtype)
-        out[plan.win :] = first.astype(out.dtype)
-
-
-def blend(plan, rest, parts):
-    height = plan.win + plan.tail
-    return pl.pallas_call(
-        functools.partial(blend_kernel, plan, len(parts)),
+        owner = jnp.bitwise_xor(bucket, i)
+        quarter = jnp.maximum(owner - 1, 0)
+        window = late[0][quarter]
+        if late_count > 1:
+            window = window + tree_sum([ref[quarter].astype(F32) for ref in late[1:]])
+        out[: plan.win] = jnp.where(owner == 0, first[: plan.win], window).astype(out.dtype)
+        out[plan.win :] = first[plan.win :].astype(out.dtype)
+
+
+def blend(plan, late, token, parts):
+    return pl.pallas_call(
+        functools.partial(blend_kernel, plan, len(late)),
         out_shape=tuple(
-            jax.ShapeDtypeStruct((height, LANES), BF if i else F32) for i in range(plan.nb)
+            jax.ShapeDtypeStruct((plan.tail, LANES), BF if i else F32) for i in range(plan.nb)
         ),
-        in_specs=[VMEM] * (1 + len(parts)),
+        in_specs=[VMEM] * (len(late) + 1 + len(parts)),
         out_specs=(VMEM,) * plan.nb,
-        compiler_params=params(8),
-    )(rest, *parts)
+        compiler_params=params(10),
+    )(*late, token, *parts)
 
 
 def add_rows_kernel(*refs):
@@ -1050,9 +1059,10 @@
 
 
 def tree_sum(parts):
-    if len(parts) == 4:
-        return (parts[0] + parts[1]) + (parts[2] + parts[3])
-    return parts[0] + parts[1]
+    if len(parts) == 1:
+        return parts[0]
+    half = len(parts) // 2
+    return tree_sum(parts[:half]) + tree_sum(parts[half:])
 
 
 def with_partners(x, axis, size, bits):
@@ -1065,8 +1075,9 @@
     for bits in more:
         column = jnp.concatenate(with_partners(column, "dp", plan.nd, bits), axis=0)
     (bits,) = groups_of(plan.nb)
-    early, late = choose(plan, with_partners(column, "bucket", plan.nb, bits))
-    return (early, swap(early, "dp", plan.nd, 1)), (late, swap(late, "dp", plan.nd, 1))
+    early, *late = choose(plan, with_partners(column, "bucket", plan.nb, bits))
+    others = [swap(x, "dp", plan.nd, 1) for x in (early, *late)]
+    return (early, others[0]), (*late, *others[1:])
 
 
 def scatter_dp(plan, pieces):
@@ -1113,18 +1124,20 @@
     wq, vec, head, kept, q, k, v, hat, rstd = project_part(plan, *early, tokens)
     o, ot, lse = forward(plan, segment_ids, seg_row, keep_row, q, k, v)
     block_output, dh1, do, near, far, tail, gvec = middle_part(
-        plan, tokens, cotangent, o, ot, *late, head, kept, vec, keep_row, bucket_patches
+        plan, late, tokens, cotangent, o, ot, head, kept, vec, keep_row, bucket_patches
     )
     *pieces, token = add_parts([near, swap(far, "dp", plan.nd, 1)], count, gvec)
     rest = scatter_dp(plan, pieces)
     low, gains = backward(
         plan, vec, segment_ids, seg_row, keep_row, lse, q, k, v, o, do, hat, rstd, token
     )
-    input_grad, near, *far = finish_part(plan, tokens, wq, vec, dh1, tail, gvec, low, gains)
-    rest, token = add_parts(rest, 1, gains)
+    da1, near, *far = finish_part(plan, tokens, wq, vec, tail, gvec, low, gains)
+    input_grad, given = input_part(tokens, vec, da1, dh1)
+    *late_parts, token = add_parts(rest[:2], 1, gains)
+    late_parts += rest[2:]
     *pieces, _ = add_parts([near, [swap(half, "dp", plan.nd, 1) for half in far]], count, token)
     first = scatter_dp(plan, pieces)
-    mine, *sent = blend(plan, rest, first)
+    mine, *sent = blend(plan, late_parts, given, first)
     parts = [mine] + [
         swap(x, "bucket", plan.nb, mask) for x, mask in zip(sent, masks_of(b_bits))
     ]

time: 161 us -> 148 us (0.919); the launches traced: 162 us -> 146 us
  starting transfers between devices: 42.5 us -> 32.6 us
  waiting for transfers between devices: 58 us -> 53.3 us
    ppermute x27 -> x30, starting transfers between devices: 42.5 us -> 32.6 us  [swap(): return lax.ppermute(x, axis, [(i, i ^ mask) for i in range(size)])]
    ppermute x27 -> x30, waiting for transfers between devices: 58 us -> 53.3 us  [swap(): return lax.ppermute(x, axis, [(i, i ^ mask) for i in range(size)])]
    pallas_call x1, Pallas kernels: 20.8 us -> 17.6 us  [middle_part(): pl.pallas_call(functools.partial(middle_kernel, plan), out_shape=(jax.Sha...]
    pallas_call x1, Pallas kernels: 6.29 us -> 3.5 us  [finish_part(): pl.pallas_call(functools.partial(finish_kernel, plan), out_shape=(jax.Sha...]
    pallas_call x1, Pallas kernels: 13.7 us -> 16.3 us  [backward(): pl.pallas_call(functools.partial(backward_kernel, plan), out_shape=(jax.S...]
    pallas_call x1 -> x2, Pallas kernels: 0.1 us -> 2.47 us  [the longest x1 2.22 us: input_part(): pl.pallas_call(input_kernel, out_shape=(jax.ShapeDtypeStruct(dh1.shape, F...]
  transfers between devices with their start and end apart: 27 -> 30, of which waited for: 16 -> 17; matrix products, arithmetic and copies ran while one was open for 1% -> 1% of each run, Pallas kernels for 20% -> 24%
where the time goes in v3:
time: 148 us; the launch traced here: 146 us
  Pallas kernels  55 us (37%)
  waiting for transfers between devices  53.3 us (36%)
  starting transfers between devices  32.6 us (22%)
  local copies, waits for them, and re-layouts  3.88 us (3%)
    ppermute x30, waiting for transfers between devices, swap(): return lax.ppermute(x, axis, [(i, i ^ mask) for i in range(size)])  53.3 us
    ppermute x30, starting transfers between devices, swap(): return lax.ppermute(x, axis, [(i, i ^ mask) for i in range(size)])  32.6 us
    pallas_call x1, Pallas kernels, middle_part(): pl.pallas_call(functools.partial(middle_kernel, plan), out_shape=(jax.Sha...  17.6 us
    pallas_call x1, Pallas kernels, backward(): pl.pallas_call(functools.partial(backward_kernel, plan), out_shape=(jax.S...  16.3 us
    pallas_call x1, Pallas kernels, forward(): pl.pallas_call(functools.partial(forward_kernel, plan), out_shape=(jax.Sh...  7.54 us
    pallas_call x1, Pallas kernels, project_part(): pl.pallas_call(functools.partial(project_kernel, plan), out_shape=(jax.Sh...  4.18 us
    pallas_call x1, Pallas kernels, finish_part(): pl.pallas_call(functools.partial(finish_kernel, plan), out_shape=(jax.Sha...  3.5 us
  transfers between devices with their start and end apart: 30, of which 17 were waited for; matrix products, arithmetic and copies ran while one was open for 1% of the time, Pallas kernels for 24%

profile of v3, /device:TPU:0, one launch (start us, length us, event | category | flops | bytes accessed | tf_op | source)
XLA Modules:
  0.0 145.7 jit_solution(3915866085311244601)
XLA Ops:
  2.5 3.1 %collective-permute-start = (bf16[448,128]{1,0:T(8,128)(2,1)S(1)}, bf16[448,128]{1,0:T(8,128)(2,1)S(1)}, u32[]{:S(2)}, u32[]{:S(2)}) collective-permute-start(bf16[448,128]{1,0:T(8,128)(2,1)S(1)} %shard_map.135.refs_0_), channel_id=1, source_target_pairs={{0,2},{1,3},{2,0},{3,1},{4,6},{5,7},{6,4},{7,5},{8,10},{9,11},{10,... | collective-permute-start | bytes 344072 | tf_op jit(solution)/shard_map/ppermute | solution.py:1058
  5.6 2.6 %collective-permute-start.1 = (bf16[448,128]{1,0:T(8,128)(2,1)S(1)}, bf16[448,128]{1,0:T(8,128)(2,1)S(1)}, u32[]{:S(2)}, u32[]{:S(2)}) collective-permute-start(bf16[448,128]{1,0:T(8,128)(2,1)S(1)} %shard_map.135.refs_0_), channel_id=1, source_target_pairs={{0,4},{1,5},{2,6},{3,7},{4,0},{5,1},{6,2},{7,3},{8,12},{9,13},{10,... | collective-permute-start | bytes 344072 | tf_op jit(solution)/shard_map/ppermute | solution.py:1058
  8.7 8.5 %collective-permute-done.1.refs_2_ = bf16[448,128]{1,0:T(8,128)(2,1)S(1)} collective-permute-done((bf16[448,128]{1,0:T(8,128)(2,1)S(1)}, bf16[448,128]{1,0:T(8,128)(2,1)S(1)}, u32[]{:S(2)}, u32[]{:S(2)}) %collective-permute-start.1) | collective-permute-done | bytes 114720 | tf_op jit(solution)/shard_map/ppermute | solution.py:1058
  17.3 1.6 %collective-permute-start.3 = (bf16[4,448,128]{2,1,0:T(8,128)(2,1)S(1)}, bf16[4,448,128]{2,1,0:T(8,128)(2,1)S(1)}, u32[]{:S(2)}, u32[]{:S(2)}) collective-permute-start(bf16[4,448,128]{2,1,0:T(8,128)(2,1)S(1)} %shard_map.136.refs_0_), channel_id=1, source_target_pairs={{0,8},{8,0},{16,24},{24,16},{1,9},{9,1},{17,25},{25,17},{2,10},{10... | collective-permute-start | bytes 1376264 | tf_op jit(solution)/shard_map/ppermute | solution.py:1058
  18.9 1.5 %collective-permute-start.4 = (bf16[4,448,128]{2,1,0:T(8,128)(2,1)S(1)}, bf16[4,448,128]{2,1,0:T(8,128)(2,1)S(1)}, u32[]{:S(2)}, u32[]{:S(2)}) collective-permute-start(bf16[4,448,128]{2,1,0:T(8,128)(2,1)S(1)} %shard_map.136.refs_0_), channel_id=1, source_target_pairs={{0,16},{8,24},{16,0},{24,8},{1,17},{9,25},{17,1},{25,9},{2,18},{10... | collective-permute-start | bytes 1376264 | tf_op jit(solution)/shard_map/ppermute | solution.py:1058
  20.9 10.0 %collective-permute-done.3.refs_1_ = bf16[4,448,128]{2,1,0:T(8,128)(2,1)S(1)} collective-permute-done((bf16[4,448,128]{2,1,0:T(8,128)(2,1)S(1)}, bf16[4,448,128]{2,1,0:T(8,128)(2,1)S(1)}, u32[]{:S(2)}, u32[]{:S(2)}) %collective-permute-start.3) | collective-permute-done | bytes 458784 | tf_op jit(solution)/shard_map/ppermute | solution.py:1058
  30.9 7.6 %collective-permute-done.4.refs_2_ = bf16[4,448,128]{2,1,0:T(8,128)(2,1)S(1)} collective-permute-done((bf16[4,448,128]{2,1,0:T(8,128)(2,1)S(1)}, bf16[4,448,128]{2,1,0:T(8,128)(2,1)S(1)}, u32[]{:S(2)}, u32[]{:S(2)}) %collective-permute-start.4) | collective-permute-done | bytes 458784 | tf_op jit(solution)/shard_map/ppermute | solution.py:1058
  40.6 4.2 %shard_map.138 = (bf16[384,1152]{1,0:T(8,128)(2,1)S(1)}, f32[8,384]{1,0:T(8,128)S(1)}, f32[8,128]{1,0:T(8,128)S(1)}, f32[8,128]{1,0:T(8,128)S(1)}, bf16[1024,384...) custom-call(bf16[4,512,128]{2,1,0:T(8,128)(2,1)S(1)} %get-tuple-elem, ...), custom_call_target="tpu_custom_call" | custom-call | flops 1000 | bytes 1000 | tf_op jit(solution)/shard_map/pallas_call | solution.py:311
  44.9 7.5 %shard_map.139 = (bf16[1024,384]{1,0:T(8,128)(2,1)S(1)}, bf16[4,384,256]{2,1,0:T(8,128)(2,1)S(1)}, f32[4,8,256]{2,1,0:T(8,128)S(1)}) custom-call(s32[1024]{0:T(1024)S(1)} %copy-done.4, s32[1,1024]{1,0:T(1,128)S(1)} %bitcast.38, s32[1,1024]{1,0:T(1,128)S(1)} %bitcast.35, bf16[1024,384]{1,0:T(8,128)(2,1)S(1)} %get-tuple-element.65.q_ref, ...), custom_call_target="tpu_custom_call" | custom-call | flops 1000 | bytes 1000 | tf_op jit(solution)/shard_map/pallas_call | solution.py:404
  52.5 17.6 %shard_map.140 = (bf16[1024,384]{1,0:T(8,128)(2,1)}, f32[1024,384]{1,0:T(8,128)S(1)}, bf16[1024,384]{1,0:T(8,128)(2,1)S(1)}, bf16[3,4,448,128]{3,2,1,0:T(8,128)(...) custom-call(bf16[4,448,128]{2,1,0:T(8,128)(2,1)S(1)} %get-tuple-element.61.refs_0_, ...), custom_call_target="tpu_custom_call" | custom-call | flops 1000 | bytes 1000 | tf_op jit(solution)/shard_map/pallas_call | solution.py:553
  70.2 3.0 %collective-permute-done.10.refs_1_ = bf16[3,4,448,128]{3,2,1,0:T(8,128)(2,1)S(1)} collective-permute-done((bf16[3,4,448,128]{3,2,1,0:T(8,128)(2,1)S(1)}, bf16[3,4,448,128]{3,2,1,0:T(8,128)(2,1)S(1)}, u32[]{:S(2)}, u32[]{:S(2)}) %collective-permute-start.10) | collective-permute-done | bytes 1376288 | tf_op jit(solution)/shard_map/ppermute | solution.py:1058
  73.5 2.8 %collective-permute-start.11 = (bf16[3,1,448,128]{3,2,0,1:T(8,128)(2,1)S(1)}, bf16[3,1,448,128]{3,2,0,1:T(8,128)(2,1)S(1)}, u32[]{:S(2)}, u32[]{:S(2)}) collective-permute-start(bf16[3,1,448,128]{3,2,0,1:T(8,128)(2,1)S(1)} %bitcast.42), channel_id=1, source_target_pairs={{0,2},{1,3},{2,0},{3,1},{4,6},{5,7},{6,4},{7,5},{8,10},{9,11},{10,... | collective-permute-start | bytes 1032200 | tf_op jit(solution)/shard_map/ppermute | solution.py:1058
  76.3 1.1 collective-permute-start.12
  77.5 1.4 collective-permute-start.13
  78.8 16.3 %shard_map.142 = (bf16[1024,1152]{1,0:T(8,128)(2,1)S(1)}, f32[8,384]{1,0:T(8,128)S(1)}) custom-call(f32[8,384]{1,0:T(8,128)S(1)} %get-tuple-element.72.refs_12_.vec_ref, s32[1024]{0:T(1024)S(1)} %copy-done.4, s32[1,1024]{1,0:T(1,128)S(1)} %bitcast.39, s32[1,1024]{1,0:T(1,128)S(1)} %bitcast.37, f32[4,8,256]{2,1,0:T(8,128)S(1)} %get-tuple-element.77.lse_ref, ...), custom_call_target="tpu_custom_call" | custom-call | flops 1000 | bytes 1000 | tf_op jit(solution)/shard_map/pallas_call | solution.py:696
  95.2 3.5 %shard_map.143 = (f32[1024,384]{1,0:T(8,128)S(1)}, bf16[4,480,128]{2,1,0:T(8,128)(2,1)S(1)}, bf16[4,160,128]{2,1,0:T(8,128)(2,1)S(1)}, bf16[4,160,128]{2,1,0:T(8,128)(2,1)S(1)}, bf16[4,160,128]{2,1,0:T(8,128)(2,1)S(1)}) custom-call(bf16[1024,384]{1,0:T(8,128)(2,1)S(1)} %copy-done, bf16[384,1152]{1,0:T(8,128)(2,1)S(1)} %get-tuple-element.74.wq_ref, ...), custom_call_target="tpu_custom_call" | custom-call | flops 1000 | bytes 1000 | tf_op jit(solution)/shard_map/pallas_call | solution.py:781
  102.3 2.0 %collective-permute-start.18 = (bf16[1,480,128]{2,1,0:T(8,128)(2,1)S(1)}, bf16[1,480,128]{2,1,0:T(8,128)(2,1)S(1)}, u32[]{:S(2)}, u32[]{:S(2)}) collective-permute-start(bf16[1,480,128]{2,1,0:T(8,128)(2,1)S(1)} %get-tuple-element.102), channel_id=1, source_target_pairs={{0,4},{1,5},{2,6},{3,7},{4,0},{5,1},{6,2},{7,3},{8,12},{9,13},{10,... | collective-permute-start | bytes 368648 | tf_op jit(solution)/shard_map/ppermute | solution.py:1058
  104.3 1.4 collective-permute-start.19
  105.7 2.2 %shard_map.144 = (f32[1024,384]{1,0:T(8,128)}, f32[8,128]{1,0:T(8,128)S(1)}) custom-call(bf16[1024,384]{1,0:T(8,128)(2,1)S(1)} %copy-done, f32[8,384]{1,0:T(8,128)S(1)} %get-tuple-element.72.refs_12_.vec_ref, f32[1024,384]{1,0:T(8,128)S(1)} %get-tuple-element.86.da1_ref, f32[1024,384]{1,0:T(8,128)S(1)} %get-tuple-element.87.dh1_ref), custom_call_target="tpu_custom_call" | custom-call | flops 1000 | bytes 1000 | tf_op jit(solution)/shard_map/pallas_call | solution.py:802
  107.9 10.3 %collective-permute-done.18 = bf16[1,480,128]{2,1,0:T(8,128)(2,1)S(1)} collective-permute-done((bf16[1,480,128]{2,1,0:T(8,128)(2,1)S(1)}, bf16[1,480,128]{2,1,0:T(8,128)(2,1)S(1)}, u32[]{:S(2)}, u32[]{:S(2)}) %collective-permute-start.18) | collective-permute-done | bytes 122912 | tf_op jit(solution)/shard_map/ppermute | solution.py:1058
  119.6 1.7 %collective-permute-start.21 = (bf16[480,128]{1,0:T(8,128)(2,1)S(1)}, bf16[480,128]{1,0:T(8,128)(2,1)S(1)}, u32[]{:S(2)}, u32[]{:S(2)}) collective-permute-start(bf16[480,128]{1,0:T(8,128)(2,1)S(1)} %get-tuple-element.106), channel_id=1, source_target_pairs={{0,16},{8,24},{16,0},{24,8},{1,17},{9,25},{17,1},{25,9},{2,18},{10... | collective-permute-start | bytes 368648 | tf_op jit(solution)/shard_map/ppermute | solution.py:1058
  122.1 2.0 %collective-permute-done.20.got0_ref = bf16[480,128]{1,0:T(8,128)(2,1)S(1)} collective-permute-done((bf16[480,128]{1,0:T(8,128)(2,1)S(1)}, bf16[480,128]{1,0:T(8,128)(2,1)S(1)}, u32[]{:S(2)}, u32[]{:S(2)}) %collective-permute-start.20) | collective-permute-done | bytes 122912 | tf_op jit(solution)/shard_map/ppermute | solution.py:1058
  124.1 1.2 collective-permute-done.21.got1_ref
  125.3 1.8 %collective-permute-done.22.got2_ref = bf16[480,128]{1,0:T(8,128)(2,1)S(1)} collective-permute-done((bf16[480,128]{1,0:T(8,128)(2,1)S(1)}, bf16[480,128]{1,0:T(8,128)(2,1)S(1)}, u32[]{:S(2)}, u32[]{:S(2)}) %collective-permute-start.22) | collective-permute-done | bytes 122912 | tf_op jit(solution)/shard_map/ppermute | solution.py:1058
  127.1 1.1 shard_map.148
  128.2 1.2 collective-permute-done.23.refs_1_
  129.4 2.3 %collective-permute-start.24 = (f32[8,128]{1,0:T(8,128)S(1)}, f32[8,128]{1,0:T(8,128)S(1)}, u32[]{:S(2)}, u32[]{:S(2)}) collective-permute-start(f32[8,128]{1,0:T(8,128)S(1)} %shard_map.149.refs_0_), channel_id=1, source_target_pairs={{0,2},{1,3},{2,0},{3,1},{4,6},{5,7},{6,4},{7,5},{8,10},{9,11},{10,... | collective-permute-start | bytes 12296 | tf_op jit(solution)/shard_map/ppermute | solution.py:1058
  132.6 1.5 %collective-permute-start.26 = (f32[8,128]{1,0:T(8,128)S(1)}, f32[8,128]{1,0:T(8,128)S(1)}, u32[]{:S(2)}, u32[]{:S(2)}) collective-permute-start(f32[8,128]{1,0:T(8,128)S(1)} %shard_map.149.refs_0_), channel_id=1, source_target_pairs={{0,6},{1,7},{2,4},{3,5},{4,2},{5,3},{6,0},{7,1},{8,14},{9,15},{10,... | collective-permute-start | bytes 12296 | tf_op jit(solution)/shard_map/ppermute | solution.py:1058
  134.1 2.2 %collective-permute-done.25.refs_2_ = f32[8,128]{1,0:T(8,128)S(1)} collective-permute-done((f32[8,128]{1,0:T(8,128)S(1)}, f32[8,128]{1,0:T(8,128)S(1)}, u32[]{:S(2)}, u32[]{:S(2)}) %collective-permute-start.25) | collective-permute-done | bytes 4128 | tf_op jit(solution)/shard_map/ppermute | solution.py:1058
  136.2 1.7 %collective-permute-done.26.refs_3_ = f32[8,128]{1,0:T(8,128)S(1)} collective-permute-done((f32[8,128]{1,0:T(8,128)S(1)}, f32[8,128]{1,0:T(8,128)S(1)}, u32[]{:S(2)}, u32[]{:S(2)}) %collective-permute-start.26) | collective-permute-done | bytes 4128 | tf_op jit(solution)/shard_map/ppermute | solution.py:1058
  139.6 1.8 %collective-permute-start.29 = (f32[8,128]{1,0:T(8,128)S(1)}, f32[8,128]{1,0:T(8,128)S(1)}, u32[]{:S(2)}, u32[]{:S(2)}) collective-permute-start(f32[8,128]{1,0:T(8,128)S(1)} %shard_map.150.refs_0_), channel_id=1, source_target_pairs={{0,24},{8,16},{16,8},{24,0},{1,25},{9,17},{17,9},{25,1},{2,26},{10... | collective-permute-start | bytes 12296 | tf_op jit(solution)/shard_map/ppermute | solution.py:1058
  142.9 1.2 collective-permute-done.29.refs_3_
  (66 shorter events, 16.9 us)
Async XLA Ops:
  1.6 39.0 %copy-start = (bf16[1024,384]{1,0:T(8,128)(2,1)S(1)}, bf16[1024,384]{1,0:T(8,128)(2,1)}, u32[]{:S(2)}) copy-start(bf16[1024,384]{1,0:T(8,128)(2,1)} %tokens_ref.5) | copy-start | bytes 2359300
  2.5 6.2 %collective-permute-start = (bf16[448,128]{1,0:T(8,128)(2,1)S(1)}, bf16[448,128]{1,0:T(8,128)(2,1)S(1)}, u32[]{:S(2)}, u32[]{:S(2)}) collective-permute-start(bf16[448,128]{1,0:T(8,128)(2,1)S(1)} %shard_map.135.refs_0_), channel_id=1, source_target_pairs={{0,2},{1,3},{2,0},{3,1},{4,6},{5,7},{6,4},{7,5},{8,10},{9,11},{10,... | collective-permute-start | bytes 344072 | tf_op jit(solution)/shard_map/ppermute | solution.py:1058
  5.6 11.7 %collective-permute-start.1 = (bf16[448,128]{1,0:T(8,128)(2,1)S(1)}, bf16[448,128]{1,0:T(8,128)(2,1)S(1)}, u32[]{:S(2)}, u32[]{:S(2)}) collective-permute-start(bf16[448,128]{1,0:T(8,128)(2,1)S(1)} %shard_map.135.refs_0_), channel_id=1, source_target_pairs={{0,4},{1,5},{2,6},{3,7},{4,0},{5,1},{6,2},{7,3},{8,12},{9,13},{10,... | collective-permute-start | bytes 344072 | tf_op jit(solution)/shard_map/ppermute | solution.py:1058
  8.2 9.1 %collective-permute-start.2 = (bf16[448,128]{1,0:T(8,128)(2,1)S(1)}, bf16[448,128]{1,0:T(8,128)(2,1)S(1)}, u32[]{:S(2)}, u32[]{:S(2)}) collective-permute-start(bf16[448,128]{1,0:T(8,128)(2,1)S(1)} %shard_map.135.refs_0_), channel_id=1, source_target_pairs={{0,6},{1,7},{2,4},{3,5},{4,2},{5,3},{6,0},{7,1},{8,14},{9,15},{10,... | collective-permute-start | bytes 344072 | tf_op jit(solution)/shard_map/ppermute | solution.py:1058
  17.3 27.5 %copy-start.3 = (s32[1024]{0:T(1024)S(1)}, s32[1024]{0:T(1024)}, u32[]{:S(2)}) copy-start(s32[1024]{0:T(1024)} %param.11) | copy-start | bytes 12292
  17.3 13.5 %collective-permute-start.3 = (bf16[4,448,128]{2,1,0:T(8,128)(2,1)S(1)}, bf16[4,448,128]{2,1,0:T(8,128)(2,1)S(1)}, u32[]{:S(2)}, u32[]{:S(2)}) collective-permute-start(bf16[4,448,128]{2,1,0:T(8,128)(2,1)S(1)} %shard_map.136.refs_0_), channel_id=1, source_target_pairs={{0,8},{8,0},{16,24},{24,16},{1,9},{9,1},{17,25},{25,17},{2,10},{10... | collective-permute-start | bytes 1376264 | tf_op jit(solution)/shard_map/ppermute | solution.py:1058
  18.9 19.5 %collective-permute-start.4 = (bf16[4,448,128]{2,1,0:T(8,128)(2,1)S(1)}, bf16[4,448,128]{2,1,0:T(8,128)(2,1)S(1)}, u32[]{:S(2)}, u32[]{:S(2)}) collective-permute-start(bf16[4,448,128]{2,1,0:T(8,128)(2,1)S(1)} %shard_map.136.refs_0_), channel_id=1, source_target_pairs={{0,16},{8,24},{16,0},{24,8},{1,17},{9,25},{17,1},{25,9},{2,18},{10... | collective-permute-start | bytes 1376264 | tf_op jit(solution)/shard_map/ppermute | solution.py:1058
  20.4 18.0 %collective-permute-start.5 = (bf16[4,448,128]{2,1,0:T(8,128)(2,1)S(1)}, bf16[4,448,128]{2,1,0:T(8,128)(2,1)S(1)}, u32[]{:S(2)}, u32[]{:S(2)}) collective-permute-start(bf16[4,448,128]{2,1,0:T(8,128)(2,1)S(1)} %shard_map.136.refs_0_), channel_id=1, source_target_pairs={{0,24},{8,16},{16,8},{24,0},{1,25},{9,17},{17,9},{25,1},{2,26},{10... | collective-permute-start | bytes 1376264 | tf_op jit(solution)/shard_map/ppermute | solution.py:1058
  38.6 2.0 %collective-permute-start.9 = (bf16[4,512,128]{2,1,0:T(8,128)(2,1)S(1)}, bf16[4,512,128]{2,1,0:T(8,128)(2,1)S(1)}, u32[]{:S(2)}, u32[]{:S(2)}) collective-permute-start(bf16[4,512,128]{2,1,0:T(8,128)(2,1)S(1)} %get-tuple-element.64.own_ref), channel_id=1, source_target_pairs={{0,1},{1,0},{2,3},{3,2},{4,5},{5,4},{6,7},{7,6},{8,9},{9,8},{10,11... | collective-permute-start | bytes 1572872 | tf_op jit(solution)/shard_map/ppermute | solution.py:1058
  38.7 13.7 %collective-permute-start.6 = (bf16[4,448,128]{2,1,0:T(8,128)(2,1)S(1)}, bf16[4,448,128]{2,1,0:T(8,128)(2,1)S(1)}, u32[]{:S(2)}, u32[]{:S(2)}) collective-permute-start(bf16[4,448,128]{2,1,0:T(8,128)(2,1)S(1)} %get-tuple-element.61.refs_0_), channel_id=1, source_target_pairs={{0,1},{1,0},{2,3},{3,2},{4,5},{5,4},{6,7},{7,6},{8,9},{9,8},{10,11... | collective-permute-start | bytes 1376264 | tf_op jit(solution)/shard_map/ppermute | solution.py:1058
  39.2 13.2 %collective-permute-start.7 = (bf16[4,448,128]{2,1,0:T(8,128)(2,1)S(1)}, bf16[4,448,128]{2,1,0:T(8,128)(2,1)S(1)}, u32[]{:S(2)}, u32[]{:S(2)}) collective-permute-start(bf16[4,448,128]{2,1,0:T(8,128)(2,1)S(1)} %get-tuple-element.62.refs_1_), channel_id=1, source_target_pairs={{0,1},{1,0},{2,3},{3,2},{4,5},{5,4},{6,7},{7,6},{8,9},{9,8},{10,11... | collective-permute-start | bytes 1376264 | tf_op jit(solution)/shard_map/ppermute | solution.py:1058
  39.3 13.1 %collective-permute-start.8 = (bf16[4,448,128]{2,1,0:T(8,128)(2,1)S(1)}, bf16[4,448,128]{2,1,0:T(8,128)(2,1)S(1)}, u32[]{:S(2)}, u32[]{:S(2)}) collective-permute-start(bf16[4,448,128]{2,1,0:T(8,128)(2,1)S(1)} %get-tuple-element.63.refs_2_), channel_id=1, source_target_pairs={{0,1},{1,0},{2,3},{3,2},{4,5},{5,4},{6,7},{7,6},{8,9},{9,8},{10,11... | collective-permute-start | bytes 1376264 | tf_op jit(solution)/shard_map/ppermute | solution.py:1058
  70.0 3.1 %collective-permute-start.10 = (bf16[3,4,448,128]{3,2,1,0:T(8,128)(2,1)S(1)}, bf16[3,4,448,128]{3,2,1,0:T(8,128)(2,1)S(1)}, u32[]{:S(2)}, u32[]{:S(2)}) collective-permute-start(bf16[3,4,448,128]{3,2,1,0:T(8,128)(2,1)S(1)} %get-tuple-element.82), channel_id=1, source_target_pairs={{0,1},{1,0},{2,3},{3,2},{4,5},{5,4},{6,7},{7,6},{8,9},{9,8},{10,11... | collective-permute-start | bytes 4128776 | tf_op jit(solution)/shard_map/ppermute | solution.py:1058
  73.5 25.7 %collective-permute-start.11 = (bf16[3,1,448,128]{3,2,0,1:T(8,128)(2,1)S(1)}, bf16[3,1,448,128]{3,2,0,1:T(8,128)(2,1)S(1)}, u32[]{:S(2)}, u32[]{:S(2)}) collective-permute-start(bf16[3,1,448,128]{3,2,0,1:T(8,128)(2,1)S(1)} %bitcast.42), channel_id=1, source_target_pairs={{0,2},{1,3},{2,0},{3,1},{4,6},{5,7},{6,4},{7,5},{8,10},{9,11},{10,... | collective-permute-start | bytes 1032200 | tf_op jit(solution)/shard_map/ppermute | solution.py:1058
  76.3 31.6 %collective-permute-start.12 = (bf16[3,1,448,128]{3,2,0,1:T(8,128)(2,1)S(1)}, bf16[3,1,448,128]{3,2,0,1:T(8,128)(2,1)S(1)}, u32[]{:S(2)}, u32[]{:S(2)}) collective-permute-start(bf16[3,1,448,128]{3,2,0,1:T(8,128)(2,1)S(1)} %bitcast.41), channel_id=1, source_target_pairs={{0,4},{1,5},{2,6},{3,7},{4,0},{5,1},{6,2},{7,3},{8,12},{9,13},{10,... | collective-permute-start | bytes 1032200 | tf_op jit(solution)/shard_map/ppermute | solution.py:1058
  77.5 30.5 %collective-permute-start.13 = (bf16[3,1,448,128]{3,2,0,1:T(8,128)(2,1)S(1)}, bf16[3,1,448,128]{3,2,0,1:T(8,128)(2,1)S(1)}, u32[]{:S(2)}, u32[]{:S(2)}) collective-permute-start(bf16[3,1,448,128]{3,2,0,1:T(8,128)(2,1)S(1)} %bitcast.40), channel_id=1, source_target_pairs={{0,6},{1,7},{2,4},{3,5},{4,2},{5,3},{6,0},{7,1},{8,14},{9,15},{10,... | collective-permute-start | bytes 1032200 | tf_op jit(solution)/shard_map/ppermute | solution.py:1058
  98.7 1.5 %collective-permute-start.14 = (bf16[4,160,128]{2,1,0:T(8,128)(2,1)S(1)}, bf16[4,160,128]{2,1,0:T(8,128)(2,1)S(1)}, u32[]{:S(2)}, u32[]{:S(2)}) collective-permute-start(bf16[4,160,128]{2,1,0:T(8,128)(2,1)S(1)} %get-tuple-element.96), channel_id=1, source_target_pairs={{0,1},{1,0},{2,3},{3,2},{4,5},{5,4},{6,7},{7,6},{8,9},{9,8},{10,11... | collective-permute-start | bytes 491528 | tf_op jit(solution)/shard_map/ppermute | solution.py:1058
  98.8 1.6 %collective-permute-start.15 = (bf16[4,160,128]{2,1,0:T(8,128)(2,1)S(1)}, bf16[4,160,128]{2,1,0:T(8,128)(2,1)S(1)}, u32[]{:S(2)}, u32[]{:S(2)}) collective-permute-start(bf16[4,160,128]{2,1,0:T(8,128)(2,1)S(1)} %get-tuple-element.97), channel_id=1, source_target_pairs={{0,1},{1,0},{2,3},{3,2},{4,5},{5,4},{6,7},{7,6},{8,9},{9,8},{10,11... | collective-permute-start | bytes 491528 | tf_op jit(solution)/shard_map/ppermute | solution.py:1058
  99.3 1.4 collective-permute-start.16
  101.3 6.6 %collective-permute-start.17 = (bf16[1,480,128]{2,1,0:T(8,128)(2,1)S(1)}, bf16[1,480,128]{2,1,0:T(8,128)(2,1)S(1)}, u32[]{:S(2)}, u32[]{:S(2)}) collective-permute-start(bf16[1,480,128]{2,1,0:T(8,128)(2,1)S(1)} %get-tuple-element.101), channel_id=1, source_target_pairs={{0,2},{1,3},{2,0},{3,1},{4,6},{5,7},{6,4},{7,5},{8,10},{9,11},{10,... | collective-permute-start | bytes 368648 | tf_op jit(solution)/shard_map/ppermute | solution.py:1058
  102.3 15.9 %collective-permute-start.18 = (bf16[1,480,128]{2,1,0:T(8,128)(2,1)S(1)}, bf16[1,480,128]{2,1,0:T(8,128)(2,1)S(1)}, u32[]{:S(2)}, u32[]{:S(2)}) collective-permute-start(bf16[1,480,128]{2,1,0:T(8,128)(2,1)S(1)} %get-tuple-element.102), channel_id=1, source_target_pairs={{0,4},{1,5},{2,6},{3,7},{4,0},{5,1},{6,2},{7,3},{8,12},{9,13},{10,... | collective-permute-start | bytes 368648 | tf_op jit(solution)/shard_map/ppermute | solution.py:1058
  104.3 13.9 %collective-permute-start.19 = (bf16[1,480,128]{2,1,0:T(8,128)(2,1)S(1)}, bf16[1,480,128]{2,1,0:T(8,128)(2,1)S(1)}, u32[]{:S(2)}, u32[]{:S(2)}) collective-permute-start(bf16[1,480,128]{2,1,0:T(8,128)(2,1)S(1)} %get-tuple-element.103), channel_id=1, source_target_pairs={{0,6},{1,7},{2,4},{3,5},{4,2},{5,3},{6,0},{7,1},{8,14},{9,15},{10,... | collective-permute-start | bytes 368648 | tf_op jit(solution)/shard_map/ppermute | solution.py:1058
  118.5 5.6 %collective-permute-start.20 = (bf16[480,128]{1,0:T(8,128)(2,1)S(1)}, bf16[480,128]{1,0:T(8,128)(2,1)S(1)}, u32[]{:S(2)}, u32[]{:S(2)}) collective-permute-start(bf16[480,128]{1,0:T(8,128)(2,1)S(1)} %get-tuple-element.105), channel_id=1, source_target_pairs={{0,8},{8,0},{16,24},{24,16},{1,9},{9,1},{17,25},{25,17},{2,10},{10... | collective-permute-start | bytes 368648 | tf_op jit(solution)/shard_map/ppermute | solution.py:1058
  119.6 5.7 %collective-permute-start.21 = (bf16[480,128]{1,0:T(8,128)(2,1)S(1)}, bf16[480,128]{1,0:T(8,128)(2,1)S(1)}, u32[]{:S(2)}, u32[]{:S(2)}) collective-permute-start(bf16[480,128]{1,0:T(8,128)(2,1)S(1)} %get-tuple-element.106), channel_id=1, source_target_pairs={{0,16},{8,24},{16,0},{24,8},{1,17},{9,25},{17,1},{25,9},{2,18},{10... | collective-permute-start | bytes 368648 | tf_op jit(solution)/shard_map/ppermute | solution.py:1058
  121.3 5.8 %collective-permute-start.22 = (bf16[480,128]{1,0:T(8,128)(2,1)S(1)}, bf16[480,128]{1,0:T(8,128)(2,1)S(1)}, u32[]{:S(2)}, u32[]{:S(2)}) collective-permute-start(bf16[480,128]{1,0:T(8,128)(2,1)S(1)} %get-tuple-element.107), channel_id=1, source_target_pairs={{0,24},{8,16},{16,8},{24,0},{1,25},{9,17},{17,9},{25,1},{2,26},{10... | collective-permute-start | bytes 368648 | tf_op jit(solution)/shard_map/ppermute | solution.py:1058
  128.2 1.2 collective-permute-start.23
  129.4 4.7 %collective-permute-start.24 = (f32[8,128]{1,0:T(8,128)S(1)}, f32[8,128]{1,0:T(8,128)S(1)}, u32[]{:S(2)}, u32[]{:S(2)}) collective-permute-start(f32[8,128]{1,0:T(8,128)S(1)} %shard_map.149.refs_0_), channel_id=1, source_target_pairs={{0,2},{1,3},{2,0},{3,1},{4,6},{5,7},{6,4},{7,5},{8,10},{9,11},{10,... | collective-permute-start | bytes 12296 | tf_op jit(solution)/shard_map/ppermute | solution.py:1058
  131.7 4.5 %collective-permute-start.25 = (f32[8,128]{1,0:T(8,128)S(1)}, f32[8,128]{1,0:T(8,128)S(1)}, u32[]{:S(2)}, u32[]{:S(2)}) collective-permute-start(f32[8,128]{1,0:T(8,128)S(1)} %shard_map.149.refs_0_), channel_id=1, source_target_pairs={{0,4},{1,5},{2,6},{3,7},{4,0},{5,1},{6,2},{7,3},{8,12},{9,13},{10,... | collective-permute-start | bytes 12296 | tf_op jit(solution)/shard_map/ppermute | solution.py:1058
  132.6 5.4 %collective-permute-start.26 = (f32[8,128]{1,0:T(8,128)S(1)}, f32[8,128]{1,0:T(8,128)S(1)}, u32[]{:S(2)}, u32[]{:S(2)}) collective-permute-start(f32[8,128]{1,0:T(8,128)S(1)} %shard_map.149.refs_0_), channel_id=1, source_target_pairs={{0,6},{1,7},{2,4},{3,5},{4,2},{5,3},{6,0},{7,1},{8,14},{9,15},{10,... | collective-permute-start | bytes 12296 | tf_op jit(solution)/shard_map/ppermute | solution.py:1058
  138.0 4.9 %collective-permute-start.27 = (f32[8,128]{1,0:T(8,128)S(1)}, f32[8,128]{1,0:T(8,128)S(1)}, u32[]{:S(2)}, u32[]{:S(2)}) collective-permute-start(f32[8,128]{1,0:T(8,128)S(1)} %shard_map.150.refs_0_), channel_id=1, source_target_pairs={{0,8},{8,0},{16,24},{24,16},{1,9},{9,1},{17,25},{25,17},{2,10},{10... | collective-permute-start | bytes 12296 | tf_op jit(solution)/shard_map/ppermute | solution.py:1058
  138.7 4.1 %collective-permute-start.28 = (f32[8,128]{1,0:T(8,128)S(1)}, f32[8,128]{1,0:T(8,128)S(1)}, u32[]{:S(2)}, u32[]{:S(2)}) collective-permute-start(f32[8,128]{1,0:T(8,128)S(1)} %shard_map.150.refs_0_), channel_id=1, source_target_pairs={{0,16},{8,24},{16,0},{24,8},{1,17},{9,25},{17,1},{25,9},{2,18},{10... | collective-permute-start | bytes 12296 | tf_op jit(solution)/shard_map/ppermute | solution.py:1058
  139.6 4.5 %collective-permute-start.29 = (f32[8,128]{1,0:T(8,128)S(1)}, f32[8,128]{1,0:T(8,128)S(1)}, u32[]{:S(2)}, u32[]{:S(2)}) collective-permute-start(f32[8,128]{1,0:T(8,128)S(1)} %shard_map.150.refs_0_), channel_id=1, source_target_pairs={{0,24},{8,16},{16,8},{24,0},{1,25},{9,17},{17,9},{25,1},{2,26},{10... | collective-permute-start | bytes 12296 | tf_op jit(solution)/shard_map/ppermute | solution.py:1058
  (6 other events, 71.8 us)

commit v4 on v3

--- a/solution.py
+++ b/solution.py
@@ -75,6 +75,7 @@
         ]
         self.win = round_up(max(self.rows) + 1, 16)
         self.tail = round_up(self.win + VEC_ROWS, 16 * FAR_PARTS)
+        self.upper = self.win * 3 // 4 // 16 * 16
         self.vec_place = ROW_VEC - self.start[-1]
         self.vec_from = self.vec_place // 16 * 16
         self.kept_row = 2 * self.win - self.vec_from
@@ -135,7 +136,7 @@
     return head_mean_low(high, matrix) + head_mean_low(rest, matrix)
 
 
-def prepare_kernel(plan, master_ref, keep_ref, out_ref):
+def prepare_kernel(plan, master_ref, keep_ref, upper_ref, lower_ref):
     me = plan.device()
     offset = lax.rem(me * plan.shard, LANES)
     values = master_ref[...]
@@ -147,17 +148,45 @@
     high = jnp.floor(count * (1.0 / 32.0))
     parts = jnp.where(lane == 0, high, jnp.where(lane == 1, count - 32.0 * high, 0.0))
     window = jnp.where(lane < offset, below, turned)
-    out_ref[...] = jnp.where(row == plan.win - 1, parts, window).astype(BF)
+    window = jnp.where(row == plan.win - 1, parts, window).astype(BF)
+    upper_ref[...] = window[: plan.upper]
+    lower_ref[...] = window[plan.upper :]
 
 
 def prepare(plan, master_rows, keep_row):
     return pl.pallas_call(
         functools.partial(prepare_kernel, plan),
-        out_shape=jax.ShapeDtypeStruct((plan.win, LANES), BF),
+        out_shape=(
+            jax.ShapeDtypeStruct((plan.upper, LANES), BF),
+            jax.ShapeDtypeStruct((plan.win - plan.upper, LANES), BF),
+        ),
         in_specs=[VMEM, VMEM],
-        out_specs=VMEM,
+        out_specs=(VMEM, VMEM),
         compiler_params=params(8),
     )(master_rows, keep_row)
+
+
+def ahead_kernel(tokens_ref, hat_ref, rstd_ref, token_ref):
+    hat, rstd = norm_parts(tokens_ref[...].astype(F32))
+    hat_ref[...] = hat
+    rstd_ref[...] = jnp.broadcast_to(rstd, rstd_ref.shape)
+    token_ref[...] = jnp.zeros_like(token_ref)
+
+
+def ahead(tokens):
+    rows = tokens.shape[0]
+    return pl.pallas_call(
+        ahead_kernel,
+        out_shape=(
+            jax.ShapeDtypeStruct((rows, D), F32),
+            jax.ShapeDtypeStruct((rows, LANES), F32),
+            jax.ShapeDtypeStruct((8, LANES), F32),
+        ),
+        in_specs=[VMEM],
+        out_specs=(VMEM,) * 3,
+        compiler_params=params(12),
+        cost_estimate=QUICK,
+    )(tokens)
 
 
 def held_window(own_ref, other_ref, rel, at):
@@ -256,7 +285,7 @@
     plan,
     own_ref,
     other_ref,
-    tokens_ref,
+    hat_in_ref,
     wq_ref,
     vec_ref,
     head_ref,
@@ -287,8 +316,7 @@
     gain1, shift1 = vec_ref[0:1, :], vec_ref[1:2, :]
     gain_q, gain_k = vec_ref[2:3, :], vec_ref[3:4, :]
 
-    hat, _ = norm_parts(tokens_ref[...].astype(F32))
-    raw = nn((hat * gain1 + shift1).astype(BF), wq_ref[...])
+    raw = nn((hat_in_ref[...] * gain1 + shift1).astype(BF), wq_ref[...])
 
     def head_norm(low_out, part, gain):
         lanes = slice(part * D, (part + 1) * D)
@@ -341,12 +369,14 @@
     v_ref,
     o_ref,
     ot_ref,
+    whole_ref,
     lse_ref,
     kab,
+    segk,
     vt,
     ot,
+    rest_t,
     sums,
-    segk,
     expo,
 ):
     seg_row = seg_ref[...].astype(F32)
@@ -360,6 +390,7 @@
 
     def query_tile(ti, carry):
         ot[...] = jnp.zeros_like(ot)
+        rest_t[...] = jnp.zeros_like(rest_t)
         sums[...] = jnp.zeros_like(sums)
         row_seg = seg_ref[:, rows_at(ti)].astype(F32)
         first, count = key_chunks(seg_smem, ti)
@@ -385,14 +416,16 @@
         def value_chunk(c, inner):
             keys = keys_at(first + 2 * c)
             for head in range(HEADS):
-                prob = (expo[c, head] * sums[head : head + 1, :]).astype(BF)
+                prob, rest = split_low(expo[c, head] * sums[head : head + 1, :])
                 at = slice(head * HD, (head + 1) * HD)
                 ot[at, :] += nn(vt[at, keys], prob)
+                rest_t[at, :] += nn(vt[at, keys], rest)
             return inner
 
         lax.fori_loop(0, count, value_chunk, 0)
         attended = ot[...]
         ot_ref[ti] = attended.astype(BF)
+        whole_ref[ti] = attended + rest_t[...]
         o_ref[rows_at(ti), :] = jnp.transpose(attended).astype(BF)
         return carry
 
@@ -406,16 +439,18 @@
         out_shape=(
             jax.ShapeDtypeStruct((rows, D), BF),
             jax.ShapeDtypeStruct((TILES, D, TILE), BF),
+            jax.ShapeDtypeStruct((TILES, D, TILE), F32),
             jax.ShapeDtypeStruct((TILES, 8, TILE), F32),
+            jax.ShapeDtypeStruct((PAIRS, BLOCKS, 2, LANES, LANES), BF),
+            jax.ShapeDtypeStruct((SEQ, LANES), F32),
         ),
         in_specs=[SMEM] + [VMEM] * 5,
-        out_specs=(VMEM,) * 3,
+        out_specs=(VMEM,) * 6,
         scratch_shapes=[
-            pltpu.VMEM((PAIRS, BLOCKS, 2, LANES, LANES), BF),
             pltpu.VMEM((D, SEQ), BF),
             pltpu.VMEM((D, TILE), F32),
+            pltpu.VMEM((D, TILE), F32),
             pltpu.VMEM((8, TILE), F32),
-            pltpu.VMEM((SEQ, LANES), F32),
             pltpu.VMEM((TILES, HEADS, TILE, TILE), F32),
         ],
         compiler_params=params(24),
@@ -577,58 +612,90 @@
     )(*late, tokens, cot, o, ot, head, kept, vec, keep_row, patches)
 
 
+def stack_kernel(
+    vec_ref,
+    hat_in_ref,
+    q_ref,
+    k_ref,
+    v_ref,
+    do_ref,
+    whole_ref,
+    vab,
+    qab,
+    dab,
+    kt,
+    inner_sums,
+    normed_ref,
+    token_ref,
+):
+    for step in range(TILES):
+        at = rows_at(step)
+        grads = do_ref[at, :]
+        for hp in range(PAIRS):
+            lanes = slice(hp * LANES, (hp + 1) * LANES)
+            put_blocks(vab, hp, step, v_ref[at, lanes])
+            qab[hp, step] = stack_heads(q_ref[at, lanes])
+            dab[hp, step] = stack_heads(grads[:, lanes])
+        kt[:, at] = jnp.transpose(k_ref[at, :].astype(F32)).astype(BF)
+        both = jnp.transpose(grads.astype(F32)) * whole_ref[step]
+        for head in range(HEADS):
+            inner_sums[step, head : head + 1, :] = jnp.sum(
+                both[head * HD : (head + 1) * HD], axis=0, keepdims=True
+            )
+        normed = hat_in_ref[at, :] * vec_ref[0:1, :] + vec_ref[1:2, :]
+        normed_ref[:, at] = jnp.transpose(normed).astype(BF)
+    token_ref[...] = jnp.zeros_like(token_ref)
+
+
+def stack_part(vec, hat_in, q, k, v, do, whole):
+    stacked = jax.ShapeDtypeStruct((PAIRS, TILES, 2 * TILE, LANES), BF)
+    return pl.pallas_call(
+        stack_kernel,
+        out_shape=(
+            jax.ShapeDtypeStruct((PAIRS, BLOCKS, 2, LANES, LANES), BF),
+            stacked,
+            stacked,
+            jax.ShapeDtypeStruct((D, SEQ), BF),
+            jax.ShapeDtypeStruct((TILES, 8, TILE), F32),
+            jax.ShapeDtypeStruct((D, SEQ), BF),
+            jax.ShapeDtypeStruct((8, LANES), F32),
+        ),
+        in_specs=[VMEM] * 7,
+        out_specs=(VMEM,) * 7,
+        compiler_params=params(16),
+        cost_estimate=QUICK,
+    )(vec, hat_in, q, k, v, do, whole)
+
+
 def backward_kernel(
     plan,
     vec_ref,
     seg_smem,
     seg_ref,
-    keep_ref,
     lse_ref,
     q_ref,
-    k_ref,
-    v_ref,
-    o_ref,
     do_ref,
     hat_ref,
     rstd_ref,
-    token_ref,
-    low_ref,
-    gains_ref,
+    segk,
     kab,
     vab,
     qab,
     dab,
     kt,
+    inner_sums,
+    token_ref,
+    low_ref,
+    gains_ref,
     dqt,
     dk,
     dv,
-    inner_sums,
-    segk,
 ):
     matrix = head_mean_matrix()
-    seg_row = seg_ref[...].astype(F32)
-    segk[...] = to_column(jnp.where(keep_ref[...] == 1, seg_row, -1.0))
-    head_row = lax.broadcasted_iota(jnp.int32, (8, D), 0)
-    head_lane = lax.broadcasted_iota(jnp.int32, (8, D), 1)
-    hot = jnp.where(head_lane // HD == head_row, 1.0, 0.0).astype(BF)
     dqt[...] = jnp.zeros_like(dqt)
     dk[...] = jnp.zeros_like(dk)
     dv[...] = jnp.zeros_like(dv)
     gains_ref[...] = jnp.zeros_like(gains_ref)
-
-    for step in range(TILES):
-        at = rows_at(step)
-        keys = k_ref[at, :]
-        grads = do_ref[at, :]
-        for hp in range(PAIRS):
-            lanes = slice(hp * LANES, (hp + 1) * LANES)
-            put_blocks(kab, hp, step, keys[:, lanes])
-            put_blocks(vab, hp, step, v_ref[at, lanes])
-            qab[hp, step] = stack_heads(q_ref[at, lanes])
-            dab[hp, step] = stack_heads(grads[:, lanes])
-        kt[:, at] = jnp.transpose(keys.astype(F32)).astype(BF)
-        high, rest = split_low(grads.astype(F32) * o_ref[at, :].astype(F32))
-        inner_sums[step] = nt(hot, high) + nt(hot, rest)
 
     def query_tile(ti, carry):
         row_seg = seg_ref[:, rows_at(ti)].astype(F32)
@@ -639,25 +706,32 @@
             keys = keys_at(block)
             column = segk[keys, :]
             bias = tile_bias(ti, block, row_seg, jnp.concatenate([column, column], axis=1))
+            raw = []
             for hp in range(PAIRS):
                 lanes = slice(hp * LANES, (hp + 1) * LANES)
-                scores = nt(two_blocks(kab, hp, block), q_ref[rows_at(ti), lanes])
-                grads = nt(two_blocks(vab, hp, block), do_ref[rows_at(ti), lanes])
-                probs, dscores = [], []
-                for side in range(2):
-                    head = 2 * hp + side
-                    prob = jnp.exp2(
-                        side_rows(scores, side) * score_scale
-                        + (bias - lse_ref[ti, head : head + 1, :])
+                raw.append(
+                    (
+                        nt(two_blocks(kab, hp, block), q_ref[rows_at(ti), lanes]),
+                        nt(two_blocks(vab, hp, block), do_ref[rows_at(ti), lanes]),
                     )
-                    dscore = prob * (side_rows(grads, side) - inner_sums[ti, head : head + 1, :])
-                    dscore = dscore.astype(BF)
-                    probs.append(prob.astype(BF))
-                    dscores.append(dscore)
+                )
+            probs, dscores = [], []
+            for head in range(HEADS):
+                scores, grads = raw[head // 2]
+                prob = jnp.exp2(
+                    side_rows(scores, head % 2) * score_scale
+                    + (bias - lse_ref[ti, head : head + 1, :])
+                )
+                dscore = prob * (side_rows(grads, head % 2) - inner_sums[ti, head : head + 1, :])
+                probs.append(prob.astype(BF))
+                dscores.append(dscore.astype(BF))
+            for hp in range(PAIRS):
+                pair = slice(2 * hp, 2 * hp + 2)
+                for head in (2 * hp, 2 * hp + 1):
                     at = slice(head * HD, (head + 1) * HD)
-                    dqt[ti, at, :] += nn(kt[at, keys], dscore)
-                dv[hp, keys] += nn(jnp.concatenate(probs, axis=1), dab[hp, ti])
-                dk[hp, keys] += nn(jnp.concatenate(dscores, axis=1), qab[hp, ti])
+                    dqt[ti, at, :] += nn(kt[at, keys], dscores[head])
+                dv[hp, keys] += nn(jnp.concatenate(probs[pair], axis=1), dab[hp, ti])
+                dk[hp, keys] += nn(jnp.concatenate(dscores[pair], axis=1), qab[hp, ti])
             return inner
 
         lax.fori_loop(0, count, key_chunk, 0)
@@ -689,40 +763,31 @@
     lax.fori_loop(0, TILES, finish, 0)
 
 
-def backward(plan, vec, seg, seg_row, keep_row, lse, q, k, v, o, do, hat, rstd, token):
+def backward(plan, vec, seg, seg_row, lse, q, do, hat, rstd, segk, stacks, token):
     rows = q.shape[0]
-    stacked = pltpu.VMEM((PAIRS, TILES, 2 * TILE, LANES), BF)
-    blocked = pltpu.VMEM((PAIRS, BLOCKS, 2, LANES, LANES), BF)
     return pl.pallas_call(
         functools.partial(backward_kernel, plan),
         out_shape=(
             jax.ShapeDtypeStruct((rows, 3 * D), BF),
             jax.ShapeDtypeStruct((8, D), F32),
         ),
-        in_specs=[VMEM, SMEM] + [VMEM] * 11,
+        in_specs=[VMEM, SMEM] + [VMEM] * 14,
         out_specs=(VMEM, VMEM),
         scratch_shapes=[
-            blocked,
-            blocked,
-            stacked,
-            stacked,
-            pltpu.VMEM((D, SEQ), BF),
             pltpu.VMEM((TILES, D, TILE), F32),
             pltpu.VMEM((PAIRS, SEQ, LANES), F32),
             pltpu.VMEM((PAIRS, SEQ, LANES), F32),
-            pltpu.VMEM((TILES, 8, TILE), F32),
-            pltpu.VMEM((SEQ, LANES), F32),
         ],
-        compiler_params=params(32),
+        compiler_params=params(26),
         cost_estimate=QUICK,
-    )(vec, seg, seg_row, keep_row, lse, q, k, v, o, do, hat, rstd, token)
+    )(vec, seg, seg_row, lse, q, do, hat, rstd, segk, *stacks, token)
 
 
 def finish_kernel(
     plan,
-    tokens_ref,
+    hat_ref,
+    normed_ref,
     wq_ref,
-    vec_ref,
     tail_ref,
     gvec_ref,
     low_ref,
@@ -732,10 +797,9 @@
     *refs,
 ):
     *far_refs, gains, flat = refs
-    hat, _ = norm_parts(tokens_ref[...].astype(F32))
-    normed = jnp.transpose(hat * vec_ref[0:1, :] + vec_ref[1:2, :]).astype(BF)
+    hat = hat_ref[...]
     for i in range(3):
-        part = nn(normed, low_ref[:, i * D : (i + 1) * D])
+        part = nn(normed_ref[...], low_ref[:, i * D : (i + 1) * D])
         for j in range(D // LANES):
             flat[pl.ds(i * (D // LANES) + j, D, stride=3 * D // LANES), :] = part[
                 :, j * LANES : (j + 1) * LANES
@@ -774,8 +838,8 @@
                 far_ref[reld] = window[i * height : (i + 1) * height]
 
 
-def finish_part(plan, tokens, wq, vec, tail, gvec, low, gains):
-    rows = tokens.shape[0]
+def finish_part(plan, hat, normed, wq, tail, gvec, low, gains):
+    rows = hat.shape[0]
     windows = jax.ShapeDtypeStruct((plan.nd // 2, plan.tail, LANES), BF)
     part = jax.ShapeDtypeStruct((plan.nd // 2, plan.tail // FAR_PARTS, LANES), BF)
     return pl.pallas_call(
@@ -789,27 +853,27 @@
         ],
         compiler_params=params(28),
         cost_estimate=QUICK,
-    )(tokens, wq, vec, tail, gvec, low, gains)
-
-
-def input_kernel(tokens_ref, vec_ref, da1_ref, dh1_ref, grad_ref, token_ref):
-    hat, rstd = norm_parts(tokens_ref[...].astype(F32))
-    grad_ref[...] = dh1_ref[...] + norm_back(hat, rstd, da1_ref[...] * vec_ref[0:1, :])
+    )(hat, normed, wq, tail, gvec, low, gains)
+
+
+def input_kernel(hat_ref, rstd_ref, vec_ref, da1_ref, dh1_ref, grad_ref, token_ref):
+    back = norm_back(hat_ref[...], rstd_ref[:, 0:1], da1_ref[...] * vec_ref[0:1, :])
+    grad_ref[...] = dh1_ref[...] + back
     token_ref[...] = jnp.zeros_like(token_ref)
 
 
-def input_part(tokens, vec, da1, dh1):
+def input_part(hat, rstd, vec, da1, dh1):
     return pl.pallas_call(
         input_kernel,
         out_shape=(
             jax.ShapeDtypeStruct(dh1.shape, F32),
             jax.ShapeDtypeStruct((8, LANES), F32),
         ),
-        in_specs=[VMEM] * 4,
+        in_specs=[VMEM] * 5,
         out_specs=(VMEM, VMEM),
         compiler_params=params(16),
         cost_estimate=QUICK,
-    )(tokens, vec, da1, dh1)
+    )(hat, rstd, vec, da1, dh1)
 
 
 def flat_place(plan, shape):
@@ -919,55 +983,50 @@
     )(*sums, master_rows, update_rows)
 
 
-def lay_column_kernel(*refs):
-    for i, part in enumerate(refs[:-1]):
+def lay_column_kernel(count, *refs):
+    for i, part in enumerate(refs[:count]):
         refs[-1][i] = part[...]
 
 
-def lay_column(parts):
-    return pl.pallas_call(
-        lay_column_kernel,
+def lay_column(parts, *after):
+    return pl.pallas_call(
+        functools.partial(lay_column_kernel, len(parts)),
         out_shape=jax.ShapeDtypeStruct((len(parts), *parts[0].shape), parts[0].dtype),
-        in_specs=[VMEM] * len(parts),
+        in_specs=[VMEM] * (len(parts) + len(after)),
         out_specs=VMEM,
         compiler_params=params(4),
-    )(*parts)
+    )(*parts, *after)
 
 
 def choose_kernel(plan, *refs):
-    columns, early_ref, late_refs = refs[: plan.nb], refs[plan.nb], refs[plan.nb + 1 :]
+    columns, (lower_ref, _, early_ref), late_refs = (
+        refs[: plan.nb],
+        refs[plan.nb : plan.nb + 3],
+        refs[plan.nb + 3 :],
+    )
     bucket = lax.axis_index("bucket")
-    early_ref[:, plan.kept_row :] = columns[0][:, plan.win - 16 :]
+    early_ref[:, plan.kept_row :] = lower_ref[:, 0, plan.win - plan.upper - 16 :]
     for i, part in enumerate(columns):
-        owner = jnp.bitwise_xor(bucket, i)
-
-        @pl.when(owner == 0)
-        def _():
-            early_ref[:, : plan.win] = part[...]
-
-        @pl.when(owner == plan.nb - 1)
-        def _():
-            early_ref[:, plan.win : plan.kept_row] = part[:, plan.vec_from :]
-
-        for quarter, late_ref in enumerate(late_refs):
-
-            @pl.when(owner == quarter + 1)
+        for owner, out_ref in enumerate((early_ref, *late_refs)):
+
+            @pl.when(jnp.bitwise_xor(bucket, i) == owner)
             def _():
-                late_ref[...] = part[...]
-
-
-def choose(plan, columns):
+                out_ref[:, : plan.upper] = part[...]
+                out_ref[:, plan.upper : plan.win] = lower_ref[:, i]
+
+    early_ref[:, plan.win : plan.kept_row] = late_refs[-1][:, plan.vec_from :]
+
+
+def choose(plan, columns, lower, token):
     step = columns[0].shape[0]
+    late = jax.ShapeDtypeStruct((step, plan.win, LANES), BF)
     return pl.pallas_call(
         functools.partial(choose_kernel, plan),
-        out_shape=(
-            jax.ShapeDtypeStruct((step, plan.early, LANES), BF),
-        )
-        + (jax.ShapeDtypeStruct(columns[0].shape, BF),) * (plan.nb - 1),
-        in_specs=[VMEM] * len(columns),
+        out_shape=(jax.ShapeDtypeStruct((step, plan.early, LANES), BF),) + (late,) * (plan.nb - 1),
+        in_specs=[VMEM] * (len(columns) + 2),
         out_specs=(VMEM,) * plan.nb,
-        compiler_params=params(8),
-    )(*columns)
+        compiler_params=params(10),
+    )(*columns, lower, token)
 
 
 def add_parts_kernel(halves, *refs):
@@ -1069,13 +1128,18 @@
     return [x] + [swap(x, axis, size, mask) for mask in masks_of(bits)]
 
 
-def gather_windows(plan, window):
+def gather_windows(plan, upper, lower, token):
     first, *more = groups_of(plan.nd, 1)
-    column = lay_column(with_partners(window, "dp", plan.nd, first))
-    for bits in more:
-        column = jnp.concatenate(with_partners(column, "dp", plan.nd, bits), axis=0)
     (bits,) = groups_of(plan.nb)
-    early, *late = choose(plan, with_partners(column, "bucket", plan.nb, bits))
+    lower = lay_column(with_partners(lower, "bucket", plan.nb, bits))
+    column = lay_column(with_partners(upper, "dp", plan.nd, first), lower)
+    for group in more:
+        column = jnp.concatenate(with_partners(column, "dp", plan.nd, group), axis=0)
+    columns = with_partners(column, "bucket", plan.nb, bits)
+    lower = lay_column(with_partners(lower, "dp", plan.nd, first))
+    for group in more:
+        lower = jnp.concatenate(with_partners(lower, "dp", plan.nd, group), axis=0)
+    early, *late = choose(plan, columns, lower, token)
     others = [swap(x, "dp", plan.nd, 1) for x in (early, *late)]
     return (early, others[0]), (*late, *others[1:])
 
@@ -1120,19 +1184,21 @@
     count = 1 << len(groups_of(plan.nd, 1)[-1])
     (b_bits,) = groups_of(plan.nb)
 
-    early, late = gather_windows(plan, prepare(plan, master_rows, keep_row))
-    wq, vec, head, kept, q, k, v, hat, rstd = project_part(plan, *early, tokens)
-    o, ot, lse = forward(plan, segment_ids, seg_row, keep_row, q, k, v)
+    hat_in, rstd_in, token = ahead(tokens)
+    early, late = gather_windows(plan, *prepare(plan, master_rows, keep_row), token)
+    wq, vec, head, kept, q, k, v, hat, rstd = project_part(plan, *early, hat_in)
+    o, ot, whole, lse, kab, segk = forward(plan, segment_ids, seg_row, keep_row, q, k, v)
     block_output, dh1, do, near, far, tail, gvec = middle_part(
         plan, late, tokens, cotangent, o, ot, head, kept, vec, keep_row, bucket_patches
     )
-    *pieces, token = add_parts([near, swap(far, "dp", plan.nd, 1)], count, gvec)
+    *stacks, normed, token = stack_part(vec, hat_in, q, k, v, do, whole)
+    *pieces, token = add_parts([near, swap(far, "dp", plan.nd, 1)], count, token)
     rest = scatter_dp(plan, pieces)
     low, gains = backward(
-        plan, vec, segment_ids, seg_row, keep_row, lse, q, k, v, o, do, hat, rstd, token
+        plan, vec, segment_ids, seg_row, lse, q, do, hat, rstd, segk, [kab, *stacks], token
     )
-    da1, near, *far = finish_part(plan, tokens, wq, vec, tail, gvec, low, gains)
-    input_grad, given = input_part(tokens, vec, da1, dh1)
+    da1, near, *far = finish_part(plan, hat_in, normed, wq, tail, gvec, low, gains)
+    input_grad, given = input_part(hat_in, rstd_in, vec, da1, dh1)
     *late_parts, token = add_parts(rest[:2], 1, gains)
     late_parts += rest[2:]
     *pieces, _ = add_parts([near, [swap(half, "dp", plan.nd, 1) for half in far]], count, token)

time: 148 us -> 142 us (0.959); the launches traced: 146 us -> 141 us
  waiting for transfers between devices: 53.3 us -> 35.6 us
  starting transfers between devices: 32.6 us -> 48.5 us
  Pallas kernels: 55 us -> 52.5 us
    ppermute x30 -> x36, waiting for transfers between devices: 53.3 us -> 35.6 us  [swap(): return lax.ppermute(x, axis, [(i, i ^ mask) for i in range(size)])]
    ppermute x30 -> x36, starting transfers between devices: 32.6 us -> 48.5 us  [swap(): return lax.ppermute(x, axis, [(i, i ^ mask) for i in range(size)])]
    pallas_call x1, Pallas kernels: 16.3 us -> 11.9 us  [backward(): pl.pallas_call(functools.partial(backward_kernel, plan), out_shape=(jax.S...]
    pallas_call x2 -> x6, Pallas kernels: 0.15 us -> 2.14 us  [the longest x1 1.51 us: stack_part(): pl.pallas_call(stack_kernel, out_shape=(jax.ShapeDtypeStruct((PAIRS, BLOC...]
  transfers between devices with their start and end apart: 30 -> 36, of which waited for: 17 -> 18; matrix products, arithmetic and copies ran while one was open for 1% -> 1% of each run, Pallas kernels for 24% -> 23%
where the time goes in v4:
time: 142 us; the launch traced here: 141 us
  Pallas kernels  52.5 us (37%)
  starting transfers between devices  48.5 us (34%)
  waiting for transfers between devices  35.6 us (25%)
  local copies, waits for them, and re-layouts  3.88 us (3%)
    ppermute x36, starting transfers between devices, swap(): return lax.ppermute(x, axis, [(i, i ^ mask) for i in range(size)])  48.5 us
    ppermute x36, waiting for transfers between devices, swap(): return lax.ppermute(x, axis, [(i, i ^ mask) for i in range(size)])  35.6 us
    pallas_call x1, Pallas kernels, middle_part(): pl.pallas_call(functools.partial(middle_kernel, plan), out_shape=(jax.Sha...  17.6 us
    pallas_call x1, Pallas kernels, backward(): pl.pallas_call(functools.partial(backward_kernel, plan), out_shape=(jax.S...  11.9 us
    pallas_call x1, Pallas kernels, forward(): pl.pallas_call(functools.partial(forward_kernel, plan), out_shape=(jax.Sh...  8.72 us
    pallas_call x1, Pallas kernels, project_part(): pl.pallas_call(functools.partial(project_kernel, plan), out_shape=(jax.Sh...  3.72 us
    pallas_call x1, Pallas kernels, finish_part(): pl.pallas_call(functools.partial(finish_kernel, plan), out_shape=(jax.Sha...  2.9 us
  transfers between devices with their start and end apart: 36, of which 18 were waited for; matrix products, arithmetic and copies ran while one was open for 1% of the time, Pallas kernels for 23%

profile of v4, /device:TPU:0, one launch (start us, length us, event | category | flops | bytes accessed | tf_op | source)
XLA Modules:
  0.0 141.4 jit_solution(13711499059811470884)
XLA Ops:
  2.5 3.1 %collective-permute-start = (bf16[336,128]{1,0:T(8,128)(2,1)S(1)}, bf16[336,128]{1,0:T(8,128)(2,1)S(1)}, u32[]{:S(2)}, u32[]{:S(2)}) collective-permute-start(bf16[336,128]{1,0:T(8,128)(2,1)S(1)} %get-tuple-element.76.refs_0_), channel_id=1, source_target_pairs={{0,2},{1,3},{2,0},{3,1},{4,6},{5,7},{6,4},{7,5},{8,10},{9,11},{10,... | collective-permute-start | bytes 258056 | tf_op jit(solution)/shard_map/ppermute | solution.py:1117
  5.6 2.6 %collective-permute-start.1 = (bf16[336,128]{1,0:T(8,128)(2,1)S(1)}, bf16[336,128]{1,0:T(8,128)(2,1)S(1)}, u32[]{:S(2)}, u32[]{:S(2)}) collective-permute-start(bf16[336,128]{1,0:T(8,128)(2,1)S(1)} %get-tuple-element.76.refs_0_), channel_id=1, source_target_pairs={{0,4},{1,5},{2,6},{3,7},{4,0},{5,1},{6,2},{7,3},{8,12},{9,13},{10,... | collective-permute-start | bytes 258056 | tf_op jit(solution)/shard_map/ppermute | solution.py:1117
  8.2 1.7 %collective-permute-start.3 = (bf16[112,128]{1,0:T(8,128)(2,1)S(1)}, bf16[112,128]{1,0:T(8,128)(2,1)S(1)}, u32[]{:S(2)}, u32[]{:S(2)}) collective-permute-start(bf16[112,128]{1,0:T(8,128)(2,1)S(1)} %get-tuple-element.77.refs_0_), channel_id=1, source_target_pairs={{0,8},{8,0},{16,24},{24,16},{1,9},{9,1},{17,25},{25,17},{2,10},{10... | collective-permute-start | bytes 86024 | tf_op jit(solution)/shard_map/ppermute | solution.py:1117
  9.9 1.5 %collective-permute-start.4 = (bf16[112,128]{1,0:T(8,128)(2,1)S(1)}, bf16[112,128]{1,0:T(8,128)(2,1)S(1)}, u32[]{:S(2)}, u32[]{:S(2)}) collective-permute-start(bf16[112,128]{1,0:T(8,128)(2,1)S(1)} %get-tuple-element.77.refs_0_), channel_id=1, source_target_pairs={{0,16},{8,24},{16,0},{24,8},{1,17},{9,25},{17,1},{25,9},{2,18},{10... | collective-permute-start | bytes 86024 | tf_op jit(solution)/shard_map/ppermute | solution.py:1117
  12.0 2.7 %collective-permute-start.5 = (bf16[112,128]{1,0:T(8,128)(2,1)S(1)}, bf16[112,128]{1,0:T(8,128)(2,1)S(1)}, u32[]{:S(2)}, u32[]{:S(2)}) collective-permute-start(bf16[112,128]{1,0:T(8,128)(2,1)S(1)} %get-tuple-element.77.refs_0_), channel_id=1, source_target_pairs={{0,24},{8,16},{16,8},{24,0},{1,25},{9,17},{17,9},{25,1},{2,26},{10... | collective-permute-start | bytes 86024 | tf_op jit(solution)/shard_map/ppermute | solution.py:1117
  14.7 2.1 %collective-permute-done.5.refs_3_ = bf16[112,128]{1,0:T(8,128)(2,1)S(1)} collective-permute-done((bf16[112,128]{1,0:T(8,128)(2,1)S(1)}, bf16[112,128]{1,0:T(8,128)(2,1)S(1)}, u32[]{:S(2)}, u32[]{:S(2)}) %collective-permute-start.5) | collective-permute-done | bytes 28704 | tf_op jit(solution)/shard_map/ppermute | solution.py:1117
  16.9 1.8 %collective-permute-start.6 = (bf16[4,336,128]{2,1,0:T(8,128)(2,1)S(1)}, bf16[4,336,128]{2,1,0:T(8,128)(2,1)S(1)}, u32[]{:S(2)}, u32[]{:S(2)}) collective-permute-start(bf16[4,336,128]{2,1,0:T(8,128)(2,1)S(1)} %shard_map.137.refs_0_), channel_id=1, source_target_pairs={{0,8},{8,0},{16,24},{24,16},{1,9},{9,1},{17,25},{25,17},{2,10},{10... | collective-permute-start | bytes 1032200 | tf_op jit(solution)/shard_map/ppermute | solution.py:1117
  18.7 1.5 %collective-permute-start.7 = (bf16[4,336,128]{2,1,0:T(8,128)(2,1)S(1)}, bf16[4,336,128]{2,1,0:T(8,128)(2,1)S(1)}, u32[]{:S(2)}, u32[]{:S(2)}) collective-permute-start(bf16[4,336,128]{2,1,0:T(8,128)(2,1)S(1)} %shard_map.137.refs_0_), channel_id=1, source_target_pairs={{0,16},{8,24},{16,0},{24,8},{1,17},{9,25},{17,1},{25,9},{2,18},{10... | collective-permute-start | bytes 1032200 | tf_op jit(solution)/shard_map/ppermute | solution.py:1117
  21.3 3.5 %collective-permute-start.10 = (bf16[4,112,128]{2,1,0:T(8,128)(2,1)S(1)}, bf16[4,112,128]{2,1,0:T(8,128)(2,1)S(1)}, u32[]{:S(2)}, u32[]{:S(2)}) collective-permute-start(bf16[4,112,128]{2,1,0:T(8,128)(2,1)S(1)} %shard_map.136.refs_4_.refs_0_), channel_id=1, source_target_pairs={{0,4},{1,5},{2,6},{3,7},{4,0},{5,1},{6,2},{7,3},{8,12},{9,13},{10,... | collective-permute-start | bytes 344072 | tf_op jit(solution)/shard_map/ppermute | solution.py:1117
  25.2 5.5 %collective-permute-start.11 = (bf16[4,112,128]{2,1,0:T(8,128)(2,1)S(1)}, bf16[4,112,128]{2,1,0:T(8,128)(2,1)S(1)}, u32[]{:S(2)}, u32[]{:S(2)}) collective-permute-start(bf16[4,112,128]{2,1,0:T(8,128)(2,1)S(1)} %shard_map.136.refs_4_.refs_0_), channel_id=1, source_target_pairs={{0,6},{1,7},{2,4},{3,5},{4,2},{5,3},{6,0},{7,1},{8,14},{9,15},{10,... | collective-permute-start | bytes 344072 | tf_op jit(solution)/shard_map/ppermute | solution.py:1117
  31.2 2.3 %collective-permute-done.11.refs_3_ = bf16[4,112,128]{2,1,0:T(8,128)(2,1)S(1)} collective-permute-done((bf16[4,112,128]{2,1,0:T(8,128)(2,1)S(1)}, bf16[4,112,128]{2,1,0:T(8,128)(2,1)S(1)}, u32[]{:S(2)}, u32[]{:S(2)}) %collective-permute-start.11) | collective-permute-done | bytes 114720 | tf_op jit(solution)/shard_map/ppermute | solution.py:1117
  35.8 3.7 %shard_map.141 = (bf16[384,1152]{1,0:T(8,128)(2,1)S(1)}, f32[8,384]{1,0:T(8,128)S(1)}, f32[8,128]{1,0:T(8,128)S(1)}, f32[8,128]{1,0:T(8,128)S(1)}, bf16[1024,384...) custom-call(bf16[4,512,128]{2,1,0:T(8,128)(2,1)S(1)} %get-tuple-elem, ...), custom_call_target="tpu_custom_call" | custom-call | flops 1000 | bytes 1000 | tf_op jit(solution)/shard_map/pallas_call | solution.py:339
  39.6 8.7 %shard_map.142 = (bf16[1024,384]{1,0:T(8,128)(2,1)S(1)}, bf16[4,384,256]{2,1,0:T(8,128)(2,1)S(1)}, f32[4,384,256]{2,1,0:T(8,128)S(1)}, f32[4,8,256]{2,1,0:T(8,12...) custom-call(s32[1024]{0:T(1024)S(1)} %copy-done.2, s32[1,1024]{1,0:T(1,128)S(1)} %bitcast.34, ...), custom_call_target="tpu_custom_call" | custom-call | flops 1000 | bytes 1000 | tf_op jit(solution)/shard_map/pallas_call | solution.py:437
  48.4 17.6 %shard_map.143 = (bf16[1024,384]{1,0:T(8,128)(2,1)}, f32[1024,384]{1,0:T(8,128)S(1)}, bf16[1024,384]{1,0:T(8,128)(2,1)S(1)}, bf16[3,4,448,128]{3,2,1,0:T(8,128)(...) custom-call(bf16[4,448,128]{2,1,0:T(8,128)(2,1)S(1)} %get-tuple-element.79.refs_0_, ...), custom_call_target="tpu_custom_call" | custom-call | flops 1000 | bytes 1000 | tf_op jit(solution)/shard_map/pallas_call | solution.py:588
  66.1 1.5 %shard_map.144 = (bf16[3,8,2,128,128]{4,3,2,1,0:T(8,128)(2,1)S(1)}, bf16[3,4,512,128]{3,2,1,0:T(8,128)(2,1)S(1)}, bf16[3,4,512,128]{3,2,1,0:T(8,128)(2,1)S(1)}, ...) custom-call(f32[8,384]{1,0:T(8,128)S(1)} %get-tuple-element.91.refs_, ...), custom_call_target="tpu_custom_call" | custom-call | flops 1000 | bytes 1000 | tf_op jit(solution)/shard_map/pallas_call | solution.py:652
  67.6 1.5 %collective-permute-done.16.refs_1_ = bf16[3,4,448,128]{3,2,1,0:T(8,128)(2,1)S(1)} collective-permute-done((bf16[3,4,448,128]{3,2,1,0:T(8,128)(2,1)S(1)}, bf16[3,4,448,128]{3,2,1,0:T(8,128)(2,1)S(1)}, u32[]{:S(2)}, u32[]{:S(2)}) %collective-permute-start.16) | collective-permute-done | bytes 1376288 | tf_op jit(solution)/shard_map/ppermute | solution.py:1117
  69.9 4.0 %collective-permute-start.18 = (bf16[3,1,448,128]{3,2,0,1:T(8,128)(2,1)S(1)}, bf16[3,1,448,128]{3,2,0,1:T(8,128)(2,1)S(1)}, u32[]{:S(2)}, u32[]{:S(2)}) collective-permute-start(bf16[3,1,448,128]{3,2,0,1:T(8,128)(2,1)S(1)} %bitcast.40), channel_id=1, source_target_pairs={{0,4},{1,5},{2,6},{3,7},{4,0},{5,1},{6,2},{7,3},{8,12},{9,13},{10,... | collective-permute-start | bytes 1032200 | tf_op jit(solution)/shard_map/ppermute | solution.py:1117
  73.9 11.9 %shard_map.146 = (bf16[1024,1152]{1,0:T(8,128)(2,1)S(1)}, f32[8,384]{1,0:T(8,128)S(1)}) custom-call(f32[8,384]{1,0:T(8,128)S(1)} %get-tuple-element.91.refs_12_.vec_ref, s32[1024]{0:T(1024)S(1)} %copy-done.2, s32[1,1024]{1,0:T(1,128)S(1)} %bitcast.35, f32[4,8,256]{2,1,0:T(8,128)S(1)} %get-tuple-element.100.lse_ref, ...), custom_call_target="tpu_custom_call" | custom-call | flops 1000 | bytes 1000 | tf_op jit(solution)/shard_map/pallas_call | solution.py:768
  85.7 2.9 %shard_map.147 = (f32[1024,384]{1,0:T(8,128)S(1)}, bf16[4,480,128]{2,1,0:T(8,128)(2,1)S(1)}, bf16[4,160,128]{2,1,0:T(8,128)(2,1)S(1)}, bf16[4,160,128]{2,1,0:T(8,128)(2,1)S(1)}, bf16[4,160,128]{2,1,0:T(8,128)(2,1)S(1)}) custom-call(f32[1024,384]{1,0:T(8,128)S(1)} %get-tuple-element.83.hat_in_ref.hat_ref, bf16[384,1024]{1,0:T(8,128)(2,1)S(1)} %get-tuple-element.96.normed_ref, ...), custom_call_target="tpu_custom_call" | custom-call | flops 1000 | bytes 1000 | tf_op jit(solution)/shard_map/pallas_call | solution.py:845
  91.9 3.8 %collective-permute-start.24 = (bf16[1,480,128]{2,1,0:T(8,128)(2,1)S(1)}, bf16[1,480,128]{2,1,0:T(8,128)(2,1)S(1)}, u32[]{:S(2)}, u32[]{:S(2)}) collective-permute-start(bf16[1,480,128]{2,1,0:T(8,128)(2,1)S(1)} %get-tuple-element.132), channel_id=1, source_target_pairs={{0,4},{1,5},{2,6},{3,7},{4,0},{5,1},{6,2},{7,3},{8,12},{9,13},{10,... | collective-permute-start | bytes 368648 | tf_op jit(solution)/shard_map/ppermute | solution.py:1117
  95.7 2.0 %shard_map.148 = (f32[1024,384]{1,0:T(8,128)}, f32[8,128]{1,0:T(8,128)S(1)}) custom-call(f32[1024,384]{1,0:T(8,128)S(1)} %get-tuple-element.83.hat_in_ref.hat_ref, f32[1024,128]{1,0:T(8,128)S(1)} %get-tuple-element.93.rstd_ref, f32[8,384]{1,0:T(8,128)S(1)} %get-tuple-element.91.refs_12_.vec_ref, f32[1024,384]{1,0:T(8,128)S(1)} %get-tuple-element.116.da1_ref, ...), custom_call_target="tpu_custom_call" | custom-call | flops 1000 | bytes 1000 | tf_op jit(solution)/shard_map/pallas_call | solution.py:866
  97.7 1.9 %collective-permute-done.23 = bf16[1,480,128]{2,1,0:T(8,128)(2,1)S(1)} collective-permute-done((bf16[1,480,128]{2,1,0:T(8,128)(2,1)S(1)}, bf16[1,480,128]{2,1,0:T(8,128)(2,1)S(1)}, u32[]{:S(2)}, u32[]{:S(2)}) %collective-permute-start.23) | collective-permute-done | bytes 122912 | tf_op jit(solution)/shard_map/ppermute | solution.py:1117
  99.7 13.2 %collective-permute-done.24 = bf16[1,480,128]{2,1,0:T(8,128)(2,1)S(1)} collective-permute-done((bf16[1,480,128]{2,1,0:T(8,128)(2,1)S(1)}, bf16[1,480,128]{2,1,0:T(8,128)(2,1)S(1)}, u32[]{:S(2)}, u32[]{:S(2)}) %collective-permute-start.24) | collective-permute-done | bytes 122912 | tf_op jit(solution)/shard_map/ppermute | solution.py:1117
  113.2 1.7 %collective-permute-start.27 = (bf16[480,128]{1,0:T(8,128)(2,1)S(1)}, bf16[480,128]{1,0:T(8,128)(2,1)S(1)}, u32[]{:S(2)}, u32[]{:S(2)}) collective-permute-start(bf16[480,128]{1,0:T(8,128)(2,1)S(1)} %get-tuple-element.136), channel_id=1, source_target_pairs={{0,16},{8,24},{16,0},{24,8},{1,17},{9,25},{17,1},{25,9},{2,18},{10... | collective-permute-start | bytes 368648 | tf_op jit(solution)/shard_map/ppermute | solution.py:1117
  114.9 1.7 %collective-permute-start.28 = (bf16[480,128]{1,0:T(8,128)(2,1)S(1)}, bf16[480,128]{1,0:T(8,128)(2,1)S(1)}, u32[]{:S(2)}, u32[]{:S(2)}) collective-permute-start(bf16[480,128]{1,0:T(8,128)(2,1)S(1)} %get-tuple-element.137), channel_id=1, source_target_pairs={{0,24},{8,16},{16,8},{24,0},{1,25},{9,17},{17,9},{25,1},{2,26},{10... | collective-permute-start | bytes 368648 | tf_op jit(solution)/shard_map/ppermute | solution.py:1117
  116.7 2.0 %collective-permute-done.26.got0_ref = bf16[480,128]{1,0:T(8,128)(2,1)S(1)} collective-permute-done((bf16[480,128]{1,0:T(8,128)(2,1)S(1)}, bf16[480,128]{1,0:T(8,128)(2,1)S(1)}, u32[]{:S(2)}, u32[]{:S(2)}) %collective-permute-start.26) | collective-permute-done | bytes 122912 | tf_op jit(solution)/shard_map/ppermute | solution.py:1117
  119.5 1.6 %collective-permute-done.28.got2_ref = bf16[480,128]{1,0:T(8,128)(2,1)S(1)} collective-permute-done((bf16[480,128]{1,0:T(8,128)(2,1)S(1)}, bf16[480,128]{1,0:T(8,128)(2,1)S(1)}, u32[]{:S(2)}, u32[]{:S(2)}) %collective-permute-start.28) | collective-permute-done | bytes 122912 | tf_op jit(solution)/shard_map/ppermute | solution.py:1117
  123.4 3.2 %collective-permute-start.30 = (f32[8,128]{1,0:T(8,128)S(1)}, f32[8,128]{1,0:T(8,128)S(1)}, u32[]{:S(2)}, u32[]{:S(2)}) collective-permute-start(f32[8,128]{1,0:T(8,128)S(1)} %shard_map.153.refs_0_), channel_id=1, source_target_pairs={{0,2},{1,3},{2,0},{3,1},{4,6},{5,7},{6,4},{7,5},{8,10},{9,11},{10,... | collective-permute-start | bytes 12296 | tf_op jit(solution)/shard_map/ppermute | solution.py:1117
  127.6 1.5 %collective-permute-start.32 = (f32[8,128]{1,0:T(8,128)S(1)}, f32[8,128]{1,0:T(8,128)S(1)}, u32[]{:S(2)}, u32[]{:S(2)}) collective-permute-start(f32[8,128]{1,0:T(8,128)S(1)} %shard_map.153.refs_0_), channel_id=1, source_target_pairs={{0,6},{1,7},{2,4},{3,5},{4,2},{5,3},{6,0},{7,1},{8,14},{9,15},{10,... | collective-permute-start | bytes 12296 | tf_op jit(solution)/shard_map/ppermute | solution.py:1117
  129.0 2.0 %collective-permute-done.31.refs_2_ = f32[8,128]{1,0:T(8,128)S(1)} collective-permute-done((f32[8,128]{1,0:T(8,128)S(1)}, f32[8,128]{1,0:T(8,128)S(1)}, u32[]{:S(2)}, u32[]{:S(2)}) %collective-permute-start.31) | collective-permute-done | bytes 4128 | tf_op jit(solution)/shard_map/ppermute | solution.py:1117
  131.1 1.9 %collective-permute-done.32.refs_3_ = f32[8,128]{1,0:T(8,128)S(1)} collective-permute-done((f32[8,128]{1,0:T(8,128)S(1)}, f32[8,128]{1,0:T(8,128)S(1)}, u32[]{:S(2)}, u32[]{:S(2)}) %collective-permute-start.32) | collective-permute-done | bytes 4128 | tf_op jit(solution)/shard_map/ppermute | solution.py:1117
  137.9 1.9 %collective-permute-done.35.refs_3_ = f32[8,128]{1,0:T(8,128)S(1)} collective-permute-done((f32[8,128]{1,0:T(8,128)S(1)}, f32[8,128]{1,0:T(8,128)S(1)}, u32[]{:S(2)}, u32[]{:S(2)}) %collective-permute-start.35) | collective-permute-done | bytes 4128 | tf_op jit(solution)/shard_map/ppermute | solution.py:1117
  (82 shorter events, 21.8 us)
Async XLA Ops:
  2.5 14.3 %collective-permute-start = (bf16[336,128]{1,0:T(8,128)(2,1)S(1)}, bf16[336,128]{1,0:T(8,128)(2,1)S(1)}, u32[]{:S(2)}, u32[]{:S(2)}) collective-permute-start(bf16[336,128]{1,0:T(8,128)(2,1)S(1)} %get-tuple-element.76.refs_0_), channel_id=1, source_target_pairs={{0,2},{1,3},{2,0},{3,1},{4,6},{5,7},{6,4},{7,5},{8,10},{9,11},{10,... | collective-permute-start | bytes 258056 | tf_op jit(solution)/shard_map/ppermute | solution.py:1117
  5.6 11.3 %collective-permute-start.1 = (bf16[336,128]{1,0:T(8,128)(2,1)S(1)}, bf16[336,128]{1,0:T(8,128)(2,1)S(1)}, u32[]{:S(2)}, u32[]{:S(2)}) collective-permute-start(bf16[336,128]{1,0:T(8,128)(2,1)S(1)} %get-tuple-element.76.refs_0_), channel_id=1, source_target_pairs={{0,4},{1,5},{2,6},{3,7},{4,0},{5,1},{6,2},{7,3},{8,12},{9,13},{10,... | collective-permute-start | bytes 258056 | tf_op jit(solution)/shard_map/ppermute | solution.py:1117
  8.2 8.7 %collective-permute-start.2 = (bf16[336,128]{1,0:T(8,128)(2,1)S(1)}, bf16[336,128]{1,0:T(8,128)(2,1)S(1)}, u32[]{:S(2)}, u32[]{:S(2)}) collective-permute-start(bf16[336,128]{1,0:T(8,128)(2,1)S(1)} %get-tuple-element.76.refs_0_), channel_id=1, source_target_pairs={{0,6},{1,7},{2,4},{3,5},{4,2},{5,3},{6,0},{7,1},{8,14},{9,15},{10,... | collective-permute-start | bytes 258056 | tf_op jit(solution)/shard_map/ppermute | solution.py:1117
  8.2 3.9 %collective-permute-start.3 = (bf16[112,128]{1,0:T(8,128)(2,1)S(1)}, bf16[112,128]{1,0:T(8,128)(2,1)S(1)}, u32[]{:S(2)}, u32[]{:S(2)}) collective-permute-start(bf16[112,128]{1,0:T(8,128)(2,1)S(1)} %get-tuple-element.77.refs_0_), channel_id=1, source_target_pairs={{0,8},{8,0},{16,24},{24,16},{1,9},{9,1},{17,25},{25,17},{2,10},{10... | collective-permute-start | bytes 86024 | tf_op jit(solution)/shard_map/ppermute | solution.py:1117
  9.9 4.8 %collective-permute-start.4 = (bf16[112,128]{1,0:T(8,128)(2,1)S(1)}, bf16[112,128]{1,0:T(8,128)(2,1)S(1)}, u32[]{:S(2)}, u32[]{:S(2)}) collective-permute-start(bf16[112,128]{1,0:T(8,128)(2,1)S(1)} %get-tuple-element.77.refs_0_), channel_id=1, source_target_pairs={{0,16},{8,24},{16,0},{24,8},{1,17},{9,25},{17,1},{25,9},{2,18},{10... | collective-permute-start | bytes 86024 | tf_op jit(solution)/shard_map/ppermute | solution.py:1117
  12.0 4.8 %collective-permute-start.5 = (bf16[112,128]{1,0:T(8,128)(2,1)S(1)}, bf16[112,128]{1,0:T(8,128)(2,1)S(1)}, u32[]{:S(2)}, u32[]{:S(2)}) collective-permute-start(bf16[112,128]{1,0:T(8,128)(2,1)S(1)} %get-tuple-element.77.refs_0_), channel_id=1, source_target_pairs={{0,24},{8,16},{16,8},{24,0},{1,25},{9,17},{17,9},{25,1},{2,26},{10... | collective-permute-start | bytes 86024 | tf_op jit(solution)/shard_map/ppermute | solution.py:1117
  16.9 16.7 %collective-permute-start.6 = (bf16[4,336,128]{2,1,0:T(8,128)(2,1)S(1)}, bf16[4,336,128]{2,1,0:T(8,128)(2,1)S(1)}, u32[]{:S(2)}, u32[]{:S(2)}) collective-permute-start(bf16[4,336,128]{2,1,0:T(8,128)(2,1)S(1)} %shard_map.137.refs_0_), channel_id=1, source_target_pairs={{0,8},{8,0},{16,24},{24,16},{1,9},{9,1},{17,25},{25,17},{2,10},{10... | collective-permute-start | bytes 1032200 | tf_op jit(solution)/shard_map/ppermute | solution.py:1117
  18.7 14.9 %collective-permute-start.7 = (bf16[4,336,128]{2,1,0:T(8,128)(2,1)S(1)}, bf16[4,336,128]{2,1,0:T(8,128)(2,1)S(1)}, u32[]{:S(2)}, u32[]{:S(2)}) collective-permute-start(bf16[4,336,128]{2,1,0:T(8,128)(2,1)S(1)} %shard_map.137.refs_0_), channel_id=1, source_target_pairs={{0,16},{8,24},{16,0},{24,8},{1,17},{9,25},{17,1},{25,9},{2,18},{10... | collective-permute-start | bytes 1032200 | tf_op jit(solution)/shard_map/ppermute | solution.py:1117
  20.2 13.4 %collective-permute-start.8 = (bf16[4,336,128]{2,1,0:T(8,128)(2,1)S(1)}, bf16[4,336,128]{2,1,0:T(8,128)(2,1)S(1)}, u32[]{:S(2)}, u32[]{:S(2)}) collective-permute-start(bf16[4,336,128]{2,1,0:T(8,128)(2,1)S(1)} %shard_map.137.refs_0_), channel_id=1, source_target_pairs={{0,24},{8,16},{16,8},{24,0},{1,25},{9,17},{17,9},{25,1},{2,26},{10... | collective-permute-start | bytes 1032200 | tf_op jit(solution)/shard_map/ppermute | solution.py:1117
  20.4 4.8 %collective-permute-start.9 = (bf16[4,112,128]{2,1,0:T(8,128)(2,1)S(1)}, bf16[4,112,128]{2,1,0:T(8,128)(2,1)S(1)}, u32[]{:S(2)}, u32[]{:S(2)}) collective-permute-start(bf16[4,112,128]{2,1,0:T(8,128)(2,1)S(1)} %shard_map.136.refs_4_.refs_0_), channel_id=1, source_target_pairs={{0,2},{1,3},{2,0},{3,1},{4,6},{5,7},{6,4},{7,5},{8,10},{9,11},{10,... | collective-permute-start | bytes 344072 | tf_op jit(solution)/shard_map/ppermute | solution.py:1117
  21.3 9.9 %collective-permute-start.10 = (bf16[4,112,128]{2,1,0:T(8,128)(2,1)S(1)}, bf16[4,112,128]{2,1,0:T(8,128)(2,1)S(1)}, u32[]{:S(2)}, u32[]{:S(2)}) collective-permute-start(bf16[4,112,128]{2,1,0:T(8,128)(2,1)S(1)} %shard_map.136.refs_4_.refs_0_), channel_id=1, source_target_pairs={{0,4},{1,5},{2,6},{3,7},{4,0},{5,1},{6,2},{7,3},{8,12},{9,13},{10,... | collective-permute-start | bytes 344072 | tf_op jit(solution)/shard_map/ppermute | solution.py:1117
  25.2 8.3 %collective-permute-start.11 = (bf16[4,112,128]{2,1,0:T(8,128)(2,1)S(1)}, bf16[4,112,128]{2,1,0:T(8,128)(2,1)S(1)}, u32[]{:S(2)}, u32[]{:S(2)}) collective-permute-start(bf16[4,112,128]{2,1,0:T(8,128)(2,1)S(1)} %shard_map.136.refs_4_.refs_0_), channel_id=1, source_target_pairs={{0,6},{1,7},{2,4},{3,5},{4,2},{5,3},{6,0},{7,1},{8,14},{9,15},{10,... | collective-permute-start | bytes 344072 | tf_op jit(solution)/shard_map/ppermute | solution.py:1117
  33.8 2.0 %collective-permute-start.15 = (bf16[4,512,128]{2,1,0:T(8,128)(2,1)S(1)}, bf16[4,512,128]{2,1,0:T(8,128)(2,1)S(1)}, u32[]{:S(2)}, u32[]{:S(2)}) collective-permute-start(bf16[4,512,128]{2,1,0:T(8,128)(2,1)S(1)} %get-tuple-element.82.own_ref), channel_id=1, source_target_pairs={{0,1},{1,0},{2,3},{3,2},{4,5},{5,4},{6,7},{7,6},{8,9},{9,8},{10,11... | collective-permute-start | bytes 1572872 | tf_op jit(solution)/shard_map/ppermute | solution.py:1117
  33.9 14.4 %collective-permute-start.12 = (bf16[4,448,128]{2,1,0:T(8,128)(2,1)S(1)}, bf16[4,448,128]{2,1,0:T(8,128)(2,1)S(1)}, u32[]{:S(2)}, u32[]{:S(2)}) collective-permute-start(bf16[4,448,128]{2,1,0:T(8,128)(2,1)S(1)} %get-tuple-element.79.refs_0_), channel_id=1, source_target_pairs={{0,1},{1,0},{2,3},{3,2},{4,5},{5,4},{6,7},{7,6},{8,9},{9,8},{10,11... | collective-permute-start | bytes 1376264 | tf_op jit(solution)/shard_map/ppermute | solution.py:1117
  34.4 13.9 %collective-permute-start.13 = (bf16[4,448,128]{2,1,0:T(8,128)(2,1)S(1)}, bf16[4,448,128]{2,1,0:T(8,128)(2,1)S(1)}, u32[]{:S(2)}, u32[]{:S(2)}) collective-permute-start(bf16[4,448,128]{2,1,0:T(8,128)(2,1)S(1)} %get-tuple-element.80.refs_1_), channel_id=1, source_target_pairs={{0,1},{1,0},{2,3},{3,2},{4,5},{5,4},{6,7},{7,6},{8,9},{9,8},{10,11... | collective-permute-start | bytes 1376264 | tf_op jit(solution)/shard_map/ppermute | solution.py:1117
  34.5 13.8 %collective-permute-start.14 = (bf16[4,448,128]{2,1,0:T(8,128)(2,1)S(1)}, bf16[4,448,128]{2,1,0:T(8,128)(2,1)S(1)}, u32[]{:S(2)}, u32[]{:S(2)}) collective-permute-start(bf16[4,448,128]{2,1,0:T(8,128)(2,1)S(1)} %get-tuple-element.81.refs_2_), channel_id=1, source_target_pairs={{0,1},{1,0},{2,3},{3,2},{4,5},{5,4},{6,7},{7,6},{8,9},{9,8},{10,11... | collective-permute-start | bytes 1376264 | tf_op jit(solution)/shard_map/ppermute | solution.py:1117
  66.0 3.1 %collective-permute-start.16 = (bf16[3,4,448,128]{3,2,1,0:T(8,128)(2,1)S(1)}, bf16[3,4,448,128]{3,2,1,0:T(8,128)(2,1)S(1)}, u32[]{:S(2)}, u32[]{:S(2)}) collective-permute-start(bf16[3,4,448,128]{3,2,1,0:T(8,128)(2,1)S(1)} %get-tuple-element.111), channel_id=1, source_target_pairs={{0,1},{1,0},{2,3},{3,2},{4,5},{5,4},{6,7},{7,6},{8,9},{9,8},{10,11... | collective-permute-start | bytes 4128776 | tf_op jit(solution)/shard_map/ppermute | solution.py:1117
  69.4 19.8 %collective-permute-start.17 = (bf16[3,1,448,128]{3,2,0,1:T(8,128)(2,1)S(1)}, bf16[3,1,448,128]{3,2,0,1:T(8,128)(2,1)S(1)}, u32[]{:S(2)}, u32[]{:S(2)}) collective-permute-start(bf16[3,1,448,128]{3,2,0,1:T(8,128)(2,1)S(1)} %bitcast.41), channel_id=1, source_target_pairs={{0,2},{1,3},{2,0},{3,1},{4,6},{5,7},{6,4},{7,5},{8,10},{9,11},{10,... | collective-permute-start | bytes 1032200 | tf_op jit(solution)/shard_map/ppermute | solution.py:1117
  69.9 27.9 %collective-permute-start.18 = (bf16[3,1,448,128]{3,2,0,1:T(8,128)(2,1)S(1)}, bf16[3,1,448,128]{3,2,0,1:T(8,128)(2,1)S(1)}, u32[]{:S(2)}, u32[]{:S(2)}) collective-permute-start(bf16[3,1,448,128]{3,2,0,1:T(8,128)(2,1)S(1)} %bitcast.40), channel_id=1, source_target_pairs={{0,4},{1,5},{2,6},{3,7},{4,0},{5,1},{6,2},{7,3},{8,12},{9,13},{10,... | collective-permute-start | bytes 1032200 | tf_op jit(solution)/shard_map/ppermute | solution.py:1117
  73.9 23.9 %collective-permute-start.19 = (bf16[3,1,448,128]{3,2,0,1:T(8,128)(2,1)S(1)}, bf16[3,1,448,128]{3,2,0,1:T(8,128)(2,1)S(1)}, u32[]{:S(2)}, u32[]{:S(2)}) collective-permute-start(bf16[3,1,448,128]{3,2,0,1:T(8,128)(2,1)S(1)} %bitcast.39), channel_id=1, source_target_pairs={{0,6},{1,7},{2,4},{3,5},{4,2},{5,3},{6,0},{7,1},{8,14},{9,15},{10,... | collective-permute-start | bytes 1032200 | tf_op jit(solution)/shard_map/ppermute | solution.py:1117
  91.3 8.4 %collective-permute-start.23 = (bf16[1,480,128]{2,1,0:T(8,128)(2,1)S(1)}, bf16[1,480,128]{2,1,0:T(8,128)(2,1)S(1)}, u32[]{:S(2)}, u32[]{:S(2)}) collective-permute-start(bf16[1,480,128]{2,1,0:T(8,128)(2,1)S(1)} %get-tuple-element.131), channel_id=1, source_target_pairs={{0,2},{1,3},{2,0},{3,1},{4,6},{5,7},{6,4},{7,5},{8,10},{9,11},{10,... | collective-permute-start | bytes 368648 | tf_op jit(solution)/shard_map/ppermute | solution.py:1117
  91.9 21.0 %collective-permute-start.24 = (bf16[1,480,128]{2,1,0:T(8,128)(2,1)S(1)}, bf16[1,480,128]{2,1,0:T(8,128)(2,1)S(1)}, u32[]{:S(2)}, u32[]{:S(2)}) collective-permute-start(bf16[1,480,128]{2,1,0:T(8,128)(2,1)S(1)} %get-tuple-element.132), channel_id=1, source_target_pairs={{0,4},{1,5},{2,6},{3,7},{4,0},{5,1},{6,2},{7,3},{8,12},{9,13},{10,... | collective-permute-start | bytes 368648 | tf_op jit(solution)/shard_map/ppermute | solution.py:1117
  95.7 17.2 %collective-permute-start.25 = (bf16[1,480,128]{2,1,0:T(8,128)(2,1)S(1)}, bf16[1,480,128]{2,1,0:T(8,128)(2,1)S(1)}, u32[]{:S(2)}, u32[]{:S(2)}) collective-permute-start(bf16[1,480,128]{2,1,0:T(8,128)(2,1)S(1)} %get-tuple-element.133), channel_id=1, source_target_pairs={{0,6},{1,7},{2,4},{3,5},{4,2},{5,3},{6,0},{7,1},{8,14},{9,15},{10,... | collective-permute-start | bytes 368648 | tf_op jit(solution)/shard_map/ppermute | solution.py:1117
  113.1 5.6 %collective-permute-start.26 = (bf16[480,128]{1,0:T(8,128)(2,1)S(1)}, bf16[480,128]{1,0:T(8,128)(2,1)S(1)}, u32[]{:S(2)}, u32[]{:S(2)}) collective-permute-start(bf16[480,128]{1,0:T(8,128)(2,1)S(1)} %get-tuple-element.135), channel_id=1, source_target_pairs={{0,8},{8,0},{16,24},{24,16},{1,9},{9,1},{17,25},{25,17},{2,10},{10... | collective-permute-start | bytes 368648 | tf_op jit(solution)/shard_map/ppermute | solution.py:1117
  113.2 6.3 %collective-permute-start.27 = (bf16[480,128]{1,0:T(8,128)(2,1)S(1)}, bf16[480,128]{1,0:T(8,128)(2,1)S(1)}, u32[]{:S(2)}, u32[]{:S(2)}) collective-permute-start(bf16[480,128]{1,0:T(8,128)(2,1)S(1)} %get-tuple-element.136), channel_id=1, source_target_pairs={{0,16},{8,24},{16,0},{24,8},{1,17},{9,25},{17,1},{25,9},{2,18},{10... | collective-permute-start | bytes 368648 | tf_op jit(solution)/shard_map/ppermute | solution.py:1117
  114.9 6.1 %collective-permute-start.28 = (bf16[480,128]{1,0:T(8,128)(2,1)S(1)}, bf16[480,128]{1,0:T(8,128)(2,1)S(1)}, u32[]{:S(2)}, u32[]{:S(2)}) collective-permute-start(bf16[480,128]{1,0:T(8,128)(2,1)S(1)} %get-tuple-element.137), channel_id=1, source_target_pairs={{0,24},{8,16},{16,8},{24,0},{1,25},{9,17},{17,9},{25,1},{2,26},{10... | collective-permute-start | bytes 368648 | tf_op jit(solution)/shard_map/ppermute | solution.py:1117
  123.4 5.7 %collective-permute-start.30 = (f32[8,128]{1,0:T(8,128)S(1)}, f32[8,128]{1,0:T(8,128)S(1)}, u32[]{:S(2)}, u32[]{:S(2)}) collective-permute-start(f32[8,128]{1,0:T(8,128)S(1)} %shard_map.153.refs_0_), channel_id=1, source_target_pairs={{0,2},{1,3},{2,0},{3,1},{4,6},{5,7},{6,4},{7,5},{8,10},{9,11},{10,... | collective-permute-start | bytes 12296 | tf_op jit(solution)/shard_map/ppermute | solution.py:1117
  126.6 4.5 %collective-permute-start.31 = (f32[8,128]{1,0:T(8,128)S(1)}, f32[8,128]{1,0:T(8,128)S(1)}, u32[]{:S(2)}, u32[]{:S(2)}) collective-permute-start(f32[8,128]{1,0:T(8,128)S(1)} %shard_map.153.refs_0_), channel_id=1, source_target_pairs={{0,4},{1,5},{2,6},{3,7},{4,0},{5,1},{6,2},{7,3},{8,12},{9,13},{10,... | collective-permute-start | bytes 12296 | tf_op jit(solution)/shard_map/ppermute | solution.py:1117
  127.6 5.4 %collective-permute-start.32 = (f32[8,128]{1,0:T(8,128)S(1)}, f32[8,128]{1,0:T(8,128)S(1)}, u32[]{:S(2)}, u32[]{:S(2)}) collective-permute-start(f32[8,128]{1,0:T(8,128)S(1)} %shard_map.153.refs_0_), channel_id=1, source_target_pairs={{0,6},{1,7},{2,4},{3,5},{4,2},{5,3},{6,0},{7,1},{8,14},{9,15},{10,... | collective-permute-start | bytes 12296 | tf_op jit(solution)/shard_map/ppermute | solution.py:1117
  133.0 4.9 %collective-permute-start.33 = (f32[8,128]{1,0:T(8,128)S(1)}, f32[8,128]{1,0:T(8,128)S(1)}, u32[]{:S(2)}, u32[]{:S(2)}) collective-permute-start(f32[8,128]{1,0:T(8,128)S(1)} %shard_map.154.refs_0_), channel_id=1, source_target_pairs={{0,8},{8,0},{16,24},{24,16},{1,9},{9,1},{17,25},{25,17},{2,10},{10... | collective-permute-start | bytes 12296 | tf_op jit(solution)/shard_map/ppermute | solution.py:1117
  133.9 3.9 %collective-permute-start.34 = (f32[8,128]{1,0:T(8,128)S(1)}, f32[8,128]{1,0:T(8,128)S(1)}, u32[]{:S(2)}, u32[]{:S(2)}) collective-permute-start(f32[8,128]{1,0:T(8,128)S(1)} %shard_map.154.refs_0_), channel_id=1, source_target_pairs={{0,16},{8,24},{16,0},{24,8},{1,17},{9,25},{17,1},{25,9},{2,18},{10... | collective-permute-start | bytes 12296 | tf_op jit(solution)/shard_map/ppermute | solution.py:1117
  135.3 4.5 %collective-permute-start.35 = (f32[8,128]{1,0:T(8,128)S(1)}, f32[8,128]{1,0:T(8,128)S(1)}, u32[]{:S(2)}, u32[]{:S(2)}) collective-permute-start(f32[8,128]{1,0:T(8,128)S(1)} %shard_map.154.refs_0_), channel_id=1, source_target_pairs={{0,24},{8,16},{16,8},{24,0},{1,25},{9,17},{17,9},{25,1},{2,26},{10... | collective-permute-start | bytes 12296 | tf_op jit(solution)/shard_map/ppermute | solution.py:1117
  (12 other events, 103.5 us)

commit v5 on v4

--- a/solution.py
+++ b/solution.py
@@ -136,57 +136,73 @@
     return head_mean_low(high, matrix) + head_mean_low(rest, matrix)
 
 
-def prepare_kernel(plan, master_ref, keep_ref, upper_ref, lower_ref):
-    me = plan.device()
-    offset = lax.rem(me * plan.shard, LANES)
-    values = master_ref[...]
+def flat_to_rows(plan, flat_ref, rows_ref):
+    full, rest = divmod(plan.shard, LANES)
+    rows_ref[full:, :] = jnp.zeros((plan.win - full, LANES), F32)
+    rows_ref[:full, :] = flat_ref[: full * LANES].reshape(full, LANES)
+    if rest:
+        rows_ref[full : full + 1, :rest] = flat_ref[full * LANES :].reshape(1, rest)
+    return rows_ref[...]
+
+
+def rows_to_flat(plan, rows, flat_ref):
+    full, rest = divmod(plan.shard, LANES)
+    flat_ref[: full * LANES] = rows[:full].reshape(full * LANES)
+    if rest:
+        flat_ref[full * LANES :] = rows[full : full + 1, :rest].reshape(rest)
+
+
+def prepare_kernel(plan, master_ref, upper_ref, lower_ref, rows_ref):
+    offset = lax.rem(plan.device() * plan.shard, LANES)
+    values = flat_to_rows(plan, master_ref, rows_ref)
     turned = pltpu.roll(values, offset, 1)
     below = pltpu.roll(turned, 1, 0)
     lane = lax.broadcasted_iota(jnp.int32, values.shape, 1)
-    row = lax.broadcasted_iota(jnp.int32, values.shape, 0)
-    count = jnp.sum(keep_ref[...].astype(F32), axis=1, keepdims=True)
-    high = jnp.floor(count * (1.0 / 32.0))
-    parts = jnp.where(lane == 0, high, jnp.where(lane == 1, count - 32.0 * high, 0.0))
-    window = jnp.where(lane < offset, below, turned)
-    window = jnp.where(row == plan.win - 1, parts, window).astype(BF)
+    window = jnp.where(lane < offset, below, turned).astype(BF)
     upper_ref[...] = window[: plan.upper]
     lower_ref[...] = window[plan.upper :]
 
 
-def prepare(plan, master_rows, keep_row):
+def prepare(plan, master):
     return pl.pallas_call(
         functools.partial(prepare_kernel, plan),
         out_shape=(
             jax.ShapeDtypeStruct((plan.upper, LANES), BF),
             jax.ShapeDtypeStruct((plan.win - plan.upper, LANES), BF),
         ),
-        in_specs=[VMEM, VMEM],
+        in_specs=[VMEM],
         out_specs=(VMEM, VMEM),
+        scratch_shapes=[pltpu.VMEM((plan.win, LANES), F32)],
         compiler_params=params(8),
-    )(master_rows, keep_row)
-
-
-def ahead_kernel(tokens_ref, hat_ref, rstd_ref, token_ref):
+    )(master)
+
+
+def ahead_kernel(tokens_ref, keep_ref, hat_ref, rstd_ref, count_ref):
     hat, rstd = norm_parts(tokens_ref[...].astype(F32))
     hat_ref[...] = hat
     rstd_ref[...] = jnp.broadcast_to(rstd, rstd_ref.shape)
-    token_ref[...] = jnp.zeros_like(token_ref)
-
-
-def ahead(tokens):
+    row = lax.broadcasted_iota(jnp.int32, count_ref.shape, 0)
+    lane = lax.broadcasted_iota(jnp.int32, count_ref.shape, 1)
+    count = jnp.sum(keep_ref[...].astype(F32), axis=1, keepdims=True)
+    high = jnp.floor(count * (1.0 / 32.0))
+    parts = jnp.where(lane == 0, high, jnp.where(lane == 1, count - 32.0 * high, 0.0))
+    count_ref[...] = jnp.where(row == 15, parts, 0.0)
+
+
+def ahead(tokens, keep_row):
     rows = tokens.shape[0]
     return pl.pallas_call(
         ahead_kernel,
         out_shape=(
             jax.ShapeDtypeStruct((rows, D), F32),
             jax.ShapeDtypeStruct((rows, LANES), F32),
-            jax.ShapeDtypeStruct((8, LANES), F32),
+            jax.ShapeDtypeStruct((16, LANES), F32),
         ),
-        in_specs=[VMEM],
+        in_specs=[VMEM, VMEM],
         out_specs=(VMEM,) * 3,
         compiler_params=params(12),
         cost_estimate=QUICK,
-    )(tokens)
+    )(tokens, keep_row)
 
 
 def held_window(own_ref, other_ref, rel, at):
@@ -897,6 +913,9 @@
     update_ref,
     sums_ref,
     window,
+    master_rows,
+    moment_rows,
+    second_rows,
 ):
     bucket = lax.axis_index("bucket")
     dp = lax.axis_index("dp")
@@ -917,16 +936,18 @@
     place, index = flat_place(plan, turned.shape)
     inside = place < plan.shard
     grad = jnp.where(inside, jnp.where(lane + offset < LANES, turned, above), 0.0)
-    master = master_ref[...]
-    moment = beta_one * moment_ref[...] + (1.0 - beta_one) * grad
-    second = beta_two * second_ref[...] + (1.0 - beta_two) * grad * grad
+    master = flat_to_rows(plan, master_ref, master_rows)
+    old_moment = flat_to_rows(plan, moment_ref, moment_rows)
+    old_second = flat_to_rows(plan, second_ref, second_rows)
+    moment = beta_one * old_moment + (1.0 - beta_one) * grad
+    second = beta_two * old_second + (1.0 - beta_two) * grad * grad
     first_hat = moment / (1.0 - beta_one**STEP)
     second_hat = second / (1.0 - beta_two**STEP)
     decay = jnp.where(index < BOUNDS[4], weight_decay, 0.0)
     update = first_hat / (jnp.sqrt(second_hat) + adam_epsilon) + decay * master
     update = jnp.where(inside, update, 0.0)
-    new_moment_ref[...] = moment
-    new_second_ref[...] = second
+    rows_to_flat(plan, moment, new_moment_ref)
+    rows_to_flat(plan, second, new_second_ref)
     update_ref[...] = update
     master_sq = jnp.where(inside, master * master, 0.0)
     update_sq = update * update
@@ -943,44 +964,46 @@
     sums_ref[...] = jnp.concatenate(rows, axis=0)
 
 
-def update_part(plan, parts, master_rows, moment_rows, second_rows):
+def update_part(plan, parts, master, moment, second):
+    flat = jax.ShapeDtypeStruct((plan.shard,), F32)
     rows = jax.ShapeDtypeStruct((plan.win, LANES), F32)
     return pl.pallas_call(
         functools.partial(update_kernel, plan),
-        out_shape=(rows, rows, rows, jax.ShapeDtypeStruct((8, LANES), F32)),
+        out_shape=(flat, flat, rows, jax.ShapeDtypeStruct((8, LANES), F32)),
         in_specs=[VMEM] * 7,
         out_specs=(VMEM,) * 4,
-        scratch_shapes=[pltpu.VMEM((plan.win, LANES), F32)],
+        scratch_shapes=[pltpu.VMEM((plan.win, LANES), F32)] * 4,
         compiler_params=params(12),
-    )(*parts, master_rows, moment_rows, second_rows)
+    )(*parts, master, moment, second)
 
 
 def apply_kernel(plan, *refs):
-    *sums_refs, master_ref, update_ref, new_ref, norms_ref, trust_ref = refs
+    *sums_refs, master_ref, update_ref, new_ref, norms_ref, trust_ref, rows_ref = refs
     roots = jnp.sqrt(tree_sum([ref[...] for ref in sums_refs]))
     trust = roots[0:1, :] / (roots[1:2, :] + adam_epsilon)
     norms_ref[...] = roots[0:2, :MATS]
     trust_ref[...] = trust[:, :MATS]
-    master = master_ref[...]
+    master = flat_to_rows(plan, master_ref, rows_ref)
     _, index = flat_place(plan, master.shape)
     factors = jnp.broadcast_to(trust[:, 0:1], master.shape)
     for t in range(1, MATS):
         factors = jnp.where(index >= BOUNDS[t], trust[:, t : t + 1], factors)
-    new_ref[...] = master - learn_rate * factors * update_ref[...]
-
-
-def apply_part(plan, sums, master_rows, update_rows):
+    rows_to_flat(plan, master - learn_rate * factors * update_ref[...], new_ref)
+
+
+def apply_part(plan, sums, master, update_rows):
     return pl.pallas_call(
         functools.partial(apply_kernel, plan),
         out_shape=(
-            jax.ShapeDtypeStruct((plan.win, LANES), F32),
+            jax.ShapeDtypeStruct((plan.shard,), F32),
             jax.ShapeDtypeStruct((2, MATS), F32),
             jax.ShapeDtypeStruct((1, MATS), F32),
         ),
         in_specs=[VMEM] * (len(sums) + 2),
         out_specs=(VMEM,) * 3,
+        scratch_shapes=[pltpu.VMEM((plan.win, LANES), F32)],
         compiler_params=params(8),
-    )(*sums, master_rows, update_rows)
+    )(*sums, master, update_rows)
 
 
 def lay_column_kernel(count, *refs):
@@ -998,11 +1021,28 @@
     )(*parts, *after)
 
 
+def lay_lower_kernel(plan, count_ref, *refs):
+    for i, part in enumerate(refs[:-1]):
+        refs[-1][i] = part[...]
+    last = refs[0][-16:, :].astype(F32)
+    refs[-1][0, plan.win - plan.upper - 16 :, :] = (last + count_ref[...]).astype(BF)
+
+
+def lay_lower(plan, parts, count):
+    return pl.pallas_call(
+        functools.partial(lay_lower_kernel, plan),
+        out_shape=jax.ShapeDtypeStruct((len(parts), *parts[0].shape), BF),
+        in_specs=[VMEM] * (1 + len(parts)),
+        out_specs=VMEM,
+        compiler_params=params(4),
+    )(count, *parts)
+
+
 def choose_kernel(plan, *refs):
-    columns, (lower_ref, _, early_ref), late_refs = (
+    columns, (lower_ref, early_ref), late_refs = (
         refs[: plan.nb],
-        refs[plan.nb : plan.nb + 3],
-        refs[plan.nb + 3 :],
+        refs[plan.nb : plan.nb + 2],
+        refs[plan.nb + 2 :],
     )
     bucket = lax.axis_index("bucket")
     early_ref[:, plan.kept_row :] = lower_ref[:, 0, plan.win - plan.upper - 16 :]
@@ -1017,16 +1057,16 @@
     early_ref[:, plan.win : plan.kept_row] = late_refs[-1][:, plan.vec_from :]
 
 
-def choose(plan, columns, lower, token):
+def choose(plan, columns, lower):
     step = columns[0].shape[0]
     late = jax.ShapeDtypeStruct((step, plan.win, LANES), BF)
     return pl.pallas_call(
         functools.partial(choose_kernel, plan),
         out_shape=(jax.ShapeDtypeStruct((step, plan.early, LANES), BF),) + (late,) * (plan.nb - 1),
-        in_specs=[VMEM] * (len(columns) + 2),
+        in_specs=[VMEM] * (len(columns) + 1),
         out_specs=(VMEM,) * plan.nb,
         compiler_params=params(10),
-    )(*columns, lower, token)
+    )(*columns, lower)
 
 
 def add_parts_kernel(halves, *refs):
@@ -1128,10 +1168,10 @@
     return [x] + [swap(x, axis, size, mask) for mask in masks_of(bits)]
 
 
-def gather_windows(plan, upper, lower, token):
+def gather_windows(plan, upper, lower, count):
     first, *more = groups_of(plan.nd, 1)
     (bits,) = groups_of(plan.nb)
-    lower = lay_column(with_partners(lower, "bucket", plan.nb, bits))
+    lower = lay_lower(plan, with_partners(lower, "bucket", plan.nb, bits), count)
     column = lay_column(with_partners(upper, "dp", plan.nd, first), lower)
     for group in more:
         column = jnp.concatenate(with_partners(column, "dp", plan.nd, group), axis=0)
@@ -1139,7 +1179,7 @@
     lower = lay_column(with_partners(lower, "dp", plan.nd, first))
     for group in more:
         lower = jnp.concatenate(with_partners(lower, "dp", plan.nd, group), axis=0)
-    early, *late = choose(plan, columns, lower, token)
+    early, *late = choose(plan, columns, lower)
     others = [swap(x, "dp", plan.nd, 1) for x in (early, *late)]
     return (early, others[0]), (*late, *others[1:])
 
@@ -1172,27 +1212,20 @@
 def local(
     plan, tokens, cotangent, segment_ids, keep_mask, bucket_patches, master, first_moment, second_moment
 ):
-    def as_rows(flat):
-        return jnp.pad(flat, (0, plan.win * LANES - plan.shard)).reshape(plan.win, LANES)
-
-    def as_flat(rows):
-        return rows.reshape(-1)[: plan.shard]
-
-    master_rows = as_rows(master)
     seg_row = segment_ids.reshape(1, SEQ)
     keep_row = keep_mask.reshape(1, SEQ)
-    count = 1 << len(groups_of(plan.nd, 1)[-1])
+    pieces_of = 1 << len(groups_of(plan.nd, 1)[-1])
     (b_bits,) = groups_of(plan.nb)
 
-    hat_in, rstd_in, token = ahead(tokens)
-    early, late = gather_windows(plan, *prepare(plan, master_rows, keep_row), token)
+    hat_in, rstd_in, count = ahead(tokens, keep_row)
+    early, late = gather_windows(plan, *prepare(plan, master), count)
     wq, vec, head, kept, q, k, v, hat, rstd = project_part(plan, *early, hat_in)
     o, ot, whole, lse, kab, segk = forward(plan, segment_ids, seg_row, keep_row, q, k, v)
     block_output, dh1, do, near, far, tail, gvec = middle_part(
         plan, late, tokens, cotangent, o, ot, head, kept, vec, keep_row, bucket_patches
     )
     *stacks, normed, token = stack_part(vec, hat_in, q, k, v, do, whole)
-    *pieces, token = add_parts([near, swap(far, "dp", plan.nd, 1)], count, token)
+    *pieces, token = add_parts([near, swap(far, "dp", plan.nd, 1)], pieces_of, token)
     rest = scatter_dp(plan, pieces)
     low, gains = backward(
         plan, vec, segment_ids, seg_row, lse, q, do, hat, rstd, segk, [kab, *stacks], token
@@ -1201,22 +1234,22 @@
     input_grad, given = input_part(hat_in, rstd_in, vec, da1, dh1)
     *late_parts, token = add_parts(rest[:2], 1, gains)
     late_parts += rest[2:]
-    *pieces, _ = add_parts([near, [swap(half, "dp", plan.nd, 1) for half in far]], count, token)
+    *pieces, _ = add_parts([near, [swap(half, "dp", plan.nd, 1) for half in far]], pieces_of, token)
     first = scatter_dp(plan, pieces)
     mine, *sent = blend(plan, late_parts, given, first)
     parts = [mine] + [
         swap(x, "bucket", plan.nb, mask) for x, mask in zip(sent, masks_of(b_bits))
     ]
-    moment_rows, second_rows, update_rows, sums = update_part(
-        plan, parts, master_rows, as_rows(first_moment), as_rows(second_moment)
+    new_first, new_second, update_rows, sums = update_part(
+        plan, parts, master, first_moment, second_moment
     )
-    new_master, norms, trust = apply_part(plan, sum_all(plan, sums), master_rows, update_rows)
+    new_master, norms, trust = apply_part(plan, sum_all(plan, sums), master, update_rows)
     return (
         block_output,
         input_grad,
-        as_flat(moment_rows),
-        as_flat(second_rows),
-        as_flat(new_master),
+        new_first,
+        new_second,
+        new_master,
         norms,
         trust.reshape(MATS),
     )

time: 142 us -> 139 us (0.979)
  starting transfers between devices: 48.5 us -> 43 us
  waiting for transfers between devices: 35.6 us -> 38.7 us
    ppermute x36, starting transfers between devices: 48.5 us -> 43 us  [swap(): return lax.ppermute(x, axis, [(i, i ^ mask) for i in range(size)])]
    ppermute x36, waiting for transfers between devices: 35.6 us -> 38.7 us  [swap(): return lax.ppermute(x, axis, [(i, i ^ mask) for i in range(size)])]
    slice x3 -> x0, local copies, waits for them, and re-layouts: 2.1 us -> none  [as_flat(): return rows.reshape(-1)[:plan.shard]]
    unnamed x16 -> x22, local copies, waits for them, and re-layouts: 0.72 us -> 2.79 us
  transfers between devices with their start and end apart: 36 -> 36, of which waited for: 18 -> 22; matrix products, arithmetic and copies ran while one was open for 1% -> 0% of each run, Pallas kernels for 23% -> 23%
where the time goes in v5:
time: 139 us
  Pallas kernels  53.2 us (38%)
  starting transfers between devices  43 us (31%)
  waiting for transfers between devices  38.7 us (28%)
  local copies, waits for them, and re-layouts  2.79 us (2%)
    ppermute x36, starting transfers between devices, swap(): return lax.ppermute(x, axis, [(i, i ^ mask) for i in range(size)])  43 us
    ppermute x36, waiting for transfers between devices, swap(): return lax.ppermute(x, axis, [(i, i ^ mask) for i in range(size)])  38.7 us
    pallas_call x1, Pallas kernels, middle_part(): pl.pallas_call(functools.partial(middle_kernel, plan), out_shape=(jax.Sha...  17.6 us
    pallas_call x1, Pallas kernels, backward(): pl.pallas_call(functools.partial(backward_kernel, plan), out_shape=(jax.S...  12 us
    pallas_call x1, Pallas kernels, forward(): pl.pallas_call(functools.partial(forward_kernel, plan), out_shape=(jax.Sh...  8.72 us
    pallas_call x1, Pallas kernels, project_part(): pl.pallas_call(functools.partial(project_kernel, plan), out_shape=(jax.Sh...  3.72 us
    pallas_call x1, Pallas kernels, finish_part(): pl.pallas_call(functools.partial(finish_kernel, plan), out_shape=(jax.Sha...  2.91 us
    unnamed x22, local copies, waits for them, and re-layouts  2.79 us
  transfers between devices with their start and end apart: 36, of which 22 were waited for; matrix products, arithmetic and copies ran while one was open for 0% of the time, Pallas kernels for 23%

profile of v5, /device:TPU:0, one launch (start us, length us, event | category | flops | bytes accessed | tf_op | source)
XLA Modules:
  0.0 138.7 jit_solution(15135911977446936016)
XLA Ops:
  1.7 5.1 %collective-permute-start.2 = (bf16[336,128]{1,0:T(8,128)(2,1)S(1)}, bf16[336,128]{1,0:T(8,128)(2,1)S(1)}, u32[]{:S(2)}, u32[]{:S(2)}) collective-permute-start(bf16[336,128]{1,0:T(8,128)(2,1)S(1)} %get-tuple-element.76.refs_0_), channel_id=1, source_target_pairs={{0,6},{1,7},{2,4},{3,5},{4,2},{5,3},{6,0},{7,1},{8,14},{9,15},{10,... | collective-permute-start | bytes 258056 | tf_op jit(solution)/shard_map/ppermute | solution.py:1157
  7.5 2.6 %collective-permute-start.5 = (bf16[112,128]{1,0:T(8,128)(2,1)S(1)}, bf16[112,128]{1,0:T(8,128)(2,1)S(1)}, u32[]{:S(2)}, u32[]{:S(2)}) collective-permute-start(bf16[112,128]{1,0:T(8,128)(2,1)S(1)} %get-tuple-element.78.refs_0_), channel_id=1, source_target_pairs={{0,24},{8,16},{16,8},{24,0},{1,25},{9,17},{17,9},{25,1},{2,26},{10... | collective-permute-start | bytes 86024 | tf_op jit(solution)/shard_map/ppermute | solution.py:1157
  10.6 1.7 %collective-permute-done.5.refs_3_ = bf16[112,128]{1,0:T(8,128)(2,1)S(1)} collective-permute-done((bf16[112,128]{1,0:T(8,128)(2,1)S(1)}, bf16[112,128]{1,0:T(8,128)(2,1)S(1)}, u32[]{:S(2)}, u32[]{:S(2)}) %collective-permute-start.5) | collective-permute-done | bytes 28704 | tf_op jit(solution)/shard_map/ppermute | solution.py:1157
  12.2 1.6 %collective-permute-start.3 = (bf16[112,128]{1,0:T(8,128)(2,1)S(1)}, bf16[112,128]{1,0:T(8,128)(2,1)S(1)}, u32[]{:S(2)}, u32[]{:S(2)}) collective-permute-start(bf16[112,128]{1,0:T(8,128)(2,1)S(1)} %get-tuple-element.78.refs_0_), channel_id=1, source_target_pairs={{0,8},{8,0},{16,24},{24,16},{1,9},{9,1},{17,25},{25,17},{2,10},{10... | collective-permute-start | bytes 86024 | tf_op jit(solution)/shard_map/ppermute | solution.py:1157
  16.2 2.8 %collective-permute-start.8 = (bf16[4,336,128]{2,1,0:T(8,128)(2,1)S(1)}, bf16[4,336,128]{2,1,0:T(8,128)(2,1)S(1)}, u32[]{:S(2)}, u32[]{:S(2)}) collective-permute-start(bf16[4,336,128]{2,1,0:T(8,128)(2,1)S(1)} %shard_map.138.refs_0_), channel_id=1, source_target_pairs={{0,24},{8,16},{16,8},{24,0},{1,25},{9,17},{17,9},{25,1},{2,26},{10... | collective-permute-start | bytes 1032200 | tf_op jit(solution)/shard_map/ppermute | solution.py:1157
  19.8 3.7 %collective-permute-start.11 = (bf16[4,112,128]{2,1,0:T(8,128)(2,1)S(1)}, bf16[4,112,128]{2,1,0:T(8,128)(2,1)S(1)}, u32[]{:S(2)}, u32[]{:S(2)}) collective-permute-start(bf16[4,112,128]{2,1,0:T(8,128)(2,1)S(1)} %shard_map.137.refs_4_.refs_0_), channel_id=1, source_target_pairs={{0,6},{1,7},{2,4},{3,5},{4,2},{5,3},{6,0},{7,1},{8,14},{9,15},{10,... | collective-permute-start | bytes 344072 | tf_op jit(solution)/shard_map/ppermute | solution.py:1157
  23.5 3.3 %collective-permute-done.11.refs_3_ = bf16[4,112,128]{2,1,0:T(8,128)(2,1)S(1)} collective-permute-done((bf16[4,112,128]{2,1,0:T(8,128)(2,1)S(1)}, bf16[4,112,128]{2,1,0:T(8,128)(2,1)S(1)}, u32[]{:S(2)}, u32[]{:S(2)}) %collective-permute-start.11) | collective-permute-done | bytes 114720 | tf_op jit(solution)/shard_map/ppermute | solution.py:1157
  26.7 2.8 %collective-permute-start.9 = (bf16[4,112,128]{2,1,0:T(8,128)(2,1)S(1)}, bf16[4,112,128]{2,1,0:T(8,128)(2,1)S(1)}, u32[]{:S(2)}, u32[]{:S(2)}) collective-permute-start(bf16[4,112,128]{2,1,0:T(8,128)(2,1)S(1)} %shard_map.137.refs_4_.refs_0_), channel_id=1, source_target_pairs={{0,2},{1,3},{2,0},{3,1},{4,6},{5,7},{6,4},{7,5},{8,10},{9,11},{10,... | collective-permute-start | bytes 344072 | tf_op jit(solution)/shard_map/ppermute | solution.py:1157
  30.2 2.1 %collective-permute-done.9.refs_1_ = bf16[4,112,128]{2,1,0:T(8,128)(2,1)S(1)} collective-permute-done((bf16[4,112,128]{2,1,0:T(8,128)(2,1)S(1)}, bf16[4,112,128]{2,1,0:T(8,128)(2,1)S(1)}, u32[]{:S(2)}, u32[]{:S(2)}) %collective-permute-start.9) | collective-permute-done | bytes 114720 | tf_op jit(solution)/shard_map/ppermute | solution.py:1157
  34.6 3.7 %shard_map.141 = (bf16[384,1152]{1,0:T(8,128)(2,1)S(1)}, f32[8,384]{1,0:T(8,128)S(1)}, f32[8,128]{1,0:T(8,128)S(1)}, f32[8,128]{1,0:T(8,128)S(1)}, bf16[1024,384...) custom-call(bf16[4,512,128]{2,1,0:T(8,128)(2,1)S(1)} %get-tuple-elem, ...), custom_call_target="tpu_custom_call" | custom-call | flops 1000 | bytes 1000 | tf_op jit(solution)/shard_map/pallas_call | solution.py:355
  38.4 8.7 %shard_map.142 = (bf16[1024,384]{1,0:T(8,128)(2,1)S(1)}, bf16[4,384,256]{2,1,0:T(8,128)(2,1)S(1)}, f32[4,384,256]{2,1,0:T(8,128)S(1)}, f32[4,8,256]{2,1,0:T(8,12...) custom-call(s32[1024]{0:T(1024)S(1)} %copy-done.7, s32[1,1024]{1,0:T(1,128)S(1)} %bitcast.22, ...), custom_call_target="tpu_custom_call" | custom-call | flops 1000 | bytes 1000 | tf_op jit(solution)/shard_map/pallas_call | solution.py:453
  47.1 17.6 %shard_map.143 = (bf16[1024,384]{1,0:T(8,128)(2,1)}, f32[1024,384]{1,0:T(8,128)S(1)}, bf16[1024,384]{1,0:T(8,128)(2,1)S(1)}, bf16[3,4,448,128]{3,2,1,0:T(8,128)(...) custom-call(bf16[4,448,128]{2,1,0:T(8,128)(2,1)S(1)} %get-tuple-element.79.refs_0_, ...), custom_call_target="tpu_custom_call" | custom-call | flops 1000 | bytes 1000 | tf_op jit(solution)/shard_map/pallas_call | solution.py:604
  64.9 1.5 %shard_map.144 = (bf16[3,8,2,128,128]{4,3,2,1,0:T(8,128)(2,1)S(1)}, bf16[3,4,512,128]{3,2,1,0:T(8,128)(2,1)S(1)}, bf16[3,4,512,128]{3,2,1,0:T(8,128)(2,1)S(1)}, ...) custom-call(f32[8,384]{1,0:T(8,128)S(1)} %get-tuple-element.91.refs_, ...), custom_call_target="tpu_custom_call" | custom-call | flops 1000 | bytes 1000 | tf_op jit(solution)/shard_map/pallas_call | solution.py:668
  66.4 1.5 %collective-permute-done.16.refs_1_ = bf16[3,4,448,128]{3,2,1,0:T(8,128)(2,1)S(1)} collective-permute-done((bf16[3,4,448,128]{3,2,1,0:T(8,128)(2,1)S(1)}, bf16[3,4,448,128]{3,2,1,0:T(8,128)(2,1)S(1)}, u32[]{:S(2)}, u32[]{:S(2)}) %collective-permute-start.16) | collective-permute-done | bytes 1376288 | tf_op jit(solution)/shard_map/ppermute | solution.py:1157
  68.2 2.1 %collective-permute-start.17 = (bf16[3,1,448,128]{3,2,0,1:T(8,128)(2,1)S(1)}, bf16[3,1,448,128]{3,2,0,1:T(8,128)(2,1)S(1)}, u32[]{:S(2)}, u32[]{:S(2)}) collective-permute-start(bf16[3,1,448,128]{3,2,0,1:T(8,128)(2,1)S(1)} %bitcast.29), channel_id=1, source_target_pairs={{0,2},{1,3},{2,0},{3,1},{4,6},{5,7},{6,4},{7,5},{8,10},{9,11},{10,... | collective-permute-start | bytes 1032200 | tf_op jit(solution)/shard_map/ppermute | solution.py:1157
  70.3 2.3 %collective-permute-start.18 = (bf16[3,1,448,128]{3,2,0,1:T(8,128)(2,1)S(1)}, bf16[3,1,448,128]{3,2,0,1:T(8,128)(2,1)S(1)}, u32[]{:S(2)}, u32[]{:S(2)}) collective-permute-start(bf16[3,1,448,128]{3,2,0,1:T(8,128)(2,1)S(1)} %bitcast.28), channel_id=1, source_target_pairs={{0,4},{1,5},{2,6},{3,7},{4,0},{5,1},{6,2},{7,3},{8,12},{9,13},{10,... | collective-permute-start | bytes 1032200 | tf_op jit(solution)/shard_map/ppermute | solution.py:1157
  72.7 12.0 %shard_map.146 = (bf16[1024,1152]{1,0:T(8,128)(2,1)S(1)}, f32[8,384]{1,0:T(8,128)S(1)}) custom-call(f32[8,384]{1,0:T(8,128)S(1)} %get-tuple-element.91.refs_12_.vec_ref, s32[1024]{0:T(1024)S(1)} %copy-done.7, s32[1,1024]{1,0:T(1,128)S(1)} %bitcast.23, f32[4,8,256]{2,1,0:T(8,128)S(1)} %get-tuple-element.100.lse_ref, ...), custom_call_target="tpu_custom_call" | custom-call | flops 1000 | bytes 1000 | tf_op jit(solution)/shard_map/pallas_call | solution.py:784
  84.7 2.9 %shard_map.147 = (f32[1024,384]{1,0:T(8,128)S(1)}, bf16[4,480,128]{2,1,0:T(8,128)(2,1)S(1)}, bf16[4,160,128]{2,1,0:T(8,128)(2,1)S(1)}, bf16[4,160,128]{2,1,0:T(8,128)(2,1)S(1)}, bf16[4,160,128]{2,1,0:T(8,128)(2,1)S(1)}) custom-call(f32[1024,384]{1,0:T(8,128)S(1)} %get-tuple-element.83.hat_in_ref.hat_ref, bf16[384,1024]{1,0:T(8,128)(2,1)S(1)} %get-tuple-element.96.normed_ref, ...), custom_call_target="tpu_custom_call" | custom-call | flops 1000 | bytes 1000 | tf_op jit(solution)/shard_map/pallas_call | solution.py:861
  91.3 3.2 %collective-permute-start.24 = (bf16[1,480,128]{2,1,0:T(8,128)(2,1)S(1)}, bf16[1,480,128]{2,1,0:T(8,128)(2,1)S(1)}, u32[]{:S(2)}, u32[]{:S(2)}) collective-permute-start(bf16[1,480,128]{2,1,0:T(8,128)(2,1)S(1)} %get-tuple-element.132), channel_id=1, source_target_pairs={{0,4},{1,5},{2,6},{3,7},{4,0},{5,1},{6,2},{7,3},{8,12},{9,13},{10,... | collective-permute-start | bytes 368648 | tf_op jit(solution)/shard_map/ppermute | solution.py:1157
  94.6 2.0 %shard_map.148 = (f32[1024,384]{1,0:T(8,128)}, f32[8,128]{1,0:T(8,128)S(1)}) custom-call(f32[1024,384]{1,0:T(8,128)S(1)} %get-tuple-element.83.hat_in_ref.hat_ref, f32[1024,128]{1,0:T(8,128)S(1)} %get-tuple-element.93.rstd_ref, f32[8,384]{1,0:T(8,128)S(1)} %get-tuple-element.91.refs_12_.vec_ref, f32[1024,384]{1,0:T(8,128)S(1)} %get-tuple-element.116.da1_ref, ...), custom_call_target="tpu_custom_call" | custom-call | flops 1000 | bytes 1000 | tf_op jit(solution)/shard_map/pallas_call | solution.py:882
  96.9 1.8 %collective-permute-done.23 = bf16[1,480,128]{2,1,0:T(8,128)(2,1)S(1)} collective-permute-done((bf16[1,480,128]{2,1,0:T(8,128)(2,1)S(1)}, bf16[1,480,128]{2,1,0:T(8,128)(2,1)S(1)}, u32[]{:S(2)}, u32[]{:S(2)}) %collective-permute-start.23) | collective-permute-done | bytes 122912 | tf_op jit(solution)/shard_map/ppermute | solution.py:1157
  98.7 13.5 %collective-permute-done.24 = bf16[1,480,128]{2,1,0:T(8,128)(2,1)S(1)} collective-permute-done((bf16[1,480,128]{2,1,0:T(8,128)(2,1)S(1)}, bf16[1,480,128]{2,1,0:T(8,128)(2,1)S(1)}, u32[]{:S(2)}, u32[]{:S(2)}) %collective-permute-start.24) | collective-permute-done | bytes 122912 | tf_op jit(solution)/shard_map/ppermute | solution.py:1157
  113.1 1.9 %collective-permute-start.27 = (bf16[480,128]{1,0:T(8,128)(2,1)S(1)}, bf16[480,128]{1,0:T(8,128)(2,1)S(1)}, u32[]{:S(2)}, u32[]{:S(2)}) collective-permute-start(bf16[480,128]{1,0:T(8,128)(2,1)S(1)} %get-tuple-element.136), channel_id=1, source_target_pairs={{0,16},{8,24},{16,0},{24,8},{1,17},{9,25},{17,1},{25,9},{2,18},{10... | collective-permute-start | bytes 368648 | tf_op jit(solution)/shard_map/ppermute | solution.py:1157
  115.0 1.3 collective-permute-start.28
  116.3 1.6 %collective-permute-done.26.got0_ref = bf16[480,128]{1,0:T(8,128)(2,1)S(1)} collective-permute-done((bf16[480,128]{1,0:T(8,128)(2,1)S(1)}, bf16[480,128]{1,0:T(8,128)(2,1)S(1)}, u32[]{:S(2)}, u32[]{:S(2)}) %collective-permute-start.26) | collective-permute-done | bytes 122912 | tf_op jit(solution)/shard_map/ppermute | solution.py:1157
  117.9 1.2 collective-permute-done.27.got1_ref
  119.1 1.7 %collective-permute-done.28.got2_ref = bf16[480,128]{1,0:T(8,128)(2,1)S(1)} collective-permute-done((bf16[480,128]{1,0:T(8,128)(2,1)S(1)}, bf16[480,128]{1,0:T(8,128)(2,1)S(1)}, u32[]{:S(2)}, u32[]{:S(2)}) %collective-permute-start.28) | collective-permute-done | bytes 122912 | tf_op jit(solution)/shard_map/ppermute | solution.py:1157
  120.8 1.6 %shard_map.152 = (f32[55368]{0:T(1024)}, f32[55368]{0:T(1024)}, f32[448,128]{1,0:T(8,128)S(1)}, f32[8,128]{1,0:T(8,128)S(1)}) custom-call(f32[480,128]{1,0:T(8,128)S(1)} %get-tuple-element.134.own_ref, bf16[480,128]{1,0:T(8,128)(2,1)S(1)} %collective-permute-done.26.got0_ref, bf16[480,128]{1,0:T(8,128)(2,1)S(1)} %collective-permute-done.27.got1_ref, ...), custom_call_target="tpu_custom_call" | custom-call | tf_op jit(solution)/shard_map/pallas_call | solution.py:970
  123.6 1.5 %collective-permute-start.32 = (f32[8,128]{1,0:T(8,128)S(1)}, f32[8,128]{1,0:T(8,128)S(1)}, u32[]{:S(2)}, u32[]{:S(2)}) collective-permute-start(f32[8,128]{1,0:T(8,128)S(1)} %shard_map.153.refs_0_), channel_id=1, source_target_pairs={{0,6},{1,7},{2,4},{3,5},{4,2},{5,3},{6,0},{7,1},{8,14},{9,15},{10,... | collective-permute-start | bytes 12296 | tf_op jit(solution)/shard_map/ppermute | solution.py:1157
  125.1 2.8 %collective-permute-start.31 = (f32[8,128]{1,0:T(8,128)S(1)}, f32[8,128]{1,0:T(8,128)S(1)}, u32[]{:S(2)}, u32[]{:S(2)}) collective-permute-start(f32[8,128]{1,0:T(8,128)S(1)} %shard_map.153.refs_0_), channel_id=1, source_target_pairs={{0,4},{1,5},{2,6},{3,7},{4,0},{5,1},{6,2},{7,3},{8,12},{9,13},{10,... | collective-permute-start | bytes 12296 | tf_op jit(solution)/shard_map/ppermute | solution.py:1157
  129.6 1.9 %collective-permute-done.30.refs_1_ = f32[8,128]{1,0:T(8,128)S(1)} collective-permute-done((f32[8,128]{1,0:T(8,128)S(1)}, f32[8,128]{1,0:T(8,128)S(1)}, u32[]{:S(2)}, u32[]{:S(2)}) %collective-permute-start.30) | collective-permute-done | bytes 4128 | tf_op jit(solution)/shard_map/ppermute | solution.py:1157
  131.5 1.6 %collective-permute-start.35 = (f32[8,128]{1,0:T(8,128)S(1)}, f32[8,128]{1,0:T(8,128)S(1)}, u32[]{:S(2)}, u32[]{:S(2)}) collective-permute-start(f32[8,128]{1,0:T(8,128)S(1)} %shard_map.154.refs_0_), channel_id=1, source_target_pairs={{0,24},{8,16},{16,8},{24,0},{1,25},{9,17},{17,9},{25,1},{2,26},{10... | collective-permute-start | bytes 12296 | tf_op jit(solution)/shard_map/ppermute | solution.py:1157
  (83 shorter events, 22.3 us)
Async XLA Ops:
  1.7 14.5 %collective-permute-start.2 = (bf16[336,128]{1,0:T(8,128)(2,1)S(1)}, bf16[336,128]{1,0:T(8,128)(2,1)S(1)}, u32[]{:S(2)}, u32[]{:S(2)}) collective-permute-start(bf16[336,128]{1,0:T(8,128)(2,1)S(1)} %get-tuple-element.76.refs_0_), channel_id=1, source_target_pairs={{0,6},{1,7},{2,4},{3,5},{4,2},{5,3},{6,0},{7,1},{8,14},{9,15},{10,... | collective-permute-start | bytes 258056 | tf_op jit(solution)/shard_map/ppermute | solution.py:1157
  6.8 9.4 %collective-permute-start.1 = (bf16[336,128]{1,0:T(8,128)(2,1)S(1)}, bf16[336,128]{1,0:T(8,128)(2,1)S(1)}, u32[]{:S(2)}, u32[]{:S(2)}) collective-permute-start(bf16[336,128]{1,0:T(8,128)(2,1)S(1)} %get-tuple-element.76.refs_0_), channel_id=1, source_target_pairs={{0,4},{1,5},{2,6},{3,7},{4,0},{5,1},{6,2},{7,3},{8,12},{9,13},{10,... | collective-permute-start | bytes 258056 | tf_op jit(solution)/shard_map/ppermute | solution.py:1157
  6.8 9.4 %collective-permute-start = (bf16[336,128]{1,0:T(8,128)(2,1)S(1)}, bf16[336,128]{1,0:T(8,128)(2,1)S(1)}, u32[]{:S(2)}, u32[]{:S(2)}) collective-permute-start(bf16[336,128]{1,0:T(8,128)(2,1)S(1)} %get-tuple-element.76.refs_0_), channel_id=1, source_target_pairs={{0,2},{1,3},{2,0},{3,1},{4,6},{5,7},{6,4},{7,5},{8,10},{9,11},{10,... | collective-permute-start | bytes 258056 | tf_op jit(solution)/shard_map/ppermute | solution.py:1157
  7.5 4.8 %collective-permute-start.5 = (bf16[112,128]{1,0:T(8,128)(2,1)S(1)}, bf16[112,128]{1,0:T(8,128)(2,1)S(1)}, u32[]{:S(2)}, u32[]{:S(2)}) collective-permute-start(bf16[112,128]{1,0:T(8,128)(2,1)S(1)} %get-tuple-element.78.refs_0_), channel_id=1, source_target_pairs={{0,24},{8,16},{16,8},{24,0},{1,25},{9,17},{17,9},{25,1},{2,26},{10... | collective-permute-start | bytes 86024 | tf_op jit(solution)/shard_map/ppermute | solution.py:1157
  10.0 6.1 %collective-permute-start.4 = (bf16[112,128]{1,0:T(8,128)(2,1)S(1)}, bf16[112,128]{1,0:T(8,128)(2,1)S(1)}, u32[]{:S(2)}, u32[]{:S(2)}) collective-permute-start(bf16[112,128]{1,0:T(8,128)(2,1)S(1)} %get-tuple-element.78.refs_0_), channel_id=1, source_target_pairs={{0,16},{8,24},{16,0},{24,8},{1,17},{9,25},{17,1},{25,9},{2,18},{10... | collective-permute-start | bytes 86024 | tf_op jit(solution)/shard_map/ppermute | solution.py:1157
  12.2 3.9 %collective-permute-start.3 = (bf16[112,128]{1,0:T(8,128)(2,1)S(1)}, bf16[112,128]{1,0:T(8,128)(2,1)S(1)}, u32[]{:S(2)}, u32[]{:S(2)}) collective-permute-start(bf16[112,128]{1,0:T(8,128)(2,1)S(1)} %get-tuple-element.78.refs_0_), channel_id=1, source_target_pairs={{0,8},{8,0},{16,24},{24,16},{1,9},{9,1},{17,25},{25,17},{2,10},{10... | collective-permute-start | bytes 86024 | tf_op jit(solution)/shard_map/ppermute | solution.py:1157
  16.2 16.1 %collective-permute-start.8 = (bf16[4,336,128]{2,1,0:T(8,128)(2,1)S(1)}, bf16[4,336,128]{2,1,0:T(8,128)(2,1)S(1)}, u32[]{:S(2)}, u32[]{:S(2)}) collective-permute-start(bf16[4,336,128]{2,1,0:T(8,128)(2,1)S(1)} %shard_map.138.refs_0_), channel_id=1, source_target_pairs={{0,24},{8,16},{16,8},{24,0},{1,25},{9,17},{17,9},{25,1},{2,26},{10... | collective-permute-start | bytes 1032200 | tf_op jit(solution)/shard_map/ppermute | solution.py:1157
  19.0 13.3 %collective-permute-start.7 = (bf16[4,336,128]{2,1,0:T(8,128)(2,1)S(1)}, bf16[4,336,128]{2,1,0:T(8,128)(2,1)S(1)}, u32[]{:S(2)}, u32[]{:S(2)}) collective-permute-start(bf16[4,336,128]{2,1,0:T(8,128)(2,1)S(1)} %shard_map.138.refs_0_), channel_id=1, source_target_pairs={{0,16},{8,24},{16,0},{24,8},{1,17},{9,25},{17,1},{25,9},{2,18},{10... | collective-permute-start | bytes 1032200 | tf_op jit(solution)/shard_map/ppermute | solution.py:1157
  19.3 13.0 %collective-permute-start.6 = (bf16[4,336,128]{2,1,0:T(8,128)(2,1)S(1)}, bf16[4,336,128]{2,1,0:T(8,128)(2,1)S(1)}, u32[]{:S(2)}, u32[]{:S(2)}) collective-permute-start(bf16[4,336,128]{2,1,0:T(8,128)(2,1)S(1)} %shard_map.138.refs_0_), channel_id=1, source_target_pairs={{0,8},{8,0},{16,24},{24,16},{1,9},{9,1},{17,25},{25,17},{2,10},{10... | collective-permute-start | bytes 1032200 | tf_op jit(solution)/shard_map/ppermute | solution.py:1157
  19.8 7.0 %collective-permute-start.11 = (bf16[4,112,128]{2,1,0:T(8,128)(2,1)S(1)}, bf16[4,112,128]{2,1,0:T(8,128)(2,1)S(1)}, u32[]{:S(2)}, u32[]{:S(2)}) collective-permute-start(bf16[4,112,128]{2,1,0:T(8,128)(2,1)S(1)} %shard_map.137.refs_4_.refs_0_), channel_id=1, source_target_pairs={{0,6},{1,7},{2,4},{3,5},{4,2},{5,3},{6,0},{7,1},{8,14},{9,15},{10,... | collective-permute-start | bytes 344072 | tf_op jit(solution)/shard_map/ppermute | solution.py:1157
  23.5 6.7 %collective-permute-start.10 = (bf16[4,112,128]{2,1,0:T(8,128)(2,1)S(1)}, bf16[4,112,128]{2,1,0:T(8,128)(2,1)S(1)}, u32[]{:S(2)}, u32[]{:S(2)}) collective-permute-start(bf16[4,112,128]{2,1,0:T(8,128)(2,1)S(1)} %shard_map.137.refs_4_.refs_0_), channel_id=1, source_target_pairs={{0,4},{1,5},{2,6},{3,7},{4,0},{5,1},{6,2},{7,3},{8,12},{9,13},{10,... | collective-permute-start | bytes 344072 | tf_op jit(solution)/shard_map/ppermute | solution.py:1157
  26.7 5.6 %collective-permute-start.9 = (bf16[4,112,128]{2,1,0:T(8,128)(2,1)S(1)}, bf16[4,112,128]{2,1,0:T(8,128)(2,1)S(1)}, u32[]{:S(2)}, u32[]{:S(2)}) collective-permute-start(bf16[4,112,128]{2,1,0:T(8,128)(2,1)S(1)} %shard_map.137.refs_4_.refs_0_), channel_id=1, source_target_pairs={{0,2},{1,3},{2,0},{3,1},{4,6},{5,7},{6,4},{7,5},{8,10},{9,11},{10,... | collective-permute-start | bytes 344072 | tf_op jit(solution)/shard_map/ppermute | solution.py:1157
  32.6 2.0 %collective-permute-start.15 = (bf16[4,512,128]{2,1,0:T(8,128)(2,1)S(1)}, bf16[4,512,128]{2,1,0:T(8,128)(2,1)S(1)}, u32[]{:S(2)}, u32[]{:S(2)}) collective-permute-start(bf16[4,512,128]{2,1,0:T(8,128)(2,1)S(1)} %get-tuple-element.82.own_ref), channel_id=1, source_target_pairs={{0,1},{1,0},{2,3},{3,2},{4,5},{5,4},{6,7},{7,6},{8,9},{9,8},{10,11... | collective-permute-start | bytes 1572872 | tf_op jit(solution)/shard_map/ppermute | solution.py:1157
  32.7 14.4 %collective-permute-start.12 = (bf16[4,448,128]{2,1,0:T(8,128)(2,1)S(1)}, bf16[4,448,128]{2,1,0:T(8,128)(2,1)S(1)}, u32[]{:S(2)}, u32[]{:S(2)}) collective-permute-start(bf16[4,448,128]{2,1,0:T(8,128)(2,1)S(1)} %get-tuple-element.79.refs_0_), channel_id=1, source_target_pairs={{0,1},{1,0},{2,3},{3,2},{4,5},{5,4},{6,7},{7,6},{8,9},{9,8},{10,11... | collective-permute-start | bytes 1376264 | tf_op jit(solution)/shard_map/ppermute | solution.py:1157
  33.2 13.9 %collective-permute-start.13 = (bf16[4,448,128]{2,1,0:T(8,128)(2,1)S(1)}, bf16[4,448,128]{2,1,0:T(8,128)(2,1)S(1)}, u32[]{:S(2)}, u32[]{:S(2)}) collective-permute-start(bf16[4,448,128]{2,1,0:T(8,128)(2,1)S(1)} %get-tuple-element.80.refs_1_), channel_id=1, source_target_pairs={{0,1},{1,0},{2,3},{3,2},{4,5},{5,4},{6,7},{7,6},{8,9},{9,8},{10,11... | collective-permute-start | bytes 1376264 | tf_op jit(solution)/shard_map/ppermute | solution.py:1157
  33.2 13.9 %collective-permute-start.14 = (bf16[4,448,128]{2,1,0:T(8,128)(2,1)S(1)}, bf16[4,448,128]{2,1,0:T(8,128)(2,1)S(1)}, u32[]{:S(2)}, u32[]{:S(2)}) collective-permute-start(bf16[4,448,128]{2,1,0:T(8,128)(2,1)S(1)} %get-tuple-element.81.refs_2_), channel_id=1, source_target_pairs={{0,1},{1,0},{2,3},{3,2},{4,5},{5,4},{6,7},{7,6},{8,9},{9,8},{10,11... | collective-permute-start | bytes 1376264 | tf_op jit(solution)/shard_map/ppermute | solution.py:1157
  64.7 3.1 %collective-permute-start.16 = (bf16[3,4,448,128]{3,2,1,0:T(8,128)(2,1)S(1)}, bf16[3,4,448,128]{3,2,1,0:T(8,128)(2,1)S(1)}, u32[]{:S(2)}, u32[]{:S(2)}) collective-permute-start(bf16[3,4,448,128]{3,2,1,0:T(8,128)(2,1)S(1)} %get-tuple-element.111), channel_id=1, source_target_pairs={{0,1},{1,0},{2,3},{3,2},{4,5},{5,4},{6,7},{7,6},{8,9},{9,8},{10,11... | collective-permute-start | bytes 4128776 | tf_op jit(solution)/shard_map/ppermute | solution.py:1157
  68.2 20.0 %collective-permute-start.17 = (bf16[3,1,448,128]{3,2,0,1:T(8,128)(2,1)S(1)}, bf16[3,1,448,128]{3,2,0,1:T(8,128)(2,1)S(1)}, u32[]{:S(2)}, u32[]{:S(2)}) collective-permute-start(bf16[3,1,448,128]{3,2,0,1:T(8,128)(2,1)S(1)} %bitcast.29), channel_id=1, source_target_pairs={{0,2},{1,3},{2,0},{3,1},{4,6},{5,7},{6,4},{7,5},{8,10},{9,11},{10,... | collective-permute-start | bytes 1032200 | tf_op jit(solution)/shard_map/ppermute | solution.py:1157
  70.3 26.6 %collective-permute-start.18 = (bf16[3,1,448,128]{3,2,0,1:T(8,128)(2,1)S(1)}, bf16[3,1,448,128]{3,2,0,1:T(8,128)(2,1)S(1)}, u32[]{:S(2)}, u32[]{:S(2)}) collective-permute-start(bf16[3,1,448,128]{3,2,0,1:T(8,128)(2,1)S(1)} %bitcast.28), channel_id=1, source_target_pairs={{0,4},{1,5},{2,6},{3,7},{4,0},{5,1},{6,2},{7,3},{8,12},{9,13},{10,... | collective-permute-start | bytes 1032200 | tf_op jit(solution)/shard_map/ppermute | solution.py:1157
  72.6 24.4 %collective-permute-start.19 = (bf16[3,1,448,128]{3,2,0,1:T(8,128)(2,1)S(1)}, bf16[3,1,448,128]{3,2,0,1:T(8,128)(2,1)S(1)}, u32[]{:S(2)}, u32[]{:S(2)}) collective-permute-start(bf16[3,1,448,128]{3,2,0,1:T(8,128)(2,1)S(1)} %bitcast.27), channel_id=1, source_target_pairs={{0,6},{1,7},{2,4},{3,5},{4,2},{5,3},{6,0},{7,1},{8,14},{9,15},{10,... | collective-permute-start | bytes 1032200 | tf_op jit(solution)/shard_map/ppermute | solution.py:1157
  90.3 8.4 %collective-permute-start.23 = (bf16[1,480,128]{2,1,0:T(8,128)(2,1)S(1)}, bf16[1,480,128]{2,1,0:T(8,128)(2,1)S(1)}, u32[]{:S(2)}, u32[]{:S(2)}) collective-permute-start(bf16[1,480,128]{2,1,0:T(8,128)(2,1)S(1)} %get-tuple-element.131), channel_id=1, source_target_pairs={{0,2},{1,3},{2,0},{3,1},{4,6},{5,7},{6,4},{7,5},{8,10},{9,11},{10,... | collective-permute-start | bytes 368648 | tf_op jit(solution)/shard_map/ppermute | solution.py:1157
  91.3 20.9 %collective-permute-start.24 = (bf16[1,480,128]{2,1,0:T(8,128)(2,1)S(1)}, bf16[1,480,128]{2,1,0:T(8,128)(2,1)S(1)}, u32[]{:S(2)}, u32[]{:S(2)}) collective-permute-start(bf16[1,480,128]{2,1,0:T(8,128)(2,1)S(1)} %get-tuple-element.132), channel_id=1, source_target_pairs={{0,4},{1,5},{2,6},{3,7},{4,0},{5,1},{6,2},{7,3},{8,12},{9,13},{10,... | collective-permute-start | bytes 368648 | tf_op jit(solution)/shard_map/ppermute | solution.py:1157
  94.5 17.7 %collective-permute-start.25 = (bf16[1,480,128]{2,1,0:T(8,128)(2,1)S(1)}, bf16[1,480,128]{2,1,0:T(8,128)(2,1)S(1)}, u32[]{:S(2)}, u32[]{:S(2)}) collective-permute-start(bf16[1,480,128]{2,1,0:T(8,128)(2,1)S(1)} %get-tuple-element.133), channel_id=1, source_target_pairs={{0,6},{1,7},{2,4},{3,5},{4,2},{5,3},{6,0},{7,1},{8,14},{9,15},{10,... | collective-permute-start | bytes 368648 | tf_op jit(solution)/shard_map/ppermute | solution.py:1157
  112.4 5.5 %collective-permute-start.26 = (bf16[480,128]{1,0:T(8,128)(2,1)S(1)}, bf16[480,128]{1,0:T(8,128)(2,1)S(1)}, u32[]{:S(2)}, u32[]{:S(2)}) collective-permute-start(bf16[480,128]{1,0:T(8,128)(2,1)S(1)} %get-tuple-element.135), channel_id=1, source_target_pairs={{0,8},{8,0},{16,24},{24,16},{1,9},{9,1},{17,25},{25,17},{2,10},{10... | collective-permute-start | bytes 368648 | tf_op jit(solution)/shard_map/ppermute | solution.py:1157
  113.1 6.0 %collective-permute-start.27 = (bf16[480,128]{1,0:T(8,128)(2,1)S(1)}, bf16[480,128]{1,0:T(8,128)(2,1)S(1)}, u32[]{:S(2)}, u32[]{:S(2)}) collective-permute-start(bf16[480,128]{1,0:T(8,128)(2,1)S(1)} %get-tuple-element.136), channel_id=1, source_target_pairs={{0,16},{8,24},{16,0},{24,8},{1,17},{9,25},{17,1},{25,9},{2,18},{10... | collective-permute-start | bytes 368648 | tf_op jit(solution)/shard_map/ppermute | solution.py:1157
  115.0 5.8 %collective-permute-start.28 = (bf16[480,128]{1,0:T(8,128)(2,1)S(1)}, bf16[480,128]{1,0:T(8,128)(2,1)S(1)}, u32[]{:S(2)}, u32[]{:S(2)}) collective-permute-start(bf16[480,128]{1,0:T(8,128)(2,1)S(1)} %get-tuple-element.137), channel_id=1, source_target_pairs={{0,24},{8,16},{16,8},{24,0},{1,25},{9,17},{17,9},{25,1},{2,26},{10... | collective-permute-start | bytes 368648 | tf_op jit(solution)/shard_map/ppermute | solution.py:1157
  123.6 5.4 %collective-permute-start.32 = (f32[8,128]{1,0:T(8,128)S(1)}, f32[8,128]{1,0:T(8,128)S(1)}, u32[]{:S(2)}, u32[]{:S(2)}) collective-permute-start(f32[8,128]{1,0:T(8,128)S(1)} %shard_map.153.refs_0_), channel_id=1, source_target_pairs={{0,6},{1,7},{2,4},{3,5},{4,2},{5,3},{6,0},{7,1},{8,14},{9,15},{10,... | collective-permute-start | bytes 12296 | tf_op jit(solution)/shard_map/ppermute | solution.py:1157
  125.1 4.5 %collective-permute-start.31 = (f32[8,128]{1,0:T(8,128)S(1)}, f32[8,128]{1,0:T(8,128)S(1)}, u32[]{:S(2)}, u32[]{:S(2)}) collective-permute-start(f32[8,128]{1,0:T(8,128)S(1)} %shard_map.153.refs_0_), channel_id=1, source_target_pairs={{0,4},{1,5},{2,6},{3,7},{4,0},{5,1},{6,2},{7,3},{8,12},{9,13},{10,... | collective-permute-start | bytes 12296 | tf_op jit(solution)/shard_map/ppermute | solution.py:1157
  127.9 3.6 %collective-permute-start.30 = (f32[8,128]{1,0:T(8,128)S(1)}, f32[8,128]{1,0:T(8,128)S(1)}, u32[]{:S(2)}, u32[]{:S(2)}) collective-permute-start(f32[8,128]{1,0:T(8,128)S(1)} %shard_map.153.refs_0_), channel_id=1, source_target_pairs={{0,2},{1,3},{2,0},{3,1},{4,6},{5,7},{6,4},{7,5},{8,10},{9,11},{10,... | collective-permute-start | bytes 12296 | tf_op jit(solution)/shard_map/ppermute | solution.py:1157
  131.5 4.5 %collective-permute-start.35 = (f32[8,128]{1,0:T(8,128)S(1)}, f32[8,128]{1,0:T(8,128)S(1)}, u32[]{:S(2)}, u32[]{:S(2)}) collective-permute-start(f32[8,128]{1,0:T(8,128)S(1)} %shard_map.154.refs_0_), channel_id=1, source_target_pairs={{0,24},{8,16},{16,8},{24,0},{1,25},{9,17},{17,9},{25,1},{2,26},{10... | collective-permute-start | bytes 12296 | tf_op jit(solution)/shard_map/ppermute | solution.py:1157
  133.1 3.6 %collective-permute-start.34 = (f32[8,128]{1,0:T(8,128)S(1)}, f32[8,128]{1,0:T(8,128)S(1)}, u32[]{:S(2)}, u32[]{:S(2)}) collective-permute-start(f32[8,128]{1,0:T(8,128)S(1)} %shard_map.154.refs_0_), channel_id=1, source_target_pairs={{0,16},{8,24},{16,0},{24,8},{1,17},{9,25},{17,1},{25,9},{2,18},{10... | collective-permute-start | bytes 12296 | tf_op jit(solution)/shard_map/ppermute | solution.py:1157
  134.1 3.6 %collective-permute-start.33 = (f32[8,128]{1,0:T(8,128)S(1)}, f32[8,128]{1,0:T(8,128)S(1)}, u32[]{:S(2)}, u32[]{:S(2)}) collective-permute-start(f32[8,128]{1,0:T(8,128)S(1)} %shard_map.154.refs_0_), channel_id=1, source_target_pairs={{0,8},{8,0},{16,24},{24,16},{1,9},{9,1},{17,25},{25,17},{2,10},{10... | collective-permute-start | bytes 12296 | tf_op jit(solution)/shard_map/ppermute | solution.py:1157
  (15 other events, 118.7 us)

commit v6 on v5

--- a/solution.py
+++ b/solution.py
@@ -1021,21 +1021,23 @@
     )(*parts, *after)
 
 
-def lay_lower_kernel(plan, count_ref, *refs):
-    for i, part in enumerate(refs[:-1]):
-        refs[-1][i] = part[...]
-    last = refs[0][-16:, :].astype(F32)
-    refs[-1][0, plan.win - plan.upper - 16 :, :] = (last + count_ref[...]).astype(BF)
-
-
-def lay_lower(plan, parts, count):
+def lay_lower_kernel(plan, mine_ref, got_ref, count_ref, out_ref):
+    half = mine_ref.shape[0]
+    out_ref[:half] = mine_ref[...]
+    out_ref[half:] = got_ref[...]
+    last = mine_ref[0, -16:, :].astype(F32)
+    out_ref[0, plan.win - plan.upper - 16 :, :] = (last + count_ref[...]).astype(BF)
+
+
+def lay_lower(plan, mine, got, count):
+    half, height, _ = mine.shape
     return pl.pallas_call(
         functools.partial(lay_lower_kernel, plan),
-        out_shape=jax.ShapeDtypeStruct((len(parts), *parts[0].shape), BF),
-        in_specs=[VMEM] * (1 + len(parts)),
+        out_shape=jax.ShapeDtypeStruct((2 * half, height, LANES), BF),
+        in_specs=[VMEM] * 3,
         out_specs=VMEM,
         compiler_params=params(4),
-    )(count, *parts)
+    )(mine, got, count)
 
 
 def choose_kernel(plan, *refs):
@@ -1171,7 +1173,9 @@
 def gather_windows(plan, upper, lower, count):
     first, *more = groups_of(plan.nd, 1)
     (bits,) = groups_of(plan.nb)
-    lower = lay_lower(plan, with_partners(lower, "bucket", plan.nb, bits), count)
+    near, distant = masks_of(bits)[:2]
+    lower = lay_column([lower, swap(lower, "bucket", plan.nb, near)])
+    lower = lay_lower(plan, lower, swap(lower, "bucket", plan.nb, distant), count)
     column = lay_column(with_partners(upper, "dp", plan.nd, first), lower)
     for group in more:
         column = jnp.concatenate(with_partners(column, "dp", plan.nd, group), axis=0)
@@ -1186,8 +1190,9 @@
 
 def scatter_dp(plan, pieces):
     *more, last = groups_of(plan.nd, 1)
+    sent = list(zip(pieces[1:], masks_of(last)))
     got = [pieces[0]] + [
-        swap(piece, "dp", plan.nd, mask) for piece, mask in zip(pieces[1:], masks_of(last))
+        swap(piece, "dp", plan.nd, mask) for piece, mask in sent[1:] + sent[:1]
     ]
     for bits in reversed(more):
         held = tree_sum([x.astype(F32) for x in got])

time: 139 us -> 138 us (level)
  waiting for transfers between devices: 38.7 us -> 42.9 us
  Pallas kernels: 53.2 us -> 49.4 us
    ppermute x36 -> x35, waiting for transfers between devices: 38.7 us -> 42.9 us  [swap(): return lax.ppermute(x, axis, [(i, i ^ mask) for i in range(size)])]
    pallas_call x1, Pallas kernels: 12 us -> 9.8 us  [backward(): pl.pallas_call(functools.partial(backward_kernel, plan), out_shape=(jax.S...]
    pallas_call x1, Pallas kernels: 8.72 us -> 7.11 us  [forward(): pl.pallas_call(functools.partial(forward_kernel, plan), out_shape=(jax.Sh...]
    ppermute x36 -> x35, starting transfers between devices: 43 us -> 41.7 us  [swap(): return lax.ppermute(x, axis, [(i, i ^ mask) for i in range(size)])]
  transfers between devices with their start and end apart: 36 -> 35, of which waited for: 22 -> 22; matrix products, arithmetic and copies ran while one was open for 0% -> 0% of each run, Pallas kernels for 23% -> 21%
where the time goes in v6:
time: 138 us
  Pallas kernels  49.4 us (36%)
  waiting for transfers between devices  42.9 us (31%)
  starting transfers between devices  41.7 us (30%)
  local copies, waits for them, and re-layouts  2.79 us (2%)
    ppermute x35, waiting for transfers between devices, swap(): return lax.ppermute(x, axis, [(i, i ^ mask) for i in range(size)])  42.9 us
    ppermute x35, starting transfers between devices, swap(): return lax.ppermute(x, axis, [(i, i ^ mask) for i in range(size)])  41.7 us
    pallas_call x1, Pallas kernels, middle_part(): pl.pallas_call(functools.partial(middle_kernel, plan), out_shape=(jax.Sha...  17.6 us
    pallas_call x1, Pallas kernels, backward(): pl.pallas_call(functools.partial(backward_kernel, plan), out_shape=(jax.S...  9.8 us
    pallas_call x1, Pallas kernels, forward(): pl.pallas_call(functools.partial(forward_kernel, plan), out_shape=(jax.Sh...  7.11 us
    pallas_call x1, Pallas kernels, project_part(): pl.pallas_call(functools.partial(project_kernel, plan), out_shape=(jax.Sh...  3.72 us
    pallas_call x1, Pallas kernels, finish_part(): pl.pallas_call(functools.partial(finish_kernel, plan), out_shape=(jax.Sha...  2.9 us
    unnamed x22, local copies, waits for them, and re-layouts  2.79 us
  transfers between devices with their start and end apart: 35, of which 22 were waited for; matrix products, arithmetic and copies ran while one was open for 0% of the time, Pallas kernels for 21%

profile of v6, /device:TPU:0, one launch (start us, length us, event | category | flops | bytes accessed | tf_op | source)
XLA Modules:
  0.0 137.7 jit_solution(5364017374099120149)
XLA Ops:
  1.7 3.0 %collective-permute-start.3 = (bf16[112,128]{1,0:T(8,128)(2,1)S(1)}, bf16[112,128]{1,0:T(8,128)(2,1)S(1)}, u32[]{:S(2)}, u32[]{:S(2)}) collective-permute-start(bf16[112,128]{1,0:T(8,128)(2,1)S(1)} %get-tuple-element.77.refs_0_), channel_id=1, source_target_pairs={{0,8},{8,0},{16,24},{24,16},{1,9},{9,1},{17,25},{25,17},{2,10},{10... | collective-permute-start | bytes 86024 | tf_op jit(solution)/shard_map/ppermute | solution.py:1159
  4.7 3.6 %collective-permute-start.2 = (bf16[336,128]{1,0:T(8,128)(2,1)S(1)}, bf16[336,128]{1,0:T(8,128)(2,1)S(1)}, u32[]{:S(2)}, u32[]{:S(2)}) collective-permute-start(bf16[336,128]{1,0:T(8,128)(2,1)S(1)} %get-tuple-element.76.refs_0_), channel_id=1, source_target_pairs={{0,6},{1,7},{2,4},{3,5},{4,2},{5,3},{6,0},{7,1},{8,14},{9,15},{10,... | collective-permute-start | bytes 258056 | tf_op jit(solution)/shard_map/ppermute | solution.py:1159
  9.1 1.6 %collective-permute-start.4 = (bf16[2,112,128]{2,1,0:T(8,128)(2,1)S(1)}, bf16[2,112,128]{2,1,0:T(8,128)(2,1)S(1)}, u32[]{:S(2)}, u32[]{:S(2)}) collective-permute-start(bf16[2,112,128]{2,1,0:T(8,128)(2,1)S(1)} %shard_map.136.mine_ref), channel_id=1, source_target_pairs={{0,16},{8,24},{16,0},{24,8},{1,17},{9,25},{17,1},{25,9},{2,18},{10... | collective-permute-start | bytes 172040 | tf_op jit(solution)/shard_map/ppermute | solution.py:1159
  13.4 1.9 %collective-permute-done.1.refs_2_ = bf16[336,128]{1,0:T(8,128)(2,1)S(1)} collective-permute-done((bf16[336,128]{1,0:T(8,128)(2,1)S(1)}, bf16[336,128]{1,0:T(8,128)(2,1)S(1)}, u32[]{:S(2)}, u32[]{:S(2)}) %collective-permute-start.1) | collective-permute-done | bytes 86048 | tf_op jit(solution)/shard_map/ppermute | solution.py:1159
  15.3 1.6 %collective-permute-start.7 = (bf16[4,336,128]{2,1,0:T(8,128)(2,1)S(1)}, bf16[4,336,128]{2,1,0:T(8,128)(2,1)S(1)}, u32[]{:S(2)}, u32[]{:S(2)}) collective-permute-start(bf16[4,336,128]{2,1,0:T(8,128)(2,1)S(1)} %shard_map.139.refs_0_), channel_id=1, source_target_pairs={{0,24},{8,16},{16,8},{24,0},{1,25},{9,17},{17,9},{25,1},{2,26},{10... | collective-permute-start | bytes 1032200 | tf_op jit(solution)/shard_map/ppermute | solution.py:1159
  17.3 1.5 %collective-permute-start.5 = (bf16[4,336,128]{2,1,0:T(8,128)(2,1)S(1)}, bf16[4,336,128]{2,1,0:T(8,128)(2,1)S(1)}, u32[]{:S(2)}, u32[]{:S(2)}) collective-permute-start(bf16[4,336,128]{2,1,0:T(8,128)(2,1)S(1)} %shard_map.139.refs_0_), channel_id=1, source_target_pairs={{0,8},{8,0},{16,24},{24,16},{1,9},{9,1},{17,25},{25,17},{2,10},{10... | collective-permute-start | bytes 1032200 | tf_op jit(solution)/shard_map/ppermute | solution.py:1159
  18.8 2.6 %collective-permute-start.10 = (bf16[4,112,128]{2,1,0:T(8,128)(2,1)S(1)}, bf16[4,112,128]{2,1,0:T(8,128)(2,1)S(1)}, u32[]{:S(2)}, u32[]{:S(2)}) collective-permute-start(bf16[4,112,128]{2,1,0:T(8,128)(2,1)S(1)} %shard_map.138.refs_4_.refs_0_), channel_id=1, source_target_pairs={{0,6},{1,7},{2,4},{3,5},{4,2},{5,3},{6,0},{7,1},{8,14},{9,15},{10,... | collective-permute-start | bytes 344072 | tf_op jit(solution)/shard_map/ppermute | solution.py:1159
  21.4 5.3 %collective-permute-done.10.refs_3_ = bf16[4,112,128]{2,1,0:T(8,128)(2,1)S(1)} collective-permute-done((bf16[4,112,128]{2,1,0:T(8,128)(2,1)S(1)}, bf16[4,112,128]{2,1,0:T(8,128)(2,1)S(1)}, u32[]{:S(2)}, u32[]{:S(2)}) %collective-permute-start.10) | collective-permute-done | bytes 114720 | tf_op jit(solution)/shard_map/ppermute | solution.py:1159
  26.7 2.9 %collective-permute-start.8 = (bf16[4,112,128]{2,1,0:T(8,128)(2,1)S(1)}, bf16[4,112,128]{2,1,0:T(8,128)(2,1)S(1)}, u32[]{:S(2)}, u32[]{:S(2)}) collective-permute-start(bf16[4,112,128]{2,1,0:T(8,128)(2,1)S(1)} %shard_map.138.refs_4_.refs_0_), channel_id=1, source_target_pairs={{0,2},{1,3},{2,0},{3,1},{4,6},{5,7},{6,4},{7,5},{8,10},{9,11},{10,... | collective-permute-start | bytes 344072 | tf_op jit(solution)/shard_map/ppermute | solution.py:1159
  30.2 2.1 %collective-permute-done.8.refs_1_ = bf16[4,112,128]{2,1,0:T(8,128)(2,1)S(1)} collective-permute-done((bf16[4,112,128]{2,1,0:T(8,128)(2,1)S(1)}, bf16[4,112,128]{2,1,0:T(8,128)(2,1)S(1)}, u32[]{:S(2)}, u32[]{:S(2)}) %collective-permute-start.8) | collective-permute-done | bytes 114720 | tf_op jit(solution)/shard_map/ppermute | solution.py:1159
  35.5 3.7 %shard_map.142 = (bf16[384,1152]{1,0:T(8,128)(2,1)S(1)}, f32[8,384]{1,0:T(8,128)S(1)}, f32[8,128]{1,0:T(8,128)S(1)}, f32[8,128]{1,0:T(8,128)S(1)}, bf16[1024,384...) custom-call(bf16[4,512,128]{2,1,0:T(8,128)(2,1)S(1)} %get-tuple-elem, ...), custom_call_target="tpu_custom_call" | custom-call | flops 1000 | bytes 1000 | tf_op jit(solution)/shard_map/pallas_call | solution.py:355
  39.3 7.1 %shard_map.143 = (bf16[1024,384]{1,0:T(8,128)(2,1)S(1)}, bf16[4,384,256]{2,1,0:T(8,128)(2,1)S(1)}, f32[4,384,256]{2,1,0:T(8,128)S(1)}, f32[4,8,256]{2,1,0:T(8,12...) custom-call(s32[1024]{0:T(1024)S(1)} %copy-done.7, s32[1,1024]{1,0:T(1,128)S(1)} %bitcast.22, ...), custom_call_target="tpu_custom_call" | custom-call | flops 1000 | bytes 1000 | tf_op jit(solution)/shard_map/pallas_call | solution.py:453
  46.5 17.6 %shard_map.144 = (bf16[1024,384]{1,0:T(8,128)(2,1)}, f32[1024,384]{1,0:T(8,128)S(1)}, bf16[1024,384]{1,0:T(8,128)(2,1)S(1)}, bf16[3,4,448,128]{3,2,1,0:T(8,128)(...) custom-call(bf16[4,448,128]{2,1,0:T(8,128)(2,1)S(1)} %get-tuple-element.79.refs_0_, ...), custom_call_target="tpu_custom_call" | custom-call | flops 1000 | bytes 1000 | tf_op jit(solution)/shard_map/pallas_call | solution.py:604
  64.1 1.8 %collective-permute-start.15 = (bf16[3,4,448,128]{3,2,1,0:T(8,128)(2,1)S(1)}, bf16[3,4,448,128]{3,2,1,0:T(8,128)(2,1)S(1)}, u32[]{:S(2)}, u32[]{:S(2)}) collective-permute-start(bf16[3,4,448,128]{3,2,1,0:T(8,128)(2,1)S(1)} %get-tuple-element.111), channel_id=1, source_target_pairs={{0,1},{1,0},{2,3},{3,2},{4,5},{5,4},{6,7},{7,6},{8,9},{9,8},{10,11... | collective-permute-start | bytes 4128776 | tf_op jit(solution)/shard_map/ppermute | solution.py:1159
  65.8 1.5 %shard_map.145 = (bf16[3,8,2,128,128]{4,3,2,1,0:T(8,128)(2,1)S(1)}, bf16[3,4,512,128]{3,2,1,0:T(8,128)(2,1)S(1)}, bf16[3,4,512,128]{3,2,1,0:T(8,128)(2,1)S(1)}, ...) custom-call(f32[8,384]{1,0:T(8,128)S(1)} %get-tuple-element.91.refs_, ...), custom_call_target="tpu_custom_call" | custom-call | flops 1000 | bytes 1000 | tf_op jit(solution)/shard_map/pallas_call | solution.py:668
  69.5 3.2 %collective-permute-start.17 = (bf16[3,1,448,128]{3,2,0,1:T(8,128)(2,1)S(1)}, bf16[3,1,448,128]{3,2,0,1:T(8,128)(2,1)S(1)}, u32[]{:S(2)}, u32[]{:S(2)}) collective-permute-start(bf16[3,1,448,128]{3,2,0,1:T(8,128)(2,1)S(1)} %bitcast.28), channel_id=1, source_target_pairs={{0,6},{1,7},{2,4},{3,5},{4,2},{5,3},{6,0},{7,1},{8,14},{9,15},{10,... | collective-permute-start | bytes 1032200 | tf_op jit(solution)/shard_map/ppermute | solution.py:1159
  72.7 9.8 %shard_map.147 = (bf16[1024,1152]{1,0:T(8,128)(2,1)S(1)}, f32[8,384]{1,0:T(8,128)S(1)}) custom-call(f32[8,384]{1,0:T(8,128)S(1)} %get-tuple-element.91.refs_12_.vec_ref, s32[1024]{0:T(1024)S(1)} %copy-done.7, s32[1,1024]{1,0:T(1,128)S(1)} %bitcast.23, f32[4,8,256]{2,1,0:T(8,128)S(1)} %get-tuple-element.100.lse_ref, ...), custom_call_target="tpu_custom_call" | custom-call | flops 1000 | bytes 1000 | tf_op jit(solution)/shard_map/pallas_call | solution.py:784
  82.5 2.9 %shard_map.148 = (f32[1024,384]{1,0:T(8,128)S(1)}, bf16[4,480,128]{2,1,0:T(8,128)(2,1)S(1)}, bf16[4,160,128]{2,1,0:T(8,128)(2,1)S(1)}, bf16[4,160,128]{2,1,0:T(8,128)(2,1)S(1)}, bf16[4,160,128]{2,1,0:T(8,128)(2,1)S(1)}) custom-call(f32[1024,384]{1,0:T(8,128)S(1)} %get-tuple-element.83.hat_in_ref.hat_ref, bf16[384,1024]{1,0:T(8,128)(2,1)S(1)} %get-tuple-element.96.normed_ref, ...), custom_call_target="tpu_custom_call" | custom-call | flops 1000 | bytes 1000 | tf_op jit(solution)/shard_map/pallas_call | solution.py:861
  85.4 1.8 %collective-permute-start.19 = (bf16[4,160,128]{2,1,0:T(8,128)(2,1)S(1)}, bf16[4,160,128]{2,1,0:T(8,128)(2,1)S(1)}, u32[]{:S(2)}, u32[]{:S(2)}) collective-permute-start(bf16[4,160,128]{2,1,0:T(8,128)(2,1)S(1)} %get-tuple-element.126), channel_id=1, source_target_pairs={{0,1},{1,0},{2,3},{3,2},{4,5},{5,4},{6,7},{7,6},{8,9},{9,8},{10,11... | collective-permute-start | bytes 491528 | tf_op jit(solution)/shard_map/ppermute | solution.py:1159
  87.4 8.2 %collective-permute-done.16 = bf16[3,1,448,128]{3,2,0,1:T(8,128)(2,1)S(1)} collective-permute-done((bf16[3,1,448,128]{3,2,0,1:T(8,128)(2,1)S(1)}, bf16[3,1,448,128]{3,2,0,1:T(8,128)(2,1)S(1)}, u32[]{:S(2)}, u32[]{:S(2)}) %collective-permute-start.16) | collective-permute-done | bytes 344096 | tf_op jit(solution)/shard_map/ppermute | solution.py:1159
  98.3 2.8 %collective-permute-start.24 = (bf16[1,480,128]{2,1,0:T(8,128)(2,1)S(1)}, bf16[1,480,128]{2,1,0:T(8,128)(2,1)S(1)}, u32[]{:S(2)}, u32[]{:S(2)}) collective-permute-start(bf16[1,480,128]{2,1,0:T(8,128)(2,1)S(1)} %get-tuple-element.133), channel_id=1, source_target_pairs={{0,2},{1,3},{2,0},{3,1},{4,6},{5,7},{6,4},{7,5},{8,10},{9,11},{10,... | collective-permute-start | bytes 368648 | tf_op jit(solution)/shard_map/ppermute | solution.py:1159
  101.1 2.0 %shard_map.149 = (f32[1024,384]{1,0:T(8,128)}, f32[8,128]{1,0:T(8,128)S(1)}) custom-call(f32[1024,384]{1,0:T(8,128)S(1)} %get-tuple-element.83.hat_in_ref.hat_ref, f32[1024,128]{1,0:T(8,128)S(1)} %get-tuple-element.93.rstd_ref, f32[8,384]{1,0:T(8,128)S(1)} %get-tuple-element.91.refs_12_.vec_ref, f32[1024,384]{1,0:T(8,128)S(1)} %get-tuple-element.116.da1_ref, ...), custom_call_target="tpu_custom_call" | custom-call | flops 1000 | bytes 1000 | tf_op jit(solution)/shard_map/pallas_call | solution.py:882
  103.2 7.7 %collective-permute-done.22 = bf16[1,480,128]{2,1,0:T(8,128)(2,1)S(1)} collective-permute-done((bf16[1,480,128]{2,1,0:T(8,128)(2,1)S(1)}, bf16[1,480,128]{2,1,0:T(8,128)(2,1)S(1)}, u32[]{:S(2)}, u32[]{:S(2)}) %collective-permute-start.22) | collective-permute-done | bytes 122912 | tf_op jit(solution)/shard_map/ppermute | solution.py:1159
  111.2 1.6 %collective-permute-start.26 = (bf16[480,128]{1,0:T(8,128)(2,1)S(1)}, bf16[480,128]{1,0:T(8,128)(2,1)S(1)}, u32[]{:S(2)}, u32[]{:S(2)}) collective-permute-start(bf16[480,128]{1,0:T(8,128)(2,1)S(1)} %get-tuple-element.136), channel_id=1, source_target_pairs={{0,16},{8,24},{16,0},{24,8},{1,17},{9,25},{17,1},{25,9},{2,18},{10... | collective-permute-start | bytes 368648 | tf_op jit(solution)/shard_map/ppermute | solution.py:1159
  112.8 1.9 %collective-permute-start.27 = (bf16[480,128]{1,0:T(8,128)(2,1)S(1)}, bf16[480,128]{1,0:T(8,128)(2,1)S(1)}, u32[]{:S(2)}, u32[]{:S(2)}) collective-permute-start(bf16[480,128]{1,0:T(8,128)(2,1)S(1)} %get-tuple-element.137), channel_id=1, source_target_pairs={{0,24},{8,16},{16,8},{24,0},{1,25},{9,17},{17,9},{25,1},{2,26},{10... | collective-permute-start | bytes 368648 | tf_op jit(solution)/shard_map/ppermute | solution.py:1159
  114.7 2.4 %collective-permute-done.25.got0_ref = bf16[480,128]{1,0:T(8,128)(2,1)S(1)} collective-permute-done((bf16[480,128]{1,0:T(8,128)(2,1)S(1)}, bf16[480,128]{1,0:T(8,128)(2,1)S(1)}, u32[]{:S(2)}, u32[]{:S(2)}) %collective-permute-start.25) | collective-permute-done | bytes 122912 | tf_op jit(solution)/shard_map/ppermute | solution.py:1159
  118.2 1.8 %collective-permute-done.27.got2_ref = bf16[480,128]{1,0:T(8,128)(2,1)S(1)} collective-permute-done((bf16[480,128]{1,0:T(8,128)(2,1)S(1)}, bf16[480,128]{1,0:T(8,128)(2,1)S(1)}, u32[]{:S(2)}, u32[]{:S(2)}) %collective-permute-start.27) | collective-permute-done | bytes 122912 | tf_op jit(solution)/shard_map/ppermute | solution.py:1159
  120.0 1.6 %shard_map.153 = (f32[55368]{0:T(1024)}, f32[55368]{0:T(1024)}, f32[448,128]{1,0:T(8,128)S(1)}, f32[8,128]{1,0:T(8,128)S(1)}) custom-call(f32[480,128]{1,0:T(8,128)S(1)} %get-tuple-element.134.own_ref, bf16[480,128]{1,0:T(8,128)(2,1)S(1)} %collective-permute-done.25.got0_ref, bf16[480,128]{1,0:T(8,128)(2,1)S(1)} %collective-permute-done.26.got1_ref, ...), custom_call_target="tpu_custom_call" | custom-call | tf_op jit(solution)/shard_map/pallas_call | solution.py:970
  122.8 4.7 %collective-permute-start.30 = (f32[8,128]{1,0:T(8,128)S(1)}, f32[8,128]{1,0:T(8,128)S(1)}, u32[]{:S(2)}, u32[]{:S(2)}) collective-permute-start(f32[8,128]{1,0:T(8,128)S(1)} %shard_map.154.refs_0_), channel_id=1, source_target_pairs={{0,4},{1,5},{2,6},{3,7},{4,0},{5,1},{6,2},{7,3},{8,12},{9,13},{10,... | collective-permute-start | bytes 12296 | tf_op jit(solution)/shard_map/ppermute | solution.py:1159
  129.1 2.0 %collective-permute-done.29.refs_1_ = f32[8,128]{1,0:T(8,128)S(1)} collective-permute-done((f32[8,128]{1,0:T(8,128)S(1)}, f32[8,128]{1,0:T(8,128)S(1)}, u32[]{:S(2)}, u32[]{:S(2)}) %collective-permute-start.29) | collective-permute-done | bytes 4128 | tf_op jit(solution)/shard_map/ppermute | solution.py:1159
  131.1 1.8 %collective-permute-start.34 = (f32[8,128]{1,0:T(8,128)S(1)}, f32[8,128]{1,0:T(8,128)S(1)}, u32[]{:S(2)}, u32[]{:S(2)}) collective-permute-start(f32[8,128]{1,0:T(8,128)S(1)} %shard_map.155.refs_0_), channel_id=1, source_target_pairs={{0,24},{8,16},{16,8},{24,0},{1,25},{9,17},{17,9},{25,1},{2,26},{10... | collective-permute-start | bytes 12296 | tf_op jit(solution)/shard_map/ppermute | solution.py:1159
  133.1 1.4 %collective-permute-start.32 = (f32[8,128]{1,0:T(8,128)S(1)}, f32[8,128]{1,0:T(8,128)S(1)}, u32[]{:S(2)}, u32[]{:S(2)}) collective-permute-start(f32[8,128]{1,0:T(8,128)S(1)} %shard_map.155.refs_0_), channel_id=1, source_target_pairs={{0,8},{8,0},{16,24},{24,16},{1,9},{9,1},{17,25},{25,17},{2,10},{10... | collective-permute-start | bytes 12296 | tf_op jit(solution)/shard_map/ppermute | solution.py:1159
  (82 shorter events, 21.5 us)
Async XLA Ops:
  1.7 7.4 %collective-permute-start.3 = (bf16[112,128]{1,0:T(8,128)(2,1)S(1)}, bf16[112,128]{1,0:T(8,128)(2,1)S(1)}, u32[]{:S(2)}, u32[]{:S(2)}) collective-permute-start(bf16[112,128]{1,0:T(8,128)(2,1)S(1)} %get-tuple-element.77.refs_0_), channel_id=1, source_target_pairs={{0,8},{8,0},{16,24},{24,16},{1,9},{9,1},{17,25},{25,17},{2,10},{10... | collective-permute-start | bytes 86024 | tf_op jit(solution)/shard_map/ppermute | solution.py:1159
  4.7 8.7 %collective-permute-start.2 = (bf16[336,128]{1,0:T(8,128)(2,1)S(1)}, bf16[336,128]{1,0:T(8,128)(2,1)S(1)}, u32[]{:S(2)}, u32[]{:S(2)}) collective-permute-start(bf16[336,128]{1,0:T(8,128)(2,1)S(1)} %get-tuple-element.76.refs_0_), channel_id=1, source_target_pairs={{0,6},{1,7},{2,4},{3,5},{4,2},{5,3},{6,0},{7,1},{8,14},{9,15},{10,... | collective-permute-start | bytes 258056 | tf_op jit(solution)/shard_map/ppermute | solution.py:1159
  8.3 6.9 %collective-permute-start.1 = (bf16[336,128]{1,0:T(8,128)(2,1)S(1)}, bf16[336,128]{1,0:T(8,128)(2,1)S(1)}, u32[]{:S(2)}, u32[]{:S(2)}) collective-permute-start(bf16[336,128]{1,0:T(8,128)(2,1)S(1)} %get-tuple-element.76.refs_0_), channel_id=1, source_target_pairs={{0,4},{1,5},{2,6},{3,7},{4,0},{5,1},{6,2},{7,3},{8,12},{9,13},{10,... | collective-permute-start | bytes 258056 | tf_op jit(solution)/shard_map/ppermute | solution.py:1159
  8.3 6.9 %collective-permute-start = (bf16[336,128]{1,0:T(8,128)(2,1)S(1)}, bf16[336,128]{1,0:T(8,128)(2,1)S(1)}, u32[]{:S(2)}, u32[]{:S(2)}) collective-permute-start(bf16[336,128]{1,0:T(8,128)(2,1)S(1)} %get-tuple-element.76.refs_0_), channel_id=1, source_target_pairs={{0,2},{1,3},{2,0},{3,1},{4,6},{5,7},{6,4},{7,5},{8,10},{9,11},{10,... | collective-permute-start | bytes 258056 | tf_op jit(solution)/shard_map/ppermute | solution.py:1159
  9.1 4.2 %collective-permute-start.4 = (bf16[2,112,128]{2,1,0:T(8,128)(2,1)S(1)}, bf16[2,112,128]{2,1,0:T(8,128)(2,1)S(1)}, u32[]{:S(2)}, u32[]{:S(2)}) collective-permute-start(bf16[2,112,128]{2,1,0:T(8,128)(2,1)S(1)} %shard_map.136.mine_ref), channel_id=1, source_target_pairs={{0,16},{8,24},{16,0},{24,8},{1,17},{9,25},{17,1},{25,9},{2,18},{10... | collective-permute-start | bytes 172040 | tf_op jit(solution)/shard_map/ppermute | solution.py:1159
  15.3 17.1 %collective-permute-start.7 = (bf16[4,336,128]{2,1,0:T(8,128)(2,1)S(1)}, bf16[4,336,128]{2,1,0:T(8,128)(2,1)S(1)}, u32[]{:S(2)}, u32[]{:S(2)}) collective-permute-start(bf16[4,336,128]{2,1,0:T(8,128)(2,1)S(1)} %shard_map.139.refs_0_), channel_id=1, source_target_pairs={{0,24},{8,16},{16,8},{24,0},{1,25},{9,17},{17,9},{25,1},{2,26},{10... | collective-permute-start | bytes 1032200 | tf_op jit(solution)/shard_map/ppermute | solution.py:1159
  16.8 16.4 %collective-permute-start.6 = (bf16[4,336,128]{2,1,0:T(8,128)(2,1)S(1)}, bf16[4,336,128]{2,1,0:T(8,128)(2,1)S(1)}, u32[]{:S(2)}, u32[]{:S(2)}) collective-permute-start(bf16[4,336,128]{2,1,0:T(8,128)(2,1)S(1)} %shard_map.139.refs_0_), channel_id=1, source_target_pairs={{0,16},{8,24},{16,0},{24,8},{1,17},{9,25},{17,1},{25,9},{2,18},{10... | collective-permute-start | bytes 1032200 | tf_op jit(solution)/shard_map/ppermute | solution.py:1159
  17.3 16.0 %collective-permute-start.5 = (bf16[4,336,128]{2,1,0:T(8,128)(2,1)S(1)}, bf16[4,336,128]{2,1,0:T(8,128)(2,1)S(1)}, u32[]{:S(2)}, u32[]{:S(2)}) collective-permute-start(bf16[4,336,128]{2,1,0:T(8,128)(2,1)S(1)} %shard_map.139.refs_0_), channel_id=1, source_target_pairs={{0,8},{8,0},{16,24},{24,16},{1,9},{9,1},{17,25},{25,17},{2,10},{10... | collective-permute-start | bytes 1032200 | tf_op jit(solution)/shard_map/ppermute | solution.py:1159
  18.8 7.9 %collective-permute-start.10 = (bf16[4,112,128]{2,1,0:T(8,128)(2,1)S(1)}, bf16[4,112,128]{2,1,0:T(8,128)(2,1)S(1)}, u32[]{:S(2)}, u32[]{:S(2)}) collective-permute-start(bf16[4,112,128]{2,1,0:T(8,128)(2,1)S(1)} %shard_map.138.refs_4_.refs_0_), channel_id=1, source_target_pairs={{0,6},{1,7},{2,4},{3,5},{4,2},{5,3},{6,0},{7,1},{8,14},{9,15},{10,... | collective-permute-start | bytes 344072 | tf_op jit(solution)/shard_map/ppermute | solution.py:1159
  21.4 8.8 %collective-permute-start.9 = (bf16[4,112,128]{2,1,0:T(8,128)(2,1)S(1)}, bf16[4,112,128]{2,1,0:T(8,128)(2,1)S(1)}, u32[]{:S(2)}, u32[]{:S(2)}) collective-permute-start(bf16[4,112,128]{2,1,0:T(8,128)(2,1)S(1)} %shard_map.138.refs_4_.refs_0_), channel_id=1, source_target_pairs={{0,4},{1,5},{2,6},{3,7},{4,0},{5,1},{6,2},{7,3},{8,12},{9,13},{10,... | collective-permute-start | bytes 344072 | tf_op jit(solution)/shard_map/ppermute | solution.py:1159
  26.7 5.6 %collective-permute-start.8 = (bf16[4,112,128]{2,1,0:T(8,128)(2,1)S(1)}, bf16[4,112,128]{2,1,0:T(8,128)(2,1)S(1)}, u32[]{:S(2)}, u32[]{:S(2)}) collective-permute-start(bf16[4,112,128]{2,1,0:T(8,128)(2,1)S(1)} %shard_map.138.refs_4_.refs_0_), channel_id=1, source_target_pairs={{0,2},{1,3},{2,0},{3,1},{4,6},{5,7},{6,4},{7,5},{8,10},{9,11},{10,... | collective-permute-start | bytes 344072 | tf_op jit(solution)/shard_map/ppermute | solution.py:1159
  33.6 12.8 %collective-permute-start.11 = (bf16[4,448,128]{2,1,0:T(8,128)(2,1)S(1)}, bf16[4,448,128]{2,1,0:T(8,128)(2,1)S(1)}, u32[]{:S(2)}, u32[]{:S(2)}) collective-permute-start(bf16[4,448,128]{2,1,0:T(8,128)(2,1)S(1)} %get-tuple-element.79.refs_0_), channel_id=1, source_target_pairs={{0,1},{1,0},{2,3},{3,2},{4,5},{5,4},{6,7},{7,6},{8,9},{9,8},{10,11... | collective-permute-start | bytes 1376264 | tf_op jit(solution)/shard_map/ppermute | solution.py:1159
  34.1 12.3 %collective-permute-start.12 = (bf16[4,448,128]{2,1,0:T(8,128)(2,1)S(1)}, bf16[4,448,128]{2,1,0:T(8,128)(2,1)S(1)}, u32[]{:S(2)}, u32[]{:S(2)}) collective-permute-start(bf16[4,448,128]{2,1,0:T(8,128)(2,1)S(1)} %get-tuple-element.80.refs_1_), channel_id=1, source_target_pairs={{0,1},{1,0},{2,3},{3,2},{4,5},{5,4},{6,7},{7,6},{8,9},{9,8},{10,11... | collective-permute-start | bytes 1376264 | tf_op jit(solution)/shard_map/ppermute | solution.py:1159
  34.2 12.2 %collective-permute-start.13 = (bf16[4,448,128]{2,1,0:T(8,128)(2,1)S(1)}, bf16[4,448,128]{2,1,0:T(8,128)(2,1)S(1)}, u32[]{:S(2)}, u32[]{:S(2)}) collective-permute-start(bf16[4,448,128]{2,1,0:T(8,128)(2,1)S(1)} %get-tuple-element.81.refs_2_), channel_id=1, source_target_pairs={{0,1},{1,0},{2,3},{3,2},{4,5},{5,4},{6,7},{7,6},{8,9},{9,8},{10,11... | collective-permute-start | bytes 1376264 | tf_op jit(solution)/shard_map/ppermute | solution.py:1159
  64.1 4.5 %collective-permute-start.15 = (bf16[3,4,448,128]{3,2,1,0:T(8,128)(2,1)S(1)}, bf16[3,4,448,128]{3,2,1,0:T(8,128)(2,1)S(1)}, u32[]{:S(2)}, u32[]{:S(2)}) collective-permute-start(bf16[3,4,448,128]{3,2,1,0:T(8,128)(2,1)S(1)} %get-tuple-element.111), channel_id=1, source_target_pairs={{0,1},{1,0},{2,3},{3,2},{4,5},{5,4},{6,7},{7,6},{8,9},{9,8},{10,11... | collective-permute-start | bytes 4128776 | tf_op jit(solution)/shard_map/ppermute | solution.py:1159
  69.0 26.6 %collective-permute-start.16 = (bf16[3,1,448,128]{3,2,0,1:T(8,128)(2,1)S(1)}, bf16[3,1,448,128]{3,2,0,1:T(8,128)(2,1)S(1)}, u32[]{:S(2)}, u32[]{:S(2)}) collective-permute-start(bf16[3,1,448,128]{3,2,0,1:T(8,128)(2,1)S(1)} %bitcast.29), channel_id=1, source_target_pairs={{0,4},{1,5},{2,6},{3,7},{4,0},{5,1},{6,2},{7,3},{8,12},{9,13},{10,... | collective-permute-start | bytes 1032200 | tf_op jit(solution)/shard_map/ppermute | solution.py:1159
  69.5 33.7 %collective-permute-start.17 = (bf16[3,1,448,128]{3,2,0,1:T(8,128)(2,1)S(1)}, bf16[3,1,448,128]{3,2,0,1:T(8,128)(2,1)S(1)}, u32[]{:S(2)}, u32[]{:S(2)}) collective-permute-start(bf16[3,1,448,128]{3,2,0,1:T(8,128)(2,1)S(1)} %bitcast.28), channel_id=1, source_target_pairs={{0,6},{1,7},{2,4},{3,5},{4,2},{5,3},{6,0},{7,1},{8,14},{9,15},{10,... | collective-permute-start | bytes 1032200 | tf_op jit(solution)/shard_map/ppermute | solution.py:1159
  72.7 30.5 %collective-permute-start.18 = (bf16[3,1,448,128]{3,2,0,1:T(8,128)(2,1)S(1)}, bf16[3,1,448,128]{3,2,0,1:T(8,128)(2,1)S(1)}, u32[]{:S(2)}, u32[]{:S(2)}) collective-permute-start(bf16[3,1,448,128]{3,2,0,1:T(8,128)(2,1)S(1)} %bitcast.27), channel_id=1, source_target_pairs={{0,2},{1,3},{2,0},{3,1},{4,6},{5,7},{6,4},{7,5},{8,10},{9,11},{10,... | collective-permute-start | bytes 1032200 | tf_op jit(solution)/shard_map/ppermute | solution.py:1159
  85.4 10.2 %collective-permute-start.19 = (bf16[4,160,128]{2,1,0:T(8,128)(2,1)S(1)}, bf16[4,160,128]{2,1,0:T(8,128)(2,1)S(1)}, u32[]{:S(2)}, u32[]{:S(2)}) collective-permute-start(bf16[4,160,128]{2,1,0:T(8,128)(2,1)S(1)} %get-tuple-element.126), channel_id=1, source_target_pairs={{0,1},{1,0},{2,3},{3,2},{4,5},{5,4},{6,7},{7,6},{8,9},{9,8},{10,11... | collective-permute-start | bytes 491528 | tf_op jit(solution)/shard_map/ppermute | solution.py:1159
  87.3 8.4 %collective-permute-start.20 = (bf16[4,160,128]{2,1,0:T(8,128)(2,1)S(1)}, bf16[4,160,128]{2,1,0:T(8,128)(2,1)S(1)}, u32[]{:S(2)}, u32[]{:S(2)}) collective-permute-start(bf16[4,160,128]{2,1,0:T(8,128)(2,1)S(1)} %get-tuple-element.127), channel_id=1, source_target_pairs={{0,1},{1,0},{2,3},{3,2},{4,5},{5,4},{6,7},{7,6},{8,9},{9,8},{10,11... | collective-permute-start | bytes 491528 | tf_op jit(solution)/shard_map/ppermute | solution.py:1159
  97.6 13.2 %collective-permute-start.22 = (bf16[1,480,128]{2,1,0:T(8,128)(2,1)S(1)}, bf16[1,480,128]{2,1,0:T(8,128)(2,1)S(1)}, u32[]{:S(2)}, u32[]{:S(2)}) collective-permute-start(bf16[1,480,128]{2,1,0:T(8,128)(2,1)S(1)} %get-tuple-element.131), channel_id=1, source_target_pairs={{0,4},{1,5},{2,6},{3,7},{4,0},{5,1},{6,2},{7,3},{8,12},{9,13},{10,... | collective-permute-start | bytes 368648 | tf_op jit(solution)/shard_map/ppermute | solution.py:1159
  97.6 13.2 %collective-permute-start.23 = (bf16[1,480,128]{2,1,0:T(8,128)(2,1)S(1)}, bf16[1,480,128]{2,1,0:T(8,128)(2,1)S(1)}, u32[]{:S(2)}, u32[]{:S(2)}) collective-permute-start(bf16[1,480,128]{2,1,0:T(8,128)(2,1)S(1)} %get-tuple-element.132), channel_id=1, source_target_pairs={{0,6},{1,7},{2,4},{3,5},{4,2},{5,3},{6,0},{7,1},{8,14},{9,15},{10,... | collective-permute-start | bytes 368648 | tf_op jit(solution)/shard_map/ppermute | solution.py:1159
  98.3 12.5 %collective-permute-start.24 = (bf16[1,480,128]{2,1,0:T(8,128)(2,1)S(1)}, bf16[1,480,128]{2,1,0:T(8,128)(2,1)S(1)}, u32[]{:S(2)}, u32[]{:S(2)}) collective-permute-start(bf16[1,480,128]{2,1,0:T(8,128)(2,1)S(1)} %get-tuple-element.133), channel_id=1, source_target_pairs={{0,2},{1,3},{2,0},{3,1},{4,6},{5,7},{6,4},{7,5},{8,10},{9,11},{10,... | collective-permute-start | bytes 368648 | tf_op jit(solution)/shard_map/ppermute | solution.py:1159
  111.1 6.0 %collective-permute-start.25 = (bf16[480,128]{1,0:T(8,128)(2,1)S(1)}, bf16[480,128]{1,0:T(8,128)(2,1)S(1)}, u32[]{:S(2)}, u32[]{:S(2)}) collective-permute-start(bf16[480,128]{1,0:T(8,128)(2,1)S(1)} %get-tuple-element.135), channel_id=1, source_target_pairs={{0,8},{8,0},{16,24},{24,16},{1,9},{9,1},{17,25},{25,17},{2,10},{10... | collective-permute-start | bytes 368648 | tf_op jit(solution)/shard_map/ppermute | solution.py:1159
  111.2 7.0 %collective-permute-start.26 = (bf16[480,128]{1,0:T(8,128)(2,1)S(1)}, bf16[480,128]{1,0:T(8,128)(2,1)S(1)}, u32[]{:S(2)}, u32[]{:S(2)}) collective-permute-start(bf16[480,128]{1,0:T(8,128)(2,1)S(1)} %get-tuple-element.136), channel_id=1, source_target_pairs={{0,16},{8,24},{16,0},{24,8},{1,17},{9,25},{17,1},{25,9},{2,18},{10... | collective-permute-start | bytes 368648 | tf_op jit(solution)/shard_map/ppermute | solution.py:1159
  112.8 7.2 %collective-permute-start.27 = (bf16[480,128]{1,0:T(8,128)(2,1)S(1)}, bf16[480,128]{1,0:T(8,128)(2,1)S(1)}, u32[]{:S(2)}, u32[]{:S(2)}) collective-permute-start(bf16[480,128]{1,0:T(8,128)(2,1)S(1)} %get-tuple-element.137), channel_id=1, source_target_pairs={{0,24},{8,16},{16,8},{24,0},{1,25},{9,17},{17,9},{25,1},{2,26},{10... | collective-permute-start | bytes 368648 | tf_op jit(solution)/shard_map/ppermute | solution.py:1159
  122.8 5.4 %collective-permute-start.31 = (f32[8,128]{1,0:T(8,128)S(1)}, f32[8,128]{1,0:T(8,128)S(1)}, u32[]{:S(2)}, u32[]{:S(2)}) collective-permute-start(f32[8,128]{1,0:T(8,128)S(1)} %shard_map.154.refs_0_), channel_id=1, source_target_pairs={{0,6},{1,7},{2,4},{3,5},{4,2},{5,3},{6,0},{7,1},{8,14},{9,15},{10,... | collective-permute-start | bytes 12296 | tf_op jit(solution)/shard_map/ppermute | solution.py:1159
  122.8 6.3 %collective-permute-start.30 = (f32[8,128]{1,0:T(8,128)S(1)}, f32[8,128]{1,0:T(8,128)S(1)}, u32[]{:S(2)}, u32[]{:S(2)}) collective-permute-start(f32[8,128]{1,0:T(8,128)S(1)} %shard_map.154.refs_0_), channel_id=1, source_target_pairs={{0,4},{1,5},{2,6},{3,7},{4,0},{5,1},{6,2},{7,3},{8,12},{9,13},{10,... | collective-permute-start | bytes 12296 | tf_op jit(solution)/shard_map/ppermute | solution.py:1159
  127.5 3.6 %collective-permute-start.29 = (f32[8,128]{1,0:T(8,128)S(1)}, f32[8,128]{1,0:T(8,128)S(1)}, u32[]{:S(2)}, u32[]{:S(2)}) collective-permute-start(f32[8,128]{1,0:T(8,128)S(1)} %shard_map.154.refs_0_), channel_id=1, source_target_pairs={{0,2},{1,3},{2,0},{3,1},{4,6},{5,7},{6,4},{7,5},{8,10},{9,11},{10,... | collective-permute-start | bytes 12296 | tf_op jit(solution)/shard_map/ppermute | solution.py:1159
  131.1 4.5 %collective-permute-start.34 = (f32[8,128]{1,0:T(8,128)S(1)}, f32[8,128]{1,0:T(8,128)S(1)}, u32[]{:S(2)}, u32[]{:S(2)}) collective-permute-start(f32[8,128]{1,0:T(8,128)S(1)} %shard_map.155.refs_0_), channel_id=1, source_target_pairs={{0,24},{8,16},{16,8},{24,0},{1,25},{9,17},{17,9},{25,1},{2,26},{10... | collective-permute-start | bytes 12296 | tf_op jit(solution)/shard_map/ppermute | solution.py:1159
  132.8 3.6 %collective-permute-start.33 = (f32[8,128]{1,0:T(8,128)S(1)}, f32[8,128]{1,0:T(8,128)S(1)}, u32[]{:S(2)}, u32[]{:S(2)}) collective-permute-start(f32[8,128]{1,0:T(8,128)S(1)} %shard_map.155.refs_0_), channel_id=1, source_target_pairs={{0,16},{8,24},{16,0},{24,8},{1,17},{9,25},{17,1},{25,9},{2,18},{10... | collective-permute-start | bytes 12296 | tf_op jit(solution)/shard_map/ppermute | solution.py:1159
  133.1 3.6 %collective-permute-start.32 = (f32[8,128]{1,0:T(8,128)S(1)}, f32[8,128]{1,0:T(8,128)S(1)}, u32[]{:S(2)}, u32[]{:S(2)}) collective-permute-start(f32[8,128]{1,0:T(8,128)S(1)} %shard_map.155.refs_0_), channel_id=1, source_target_pairs={{0,8},{8,0},{16,24},{24,16},{1,9},{9,1},{17,25},{25,17},{2,10},{10... | collective-permute-start | bytes 12296 | tf_op jit(solution)/shard_map/ppermute | solution.py:1159
  (14 other events, 90.9 us)

commit v7 on v6

--- a/solution.py
+++ b/solution.py
@@ -41,6 +41,7 @@
 ROW_DOWN = BOUNDS[3] // LANES
 ROW_VEC = BOUNDS[4] // LANES
 VEC_ROWS = 6 * D // LANES
+EARLY_VEC_ROWS = 4 * D // LANES
 ROWS_ALL = PARAMS // LANES
 
 score_scale = HD ** (-0.5) * math.log2(math.e)
@@ -74,7 +75,11 @@
             -(-((k + 1) * shard) // LANES) - self.start[k] for k in range(self.n)
         ]
         self.win = round_up(max(self.rows) + 1, 16)
-        self.tail = round_up(self.win + VEC_ROWS, 16 * FAR_PARTS)
+        self.most = max(self.rows)
+        self.tail = round_up(self.most + EARLY_VEC_ROWS, 16)
+        units = self.tail // 16
+        ends = [units * (i + 1) // FAR_PARTS * 16 for i in range(FAR_PARTS)]
+        self.far = list(zip([0] + ends[:-1], ends))
         self.upper = self.win * 3 // 4 // 16 * 16
         self.vec_place = ROW_VEC - self.start[-1]
         self.vec_from = self.vec_place // 16 * 16
@@ -581,6 +586,11 @@
             flat[
                 pl.ds(ROW_DOWN - base + i * block * (D // LANES) + j, block, stride=D // LANES), :
             ] = part[:, j * LANES : (j + 1) * LANES]
+    flat[ROW_VEC - base :, :] = jnp.zeros((flat.shape[0] - ROW_VEC + base, LANES), F32)
+    for t in range(2):
+        for j in range(D // LANES):
+            row = ROW_VEC - base + EARLY_VEC_ROWS + t * (D // LANES) + j
+            flat[row : row + 1, :] = gvec_ref[t : t + 1, j * LANES : (j + 1) * LANES]
     tail_ref[...] = flat[0:8, :]
     side = jnp.bitwise_and(dp, 1)
     for k in range(plan.nd, plan.n):
@@ -805,7 +815,6 @@
     normed_ref,
     wq_ref,
     tail_ref,
-    gvec_ref,
     low_ref,
     gqk_ref,
     da1_ref,
@@ -826,22 +835,23 @@
     gains[0:1, :] = jnp.sum(da1 * hat, axis=0, keepdims=True)
     gains[1:2, :] = jnp.sum(da1, axis=0, keepdims=True)
     gains[2:4, :] = gqk_ref[0:2, :]
-    gains[4:6, :] = gvec_ref[0:2, :]
     flat[ROW_OUT : ROW_OUT + 8, :] = tail_ref[...]
     dp = lax.axis_index("dp")
     side = jnp.bitwise_and(dp, 1)
-    rest = jnp.zeros((plan.tail - plan.win, LANES), BF)
     vector_rows = []
-    for t in range(6):
+    for t in range(4):
         for j in range(D // LANES):
             vector_rows.append(gains[t : t + 1, j * LANES : (j + 1) * LANES])
-    vector_rows.append(jnp.zeros((plan.tail - plan.win - VEC_ROWS, LANES), F32))
-    vectors = jnp.concatenate(vector_rows, axis=0).astype(BF)
+    spare = plan.tail - plan.most - EARLY_VEC_ROWS
+    if spare:
+        vector_rows.append(jnp.zeros((spare, LANES), F32))
     for k in range(plan.nd):
         first = plan.start[k]
         reld = jnp.right_shift(jnp.bitwise_xor(dp, k), 1)
-        window = flat[first : first + plan.win, :].astype(BF)
-        window = jnp.concatenate([window, vectors if k == plan.nd - 1 else rest], axis=0)
+        window = flat[first : first + plan.tail, :]
+        if k == plan.nd - 1:
+            window = jnp.concatenate([window[: plan.most], *vector_rows], axis=0)
+        window = window.astype(BF)
 
         @pl.when(side == k % 2)
         def _():
@@ -849,27 +859,28 @@
 
         @pl.when(side != k % 2)
         def _():
-            height = plan.tail // FAR_PARTS
-            for i, far_ref in enumerate(far_refs):
-                far_ref[reld] = window[i * height : (i + 1) * height]
-
-
-def finish_part(plan, hat, normed, wq, tail, gvec, low, gains):
+            for (low, high), far_ref in zip(plan.far, far_refs):
+                far_ref[reld] = window[low:high]
+
+
+def finish_part(plan, hat, normed, wq, tail, low, gains):
     rows = hat.shape[0]
     windows = jax.ShapeDtypeStruct((plan.nd // 2, plan.tail, LANES), BF)
-    part = jax.ShapeDtypeStruct((plan.nd // 2, plan.tail // FAR_PARTS, LANES), BF)
+    parts = tuple(
+        jax.ShapeDtypeStruct((plan.nd // 2, high - low, LANES), BF) for low, high in plan.far
+    )
     return pl.pallas_call(
         functools.partial(finish_kernel, plan),
-        out_shape=(jax.ShapeDtypeStruct((rows, D), F32), windows) + (part,) * FAR_PARTS,
-        in_specs=[VMEM] * 7,
+        out_shape=(jax.ShapeDtypeStruct((rows, D), F32), windows) + parts,
+        in_specs=[VMEM] * 6,
         out_specs=(VMEM,) * (2 + FAR_PARTS),
         scratch_shapes=[
             pltpu.VMEM((8, D), F32),
-            pltpu.VMEM((round_up(plan.start[plan.nd - 1] + plan.win, 8), LANES), F32),
+            pltpu.VMEM((round_up(plan.start[plan.nd - 1] + plan.tail, 8), LANES), F32),
         ],
         compiler_params=params(28),
         cost_estimate=QUICK,
-    )(hat, normed, wq, tail, gvec, low, gains)
+    )(hat, normed, wq, tail, low, gains)
 
 
 def input_kernel(hat_ref, rstd_ref, vec_ref, da1_ref, dh1_ref, grad_ref, token_ref):
@@ -924,8 +935,8 @@
 
     @pl.when(jnp.logical_and(bucket == plan.nb - 1, dp == plan.nd - 1))
     def _():
-        window[plan.vec_place : plan.vec_place + VEC_ROWS, :] = total[
-            plan.win : plan.win + VEC_ROWS
+        window[plan.vec_place : plan.vec_place + EARLY_VEC_ROWS, :] = total[
+            plan.most : plan.most + EARLY_VEC_ROWS
         ]
 
     offset = lax.rem(plan.device() * plan.shard, LANES)
@@ -1113,8 +1124,12 @@
         window = late[0][quarter]
         if late_count > 1:
             window = window + tree_sum([ref[quarter].astype(F32) for ref in late[1:]])
-        out[: plan.win] = jnp.where(owner == 0, first[: plan.win], window).astype(out.dtype)
-        out[plan.win :] = first[plan.win :].astype(out.dtype)
+        if plan.tail > plan.win:
+            empty = jnp.zeros((plan.tail - plan.win, LANES), F32)
+            window = jnp.concatenate([window, empty], axis=0)
+        row = lax.broadcasted_iota(jnp.int32, first.shape, 0)
+        takes_first = jnp.logical_or(row >= plan.most, owner == 0)
+        out[...] = jnp.where(takes_first, first, window).astype(out.dtype)
 
 
 def blend(plan, late, token, parts):
@@ -1226,7 +1241,7 @@
     early, late = gather_windows(plan, *prepare(plan, master), count)
     wq, vec, head, kept, q, k, v, hat, rstd = project_part(plan, *early, hat_in)
     o, ot, whole, lse, kab, segk = forward(plan, segment_ids, seg_row, keep_row, q, k, v)
-    block_output, dh1, do, near, far, tail, gvec = middle_part(
+    block_output, dh1, do, near, far, tail, _ = middle_part(
         plan, late, tokens, cotangent, o, ot, head, kept, vec, keep_row, bucket_patches
     )
     *stacks, normed, token = stack_part(vec, hat_in, q, k, v, do, whole)
@@ -1235,16 +1250,15 @@
     low, gains = backward(
         plan, vec, segment_ids, seg_row, lse, q, do, hat, rstd, segk, [kab, *stacks], token
     )
-    da1, near, *far = finish_part(plan, hat_in, normed, wq, tail, gvec, low, gains)
+    da1, near, *far = finish_part(plan, hat_in, normed, wq, tail, low, gains)
     input_grad, given = input_part(hat_in, rstd_in, vec, da1, dh1)
     *late_parts, token = add_parts(rest[:2], 1, gains)
     late_parts += rest[2:]
     *pieces, _ = add_parts([near, [swap(half, "dp", plan.nd, 1) for half in far]], pieces_of, token)
     first = scatter_dp(plan, pieces)
     mine, *sent = blend(plan, late_parts, given, first)
-    parts = [mine] + [
-        swap(x, "bucket", plan.nb, mask) for x, mask in zip(sent, masks_of(b_bits))
-    ]
+    sent = list(zip(sent, masks_of(b_bits)))
+    parts = [mine] + [swap(x, "bucket", plan.nb, mask) for x, mask in sent[::-1]]
     new_first, new_second, update_rows, sums = update_part(
         plan, parts, master, first_moment, second_moment
     )

time: 138 us -> 136 us (0.986)
  Pallas kernels: 49.4 us -> 53.2 us
  starting transfers between devices: 41.7 us -> 38.3 us
  waiting for transfers between devices: 42.9 us -> 40.3 us
    ppermute x35, starting transfers between devices: 41.7 us -> 38.3 us  [swap(): return lax.ppermute(x, axis, [(i, i ^ mask) for i in range(size)])]
    ppermute x35, waiting for transfers between devices: 42.9 us -> 40.3 us  [swap(): return lax.ppermute(x, axis, [(i, i ^ mask) for i in range(size)])]
    pallas_call x1, Pallas kernels: 9.8 us -> 12 us  [backward(): pl.pallas_call(functools.partial(backward_kernel, plan), out_shape=(jax.S...]
    pallas_call x1, Pallas kernels: 7.11 us -> 8.71 us  [forward(): pl.pallas_call(functools.partial(forward_kernel, plan), out_shape=(jax.Sh...]
  transfers between devices with their start and end apart: 35 -> 35, of which waited for: 22 -> 22; matrix products, arithmetic and copies ran while one was open for 0% -> 0% of each run, Pallas kernels for 21% -> 24%
where the time goes in v7:
time: 136 us
  Pallas kernels  53.2 us (39%)
  waiting for transfers between devices  40.3 us (30%)
  starting transfers between devices  38.3 us (28%)
  local copies, waits for them, and re-layouts  2.79 us (2%)
    ppermute x35, waiting for transfers between devices, swap(): return lax.ppermute(x, axis, [(i, i ^ mask) for i in range(size)])  40.3 us
    ppermute x35, starting transfers between devices, swap(): return lax.ppermute(x, axis, [(i, i ^ mask) for i in range(size)])  38.3 us
    pallas_call x1, Pallas kernels, middle_part(): pl.pallas_call(functools.partial(middle_kernel, plan), out_shape=(jax.Sha...  17.6 us
    pallas_call x1, Pallas kernels, backward(): pl.pallas_call(functools.partial(backward_kernel, plan), out_shape=(jax.S...  12 us
    pallas_call x1, Pallas kernels, forward(): pl.pallas_call(functools.partial(forward_kernel, plan), out_shape=(jax.Sh...  8.71 us
    pallas_call x1, Pallas kernels, project_part(): pl.pallas_call(functools.partial(project_kernel, plan), out_shape=(jax.Sh...  3.72 us
    pallas_call x1, Pallas kernels, finish_part(): pl.pallas_call(functools.partial(finish_kernel, plan), out_shape=(jax.Sha...  2.9 us
    unnamed x22, local copies, waits for them, and re-layouts  2.79 us
  transfers between devices with their start and end apart: 35, of which 22 were waited for; matrix products, arithmetic and copies ran while one was open for 0% of the time, Pallas kernels for 24%

profile of v7, /device:TPU:0, one launch (start us, length us, event | category | flops | bytes accessed | tf_op | source)
XLA Modules:
  0.0 135.5 jit_solution(7880588444597118546)
XLA Ops:
  1.7 3.0 %collective-permute-start.3 = (bf16[112,128]{1,0:T(8,128)(2,1)S(1)}, bf16[112,128]{1,0:T(8,128)(2,1)S(1)}, u32[]{:S(2)}, u32[]{:S(2)}) collective-permute-start(bf16[112,128]{1,0:T(8,128)(2,1)S(1)} %get-tuple-element.76.refs_0_), channel_id=1, source_target_pairs={{0,8},{8,0},{16,24},{24,16},{1,9},{9,1},{17,25},{25,17},{2,10},{10... | collective-permute-start | bytes 86024 | tf_op jit(solution)/shard_map/ppermute | solution.py:1174
  4.7 3.6 %collective-permute-start.2 = (bf16[336,128]{1,0:T(8,128)(2,1)S(1)}, bf16[336,128]{1,0:T(8,128)(2,1)S(1)}, u32[]{:S(2)}, u32[]{:S(2)}) collective-permute-start(bf16[336,128]{1,0:T(8,128)(2,1)S(1)} %get-tuple-element.75.refs_0_), channel_id=1, source_target_pairs={{0,6},{1,7},{2,4},{3,5},{4,2},{5,3},{6,0},{7,1},{8,14},{9,15},{10,... | collective-permute-start | bytes 258056 | tf_op jit(solution)/shard_map/ppermute | solution.py:1174
  9.1 1.6 %collective-permute-start.4 = (bf16[2,112,128]{2,1,0:T(8,128)(2,1)S(1)}, bf16[2,112,128]{2,1,0:T(8,128)(2,1)S(1)}, u32[]{:S(2)}, u32[]{:S(2)}) collective-permute-start(bf16[2,112,128]{2,1,0:T(8,128)(2,1)S(1)} %shard_map.136.mine_ref), channel_id=1, source_target_pairs={{0,16},{8,24},{16,0},{24,8},{1,17},{9,25},{17,1},{25,9},{2,18},{10... | collective-permute-start | bytes 172040 | tf_op jit(solution)/shard_map/ppermute | solution.py:1174
  13.4 1.9 %collective-permute-done.1.refs_2_ = bf16[336,128]{1,0:T(8,128)(2,1)S(1)} collective-permute-done((bf16[336,128]{1,0:T(8,128)(2,1)S(1)}, bf16[336,128]{1,0:T(8,128)(2,1)S(1)}, u32[]{:S(2)}, u32[]{:S(2)}) %collective-permute-start.1) | collective-permute-done | bytes 86048 | tf_op jit(solution)/shard_map/ppermute | solution.py:1174
  15.3 1.6 %collective-permute-start.7 = (bf16[4,336,128]{2,1,0:T(8,128)(2,1)S(1)}, bf16[4,336,128]{2,1,0:T(8,128)(2,1)S(1)}, u32[]{:S(2)}, u32[]{:S(2)}) collective-permute-start(bf16[4,336,128]{2,1,0:T(8,128)(2,1)S(1)} %shard_map.139.refs_0_), channel_id=1, source_target_pairs={{0,24},{8,16},{16,8},{24,0},{1,25},{9,17},{17,9},{25,1},{2,26},{10... | collective-permute-start | bytes 1032200 | tf_op jit(solution)/shard_map/ppermute | solution.py:1174
  17.3 1.5 %collective-permute-start.5 = (bf16[4,336,128]{2,1,0:T(8,128)(2,1)S(1)}, bf16[4,336,128]{2,1,0:T(8,128)(2,1)S(1)}, u32[]{:S(2)}, u32[]{:S(2)}) collective-permute-start(bf16[4,336,128]{2,1,0:T(8,128)(2,1)S(1)} %shard_map.139.refs_0_), channel_id=1, source_target_pairs={{0,8},{8,0},{16,24},{24,16},{1,9},{9,1},{17,25},{25,17},{2,10},{10... | collective-permute-start | bytes 1032200 | tf_op jit(solution)/shard_map/ppermute | solution.py:1174
  18.8 2.6 %collective-permute-start.10 = (bf16[4,112,128]{2,1,0:T(8,128)(2,1)S(1)}, bf16[4,112,128]{2,1,0:T(8,128)(2,1)S(1)}, u32[]{:S(2)}, u32[]{:S(2)}) collective-permute-start(bf16[4,112,128]{2,1,0:T(8,128)(2,1)S(1)} %shard_map.138.refs_4_.refs_0_), channel_id=1, source_target_pairs={{0,6},{1,7},{2,4},{3,5},{4,2},{5,3},{6,0},{7,1},{8,14},{9,15},{10,... | collective-permute-start | bytes 344072 | tf_op jit(solution)/shard_map/ppermute | solution.py:1174
  21.4 5.3 %collective-permute-done.10.refs_3_ = bf16[4,112,128]{2,1,0:T(8,128)(2,1)S(1)} collective-permute-done((bf16[4,112,128]{2,1,0:T(8,128)(2,1)S(1)}, bf16[4,112,128]{2,1,0:T(8,128)(2,1)S(1)}, u32[]{:S(2)}, u32[]{:S(2)}) %collective-permute-start.10) | collective-permute-done | bytes 114720 | tf_op jit(solution)/shard_map/ppermute | solution.py:1174
  26.7 2.9 %collective-permute-start.8 = (bf16[4,112,128]{2,1,0:T(8,128)(2,1)S(1)}, bf16[4,112,128]{2,1,0:T(8,128)(2,1)S(1)}, u32[]{:S(2)}, u32[]{:S(2)}) collective-permute-start(bf16[4,112,128]{2,1,0:T(8,128)(2,1)S(1)} %shard_map.138.refs_4_.refs_0_), channel_id=1, source_target_pairs={{0,2},{1,3},{2,0},{3,1},{4,6},{5,7},{6,4},{7,5},{8,10},{9,11},{10,... | collective-permute-start | bytes 344072 | tf_op jit(solution)/shard_map/ppermute | solution.py:1174
  30.2 2.1 %collective-permute-done.8.refs_1_ = bf16[4,112,128]{2,1,0:T(8,128)(2,1)S(1)} collective-permute-done((bf16[4,112,128]{2,1,0:T(8,128)(2,1)S(1)}, bf16[4,112,128]{2,1,0:T(8,128)(2,1)S(1)}, u32[]{:S(2)}, u32[]{:S(2)}) %collective-permute-start.8) | collective-permute-done | bytes 114720 | tf_op jit(solution)/shard_map/ppermute | solution.py:1174
  35.5 3.7 %shard_map.142 = (bf16[384,1152]{1,0:T(8,128)(2,1)S(1)}, f32[8,384]{1,0:T(8,128)S(1)}, f32[8,128]{1,0:T(8,128)S(1)}, f32[8,128]{1,0:T(8,128)S(1)}, bf16[1024,384...) custom-call(bf16[4,512,128]{2,1,0:T(8,128)(2,1)S(1)} %get-tuple-elem, ...), custom_call_target="tpu_custom_call" | custom-call | flops 1000 | bytes 1000 | tf_op jit(solution)/shard_map/pallas_call | solution.py:360
  39.3 8.7 %shard_map.143 = (bf16[1024,384]{1,0:T(8,128)(2,1)S(1)}, bf16[4,384,256]{2,1,0:T(8,128)(2,1)S(1)}, f32[4,384,256]{2,1,0:T(8,128)S(1)}, f32[4,8,256]{2,1,0:T(8,12...) custom-call(s32[1024]{0:T(1024)S(1)} %copy-done.7, s32[1,1024]{1,0:T(1,128)S(1)} %bitcast.22, ...), custom_call_target="tpu_custom_call" | custom-call | flops 1000 | bytes 1000 | tf_op jit(solution)/shard_map/pallas_call | solution.py:458
  48.1 17.6 %shard_map.144 = (bf16[1024,384]{1,0:T(8,128)(2,1)}, f32[1024,384]{1,0:T(8,128)S(1)}, bf16[1024,384]{1,0:T(8,128)(2,1)S(1)}, bf16[3,4,448,128]{3,2,1,0:T(8,128)(...) custom-call(bf16[4,448,128]{2,1,0:T(8,128)(2,1)S(1)} %get-tuple-element.78.refs_0_, ...), custom_call_target="tpu_custom_call" | custom-call | flops 1000 | bytes 1000 | tf_op jit(solution)/shard_map/pallas_call | solution.py:614
  65.9 1.5 %shard_map.145 = (bf16[3,8,2,128,128]{4,3,2,1,0:T(8,128)(2,1)S(1)}, bf16[3,4,512,128]{3,2,1,0:T(8,128)(2,1)S(1)}, bf16[3,4,512,128]{3,2,1,0:T(8,128)(2,1)S(1)}, ...) custom-call(f32[8,384]{1,0:T(8,128)S(1)} %get-tuple-element.90.refs_, ...), custom_call_target="tpu_custom_call" | custom-call | flops 1000 | bytes 1000 | tf_op jit(solution)/shard_map/pallas_call | solution.py:678
  67.4 1.5 %collective-permute-done.15.refs_1_ = bf16[3,4,448,128]{3,2,1,0:T(8,128)(2,1)S(1)} collective-permute-done((bf16[3,4,448,128]{3,2,1,0:T(8,128)(2,1)S(1)}, bf16[3,4,448,128]{3,2,1,0:T(8,128)(2,1)S(1)}, u32[]{:S(2)}, u32[]{:S(2)}) %collective-permute-start.15) | collective-permute-done | bytes 1376288 | tf_op jit(solution)/shard_map/ppermute | solution.py:1174
  69.5 3.2 %collective-permute-start.17 = (bf16[3,1,448,128]{3,2,0,1:T(8,128)(2,1)S(1)}, bf16[3,1,448,128]{3,2,0,1:T(8,128)(2,1)S(1)}, u32[]{:S(2)}, u32[]{:S(2)}) collective-permute-start(bf16[3,1,448,128]{3,2,0,1:T(8,128)(2,1)S(1)} %bitcast.28), channel_id=1, source_target_pairs={{0,6},{1,7},{2,4},{3,5},{4,2},{5,3},{6,0},{7,1},{8,14},{9,15},{10,... | collective-permute-start | bytes 1032200 | tf_op jit(solution)/shard_map/ppermute | solution.py:1174
  72.7 12.0 %shard_map.147 = (bf16[1024,1152]{1,0:T(8,128)(2,1)S(1)}, f32[8,384]{1,0:T(8,128)S(1)}) custom-call(f32[8,384]{1,0:T(8,128)S(1)} %get-tuple-element.90.refs_12_.vec_ref, s32[1024]{0:T(1024)S(1)} %copy-done.7, s32[1,1024]{1,0:T(1,128)S(1)} %bitcast.23, f32[4,8,256]{2,1,0:T(8,128)S(1)} %get-tuple-element.98.lse_ref, ...), custom_call_target="tpu_custom_call" | custom-call | flops 1000 | bytes 1000 | tf_op jit(solution)/shard_map/pallas_call | solution.py:794
  84.7 2.9 %shard_map.148 = (f32[1024,384]{1,0:T(8,128)S(1)}, bf16[4,448,128]{2,1,0:T(8,128)(2,1)S(1)}, bf16[4,144,128]{2,1,0:T(8,128)(2,1)S(1)}, bf16[4,144,128]{2,1,0:T(8,128)(2,1)S(1)}, bf16[4,160,128]{2,1,0:T(8,128)(2,1)S(1)}) custom-call(f32[1024,384]{1,0:T(8,128)S(1)} %get-tuple-element.82.hat_in_ref.hat_ref, bf16[384,1024]{1,0:T(8,128)(2,1)S(1)} %get-tuple-element.95.normed_ref, ...), custom_call_target="tpu_custom_call" | custom-call | flops 1000 | bytes 1000 | tf_op jit(solution)/shard_map/pallas_call | solution.py:872
  88.2 7.5 %collective-permute-done.16 = bf16[3,1,448,128]{3,2,0,1:T(8,128)(2,1)S(1)} collective-permute-done((bf16[3,1,448,128]{3,2,0,1:T(8,128)(2,1)S(1)}, bf16[3,1,448,128]{3,2,0,1:T(8,128)(2,1)S(1)}, u32[]{:S(2)}, u32[]{:S(2)}) %collective-permute-start.16) | collective-permute-done | bytes 344096 | tf_op jit(solution)/shard_map/ppermute | solution.py:1174
  95.8 1.3 collective-permute-done.20.refs_2_
  98.3 2.9 %collective-permute-start.24 = (bf16[1,448,128]{2,1,0:T(8,128)(2,1)S(1)}, bf16[1,448,128]{2,1,0:T(8,128)(2,1)S(1)}, u32[]{:S(2)}, u32[]{:S(2)}) collective-permute-start(bf16[1,448,128]{2,1,0:T(8,128)(2,1)S(1)} %get-tuple-element.131), channel_id=1, source_target_pairs={{0,2},{1,3},{2,0},{3,1},{4,6},{5,7},{6,4},{7,5},{8,10},{9,11},{10,... | collective-permute-start | bytes 344072 | tf_op jit(solution)/shard_map/ppermute | solution.py:1174
  101.2 2.0 %shard_map.149 = (f32[1024,384]{1,0:T(8,128)}, f32[8,128]{1,0:T(8,128)S(1)}) custom-call(f32[1024,384]{1,0:T(8,128)S(1)} %get-tuple-element.82.hat_in_ref.hat_ref, f32[1024,128]{1,0:T(8,128)S(1)} %get-tuple-element.92.rstd_ref, f32[8,384]{1,0:T(8,128)S(1)} %get-tuple-element.90.refs_12_.vec_ref, f32[1024,384]{1,0:T(8,128)S(1)} %get-tuple-element.114.da1_ref, ...), custom_call_target="tpu_custom_call" | custom-call | flops 1000 | bytes 1000 | tf_op jit(solution)/shard_map/pallas_call | solution.py:893
  103.3 7.2 %collective-permute-done.22 = bf16[1,448,128]{2,1,0:T(8,128)(2,1)S(1)} collective-permute-done((bf16[1,448,128]{2,1,0:T(8,128)(2,1)S(1)}, bf16[1,448,128]{2,1,0:T(8,128)(2,1)S(1)}, u32[]{:S(2)}, u32[]{:S(2)}) %collective-permute-start.22) | collective-permute-done | bytes 114720 | tf_op jit(solution)/shard_map/ppermute | solution.py:1174
  110.7 2.0 %collective-permute-start.26 = (bf16[448,128]{1,0:T(8,128)(2,1)S(1)}, bf16[448,128]{1,0:T(8,128)(2,1)S(1)}, u32[]{:S(2)}, u32[]{:S(2)}) collective-permute-start(bf16[448,128]{1,0:T(8,128)(2,1)S(1)} %get-tuple-element.134), channel_id=1, source_target_pairs={{0,16},{8,24},{16,0},{24,8},{1,17},{9,25},{17,1},{25,9},{2,18},{10... | collective-permute-start | bytes 344072 | tf_op jit(solution)/shard_map/ppermute | solution.py:1174
  112.7 1.5 %collective-permute-start.27 = (bf16[448,128]{1,0:T(8,128)(2,1)S(1)}, bf16[448,128]{1,0:T(8,128)(2,1)S(1)}, u32[]{:S(2)}, u32[]{:S(2)}) collective-permute-start(bf16[448,128]{1,0:T(8,128)(2,1)S(1)} %get-tuple-element.135), channel_id=1, source_target_pairs={{0,8},{8,0},{16,24},{24,16},{1,9},{9,1},{17,25},{25,17},{2,10},{10... | collective-permute-start | bytes 344072 | tf_op jit(solution)/shard_map/ppermute | solution.py:1174
  114.2 2.7 %collective-permute-done.25.got0_ref = bf16[448,128]{1,0:T(8,128)(2,1)S(1)} collective-permute-done((bf16[448,128]{1,0:T(8,128)(2,1)S(1)}, bf16[448,128]{1,0:T(8,128)(2,1)S(1)}, u32[]{:S(2)}, u32[]{:S(2)}) %collective-permute-start.25) | collective-permute-done | bytes 114720 | tf_op jit(solution)/shard_map/ppermute | solution.py:1174
  117.6 1.6 %shard_map.153 = (f32[55368]{0:T(1024)}, f32[55368]{0:T(1024)}, f32[448,128]{1,0:T(8,128)S(1)}, f32[8,128]{1,0:T(8,128)S(1)}) custom-call(f32[448,128]{1,0:T(8,128)S(1)} %get-tuple-element.132.own_ref, bf16[448,128]{1,0:T(8,128)(2,1)S(1)} %collective-permute-done.25.got0_ref, bf16[448,128]{1,0:T(8,128)(2,1)S(1)} %collective-permute-done.26.got1_ref, ...), custom_call_target="tpu_custom_call" | custom-call | tf_op jit(solution)/shard_map/pallas_call | solution.py:981
  119.3 1.2 collective-permute-done.28.refs_1_
  121.3 3.7 %collective-permute-start.30 = (f32[8,128]{1,0:T(8,128)S(1)}, f32[8,128]{1,0:T(8,128)S(1)}, u32[]{:S(2)}, u32[]{:S(2)}) collective-permute-start(f32[8,128]{1,0:T(8,128)S(1)} %shard_map.154.refs_0_), channel_id=1, source_target_pairs={{0,4},{1,5},{2,6},{3,7},{4,0},{5,1},{6,2},{7,3},{8,12},{9,13},{10,... | collective-permute-start | bytes 12296 | tf_op jit(solution)/shard_map/ppermute | solution.py:1174
  126.6 2.0 %collective-permute-done.29.refs_1_ = f32[8,128]{1,0:T(8,128)S(1)} collective-permute-done((f32[8,128]{1,0:T(8,128)S(1)}, f32[8,128]{1,0:T(8,128)S(1)}, u32[]{:S(2)}, u32[]{:S(2)}) %collective-permute-start.29) | collective-permute-done | bytes 4128 | tf_op jit(solution)/shard_map/ppermute | solution.py:1174
  129.7 1.2 collective-permute-start.33
  133.3 1.2 collective-permute-done.32.refs_1_
  (82 shorter events, 19.6 us)
Async XLA Ops:
  1.7 7.4 %collective-permute-start.3 = (bf16[112,128]{1,0:T(8,128)(2,1)S(1)}, bf16[112,128]{1,0:T(8,128)(2,1)S(1)}, u32[]{:S(2)}, u32[]{:S(2)}) collective-permute-start(bf16[112,128]{1,0:T(8,128)(2,1)S(1)} %get-tuple-element.76.refs_0_), channel_id=1, source_target_pairs={{0,8},{8,0},{16,24},{24,16},{1,9},{9,1},{17,25},{25,17},{2,10},{10... | collective-permute-start | bytes 86024 | tf_op jit(solution)/shard_map/ppermute | solution.py:1174
  4.7 8.7 %collective-permute-start.2 = (bf16[336,128]{1,0:T(8,128)(2,1)S(1)}, bf16[336,128]{1,0:T(8,128)(2,1)S(1)}, u32[]{:S(2)}, u32[]{:S(2)}) collective-permute-start(bf16[336,128]{1,0:T(8,128)(2,1)S(1)} %get-tuple-element.75.refs_0_), channel_id=1, source_target_pairs={{0,6},{1,7},{2,4},{3,5},{4,2},{5,3},{6,0},{7,1},{8,14},{9,15},{10,... | collective-permute-start | bytes 258056 | tf_op jit(solution)/shard_map/ppermute | solution.py:1174
  8.3 6.9 %collective-permute-start.1 = (bf16[336,128]{1,0:T(8,128)(2,1)S(1)}, bf16[336,128]{1,0:T(8,128)(2,1)S(1)}, u32[]{:S(2)}, u32[]{:S(2)}) collective-permute-start(bf16[336,128]{1,0:T(8,128)(2,1)S(1)} %get-tuple-element.75.refs_0_), channel_id=1, source_target_pairs={{0,4},{1,5},{2,6},{3,7},{4,0},{5,1},{6,2},{7,3},{8,12},{9,13},{10,... | collective-permute-start | bytes 258056 | tf_op jit(solution)/shard_map/ppermute | solution.py:1174
  8.3 6.9 %collective-permute-start = (bf16[336,128]{1,0:T(8,128)(2,1)S(1)}, bf16[336,128]{1,0:T(8,128)(2,1)S(1)}, u32[]{:S(2)}, u32[]{:S(2)}) collective-permute-start(bf16[336,128]{1,0:T(8,128)(2,1)S(1)} %get-tuple-element.75.refs_0_), channel_id=1, source_target_pairs={{0,2},{1,3},{2,0},{3,1},{4,6},{5,7},{6,4},{7,5},{8,10},{9,11},{10,... | collective-permute-start | bytes 258056 | tf_op jit(solution)/shard_map/ppermute | solution.py:1174
  9.1 4.2 %collective-permute-start.4 = (bf16[2,112,128]{2,1,0:T(8,128)(2,1)S(1)}, bf16[2,112,128]{2,1,0:T(8,128)(2,1)S(1)}, u32[]{:S(2)}, u32[]{:S(2)}) collective-permute-start(bf16[2,112,128]{2,1,0:T(8,128)(2,1)S(1)} %shard_map.136.mine_ref), channel_id=1, source_target_pairs={{0,16},{8,24},{16,0},{24,8},{1,17},{9,25},{17,1},{25,9},{2,18},{10... | collective-permute-start | bytes 172040 | tf_op jit(solution)/shard_map/ppermute | solution.py:1174
  15.3 17.1 %collective-permute-start.7 = (bf16[4,336,128]{2,1,0:T(8,128)(2,1)S(1)}, bf16[4,336,128]{2,1,0:T(8,128)(2,1)S(1)}, u32[]{:S(2)}, u32[]{:S(2)}) collective-permute-start(bf16[4,336,128]{2,1,0:T(8,128)(2,1)S(1)} %shard_map.139.refs_0_), channel_id=1, source_target_pairs={{0,24},{8,16},{16,8},{24,0},{1,25},{9,17},{17,9},{25,1},{2,26},{10... | collective-permute-start | bytes 1032200 | tf_op jit(solution)/shard_map/ppermute | solution.py:1174
  16.8 16.4 %collective-permute-start.6 = (bf16[4,336,128]{2,1,0:T(8,128)(2,1)S(1)}, bf16[4,336,128]{2,1,0:T(8,128)(2,1)S(1)}, u32[]{:S(2)}, u32[]{:S(2)}) collective-permute-start(bf16[4,336,128]{2,1,0:T(8,128)(2,1)S(1)} %shard_map.139.refs_0_), channel_id=1, source_target_pairs={{0,16},{8,24},{16,0},{24,8},{1,17},{9,25},{17,1},{25,9},{2,18},{10... | collective-permute-start | bytes 1032200 | tf_op jit(solution)/shard_map/ppermute | solution.py:1174
  17.3 16.0 %collective-permute-start.5 = (bf16[4,336,128]{2,1,0:T(8,128)(2,1)S(1)}, bf16[4,336,128]{2,1,0:T(8,128)(2,1)S(1)}, u32[]{:S(2)}, u32[]{:S(2)}) collective-permute-start(bf16[4,336,128]{2,1,0:T(8,128)(2,1)S(1)} %shard_map.139.refs_0_), channel_id=1, source_target_pairs={{0,8},{8,0},{16,24},{24,16},{1,9},{9,1},{17,25},{25,17},{2,10},{10... | collective-permute-start | bytes 1032200 | tf_op jit(solution)/shard_map/ppermute | solution.py:1174
  18.8 7.9 %collective-permute-start.10 = (bf16[4,112,128]{2,1,0:T(8,128)(2,1)S(1)}, bf16[4,112,128]{2,1,0:T(8,128)(2,1)S(1)}, u32[]{:S(2)}, u32[]{:S(2)}) collective-permute-start(bf16[4,112,128]{2,1,0:T(8,128)(2,1)S(1)} %shard_map.138.refs_4_.refs_0_), channel_id=1, source_target_pairs={{0,6},{1,7},{2,4},{3,5},{4,2},{5,3},{6,0},{7,1},{8,14},{9,15},{10,... | collective-permute-start | bytes 344072 | tf_op jit(solution)/shard_map/ppermute | solution.py:1174
  21.4 8.8 %collective-permute-start.9 = (bf16[4,112,128]{2,1,0:T(8,128)(2,1)S(1)}, bf16[4,112,128]{2,1,0:T(8,128)(2,1)S(1)}, u32[]{:S(2)}, u32[]{:S(2)}) collective-permute-start(bf16[4,112,128]{2,1,0:T(8,128)(2,1)S(1)} %shard_map.138.refs_4_.refs_0_), channel_id=1, source_target_pairs={{0,4},{1,5},{2,6},{3,7},{4,0},{5,1},{6,2},{7,3},{8,12},{9,13},{10,... | collective-permute-start | bytes 344072 | tf_op jit(solution)/shard_map/ppermute | solution.py:1174
  26.7 5.6 %collective-permute-start.8 = (bf16[4,112,128]{2,1,0:T(8,128)(2,1)S(1)}, bf16[4,112,128]{2,1,0:T(8,128)(2,1)S(1)}, u32[]{:S(2)}, u32[]{:S(2)}) collective-permute-start(bf16[4,112,128]{2,1,0:T(8,128)(2,1)S(1)} %shard_map.138.refs_4_.refs_0_), channel_id=1, source_target_pairs={{0,2},{1,3},{2,0},{3,1},{4,6},{5,7},{6,4},{7,5},{8,10},{9,11},{10,... | collective-permute-start | bytes 344072 | tf_op jit(solution)/shard_map/ppermute | solution.py:1174
  33.6 14.4 %collective-permute-start.11 = (bf16[4,448,128]{2,1,0:T(8,128)(2,1)S(1)}, bf16[4,448,128]{2,1,0:T(8,128)(2,1)S(1)}, u32[]{:S(2)}, u32[]{:S(2)}) collective-permute-start(bf16[4,448,128]{2,1,0:T(8,128)(2,1)S(1)} %get-tuple-element.78.refs_0_), channel_id=1, source_target_pairs={{0,1},{1,0},{2,3},{3,2},{4,5},{5,4},{6,7},{7,6},{8,9},{9,8},{10,11... | collective-permute-start | bytes 1376264 | tf_op jit(solution)/shard_map/ppermute | solution.py:1174
  34.1 13.9 %collective-permute-start.12 = (bf16[4,448,128]{2,1,0:T(8,128)(2,1)S(1)}, bf16[4,448,128]{2,1,0:T(8,128)(2,1)S(1)}, u32[]{:S(2)}, u32[]{:S(2)}) collective-permute-start(bf16[4,448,128]{2,1,0:T(8,128)(2,1)S(1)} %get-tuple-element.79.refs_1_), channel_id=1, source_target_pairs={{0,1},{1,0},{2,3},{3,2},{4,5},{5,4},{6,7},{7,6},{8,9},{9,8},{10,11... | collective-permute-start | bytes 1376264 | tf_op jit(solution)/shard_map/ppermute | solution.py:1174
  34.2 13.9 %collective-permute-start.13 = (bf16[4,448,128]{2,1,0:T(8,128)(2,1)S(1)}, bf16[4,448,128]{2,1,0:T(8,128)(2,1)S(1)}, u32[]{:S(2)}, u32[]{:S(2)}) collective-permute-start(bf16[4,448,128]{2,1,0:T(8,128)(2,1)S(1)} %get-tuple-element.80.refs_2_), channel_id=1, source_target_pairs={{0,1},{1,0},{2,3},{3,2},{4,5},{5,4},{6,7},{7,6},{8,9},{9,8},{10,11... | collective-permute-start | bytes 1376264 | tf_op jit(solution)/shard_map/ppermute | solution.py:1174
  65.7 3.1 %collective-permute-start.15 = (bf16[3,4,448,128]{3,2,1,0:T(8,128)(2,1)S(1)}, bf16[3,4,448,128]{3,2,1,0:T(8,128)(2,1)S(1)}, u32[]{:S(2)}, u32[]{:S(2)}) collective-permute-start(bf16[3,4,448,128]{3,2,1,0:T(8,128)(2,1)S(1)} %get-tuple-element.109), channel_id=1, source_target_pairs={{0,1},{1,0},{2,3},{3,2},{4,5},{5,4},{6,7},{7,6},{8,9},{9,8},{10,11... | collective-permute-start | bytes 4128776 | tf_op jit(solution)/shard_map/ppermute | solution.py:1174
  69.2 26.5 %collective-permute-start.16 = (bf16[3,1,448,128]{3,2,0,1:T(8,128)(2,1)S(1)}, bf16[3,1,448,128]{3,2,0,1:T(8,128)(2,1)S(1)}, u32[]{:S(2)}, u32[]{:S(2)}) collective-permute-start(bf16[3,1,448,128]{3,2,0,1:T(8,128)(2,1)S(1)} %bitcast.29), channel_id=1, source_target_pairs={{0,4},{1,5},{2,6},{3,7},{4,0},{5,1},{6,2},{7,3},{8,12},{9,13},{10,... | collective-permute-start | bytes 1032200 | tf_op jit(solution)/shard_map/ppermute | solution.py:1174
  69.5 33.7 %collective-permute-start.17 = (bf16[3,1,448,128]{3,2,0,1:T(8,128)(2,1)S(1)}, bf16[3,1,448,128]{3,2,0,1:T(8,128)(2,1)S(1)}, u32[]{:S(2)}, u32[]{:S(2)}) collective-permute-start(bf16[3,1,448,128]{3,2,0,1:T(8,128)(2,1)S(1)} %bitcast.28), channel_id=1, source_target_pairs={{0,6},{1,7},{2,4},{3,5},{4,2},{5,3},{6,0},{7,1},{8,14},{9,15},{10,... | collective-permute-start | bytes 1032200 | tf_op jit(solution)/shard_map/ppermute | solution.py:1174
  72.7 30.5 %collective-permute-start.18 = (bf16[3,1,448,128]{3,2,0,1:T(8,128)(2,1)S(1)}, bf16[3,1,448,128]{3,2,0,1:T(8,128)(2,1)S(1)}, u32[]{:S(2)}, u32[]{:S(2)}) collective-permute-start(bf16[3,1,448,128]{3,2,0,1:T(8,128)(2,1)S(1)} %bitcast.27), channel_id=1, source_target_pairs={{0,2},{1,3},{2,0},{3,1},{4,6},{5,7},{6,4},{7,5},{8,10},{9,11},{10,... | collective-permute-start | bytes 1032200 | tf_op jit(solution)/shard_map/ppermute | solution.py:1174
  87.6 9.4 %collective-permute-start.21 = (bf16[4,160,128]{2,1,0:T(8,128)(2,1)S(1)}, bf16[4,160,128]{2,1,0:T(8,128)(2,1)S(1)}, u32[]{:S(2)}, u32[]{:S(2)}) collective-permute-start(bf16[4,160,128]{2,1,0:T(8,128)(2,1)S(1)} %get-tuple-element.126), channel_id=1, source_target_pairs={{0,1},{1,0},{2,3},{3,2},{4,5},{5,4},{6,7},{7,6},{8,9},{9,8},{10,11... | collective-permute-start | bytes 491528 | tf_op jit(solution)/shard_map/ppermute | solution.py:1174
  87.7 8.1 %collective-permute-start.19 = (bf16[4,144,128]{2,1,0:T(8,128)(2,1)S(1)}, bf16[4,144,128]{2,1,0:T(8,128)(2,1)S(1)}, u32[]{:S(2)}, u32[]{:S(2)}) collective-permute-start(bf16[4,144,128]{2,1,0:T(8,128)(2,1)S(1)} %get-tuple-element.124), channel_id=1, source_target_pairs={{0,1},{1,0},{2,3},{3,2},{4,5},{5,4},{6,7},{7,6},{8,9},{9,8},{10,11... | collective-permute-start | bytes 442376 | tf_op jit(solution)/shard_map/ppermute | solution.py:1174
  97.7 12.7 %collective-permute-start.22 = (bf16[1,448,128]{2,1,0:T(8,128)(2,1)S(1)}, bf16[1,448,128]{2,1,0:T(8,128)(2,1)S(1)}, u32[]{:S(2)}, u32[]{:S(2)}) collective-permute-start(bf16[1,448,128]{2,1,0:T(8,128)(2,1)S(1)} %get-tuple-element.129), channel_id=1, source_target_pairs={{0,4},{1,5},{2,6},{3,7},{4,0},{5,1},{6,2},{7,3},{8,12},{9,13},{10,... | collective-permute-start | bytes 344072 | tf_op jit(solution)/shard_map/ppermute | solution.py:1174
  97.7 12.7 %collective-permute-start.23 = (bf16[1,448,128]{2,1,0:T(8,128)(2,1)S(1)}, bf16[1,448,128]{2,1,0:T(8,128)(2,1)S(1)}, u32[]{:S(2)}, u32[]{:S(2)}) collective-permute-start(bf16[1,448,128]{2,1,0:T(8,128)(2,1)S(1)} %get-tuple-element.130), channel_id=1, source_target_pairs={{0,6},{1,7},{2,4},{3,5},{4,2},{5,3},{6,0},{7,1},{8,14},{9,15},{10,... | collective-permute-start | bytes 344072 | tf_op jit(solution)/shard_map/ppermute | solution.py:1174
  98.3 12.1 %collective-permute-start.24 = (bf16[1,448,128]{2,1,0:T(8,128)(2,1)S(1)}, bf16[1,448,128]{2,1,0:T(8,128)(2,1)S(1)}, u32[]{:S(2)}, u32[]{:S(2)}) collective-permute-start(bf16[1,448,128]{2,1,0:T(8,128)(2,1)S(1)} %get-tuple-element.131), channel_id=1, source_target_pairs={{0,2},{1,3},{2,0},{3,1},{4,6},{5,7},{6,4},{7,5},{8,10},{9,11},{10,... | collective-permute-start | bytes 344072 | tf_op jit(solution)/shard_map/ppermute | solution.py:1174
  110.7 6.2 %collective-permute-start.25 = (bf16[448,128]{1,0:T(8,128)(2,1)S(1)}, bf16[448,128]{1,0:T(8,128)(2,1)S(1)}, u32[]{:S(2)}, u32[]{:S(2)}) collective-permute-start(bf16[448,128]{1,0:T(8,128)(2,1)S(1)} %get-tuple-element.133), channel_id=1, source_target_pairs={{0,24},{8,16},{16,8},{24,0},{1,25},{9,17},{17,9},{25,1},{2,26},{10... | collective-permute-start | bytes 344072 | tf_op jit(solution)/shard_map/ppermute | solution.py:1174
  110.7 6.4 %collective-permute-start.26 = (bf16[448,128]{1,0:T(8,128)(2,1)S(1)}, bf16[448,128]{1,0:T(8,128)(2,1)S(1)}, u32[]{:S(2)}, u32[]{:S(2)}) collective-permute-start(bf16[448,128]{1,0:T(8,128)(2,1)S(1)} %get-tuple-element.134), channel_id=1, source_target_pairs={{0,16},{8,24},{16,0},{24,8},{1,17},{9,25},{17,1},{25,9},{2,18},{10... | collective-permute-start | bytes 344072 | tf_op jit(solution)/shard_map/ppermute | solution.py:1174
  112.7 4.9 %collective-permute-start.27 = (bf16[448,128]{1,0:T(8,128)(2,1)S(1)}, bf16[448,128]{1,0:T(8,128)(2,1)S(1)}, u32[]{:S(2)}, u32[]{:S(2)}) collective-permute-start(bf16[448,128]{1,0:T(8,128)(2,1)S(1)} %get-tuple-element.135), channel_id=1, source_target_pairs={{0,8},{8,0},{16,24},{24,16},{1,9},{9,1},{17,25},{25,17},{2,10},{10... | collective-permute-start | bytes 344072 | tf_op jit(solution)/shard_map/ppermute | solution.py:1174
  120.5 5.4 %collective-permute-start.31 = (f32[8,128]{1,0:T(8,128)S(1)}, f32[8,128]{1,0:T(8,128)S(1)}, u32[]{:S(2)}, u32[]{:S(2)}) collective-permute-start(f32[8,128]{1,0:T(8,128)S(1)} %shard_map.154.refs_0_), channel_id=1, source_target_pairs={{0,6},{1,7},{2,4},{3,5},{4,2},{5,3},{6,0},{7,1},{8,14},{9,15},{10,... | collective-permute-start | bytes 12296 | tf_op jit(solution)/shard_map/ppermute | solution.py:1174
  121.3 5.3 %collective-permute-start.30 = (f32[8,128]{1,0:T(8,128)S(1)}, f32[8,128]{1,0:T(8,128)S(1)}, u32[]{:S(2)}, u32[]{:S(2)}) collective-permute-start(f32[8,128]{1,0:T(8,128)S(1)} %shard_map.154.refs_0_), channel_id=1, source_target_pairs={{0,4},{1,5},{2,6},{3,7},{4,0},{5,1},{6,2},{7,3},{8,12},{9,13},{10,... | collective-permute-start | bytes 12296 | tf_op jit(solution)/shard_map/ppermute | solution.py:1174
  124.9 3.6 %collective-permute-start.29 = (f32[8,128]{1,0:T(8,128)S(1)}, f32[8,128]{1,0:T(8,128)S(1)}, u32[]{:S(2)}, u32[]{:S(2)}) collective-permute-start(f32[8,128]{1,0:T(8,128)S(1)} %shard_map.154.refs_0_), channel_id=1, source_target_pairs={{0,2},{1,3},{2,0},{3,1},{4,6},{5,7},{6,4},{7,5},{8,10},{9,11},{10,... | collective-permute-start | bytes 12296 | tf_op jit(solution)/shard_map/ppermute | solution.py:1174
  128.6 4.5 %collective-permute-start.34 = (f32[8,128]{1,0:T(8,128)S(1)}, f32[8,128]{1,0:T(8,128)S(1)}, u32[]{:S(2)}, u32[]{:S(2)}) collective-permute-start(f32[8,128]{1,0:T(8,128)S(1)} %shard_map.155.refs_0_), channel_id=1, source_target_pairs={{0,24},{8,16},{16,8},{24,0},{1,25},{9,17},{17,9},{25,1},{2,26},{10... | collective-permute-start | bytes 12296 | tf_op jit(solution)/shard_map/ppermute | solution.py:1174
  129.7 3.6 %collective-permute-start.33 = (f32[8,128]{1,0:T(8,128)S(1)}, f32[8,128]{1,0:T(8,128)S(1)}, u32[]{:S(2)}, u32[]{:S(2)}) collective-permute-start(f32[8,128]{1,0:T(8,128)S(1)} %shard_map.155.refs_0_), channel_id=1, source_target_pairs={{0,16},{8,24},{16,0},{24,8},{1,17},{9,25},{17,1},{25,9},{2,18},{10... | collective-permute-start | bytes 12296 | tf_op jit(solution)/shard_map/ppermute | solution.py:1174
  130.9 3.6 %collective-permute-start.32 = (f32[8,128]{1,0:T(8,128)S(1)}, f32[8,128]{1,0:T(8,128)S(1)}, u32[]{:S(2)}, u32[]{:S(2)}) collective-permute-start(f32[8,128]{1,0:T(8,128)S(1)} %shard_map.155.refs_0_), channel_id=1, source_target_pairs={{0,8},{8,0},{16,24},{24,16},{1,9},{9,1},{17,25},{25,17},{2,10},{10... | collective-permute-start | bytes 12296 | tf_op jit(solution)/shard_map/ppermute | solution.py:1174
  (14 other events, 88.4 us)

commit v8 on v7

--- a/solution.py
+++ b/solution.py
@@ -883,24 +883,47 @@
     )(hat, normed, wq, tail, low, gains)
 
 
-def input_kernel(hat_ref, rstd_ref, vec_ref, da1_ref, dh1_ref, grad_ref, token_ref):
+def input_kernel(
+    plan,
+    hat_ref,
+    rstd_ref,
+    vec_ref,
+    da1_ref,
+    dh1_ref,
+    master_ref,
+    moment_ref,
+    second_ref,
+    grad_ref,
+    master_rows,
+    moment_rows,
+    second_rows,
+    squares_ref,
+):
     back = norm_back(hat_ref[...], rstd_ref[:, 0:1], da1_ref[...] * vec_ref[0:1, :])
     grad_ref[...] = dh1_ref[...] + back
-    token_ref[...] = jnp.zeros_like(token_ref)
-
-
-def input_part(hat, rstd, vec, da1, dh1):
-    return pl.pallas_call(
-        input_kernel,
+    master = flat_to_rows(plan, master_ref, master_rows)
+    flat_to_rows(plan, moment_ref, moment_rows)
+    flat_to_rows(plan, second_ref, second_rows)
+    _, index = flat_place(plan, master.shape)
+    squares_ref[...] = jnp.broadcast_to(tensor_sums(master * master, index), squares_ref.shape)
+
+
+def input_part(plan, hat, rstd, vec, da1, dh1, master, moment, second):
+    rows = jax.ShapeDtypeStruct((plan.win, LANES), F32)
+    return pl.pallas_call(
+        functools.partial(input_kernel, plan),
         out_shape=(
             jax.ShapeDtypeStruct(dh1.shape, F32),
+            rows,
+            rows,
+            rows,
             jax.ShapeDtypeStruct((8, LANES), F32),
         ),
-        in_specs=[VMEM] * 5,
-        out_specs=(VMEM, VMEM),
+        in_specs=[VMEM] * 8,
+        out_specs=(VMEM,) * 5,
         compiler_params=params(16),
         cost_estimate=QUICK,
-    )(hat, rstd, vec, da1, dh1)
+    )(hat, rstd, vec, da1, dh1, master, moment, second)
 
 
 def flat_place(plan, shape):
@@ -908,6 +931,16 @@
     lane = lax.broadcasted_iota(jnp.int32, shape, 1)
     place = row * LANES + lane
     return place, plan.device() * plan.shard + place
+
+
+def tensor_sums(squares, index):
+    lanes = lax.broadcasted_iota(jnp.int32, (1, LANES), 1)
+    row = jnp.zeros((1, LANES), F32)
+    for t in range(MATS):
+        mine = jnp.logical_and(index >= BOUNDS[t], index < BOUNDS[t + 1])
+        part = jnp.sum(jnp.where(mine, squares, 0.0), axis=0, keepdims=True)
+        row = jnp.where(lanes == t, jnp.sum(part, axis=1, keepdims=True), row)
+    return row
 
 
 def update_kernel(
@@ -919,14 +952,12 @@
     master_ref,
     moment_ref,
     second_ref,
+    squares_ref,
     new_moment_ref,
     new_second_ref,
     update_ref,
     sums_ref,
     window,
-    master_rows,
-    moment_rows,
-    second_rows,
 ):
     bucket = lax.axis_index("bucket")
     dp = lax.axis_index("dp")
@@ -947,54 +978,58 @@
     place, index = flat_place(plan, turned.shape)
     inside = place < plan.shard
     grad = jnp.where(inside, jnp.where(lane + offset < LANES, turned, above), 0.0)
-    master = flat_to_rows(plan, master_ref, master_rows)
-    old_moment = flat_to_rows(plan, moment_ref, moment_rows)
-    old_second = flat_to_rows(plan, second_ref, second_rows)
-    moment = beta_one * old_moment + (1.0 - beta_one) * grad
-    second = beta_two * old_second + (1.0 - beta_two) * grad * grad
+    master = master_ref[...]
+    moment = beta_one * moment_ref[...] + (1.0 - beta_one) * grad
+    second = beta_two * second_ref[...] + (1.0 - beta_two) * grad * grad
     first_hat = moment / (1.0 - beta_one**STEP)
     second_hat = second / (1.0 - beta_two**STEP)
     decay = jnp.where(index < BOUNDS[4], weight_decay, 0.0)
     update = first_hat / (jnp.sqrt(second_hat) + adam_epsilon) + decay * master
     update = jnp.where(inside, update, 0.0)
-    rows_to_flat(plan, moment, new_moment_ref)
-    rows_to_flat(plan, second, new_second_ref)
+    new_moment_ref[...] = moment
+    new_second_ref[...] = second
     update_ref[...] = update
-    master_sq = jnp.where(inside, master * master, 0.0)
-    update_sq = update * update
-    lanes = lax.broadcasted_iota(jnp.int32, (1, LANES), 1)
-    rows = []
-    for squares in (master_sq, update_sq):
-        row = jnp.zeros((1, LANES), F32)
-        for t in range(MATS):
-            mine = jnp.logical_and(index >= BOUNDS[t], index < BOUNDS[t + 1])
-            part = jnp.sum(jnp.where(mine, squares, 0.0), axis=0, keepdims=True)
-            row = jnp.where(lanes == t, jnp.sum(part, axis=1, keepdims=True), row)
-        rows.append(row)
-    rows.append(jnp.zeros((6, LANES), F32))
+    rows = [squares_ref[0:1, :], tensor_sums(update * update, index), jnp.zeros((6, LANES), F32)]
     sums_ref[...] = jnp.concatenate(rows, axis=0)
 
 
-def update_part(plan, parts, master, moment, second):
+def update_part(plan, parts, master, moment, second, squares):
+    rows = jax.ShapeDtypeStruct((plan.win, LANES), F32)
+    return pl.pallas_call(
+        functools.partial(update_kernel, plan),
+        out_shape=(rows, rows, rows, jax.ShapeDtypeStruct((8, LANES), F32)),
+        in_specs=[VMEM] * 8,
+        out_specs=(VMEM,) * 4,
+        scratch_shapes=[pltpu.VMEM((plan.win, LANES), F32)],
+        compiler_params=params(12),
+    )(*parts, master, moment, second, squares)
+
+
+def flatten_kernel(plan, moment_ref, second_ref, new_moment_ref, new_second_ref, token_ref):
+    rows_to_flat(plan, moment_ref[...], new_moment_ref)
+    rows_to_flat(plan, second_ref[...], new_second_ref)
+    token_ref[...] = jnp.zeros_like(token_ref)
+
+
+def flatten_part(plan, moment, second):
     flat = jax.ShapeDtypeStruct((plan.shard,), F32)
-    rows = jax.ShapeDtypeStruct((plan.win, LANES), F32)
-    return pl.pallas_call(
-        functools.partial(update_kernel, plan),
-        out_shape=(flat, flat, rows, jax.ShapeDtypeStruct((8, LANES), F32)),
-        in_specs=[VMEM] * 7,
-        out_specs=(VMEM,) * 4,
-        scratch_shapes=[pltpu.VMEM((plan.win, LANES), F32)] * 4,
-        compiler_params=params(12),
-    )(*parts, master, moment, second)
+    return pl.pallas_call(
+        functools.partial(flatten_kernel, plan),
+        out_shape=(flat, flat, jax.ShapeDtypeStruct((8, LANES), F32)),
+        in_specs=[VMEM] * 2,
+        out_specs=(VMEM,) * 3,
+        compiler_params=params(8),
+        cost_estimate=QUICK,
+    )(moment, second)
 
 
 def apply_kernel(plan, *refs):
-    *sums_refs, master_ref, update_ref, new_ref, norms_ref, trust_ref, rows_ref = refs
+    *sums_refs, master_ref, update_ref, _, new_ref, norms_ref, trust_ref = refs
     roots = jnp.sqrt(tree_sum([ref[...] for ref in sums_refs]))
     trust = roots[0:1, :] / (roots[1:2, :] + adam_epsilon)
     norms_ref[...] = roots[0:2, :MATS]
     trust_ref[...] = trust[:, :MATS]
-    master = flat_to_rows(plan, master_ref, rows_ref)
+    master = master_ref[...]
     _, index = flat_place(plan, master.shape)
     factors = jnp.broadcast_to(trust[:, 0:1], master.shape)
     for t in range(1, MATS):
@@ -1002,7 +1037,7 @@
     rows_to_flat(plan, master - learn_rate * factors * update_ref[...], new_ref)
 
 
-def apply_part(plan, sums, master, update_rows):
+def apply_part(plan, sums, master, update_rows, token):
     return pl.pallas_call(
         functools.partial(apply_kernel, plan),
         out_shape=(
@@ -1010,11 +1045,10 @@
             jax.ShapeDtypeStruct((2, MATS), F32),
             jax.ShapeDtypeStruct((1, MATS), F32),
         ),
-        in_specs=[VMEM] * (len(sums) + 2),
+        in_specs=[VMEM] * (len(sums) + 3),
         out_specs=(VMEM,) * 3,
-        scratch_shapes=[pltpu.VMEM((plan.win, LANES), F32)],
         compiler_params=params(8),
-    )(*sums, master, update_rows)
+    )(*sums, master, update_rows, token)
 
 
 def lay_column_kernel(count, *refs):
@@ -1251,18 +1285,21 @@
         plan, vec, segment_ids, seg_row, lse, q, do, hat, rstd, segk, [kab, *stacks], token
     )
     da1, near, *far = finish_part(plan, hat_in, normed, wq, tail, low, gains)
-    input_grad, given = input_part(hat_in, rstd_in, vec, da1, dh1)
+    input_grad, *old_rows, squares = input_part(
+        plan, hat_in, rstd_in, vec, da1, dh1, master, first_moment, second_moment
+    )
     *late_parts, token = add_parts(rest[:2], 1, gains)
     late_parts += rest[2:]
     *pieces, _ = add_parts([near, [swap(half, "dp", plan.nd, 1) for half in far]], pieces_of, token)
     first = scatter_dp(plan, pieces)
-    mine, *sent = blend(plan, late_parts, given, first)
+    mine, *sent = blend(plan, late_parts, squares, first)
     sent = list(zip(sent, masks_of(b_bits)))
     parts = [mine] + [swap(x, "bucket", plan.nb, mask) for x, mask in sent[::-1]]
-    new_first, new_second, update_rows, sums = update_part(
-        plan, parts, master, first_moment, second_moment
+    first_rows, second_rows, update_rows, sums = update_part(plan, parts, *old_rows, squares)
+    new_first, new_second, token = flatten_part(plan, first_rows, second_rows)
+    new_master, norms, trust = apply_part(
+        plan, sum_all(plan, sums), old_rows[0], update_rows, token
     )
-    new_master, norms, trust = apply_part(plan, sum_all(plan, sums), master, update_rows)
     return (
         block_output,
         input_grad,

time: 136 us -> 135 us (level)
    pallas_call x2 -> x3, Pallas kernels: 3.69 us -> 4.14 us  [the longest x1 2.5 us: input_part(): pl.pallas_call(functools.partial(input_kernel, plan), out_shape=(jax.Shap...]
  transfers between devices with their start and end apart: 35 -> 35, of which waited for: 22 -> 22; matrix products, arithmetic and copies ran while one was open for 0% -> 0% of each run, Pallas kernels for 24% -> 25%
where the time goes in v8:
time: 135 us
  Pallas kernels  53.7 us (40%)
  waiting for transfers between devices  39.1 us (29%)
  starting transfers between devices  38.3 us (28%)
  local copies, waits for them, and re-layouts  2.8 us (2%)
    ppermute x35, waiting for transfers between devices, swap(): return lax.ppermute(x, axis, [(i, i ^ mask) for i in range(size)])  39.1 us
    ppermute x35, starting transfers between devices, swap(): return lax.ppermute(x, axis, [(i, i ^ mask) for i in range(size)])  38.3 us
    pallas_call x1, Pallas kernels, middle_part(): pl.pallas_call(functools.partial(middle_kernel, plan), out_shape=(jax.Sha...  17.6 us
    pallas_call x1, Pallas kernels, backward(): pl.pallas_call(functools.partial(backward_kernel, plan), out_shape=(jax.S...  12 us
    pallas_call x1, Pallas kernels, forward(): pl.pallas_call(functools.partial(forward_kernel, plan), out_shape=(jax.Sh...  8.71 us
    pallas_call x1, Pallas kernels, project_part(): pl.pallas_call(functools.partial(project_kernel, plan), out_shape=(jax.Sh...  3.72 us
    pallas_call x1, Pallas kernels, finish_part(): pl.pallas_call(functools.partial(finish_kernel, plan), out_shape=(jax.Sha...  2.9 us
    unnamed x22, local copies, waits for them, and re-layouts  2.8 us
  transfers between devices with their start and end apart: 35, of which 22 were waited for; matrix products, arithmetic and copies ran while one was open for 0% of the time, Pallas kernels for 25%

profile of v8, /device:TPU:0, one launch (start us, length us, event | category | flops | bytes accessed | tf_op | source)
XLA Modules:
  0.0 134.8 jit_solution(14254413753175272187)
XLA Ops:
  1.7 3.0 %collective-permute-start.3 = (bf16[112,128]{1,0:T(8,128)(2,1)S(1)}, bf16[112,128]{1,0:T(8,128)(2,1)S(1)}, u32[]{:S(2)}, u32[]{:S(2)}) collective-permute-start(bf16[112,128]{1,0:T(8,128)(2,1)S(1)} %get-tuple-element.82.refs_0_), channel_id=1, source_target_pairs={{0,8},{8,0},{16,24},{24,16},{1,9},{9,1},{17,25},{25,17},{2,10},{10... | collective-permute-start | bytes 86024 | tf_op jit(solution)/shard_map/ppermute | solution.py:1208
  4.7 3.6 %collective-permute-start.2 = (bf16[336,128]{1,0:T(8,128)(2,1)S(1)}, bf16[336,128]{1,0:T(8,128)(2,1)S(1)}, u32[]{:S(2)}, u32[]{:S(2)}) collective-permute-start(bf16[336,128]{1,0:T(8,128)(2,1)S(1)} %get-tuple-element.81.refs_0_), channel_id=1, source_target_pairs={{0,6},{1,7},{2,4},{3,5},{4,2},{5,3},{6,0},{7,1},{8,14},{9,15},{10,... | collective-permute-start | bytes 258056 | tf_op jit(solution)/shard_map/ppermute | solution.py:1208
  9.1 1.6 %collective-permute-start.4 = (bf16[2,112,128]{2,1,0:T(8,128)(2,1)S(1)}, bf16[2,112,128]{2,1,0:T(8,128)(2,1)S(1)}, u32[]{:S(2)}, u32[]{:S(2)}) collective-permute-start(bf16[2,112,128]{2,1,0:T(8,128)(2,1)S(1)} %shard_map.136.mine_ref), channel_id=1, source_target_pairs={{0,16},{8,24},{16,0},{24,8},{1,17},{9,25},{17,1},{25,9},{2,18},{10... | collective-permute-start | bytes 172040 | tf_op jit(solution)/shard_map/ppermute | solution.py:1208
  13.4 1.9 %collective-permute-done.1.refs_2_ = bf16[336,128]{1,0:T(8,128)(2,1)S(1)} collective-permute-done((bf16[336,128]{1,0:T(8,128)(2,1)S(1)}, bf16[336,128]{1,0:T(8,128)(2,1)S(1)}, u32[]{:S(2)}, u32[]{:S(2)}) %collective-permute-start.1) | collective-permute-done | bytes 86048 | tf_op jit(solution)/shard_map/ppermute | solution.py:1208
  15.3 1.6 %collective-permute-start.7 = (bf16[4,336,128]{2,1,0:T(8,128)(2,1)S(1)}, bf16[4,336,128]{2,1,0:T(8,128)(2,1)S(1)}, u32[]{:S(2)}, u32[]{:S(2)}) collective-permute-start(bf16[4,336,128]{2,1,0:T(8,128)(2,1)S(1)} %shard_map.139.refs_0_), channel_id=1, source_target_pairs={{0,24},{8,16},{16,8},{24,0},{1,25},{9,17},{17,9},{25,1},{2,26},{10... | collective-permute-start | bytes 1032200 | tf_op jit(solution)/shard_map/ppermute | solution.py:1208
  17.3 1.5 %collective-permute-start.5 = (bf16[4,336,128]{2,1,0:T(8,128)(2,1)S(1)}, bf16[4,336,128]{2,1,0:T(8,128)(2,1)S(1)}, u32[]{:S(2)}, u32[]{:S(2)}) collective-permute-start(bf16[4,336,128]{2,1,0:T(8,128)(2,1)S(1)} %shard_map.139.refs_0_), channel_id=1, source_target_pairs={{0,8},{8,0},{16,24},{24,16},{1,9},{9,1},{17,25},{25,17},{2,10},{10... | collective-permute-start | bytes 1032200 | tf_op jit(solution)/shard_map/ppermute | solution.py:1208
  18.8 2.6 %collective-permute-start.10 = (bf16[4,112,128]{2,1,0:T(8,128)(2,1)S(1)}, bf16[4,112,128]{2,1,0:T(8,128)(2,1)S(1)}, u32[]{:S(2)}, u32[]{:S(2)}) collective-permute-start(bf16[4,112,128]{2,1,0:T(8,128)(2,1)S(1)} %shard_map.138.refs_4_.refs_0_), channel_id=1, source_target_pairs={{0,6},{1,7},{2,4},{3,5},{4,2},{5,3},{6,0},{7,1},{8,14},{9,15},{10,... | collective-permute-start | bytes 344072 | tf_op jit(solution)/shard_map/ppermute | solution.py:1208
  21.4 5.3 %collective-permute-done.10.refs_3_ = bf16[4,112,128]{2,1,0:T(8,128)(2,1)S(1)} collective-permute-done((bf16[4,112,128]{2,1,0:T(8,128)(2,1)S(1)}, bf16[4,112,128]{2,1,0:T(8,128)(2,1)S(1)}, u32[]{:S(2)}, u32[]{:S(2)}) %collective-permute-start.10) | collective-permute-done | bytes 114720 | tf_op jit(solution)/shard_map/ppermute | solution.py:1208
  26.7 2.9 %collective-permute-start.8 = (bf16[4,112,128]{2,1,0:T(8,128)(2,1)S(1)}, bf16[4,112,128]{2,1,0:T(8,128)(2,1)S(1)}, u32[]{:S(2)}, u32[]{:S(2)}) collective-permute-start(bf16[4,112,128]{2,1,0:T(8,128)(2,1)S(1)} %shard_map.138.refs_4_.refs_0_), channel_id=1, source_target_pairs={{0,2},{1,3},{2,0},{3,1},{4,6},{5,7},{6,4},{7,5},{8,10},{9,11},{10,... | collective-permute-start | bytes 344072 | tf_op jit(solution)/shard_map/ppermute | solution.py:1208
  30.2 2.1 %collective-permute-done.8.refs_1_ = bf16[4,112,128]{2,1,0:T(8,128)(2,1)S(1)} collective-permute-done((bf16[4,112,128]{2,1,0:T(8,128)(2,1)S(1)}, bf16[4,112,128]{2,1,0:T(8,128)(2,1)S(1)}, u32[]{:S(2)}, u32[]{:S(2)}) %collective-permute-start.8) | collective-permute-done | bytes 114720 | tf_op jit(solution)/shard_map/ppermute | solution.py:1208
  35.5 3.7 %shard_map.142 = (bf16[384,1152]{1,0:T(8,128)(2,1)S(1)}, f32[8,384]{1,0:T(8,128)S(1)}, f32[8,128]{1,0:T(8,128)S(1)}, f32[8,128]{1,0:T(8,128)S(1)}, bf16[1024,384...) custom-call(bf16[4,512,128]{2,1,0:T(8,128)(2,1)S(1)} %get-tuple-elem, ...), custom_call_target="tpu_custom_call" | custom-call | flops 1000 | bytes 1000 | tf_op jit(solution)/shard_map/pallas_call | solution.py:360
  39.3 8.7 %shard_map.143 = (bf16[1024,384]{1,0:T(8,128)(2,1)S(1)}, bf16[4,384,256]{2,1,0:T(8,128)(2,1)S(1)}, f32[4,384,256]{2,1,0:T(8,128)S(1)}, f32[4,8,256]{2,1,0:T(8,12...) custom-call(s32[1024]{0:T(1024)S(1)} %copy-done.7, s32[1,1024]{1,0:T(1,128)S(1)} %bitcast.22, ...), custom_call_target="tpu_custom_call" | custom-call | flops 1000 | bytes 1000 | tf_op jit(solution)/shard_map/pallas_call | solution.py:458
  48.1 17.6 %shard_map.144 = (bf16[1024,384]{1,0:T(8,128)(2,1)}, f32[1024,384]{1,0:T(8,128)S(1)}, bf16[1024,384]{1,0:T(8,128)(2,1)S(1)}, bf16[3,4,448,128]{3,2,1,0:T(8,128)(...) custom-call(bf16[4,448,128]{2,1,0:T(8,128)(2,1)S(1)} %get-tuple-element.84.refs_0_, ...), custom_call_target="tpu_custom_call" | custom-call | flops 1000 | bytes 1000 | tf_op jit(solution)/shard_map/pallas_call | solution.py:614
  65.8 1.5 %shard_map.145 = (bf16[3,8,2,128,128]{4,3,2,1,0:T(8,128)(2,1)S(1)}, bf16[3,4,512,128]{3,2,1,0:T(8,128)(2,1)S(1)}, bf16[3,4,512,128]{3,2,1,0:T(8,128)(2,1)S(1)}, ...) custom-call(f32[8,384]{1,0:T(8,128)S(1)} %get-tuple-element.96.refs_, ...), custom_call_target="tpu_custom_call" | custom-call | flops 1000 | bytes 1000 | tf_op jit(solution)/shard_map/pallas_call | solution.py:678
  67.4 1.5 %collective-permute-done.15.refs_1_ = bf16[3,4,448,128]{3,2,1,0:T(8,128)(2,1)S(1)} collective-permute-done((bf16[3,4,448,128]{3,2,1,0:T(8,128)(2,1)S(1)}, bf16[3,4,448,128]{3,2,1,0:T(8,128)(2,1)S(1)}, u32[]{:S(2)}, u32[]{:S(2)}) %collective-permute-start.15) | collective-permute-done | bytes 1376288 | tf_op jit(solution)/shard_map/ppermute | solution.py:1208
  69.5 3.2 %collective-permute-start.17 = (bf16[3,1,448,128]{3,2,0,1:T(8,128)(2,1)S(1)}, bf16[3,1,448,128]{3,2,0,1:T(8,128)(2,1)S(1)}, u32[]{:S(2)}, u32[]{:S(2)}) collective-permute-start(bf16[3,1,448,128]{3,2,0,1:T(8,128)(2,1)S(1)} %bitcast.28), channel_id=1, source_target_pairs={{0,6},{1,7},{2,4},{3,5},{4,2},{5,3},{6,0},{7,1},{8,14},{9,15},{10,... | collective-permute-start | bytes 1032200 | tf_op jit(solution)/shard_map/ppermute | solution.py:1208
  72.8 12.0 %shard_map.147 = (bf16[1024,1152]{1,0:T(8,128)(2,1)S(1)}, f32[8,384]{1,0:T(8,128)S(1)}) custom-call(f32[8,384]{1,0:T(8,128)S(1)} %get-tuple-element.96.refs_12_.vec_ref, s32[1024]{0:T(1024)S(1)} %copy-done.7, s32[1,1024]{1,0:T(1,128)S(1)} %bitcast.23, f32[4,8,256]{2,1,0:T(8,128)S(1)} %get-tuple-element.104.lse_ref, ...), custom_call_target="tpu_custom_call" | custom-call | flops 1000 | bytes 1000 | tf_op jit(solution)/shard_map/pallas_call | solution.py:794
  84.7 2.9 %shard_map.148 = (f32[1024,384]{1,0:T(8,128)S(1)}, bf16[4,448,128]{2,1,0:T(8,128)(2,1)S(1)}, bf16[4,144,128]{2,1,0:T(8,128)(2,1)S(1)}, bf16[4,144,128]{2,1,0:T(8,128)(2,1)S(1)}, bf16[4,160,128]{2,1,0:T(8,128)(2,1)S(1)}) custom-call(f32[1024,384]{1,0:T(8,128)S(1)} %get-tuple-element.88.hat_in_ref.hat_ref, ...), custom_call_target="tpu_custom_call" | custom-call | flops 1000 | bytes 1000 | tf_op jit(solution)/shard_map/pallas_call | solution.py:872
  88.3 7.4 %collective-permute-done.16 = bf16[3,1,448,128]{3,2,0,1:T(8,128)(2,1)S(1)} collective-permute-done((bf16[3,1,448,128]{3,2,0,1:T(8,128)(2,1)S(1)}, bf16[3,1,448,128]{3,2,0,1:T(8,128)(2,1)S(1)}, u32[]{:S(2)}, u32[]{:S(2)}) %collective-permute-start.16) | collective-permute-done | bytes 344096 | tf_op jit(solution)/shard_map/ppermute | solution.py:1208
  95.8 1.3 collective-permute-done.20.refs_2_
  98.3 2.9 %collective-permute-start.24 = (bf16[1,448,128]{2,1,0:T(8,128)(2,1)S(1)}, bf16[1,448,128]{2,1,0:T(8,128)(2,1)S(1)}, u32[]{:S(2)}, u32[]{:S(2)}) collective-permute-start(bf16[1,448,128]{2,1,0:T(8,128)(2,1)S(1)} %get-tuple-element.137), channel_id=1, source_target_pairs={{0,2},{1,3},{2,0},{3,1},{4,6},{5,7},{6,4},{7,5},{8,10},{9,11},{10,... | collective-permute-start | bytes 344072 | tf_op jit(solution)/shard_map/ppermute | solution.py:1208
  101.2 2.5 %shard_map.149 = (f32[1024,384]{1,0:T(8,128)}, f32[448,128]{1,0:T(8,128)S(1)}, f32[448,128]{1,0:T(8,128)S(1)}, f32[448,128]{1,0:T(8,128)S(1)}, f32[8,128]{1,0:T(8,128)S(1)}) custom-call(f32[1024,384]{1,0:T(8,128)S(1)} %get-tuple-element.88.hat_in_ref.hat_ref, f32[1024,128]{1,0:T(8,128)S(1)} %get-tuple-element.98.rstd_ref, ...), custom_call_target="tpu_custom_call" | custom-call | flops 1000 | bytes 1000 | tf_op jit(solution)/shard_map/pallas_call | solution.py:913
  103.7 6.7 %collective-permute-done.22 = bf16[1,448,128]{2,1,0:T(8,128)(2,1)S(1)} collective-permute-done((bf16[1,448,128]{2,1,0:T(8,128)(2,1)S(1)}, bf16[1,448,128]{2,1,0:T(8,128)(2,1)S(1)}, u32[]{:S(2)}, u32[]{:S(2)}) %collective-permute-start.22) | collective-permute-done | bytes 114720 | tf_op jit(solution)/shard_map/ppermute | solution.py:1208
  110.8 1.9 %collective-permute-start.26 = (bf16[448,128]{1,0:T(8,128)(2,1)S(1)}, bf16[448,128]{1,0:T(8,128)(2,1)S(1)}, u32[]{:S(2)}, u32[]{:S(2)}) collective-permute-start(bf16[448,128]{1,0:T(8,128)(2,1)S(1)} %get-tuple-element.140), channel_id=1, source_target_pairs={{0,16},{8,24},{16,0},{24,8},{1,17},{9,25},{17,1},{25,9},{2,18},{10... | collective-permute-start | bytes 344072 | tf_op jit(solution)/shard_map/ppermute | solution.py:1208
  112.7 1.6 %collective-permute-start.27 = (bf16[448,128]{1,0:T(8,128)(2,1)S(1)}, bf16[448,128]{1,0:T(8,128)(2,1)S(1)}, u32[]{:S(2)}, u32[]{:S(2)}) collective-permute-start(bf16[448,128]{1,0:T(8,128)(2,1)S(1)} %get-tuple-element.141), channel_id=1, source_target_pairs={{0,8},{8,0},{16,24},{24,16},{1,9},{9,1},{17,25},{25,17},{2,10},{10... | collective-permute-start | bytes 344072 | tf_op jit(solution)/shard_map/ppermute | solution.py:1208
  114.2 2.7 %collective-permute-done.25.got0_ref = bf16[448,128]{1,0:T(8,128)(2,1)S(1)} collective-permute-done((bf16[448,128]{1,0:T(8,128)(2,1)S(1)}, bf16[448,128]{1,0:T(8,128)(2,1)S(1)}, u32[]{:S(2)}, u32[]{:S(2)}) %collective-permute-start.25) | collective-permute-done | bytes 114720 | tf_op jit(solution)/shard_map/ppermute | solution.py:1208
  118.4 1.2 collective-permute-done.28.refs_1_
  120.5 3.2 %collective-permute-start.30 = (f32[8,128]{1,0:T(8,128)S(1)}, f32[8,128]{1,0:T(8,128)S(1)}, u32[]{:S(2)}, u32[]{:S(2)}) collective-permute-start(f32[8,128]{1,0:T(8,128)S(1)} %shard_map.155.refs_0_), channel_id=1, source_target_pairs={{0,4},{1,5},{2,6},{3,7},{4,0},{5,1},{6,2},{7,3},{8,12},{9,13},{10,... | collective-permute-start | bytes 12296 | tf_op jit(solution)/shard_map/ppermute | solution.py:1208
  125.3 2.0 %collective-permute-done.29.refs_1_ = f32[8,128]{1,0:T(8,128)S(1)} collective-permute-done((f32[8,128]{1,0:T(8,128)S(1)}, f32[8,128]{1,0:T(8,128)S(1)}, u32[]{:S(2)}, u32[]{:S(2)}) %collective-permute-start.29) | collective-permute-done | bytes 4128 | tf_op jit(solution)/shard_map/ppermute | solution.py:1208
  127.3 1.5 %collective-permute-start.34 = (f32[8,128]{1,0:T(8,128)S(1)}, f32[8,128]{1,0:T(8,128)S(1)}, u32[]{:S(2)}, u32[]{:S(2)}) collective-permute-start(f32[8,128]{1,0:T(8,128)S(1)} %shard_map.156.refs_0_), channel_id=1, source_target_pairs={{0,24},{8,16},{16,8},{24,0},{1,25},{9,17},{17,9},{25,1},{2,26},{10... | collective-permute-start | bytes 12296 | tf_op jit(solution)/shard_map/ppermute | solution.py:1208
  128.8 1.3 collective-permute-start.33
  132.4 1.3 collective-permute-done.32.refs_1_
  (83 shorter events, 19.2 us)
Async XLA Ops:
  1.7 7.4 %collective-permute-start.3 = (bf16[112,128]{1,0:T(8,128)(2,1)S(1)}, bf16[112,128]{1,0:T(8,128)(2,1)S(1)}, u32[]{:S(2)}, u32[]{:S(2)}) collective-permute-start(bf16[112,128]{1,0:T(8,128)(2,1)S(1)} %get-tuple-element.82.refs_0_), channel_id=1, source_target_pairs={{0,8},{8,0},{16,24},{24,16},{1,9},{9,1},{17,25},{25,17},{2,10},{10... | collective-permute-start | bytes 86024 | tf_op jit(solution)/shard_map/ppermute | solution.py:1208
  4.7 8.7 %collective-permute-start.2 = (bf16[336,128]{1,0:T(8,128)(2,1)S(1)}, bf16[336,128]{1,0:T(8,128)(2,1)S(1)}, u32[]{:S(2)}, u32[]{:S(2)}) collective-permute-start(bf16[336,128]{1,0:T(8,128)(2,1)S(1)} %get-tuple-element.81.refs_0_), channel_id=1, source_target_pairs={{0,6},{1,7},{2,4},{3,5},{4,2},{5,3},{6,0},{7,1},{8,14},{9,15},{10,... | collective-permute-start | bytes 258056 | tf_op jit(solution)/shard_map/ppermute | solution.py:1208
  8.3 6.9 %collective-permute-start.1 = (bf16[336,128]{1,0:T(8,128)(2,1)S(1)}, bf16[336,128]{1,0:T(8,128)(2,1)S(1)}, u32[]{:S(2)}, u32[]{:S(2)}) collective-permute-start(bf16[336,128]{1,0:T(8,128)(2,1)S(1)} %get-tuple-element.81.refs_0_), channel_id=1, source_target_pairs={{0,4},{1,5},{2,6},{3,7},{4,0},{5,1},{6,2},{7,3},{8,12},{9,13},{10,... | collective-permute-start | bytes 258056 | tf_op jit(solution)/shard_map/ppermute | solution.py:1208
  8.3 6.9 %collective-permute-start = (bf16[336,128]{1,0:T(8,128)(2,1)S(1)}, bf16[336,128]{1,0:T(8,128)(2,1)S(1)}, u32[]{:S(2)}, u32[]{:S(2)}) collective-permute-start(bf16[336,128]{1,0:T(8,128)(2,1)S(1)} %get-tuple-element.81.refs_0_), channel_id=1, source_target_pairs={{0,2},{1,3},{2,0},{3,1},{4,6},{5,7},{6,4},{7,5},{8,10},{9,11},{10,... | collective-permute-start | bytes 258056 | tf_op jit(solution)/shard_map/ppermute | solution.py:1208
  9.1 4.2 %collective-permute-start.4 = (bf16[2,112,128]{2,1,0:T(8,128)(2,1)S(1)}, bf16[2,112,128]{2,1,0:T(8,128)(2,1)S(1)}, u32[]{:S(2)}, u32[]{:S(2)}) collective-permute-start(bf16[2,112,128]{2,1,0:T(8,128)(2,1)S(1)} %shard_map.136.mine_ref), channel_id=1, source_target_pairs={{0,16},{8,24},{16,0},{24,8},{1,17},{9,25},{17,1},{25,9},{2,18},{10... | collective-permute-start | bytes 172040 | tf_op jit(solution)/shard_map/ppermute | solution.py:1208
  15.3 17.1 %collective-permute-start.7 = (bf16[4,336,128]{2,1,0:T(8,128)(2,1)S(1)}, bf16[4,336,128]{2,1,0:T(8,128)(2,1)S(1)}, u32[]{:S(2)}, u32[]{:S(2)}) collective-permute-start(bf16[4,336,128]{2,1,0:T(8,128)(2,1)S(1)} %shard_map.139.refs_0_), channel_id=1, source_target_pairs={{0,24},{8,16},{16,8},{24,0},{1,25},{9,17},{17,9},{25,1},{2,26},{10... | collective-permute-start | bytes 1032200 | tf_op jit(solution)/shard_map/ppermute | solution.py:1208
  16.8 16.4 %collective-permute-start.6 = (bf16[4,336,128]{2,1,0:T(8,128)(2,1)S(1)}, bf16[4,336,128]{2,1,0:T(8,128)(2,1)S(1)}, u32[]{:S(2)}, u32[]{:S(2)}) collective-permute-start(bf16[4,336,128]{2,1,0:T(8,128)(2,1)S(1)} %shard_map.139.refs_0_), channel_id=1, source_target_pairs={{0,16},{8,24},{16,0},{24,8},{1,17},{9,25},{17,1},{25,9},{2,18},{10... | collective-permute-start | bytes 1032200 | tf_op jit(solution)/shard_map/ppermute | solution.py:1208
  17.3 16.0 %collective-permute-start.5 = (bf16[4,336,128]{2,1,0:T(8,128)(2,1)S(1)}, bf16[4,336,128]{2,1,0:T(8,128)(2,1)S(1)}, u32[]{:S(2)}, u32[]{:S(2)}) collective-permute-start(bf16[4,336,128]{2,1,0:T(8,128)(2,1)S(1)} %shard_map.139.refs_0_), channel_id=1, source_target_pairs={{0,8},{8,0},{16,24},{24,16},{1,9},{9,1},{17,25},{25,17},{2,10},{10... | collective-permute-start | bytes 1032200 | tf_op jit(solution)/shard_map/ppermute | solution.py:1208
  18.8 7.9 %collective-permute-start.10 = (bf16[4,112,128]{2,1,0:T(8,128)(2,1)S(1)}, bf16[4,112,128]{2,1,0:T(8,128)(2,1)S(1)}, u32[]{:S(2)}, u32[]{:S(2)}) collective-permute-start(bf16[4,112,128]{2,1,0:T(8,128)(2,1)S(1)} %shard_map.138.refs_4_.refs_0_), channel_id=1, source_target_pairs={{0,6},{1,7},{2,4},{3,5},{4,2},{5,3},{6,0},{7,1},{8,14},{9,15},{10,... | collective-permute-start | bytes 344072 | tf_op jit(solution)/shard_map/ppermute | solution.py:1208
  21.4 8.8 %collective-permute-start.9 = (bf16[4,112,128]{2,1,0:T(8,128)(2,1)S(1)}, bf16[4,112,128]{2,1,0:T(8,128)(2,1)S(1)}, u32[]{:S(2)}, u32[]{:S(2)}) collective-permute-start(bf16[4,112,128]{2,1,0:T(8,128)(2,1)S(1)} %shard_map.138.refs_4_.refs_0_), channel_id=1, source_target_pairs={{0,4},{1,5},{2,6},{3,7},{4,0},{5,1},{6,2},{7,3},{8,12},{9,13},{10,... | collective-permute-start | bytes 344072 | tf_op jit(solution)/shard_map/ppermute | solution.py:1208
  26.7 5.6 %collective-permute-start.8 = (bf16[4,112,128]{2,1,0:T(8,128)(2,1)S(1)}, bf16[4,112,128]{2,1,0:T(8,128)(2,1)S(1)}, u32[]{:S(2)}, u32[]{:S(2)}) collective-permute-start(bf16[4,112,128]{2,1,0:T(8,128)(2,1)S(1)} %shard_map.138.refs_4_.refs_0_), channel_id=1, source_target_pairs={{0,2},{1,3},{2,0},{3,1},{4,6},{5,7},{6,4},{7,5},{8,10},{9,11},{10,... | collective-permute-start | bytes 344072 | tf_op jit(solution)/shard_map/ppermute | solution.py:1208
  33.6 14.4 %collective-permute-start.11 = (bf16[4,448,128]{2,1,0:T(8,128)(2,1)S(1)}, bf16[4,448,128]{2,1,0:T(8,128)(2,1)S(1)}, u32[]{:S(2)}, u32[]{:S(2)}) collective-permute-start(bf16[4,448,128]{2,1,0:T(8,128)(2,1)S(1)} %get-tuple-element.84.refs_0_), channel_id=1, source_target_pairs={{0,1},{1,0},{2,3},{3,2},{4,5},{5,4},{6,7},{7,6},{8,9},{9,8},{10,11... | collective-permute-start | bytes 1376264 | tf_op jit(solution)/shard_map/ppermute | solution.py:1208
  34.1 13.9 %collective-permute-start.12 = (bf16[4,448,128]{2,1,0:T(8,128)(2,1)S(1)}, bf16[4,448,128]{2,1,0:T(8,128)(2,1)S(1)}, u32[]{:S(2)}, u32[]{:S(2)}) collective-permute-start(bf16[4,448,128]{2,1,0:T(8,128)(2,1)S(1)} %get-tuple-element.85.refs_1_), channel_id=1, source_target_pairs={{0,1},{1,0},{2,3},{3,2},{4,5},{5,4},{6,7},{7,6},{8,9},{9,8},{10,11... | collective-permute-start | bytes 1376264 | tf_op jit(solution)/shard_map/ppermute | solution.py:1208
  34.2 13.9 %collective-permute-start.13 = (bf16[4,448,128]{2,1,0:T(8,128)(2,1)S(1)}, bf16[4,448,128]{2,1,0:T(8,128)(2,1)S(1)}, u32[]{:S(2)}, u32[]{:S(2)}) collective-permute-start(bf16[4,448,128]{2,1,0:T(8,128)(2,1)S(1)} %get-tuple-element.86.refs_2_), channel_id=1, source_target_pairs={{0,1},{1,0},{2,3},{3,2},{4,5},{5,4},{6,7},{7,6},{8,9},{9,8},{10,11... | collective-permute-start | bytes 1376264 | tf_op jit(solution)/shard_map/ppermute | solution.py:1208
  65.7 3.1 %collective-permute-start.15 = (bf16[3,4,448,128]{3,2,1,0:T(8,128)(2,1)S(1)}, bf16[3,4,448,128]{3,2,1,0:T(8,128)(2,1)S(1)}, u32[]{:S(2)}, u32[]{:S(2)}) collective-permute-start(bf16[3,4,448,128]{3,2,1,0:T(8,128)(2,1)S(1)} %get-tuple-element.115), channel_id=1, source_target_pairs={{0,1},{1,0},{2,3},{3,2},{4,5},{5,4},{6,7},{7,6},{8,9},{9,8},{10,11... | collective-permute-start | bytes 4128776 | tf_op jit(solution)/shard_map/ppermute | solution.py:1208
  69.2 26.5 %collective-permute-start.16 = (bf16[3,1,448,128]{3,2,0,1:T(8,128)(2,1)S(1)}, bf16[3,1,448,128]{3,2,0,1:T(8,128)(2,1)S(1)}, u32[]{:S(2)}, u32[]{:S(2)}) collective-permute-start(bf16[3,1,448,128]{3,2,0,1:T(8,128)(2,1)S(1)} %bitcast.29), channel_id=1, source_target_pairs={{0,4},{1,5},{2,6},{3,7},{4,0},{5,1},{6,2},{7,3},{8,12},{9,13},{10,... | collective-permute-start | bytes 1032200 | tf_op jit(solution)/shard_map/ppermute | solution.py:1208
  69.5 34.2 %collective-permute-start.17 = (bf16[3,1,448,128]{3,2,0,1:T(8,128)(2,1)S(1)}, bf16[3,1,448,128]{3,2,0,1:T(8,128)(2,1)S(1)}, u32[]{:S(2)}, u32[]{:S(2)}) collective-permute-start(bf16[3,1,448,128]{3,2,0,1:T(8,128)(2,1)S(1)} %bitcast.28), channel_id=1, source_target_pairs={{0,6},{1,7},{2,4},{3,5},{4,2},{5,3},{6,0},{7,1},{8,14},{9,15},{10,... | collective-permute-start | bytes 1032200 | tf_op jit(solution)/shard_map/ppermute | solution.py:1208
  72.7 31.0 %collective-permute-start.18 = (bf16[3,1,448,128]{3,2,0,1:T(8,128)(2,1)S(1)}, bf16[3,1,448,128]{3,2,0,1:T(8,128)(2,1)S(1)}, u32[]{:S(2)}, u32[]{:S(2)}) collective-permute-start(bf16[3,1,448,128]{3,2,0,1:T(8,128)(2,1)S(1)} %bitcast.27), channel_id=1, source_target_pairs={{0,2},{1,3},{2,0},{3,1},{4,6},{5,7},{6,4},{7,5},{8,10},{9,11},{10,... | collective-permute-start | bytes 1032200 | tf_op jit(solution)/shard_map/ppermute | solution.py:1208
  87.7 9.4 %collective-permute-start.21 = (bf16[4,160,128]{2,1,0:T(8,128)(2,1)S(1)}, bf16[4,160,128]{2,1,0:T(8,128)(2,1)S(1)}, u32[]{:S(2)}, u32[]{:S(2)}) collective-permute-start(bf16[4,160,128]{2,1,0:T(8,128)(2,1)S(1)} %get-tuple-element.132), channel_id=1, source_target_pairs={{0,1},{1,0},{2,3},{3,2},{4,5},{5,4},{6,7},{7,6},{8,9},{9,8},{10,11... | collective-permute-start | bytes 491528 | tf_op jit(solution)/shard_map/ppermute | solution.py:1208
  87.8 8.0 %collective-permute-start.19 = (bf16[4,144,128]{2,1,0:T(8,128)(2,1)S(1)}, bf16[4,144,128]{2,1,0:T(8,128)(2,1)S(1)}, u32[]{:S(2)}, u32[]{:S(2)}) collective-permute-start(bf16[4,144,128]{2,1,0:T(8,128)(2,1)S(1)} %get-tuple-element.130), channel_id=1, source_target_pairs={{0,1},{1,0},{2,3},{3,2},{4,5},{5,4},{6,7},{7,6},{8,9},{9,8},{10,11... | collective-permute-start | bytes 442376 | tf_op jit(solution)/shard_map/ppermute | solution.py:1208
  97.7 12.7 %collective-permute-start.22 = (bf16[1,448,128]{2,1,0:T(8,128)(2,1)S(1)}, bf16[1,448,128]{2,1,0:T(8,128)(2,1)S(1)}, u32[]{:S(2)}, u32[]{:S(2)}) collective-permute-start(bf16[1,448,128]{2,1,0:T(8,128)(2,1)S(1)} %get-tuple-element.135), channel_id=1, source_target_pairs={{0,4},{1,5},{2,6},{3,7},{4,0},{5,1},{6,2},{7,3},{8,12},{9,13},{10,... | collective-permute-start | bytes 344072 | tf_op jit(solution)/shard_map/ppermute | solution.py:1208
  97.7 12.7 %collective-permute-start.23 = (bf16[1,448,128]{2,1,0:T(8,128)(2,1)S(1)}, bf16[1,448,128]{2,1,0:T(8,128)(2,1)S(1)}, u32[]{:S(2)}, u32[]{:S(2)}) collective-permute-start(bf16[1,448,128]{2,1,0:T(8,128)(2,1)S(1)} %get-tuple-element.136), channel_id=1, source_target_pairs={{0,6},{1,7},{2,4},{3,5},{4,2},{5,3},{6,0},{7,1},{8,14},{9,15},{10,... | collective-permute-start | bytes 344072 | tf_op jit(solution)/shard_map/ppermute | solution.py:1208
  98.3 12.1 %collective-permute-start.24 = (bf16[1,448,128]{2,1,0:T(8,128)(2,1)S(1)}, bf16[1,448,128]{2,1,0:T(8,128)(2,1)S(1)}, u32[]{:S(2)}, u32[]{:S(2)}) collective-permute-start(bf16[1,448,128]{2,1,0:T(8,128)(2,1)S(1)} %get-tuple-element.137), channel_id=1, source_target_pairs={{0,2},{1,3},{2,0},{3,1},{4,6},{5,7},{6,4},{7,5},{8,10},{9,11},{10,... | collective-permute-start | bytes 344072 | tf_op jit(solution)/shard_map/ppermute | solution.py:1208
  110.7 6.2 %collective-permute-start.25 = (bf16[448,128]{1,0:T(8,128)(2,1)S(1)}, bf16[448,128]{1,0:T(8,128)(2,1)S(1)}, u32[]{:S(2)}, u32[]{:S(2)}) collective-permute-start(bf16[448,128]{1,0:T(8,128)(2,1)S(1)} %get-tuple-element.139), channel_id=1, source_target_pairs={{0,24},{8,16},{16,8},{24,0},{1,25},{9,17},{17,9},{25,1},{2,26},{10... | collective-permute-start | bytes 344072 | tf_op jit(solution)/shard_map/ppermute | solution.py:1208
  110.8 6.4 %collective-permute-start.26 = (bf16[448,128]{1,0:T(8,128)(2,1)S(1)}, bf16[448,128]{1,0:T(8,128)(2,1)S(1)}, u32[]{:S(2)}, u32[]{:S(2)}) collective-permute-start(bf16[448,128]{1,0:T(8,128)(2,1)S(1)} %get-tuple-element.140), channel_id=1, source_target_pairs={{0,16},{8,24},{16,0},{24,8},{1,17},{9,25},{17,1},{25,9},{2,18},{10... | collective-permute-start | bytes 344072 | tf_op jit(solution)/shard_map/ppermute | solution.py:1208
  112.7 4.8 %collective-permute-start.27 = (bf16[448,128]{1,0:T(8,128)(2,1)S(1)}, bf16[448,128]{1,0:T(8,128)(2,1)S(1)}, u32[]{:S(2)}, u32[]{:S(2)}) collective-permute-start(bf16[448,128]{1,0:T(8,128)(2,1)S(1)} %get-tuple-element.141), channel_id=1, source_target_pairs={{0,8},{8,0},{16,24},{24,16},{1,9},{9,1},{17,25},{25,17},{2,10},{10... | collective-permute-start | bytes 344072 | tf_op jit(solution)/shard_map/ppermute | solution.py:1208
  119.5 5.4 %collective-permute-start.31 = (f32[8,128]{1,0:T(8,128)S(1)}, f32[8,128]{1,0:T(8,128)S(1)}, u32[]{:S(2)}, u32[]{:S(2)}) collective-permute-start(f32[8,128]{1,0:T(8,128)S(1)} %shard_map.155.refs_0_), channel_id=1, source_target_pairs={{0,6},{1,7},{2,4},{3,5},{4,2},{5,3},{6,0},{7,1},{8,14},{9,15},{10,... | collective-permute-start | bytes 12296 | tf_op jit(solution)/shard_map/ppermute | solution.py:1208
  120.5 4.9 %collective-permute-start.30 = (f32[8,128]{1,0:T(8,128)S(1)}, f32[8,128]{1,0:T(8,128)S(1)}, u32[]{:S(2)}, u32[]{:S(2)}) collective-permute-start(f32[8,128]{1,0:T(8,128)S(1)} %shard_map.155.refs_0_), channel_id=1, source_target_pairs={{0,4},{1,5},{2,6},{3,7},{4,0},{5,1},{6,2},{7,3},{8,12},{9,13},{10,... | collective-permute-start | bytes 12296 | tf_op jit(solution)/shard_map/ppermute | solution.py:1208
  123.7 3.6 %collective-permute-start.29 = (f32[8,128]{1,0:T(8,128)S(1)}, f32[8,128]{1,0:T(8,128)S(1)}, u32[]{:S(2)}, u32[]{:S(2)}) collective-permute-start(f32[8,128]{1,0:T(8,128)S(1)} %shard_map.155.refs_0_), channel_id=1, source_target_pairs={{0,2},{1,3},{2,0},{3,1},{4,6},{5,7},{6,4},{7,5},{8,10},{9,11},{10,... | collective-permute-start | bytes 12296 | tf_op jit(solution)/shard_map/ppermute | solution.py:1208
  127.3 4.5 %collective-permute-start.34 = (f32[8,128]{1,0:T(8,128)S(1)}, f32[8,128]{1,0:T(8,128)S(1)}, u32[]{:S(2)}, u32[]{:S(2)}) collective-permute-start(f32[8,128]{1,0:T(8,128)S(1)} %shard_map.156.refs_0_), channel_id=1, source_target_pairs={{0,24},{8,16},{16,8},{24,0},{1,25},{9,17},{17,9},{25,1},{2,26},{10... | collective-permute-start | bytes 12296 | tf_op jit(solution)/shard_map/ppermute | solution.py:1208
  128.8 3.6 %collective-permute-start.33 = (f32[8,128]{1,0:T(8,128)S(1)}, f32[8,128]{1,0:T(8,128)S(1)}, u32[]{:S(2)}, u32[]{:S(2)}) collective-permute-start(f32[8,128]{1,0:T(8,128)S(1)} %shard_map.156.refs_0_), channel_id=1, source_target_pairs={{0,16},{8,24},{16,0},{24,8},{1,17},{9,25},{17,1},{25,9},{2,18},{10... | collective-permute-start | bytes 12296 | tf_op jit(solution)/shard_map/ppermute | solution.py:1208
  130.2 3.6 %collective-permute-start.32 = (f32[8,128]{1,0:T(8,128)S(1)}, f32[8,128]{1,0:T(8,128)S(1)}, u32[]{:S(2)}, u32[]{:S(2)}) collective-permute-start(f32[8,128]{1,0:T(8,128)S(1)} %shard_map.156.refs_0_), channel_id=1, source_target_pairs={{0,8},{8,0},{16,24},{24,16},{1,9},{9,1},{17,25},{25,17},{2,10},{10... | collective-permute-start | bytes 12296 | tf_op jit(solution)/shard_map/ppermute | solution.py:1208
  (14 other events, 85.9 us)

commit v9 on v8

--- a/solution.py
+++ b/solution.py
@@ -80,7 +80,7 @@
         units = self.tail // 16
         ends = [units * (i + 1) // FAR_PARTS * 16 for i in range(FAR_PARTS)]
         self.far = list(zip([0] + ends[:-1], ends))
-        self.upper = self.win * 3 // 4 // 16 * 16
+        self.upper = self.win * 13 // 16 // 16 * 16
         self.vec_place = ROW_VEC - self.start[-1]
         self.vec_from = self.vec_place // 16 * 16
         self.kept_row = 2 * self.win - self.vec_from

time: 135 us -> 135 us (level)
  transfers between devices with their start and end apart: 35 -> 35, of which waited for: 22 -> 21; matrix products, arithmetic and copies ran while one was open for 0% -> 0% of each run, Pallas kernels for 25% -> 25%
where the time goes in v9:
time: 135 us
  Pallas kernels  53.7 us (40%)
  starting transfers between devices  39.1 us (29%)
  waiting for transfers between devices  38.7 us (29%)
  local copies, waits for them, and re-layouts  2.8 us (2%)
    ppermute x35, starting transfers between devices, swap(): return lax.ppermute(x, axis, [(i, i ^ mask) for i in range(size)])  39.1 us
    ppermute x35, waiting for transfers between devices, swap(): return lax.ppermute(x, axis, [(i, i ^ mask) for i in range(size)])  38.7 us
    pallas_call x1, Pallas kernels, middle_part(): pl.pallas_call(functools.partial(middle_kernel, plan), out_shape=(jax.Sha...  17.6 us
    pallas_call x1, Pallas kernels, backward(): pl.pallas_call(functools.partial(backward_kernel, plan), out_shape=(jax.S...  12 us
    pallas_call x1, Pallas kernels, forward(): pl.pallas_call(functools.partial(forward_kernel, plan), out_shape=(jax.Sh...  8.72 us
    pallas_call x1, Pallas kernels, project_part(): pl.pallas_call(functools.partial(project_kernel, plan), out_shape=(jax.Sh...  3.72 us
    pallas_call x1, Pallas kernels, finish_part(): pl.pallas_call(functools.partial(finish_kernel, plan), out_shape=(jax.Sha...  2.9 us
    unnamed x22, local copies, waits for them, and re-layouts  2.8 us
  transfers between devices with their start and end apart: 35, of which 21 were waited for; matrix products, arithmetic and copies ran while one was open for 0% of the time, Pallas kernels for 25%

profile of v9, /device:TPU:0, one launch (start us, length us, event | category | flops | bytes accessed | tf_op | source)
XLA Modules:
  0.0 135.2 jit_solution(4349512362183624252)
XLA Ops:
  1.7 5.1 %collective-permute-start.2 = (bf16[352,128]{1,0:T(8,128)(2,1)S(1)}, bf16[352,128]{1,0:T(8,128)(2,1)S(1)}, u32[]{:S(2)}, u32[]{:S(2)}) collective-permute-start(bf16[352,128]{1,0:T(8,128)(2,1)S(1)} %get-tuple-element.81.refs_0_), channel_id=1, source_target_pairs={{0,6},{1,7},{2,4},{3,5},{4,2},{5,3},{6,0},{7,1},{8,14},{9,15},{10,... | collective-permute-start | bytes 270344 | tf_op jit(solution)/shard_map/ppermute | solution.py:1208
  7.5 1.6 %collective-permute-start.3 = (bf16[96,128]{1,0:T(8,128)(2,1)S(1)}, bf16[96,128]{1,0:T(8,128)(2,1)S(1)}, u32[]{:S(2)}, u32[]{:S(2)}) collective-permute-start(bf16[96,128]{1,0:T(8,128)(2,1)S(1)} %get-tuple-element.82.refs_0_), channel_id=1, source_target_pairs={{0,8},{8,0},{16,24},{24,16},{1,9},{9,1},{17,25},{25,17},{2,10},{10... | collective-permute-start | bytes 73736 | tf_op jit(solution)/shard_map/ppermute | solution.py:1208
  9.1 2.2 %collective-permute-done.3.refs_1_ = bf16[96,128]{1,0:T(8,128)(2,1)S(1)} collective-permute-done((bf16[96,128]{1,0:T(8,128)(2,1)S(1)}, bf16[96,128]{1,0:T(8,128)(2,1)S(1)}, u32[]{:S(2)}, u32[]{:S(2)}) %collective-permute-start.3) | collective-permute-done | bytes 24608 | tf_op jit(solution)/shard_map/ppermute | solution.py:1208
  11.3 1.7 %collective-permute-start.4 = (bf16[2,96,128]{2,1,0:T(8,128)(2,1)S(1)}, bf16[2,96,128]{2,1,0:T(8,128)(2,1)S(1)}, u32[]{:S(2)}, u32[]{:S(2)}) collective-permute-start(bf16[2,96,128]{2,1,0:T(8,128)(2,1)S(1)} %shard_map.136.mine_ref), channel_id=1, source_target_pairs={{0,16},{8,24},{16,0},{24,8},{1,17},{9,25},{17,1},{25,9},{2,18},{10... | collective-permute-start | bytes 147464 | tf_op jit(solution)/shard_map/ppermute | solution.py:1208
  15.5 2.7 %collective-permute-start.7 = (bf16[4,352,128]{2,1,0:T(8,128)(2,1)S(1)}, bf16[4,352,128]{2,1,0:T(8,128)(2,1)S(1)}, u32[]{:S(2)}, u32[]{:S(2)}) collective-permute-start(bf16[4,352,128]{2,1,0:T(8,128)(2,1)S(1)} %shard_map.139.refs_0_), channel_id=1, source_target_pairs={{0,24},{8,16},{16,8},{24,0},{1,25},{9,17},{17,9},{25,1},{2,26},{10... | collective-permute-start | bytes 1081352 | tf_op jit(solution)/shard_map/ppermute | solution.py:1208
  19.0 3.7 %collective-permute-start.10 = (bf16[4,96,128]{2,1,0:T(8,128)(2,1)S(1)}, bf16[4,96,128]{2,1,0:T(8,128)(2,1)S(1)}, u32[]{:S(2)}, u32[]{:S(2)}) collective-permute-start(bf16[4,96,128]{2,1,0:T(8,128)(2,1)S(1)} %shard_map.138.refs_4_.refs_0_), channel_id=1, source_target_pairs={{0,6},{1,7},{2,4},{3,5},{4,2},{5,3},{6,0},{7,1},{8,14},{9,15},{10,... | collective-permute-start | bytes 294920 | tf_op jit(solution)/shard_map/ppermute | solution.py:1208
  22.8 2.8 %collective-permute-done.10.refs_3_ = bf16[4,96,128]{2,1,0:T(8,128)(2,1)S(1)} collective-permute-done((bf16[4,96,128]{2,1,0:T(8,128)(2,1)S(1)}, bf16[4,96,128]{2,1,0:T(8,128)(2,1)S(1)}, u32[]{:S(2)}, u32[]{:S(2)}) %collective-permute-start.10) | collective-permute-done | bytes 98336 | tf_op jit(solution)/shard_map/ppermute | solution.py:1208
  26.5 2.1 %collective-permute-done.9.refs_2_ = bf16[4,96,128]{2,1,0:T(8,128)(2,1)S(1)} collective-permute-done((bf16[4,96,128]{2,1,0:T(8,128)(2,1)S(1)}, bf16[4,96,128]{2,1,0:T(8,128)(2,1)S(1)}, u32[]{:S(2)}, u32[]{:S(2)}) %collective-permute-start.9) | collective-permute-done | bytes 98336 | tf_op jit(solution)/shard_map/ppermute | solution.py:1208
  28.6 1.6 %collective-permute-done.8.refs_1_ = bf16[4,96,128]{2,1,0:T(8,128)(2,1)S(1)} collective-permute-done((bf16[4,96,128]{2,1,0:T(8,128)(2,1)S(1)}, bf16[4,96,128]{2,1,0:T(8,128)(2,1)S(1)}, u32[]{:S(2)}, u32[]{:S(2)}) %collective-permute-start.8) | collective-permute-done | bytes 98336 | tf_op jit(solution)/shard_map/ppermute | solution.py:1208
  30.2 2.2 %collective-permute-done.6.refs_2_ = bf16[4,352,128]{2,1,0:T(8,128)(2,1)S(1)} collective-permute-done((bf16[4,352,128]{2,1,0:T(8,128)(2,1)S(1)}, bf16[4,352,128]{2,1,0:T(8,128)(2,1)S(1)}, u32[]{:S(2)}, u32[]{:S(2)}) %collective-permute-start.6) | collective-permute-done | bytes 360480 | tf_op jit(solution)/shard_map/ppermute | solution.py:1208
  34.9 3.7 %shard_map.142 = (bf16[384,1152]{1,0:T(8,128)(2,1)S(1)}, f32[8,384]{1,0:T(8,128)S(1)}, f32[8,128]{1,0:T(8,128)S(1)}, f32[8,128]{1,0:T(8,128)S(1)}, bf16[1024,384...) custom-call(bf16[4,512,128]{2,1,0:T(8,128)(2,1)S(1)} %get-tuple-elem, ...), custom_call_target="tpu_custom_call" | custom-call | flops 1000 | bytes 1000 | tf_op jit(solution)/shard_map/pallas_call | solution.py:360
  38.7 8.7 %shard_map.143 = (bf16[1024,384]{1,0:T(8,128)(2,1)S(1)}, bf16[4,384,256]{2,1,0:T(8,128)(2,1)S(1)}, f32[4,384,256]{2,1,0:T(8,128)S(1)}, f32[4,8,256]{2,1,0:T(8,12...) custom-call(s32[1024]{0:T(1024)S(1)} %copy-done.7, s32[1,1024]{1,0:T(1,128)S(1)} %bitcast.22, ...), custom_call_target="tpu_custom_call" | custom-call | flops 1000 | bytes 1000 | tf_op jit(solution)/shard_map/pallas_call | solution.py:458
  47.5 17.6 %shard_map.144 = (bf16[1024,384]{1,0:T(8,128)(2,1)}, f32[1024,384]{1,0:T(8,128)S(1)}, bf16[1024,384]{1,0:T(8,128)(2,1)S(1)}, bf16[3,4,448,128]{3,2,1,0:T(8,128)(...) custom-call(bf16[4,448,128]{2,1,0:T(8,128)(2,1)S(1)} %get-tuple-element.84.refs_0_, ...), custom_call_target="tpu_custom_call" | custom-call | flops 1000 | bytes 1000 | tf_op jit(solution)/shard_map/pallas_call | solution.py:614
  65.1 1.5 %shard_map.145 = (bf16[3,8,2,128,128]{4,3,2,1,0:T(8,128)(2,1)S(1)}, bf16[3,4,512,128]{3,2,1,0:T(8,128)(2,1)S(1)}, bf16[3,4,512,128]{3,2,1,0:T(8,128)(2,1)S(1)}, ...) custom-call(f32[8,384]{1,0:T(8,128)S(1)} %get-tuple-element.96.refs_, ...), custom_call_target="tpu_custom_call" | custom-call | flops 1000 | bytes 1000 | tf_op jit(solution)/shard_map/pallas_call | solution.py:678
  66.6 1.6 %collective-permute-done.15.refs_1_ = bf16[3,4,448,128]{3,2,1,0:T(8,128)(2,1)S(1)} collective-permute-done((bf16[3,4,448,128]{3,2,1,0:T(8,128)(2,1)S(1)}, bf16[3,4,448,128]{3,2,1,0:T(8,128)(2,1)S(1)}, u32[]{:S(2)}, u32[]{:S(2)}) %collective-permute-start.15) | collective-permute-done | bytes 1376288 | tf_op jit(solution)/shard_map/ppermute | solution.py:1208
  68.6 2.0 %collective-permute-start.16 = (bf16[3,1,448,128]{3,2,0,1:T(8,128)(2,1)S(1)}, bf16[3,1,448,128]{3,2,0,1:T(8,128)(2,1)S(1)}, u32[]{:S(2)}, u32[]{:S(2)}) collective-permute-start(bf16[3,1,448,128]{3,2,0,1:T(8,128)(2,1)S(1)} %bitcast.29), channel_id=1, source_target_pairs={{0,4},{1,5},{2,6},{3,7},{4,0},{5,1},{6,2},{7,3},{8,12},{9,13},{10,... | collective-permute-start | bytes 1032200 | tf_op jit(solution)/shard_map/ppermute | solution.py:1208
  70.5 1.5 %collective-permute-start.17 = (bf16[3,1,448,128]{3,2,0,1:T(8,128)(2,1)S(1)}, bf16[3,1,448,128]{3,2,0,1:T(8,128)(2,1)S(1)}, u32[]{:S(2)}, u32[]{:S(2)}) collective-permute-start(bf16[3,1,448,128]{3,2,0,1:T(8,128)(2,1)S(1)} %bitcast.28), channel_id=1, source_target_pairs={{0,6},{1,7},{2,4},{3,5},{4,2},{5,3},{6,0},{7,1},{8,14},{9,15},{10,... | collective-permute-start | bytes 1032200 | tf_op jit(solution)/shard_map/ppermute | solution.py:1208
  72.3 12.0 %shard_map.147 = (bf16[1024,1152]{1,0:T(8,128)(2,1)S(1)}, f32[8,384]{1,0:T(8,128)S(1)}) custom-call(f32[8,384]{1,0:T(8,128)S(1)} %get-tuple-element.96.refs_12_.vec_ref, s32[1024]{0:T(1024)S(1)} %copy-done.7, s32[1,1024]{1,0:T(1,128)S(1)} %bitcast.23, f32[4,8,256]{2,1,0:T(8,128)S(1)} %get-tuple-element.104.lse_ref, ...), custom_call_target="tpu_custom_call" | custom-call | flops 1000 | bytes 1000 | tf_op jit(solution)/shard_map/pallas_call | solution.py:794
  84.3 2.9 %shard_map.148 = (f32[1024,384]{1,0:T(8,128)S(1)}, bf16[4,448,128]{2,1,0:T(8,128)(2,1)S(1)}, bf16[4,144,128]{2,1,0:T(8,128)(2,1)S(1)}, bf16[4,144,128]{2,1,0:T(8,128)(2,1)S(1)}, bf16[4,160,128]{2,1,0:T(8,128)(2,1)S(1)}) custom-call(f32[1024,384]{1,0:T(8,128)S(1)} %get-tuple-element.88.hat_in_ref.hat_ref, ...), custom_call_target="tpu_custom_call" | custom-call | flops 1000 | bytes 1000 | tf_op jit(solution)/shard_map/pallas_call | solution.py:872
  87.8 7.1 %collective-permute-done.16 = bf16[3,1,448,128]{3,2,0,1:T(8,128)(2,1)S(1)} collective-permute-done((bf16[3,1,448,128]{3,2,0,1:T(8,128)(2,1)S(1)}, bf16[3,1,448,128]{3,2,0,1:T(8,128)(2,1)S(1)}, u32[]{:S(2)}, u32[]{:S(2)}) %collective-permute-start.16) | collective-permute-done | bytes 344096 | tf_op jit(solution)/shard_map/ppermute | solution.py:1208
  95.0 1.3 collective-permute-done.20.refs_2_
  97.0 2.4 %collective-permute-start.23 = (bf16[1,448,128]{2,1,0:T(8,128)(2,1)S(1)}, bf16[1,448,128]{2,1,0:T(8,128)(2,1)S(1)}, u32[]{:S(2)}, u32[]{:S(2)}) collective-permute-start(bf16[1,448,128]{2,1,0:T(8,128)(2,1)S(1)} %get-tuple-element.136), channel_id=1, source_target_pairs={{0,6},{1,7},{2,4},{3,5},{4,2},{5,3},{6,0},{7,1},{8,14},{9,15},{10,... | collective-permute-start | bytes 344072 | tf_op jit(solution)/shard_map/ppermute | solution.py:1208
  99.3 1.1 collective-permute-start.24
  100.5 2.5 %shard_map.149 = (f32[1024,384]{1,0:T(8,128)}, f32[448,128]{1,0:T(8,128)S(1)}, f32[448,128]{1,0:T(8,128)S(1)}, f32[448,128]{1,0:T(8,128)S(1)}, f32[8,128]{1,0:T(8,128)S(1)}) custom-call(f32[1024,384]{1,0:T(8,128)S(1)} %get-tuple-element.88.hat_in_ref.hat_ref, f32[1024,128]{1,0:T(8,128)S(1)} %get-tuple-element.98.rstd_ref, ...), custom_call_target="tpu_custom_call" | custom-call | flops 1000 | bytes 1000 | tf_op jit(solution)/shard_map/pallas_call | solution.py:913
  103.0 6.7 %collective-permute-done.22 = bf16[1,448,128]{2,1,0:T(8,128)(2,1)S(1)} collective-permute-done((bf16[1,448,128]{2,1,0:T(8,128)(2,1)S(1)}, bf16[1,448,128]{2,1,0:T(8,128)(2,1)S(1)}, u32[]{:S(2)}, u32[]{:S(2)}) %collective-permute-start.22) | collective-permute-done | bytes 114720 | tf_op jit(solution)/shard_map/ppermute | solution.py:1208
  110.2 2.8 %collective-permute-start.26 = (bf16[448,128]{1,0:T(8,128)(2,1)S(1)}, bf16[448,128]{1,0:T(8,128)(2,1)S(1)}, u32[]{:S(2)}, u32[]{:S(2)}) collective-permute-start(bf16[448,128]{1,0:T(8,128)(2,1)S(1)} %get-tuple-element.140), channel_id=1, source_target_pairs={{0,16},{8,24},{16,0},{24,8},{1,17},{9,25},{17,1},{25,9},{2,18},{10... | collective-permute-start | bytes 344072 | tf_op jit(solution)/shard_map/ppermute | solution.py:1208
  114.0 2.8 %collective-permute-done.25.got0_ref = bf16[448,128]{1,0:T(8,128)(2,1)S(1)} collective-permute-done((bf16[448,128]{1,0:T(8,128)(2,1)S(1)}, bf16[448,128]{1,0:T(8,128)(2,1)S(1)}, u32[]{:S(2)}, u32[]{:S(2)}) %collective-permute-start.25) | collective-permute-done | bytes 114720 | tf_op jit(solution)/shard_map/ppermute | solution.py:1208
  119.0 1.2 collective-permute-done.28.refs_1_
  120.2 3.3 %collective-permute-start.31 = (f32[8,128]{1,0:T(8,128)S(1)}, f32[8,128]{1,0:T(8,128)S(1)}, u32[]{:S(2)}, u32[]{:S(2)}) collective-permute-start(f32[8,128]{1,0:T(8,128)S(1)} %shard_map.155.refs_0_), channel_id=1, source_target_pairs={{0,6},{1,7},{2,4},{3,5},{4,2},{5,3},{6,0},{7,1},{8,14},{9,15},{10,... | collective-permute-start | bytes 12296 | tf_op jit(solution)/shard_map/ppermute | solution.py:1208
  123.4 1.6 %collective-permute-start.30 = (f32[8,128]{1,0:T(8,128)S(1)}, f32[8,128]{1,0:T(8,128)S(1)}, u32[]{:S(2)}, u32[]{:S(2)}) collective-permute-start(f32[8,128]{1,0:T(8,128)S(1)} %shard_map.155.refs_0_), channel_id=1, source_target_pairs={{0,4},{1,5},{2,6},{3,7},{4,0},{5,1},{6,2},{7,3},{8,12},{9,13},{10,... | collective-permute-start | bytes 12296 | tf_op jit(solution)/shard_map/ppermute | solution.py:1208
  125.6 2.4 %collective-permute-done.30.refs_2_ = f32[8,128]{1,0:T(8,128)S(1)} collective-permute-done((f32[8,128]{1,0:T(8,128)S(1)}, f32[8,128]{1,0:T(8,128)S(1)}, u32[]{:S(2)}, u32[]{:S(2)}) %collective-permute-start.30) | collective-permute-done | bytes 4128 | tf_op jit(solution)/shard_map/ppermute | solution.py:1208
  130.6 1.5 %collective-permute-start.32 = (f32[8,128]{1,0:T(8,128)S(1)}, f32[8,128]{1,0:T(8,128)S(1)}, u32[]{:S(2)}, u32[]{:S(2)}) collective-permute-start(f32[8,128]{1,0:T(8,128)S(1)} %shard_map.156.refs_0_), channel_id=1, source_target_pairs={{0,8},{8,0},{16,24},{24,16},{1,9},{9,1},{17,25},{25,17},{2,10},{10... | collective-permute-start | bytes 12296 | tf_op jit(solution)/shard_map/ppermute | solution.py:1208
  (83 shorter events, 20.6 us)
Async XLA Ops:
  1.7 13.7 %collective-permute-start.2 = (bf16[352,128]{1,0:T(8,128)(2,1)S(1)}, bf16[352,128]{1,0:T(8,128)(2,1)S(1)}, u32[]{:S(2)}, u32[]{:S(2)}) collective-permute-start(bf16[352,128]{1,0:T(8,128)(2,1)S(1)} %get-tuple-element.81.refs_0_), channel_id=1, source_target_pairs={{0,6},{1,7},{2,4},{3,5},{4,2},{5,3},{6,0},{7,1},{8,14},{9,15},{10,... | collective-permute-start | bytes 270344 | tf_op jit(solution)/shard_map/ppermute | solution.py:1208
  6.8 8.6 %collective-permute-start.1 = (bf16[352,128]{1,0:T(8,128)(2,1)S(1)}, bf16[352,128]{1,0:T(8,128)(2,1)S(1)}, u32[]{:S(2)}, u32[]{:S(2)}) collective-permute-start(bf16[352,128]{1,0:T(8,128)(2,1)S(1)} %get-tuple-element.81.refs_0_), channel_id=1, source_target_pairs={{0,4},{1,5},{2,6},{3,7},{4,0},{5,1},{6,2},{7,3},{8,12},{9,13},{10,... | collective-permute-start | bytes 270344 | tf_op jit(solution)/shard_map/ppermute | solution.py:1208
  6.8 8.6 %collective-permute-start = (bf16[352,128]{1,0:T(8,128)(2,1)S(1)}, bf16[352,128]{1,0:T(8,128)(2,1)S(1)}, u32[]{:S(2)}, u32[]{:S(2)}) collective-permute-start(bf16[352,128]{1,0:T(8,128)(2,1)S(1)} %get-tuple-element.81.refs_0_), channel_id=1, source_target_pairs={{0,2},{1,3},{2,0},{3,1},{4,6},{5,7},{6,4},{7,5},{8,10},{9,11},{10,... | collective-permute-start | bytes 270344 | tf_op jit(solution)/shard_map/ppermute | solution.py:1208
  7.5 3.8 %collective-permute-start.3 = (bf16[96,128]{1,0:T(8,128)(2,1)S(1)}, bf16[96,128]{1,0:T(8,128)(2,1)S(1)}, u32[]{:S(2)}, u32[]{:S(2)}) collective-permute-start(bf16[96,128]{1,0:T(8,128)(2,1)S(1)} %get-tuple-element.82.refs_0_), channel_id=1, source_target_pairs={{0,8},{8,0},{16,24},{24,16},{1,9},{9,1},{17,25},{25,17},{2,10},{10... | collective-permute-start | bytes 73736 | tf_op jit(solution)/shard_map/ppermute | solution.py:1208
  11.3 4.1 %collective-permute-start.4 = (bf16[2,96,128]{2,1,0:T(8,128)(2,1)S(1)}, bf16[2,96,128]{2,1,0:T(8,128)(2,1)S(1)}, u32[]{:S(2)}, u32[]{:S(2)}) collective-permute-start(bf16[2,96,128]{2,1,0:T(8,128)(2,1)S(1)} %shard_map.136.mine_ref), channel_id=1, source_target_pairs={{0,16},{8,24},{16,0},{24,8},{1,17},{9,25},{17,1},{25,9},{2,18},{10... | collective-permute-start | bytes 147464 | tf_op jit(solution)/shard_map/ppermute | solution.py:1208
  15.5 14.8 %collective-permute-start.7 = (bf16[4,352,128]{2,1,0:T(8,128)(2,1)S(1)}, bf16[4,352,128]{2,1,0:T(8,128)(2,1)S(1)}, u32[]{:S(2)}, u32[]{:S(2)}) collective-permute-start(bf16[4,352,128]{2,1,0:T(8,128)(2,1)S(1)} %shard_map.139.refs_0_), channel_id=1, source_target_pairs={{0,24},{8,16},{16,8},{24,0},{1,25},{9,17},{17,9},{25,1},{2,26},{10... | collective-permute-start | bytes 1081352 | tf_op jit(solution)/shard_map/ppermute | solution.py:1208
  18.1 14.3 %collective-permute-start.6 = (bf16[4,352,128]{2,1,0:T(8,128)(2,1)S(1)}, bf16[4,352,128]{2,1,0:T(8,128)(2,1)S(1)}, u32[]{:S(2)}, u32[]{:S(2)}) collective-permute-start(bf16[4,352,128]{2,1,0:T(8,128)(2,1)S(1)} %shard_map.139.refs_0_), channel_id=1, source_target_pairs={{0,16},{8,24},{16,0},{24,8},{1,17},{9,25},{17,1},{25,9},{2,18},{10... | collective-permute-start | bytes 1081352 | tf_op jit(solution)/shard_map/ppermute | solution.py:1208
  18.6 14.1 %collective-permute-start.5 = (bf16[4,352,128]{2,1,0:T(8,128)(2,1)S(1)}, bf16[4,352,128]{2,1,0:T(8,128)(2,1)S(1)}, u32[]{:S(2)}, u32[]{:S(2)}) collective-permute-start(bf16[4,352,128]{2,1,0:T(8,128)(2,1)S(1)} %shard_map.139.refs_0_), channel_id=1, source_target_pairs={{0,8},{8,0},{16,24},{24,16},{1,9},{9,1},{17,25},{25,17},{2,10},{10... | collective-permute-start | bytes 1081352 | tf_op jit(solution)/shard_map/ppermute | solution.py:1208
  19.0 6.6 %collective-permute-start.10 = (bf16[4,96,128]{2,1,0:T(8,128)(2,1)S(1)}, bf16[4,96,128]{2,1,0:T(8,128)(2,1)S(1)}, u32[]{:S(2)}, u32[]{:S(2)}) collective-permute-start(bf16[4,96,128]{2,1,0:T(8,128)(2,1)S(1)} %shard_map.138.refs_4_.refs_0_), channel_id=1, source_target_pairs={{0,6},{1,7},{2,4},{3,5},{4,2},{5,3},{6,0},{7,1},{8,14},{9,15},{10,... | collective-permute-start | bytes 294920 | tf_op jit(solution)/shard_map/ppermute | solution.py:1208
  22.8 5.8 %collective-permute-start.9 = (bf16[4,96,128]{2,1,0:T(8,128)(2,1)S(1)}, bf16[4,96,128]{2,1,0:T(8,128)(2,1)S(1)}, u32[]{:S(2)}, u32[]{:S(2)}) collective-permute-start(bf16[4,96,128]{2,1,0:T(8,128)(2,1)S(1)} %shard_map.138.refs_4_.refs_0_), channel_id=1, source_target_pairs={{0,4},{1,5},{2,6},{3,7},{4,0},{5,1},{6,2},{7,3},{8,12},{9,13},{10,... | collective-permute-start | bytes 294920 | tf_op jit(solution)/shard_map/ppermute | solution.py:1208
  25.6 4.6 %collective-permute-start.8 = (bf16[4,96,128]{2,1,0:T(8,128)(2,1)S(1)}, bf16[4,96,128]{2,1,0:T(8,128)(2,1)S(1)}, u32[]{:S(2)}, u32[]{:S(2)}) collective-permute-start(bf16[4,96,128]{2,1,0:T(8,128)(2,1)S(1)} %shard_map.138.refs_4_.refs_0_), channel_id=1, source_target_pairs={{0,2},{1,3},{2,0},{3,1},{4,6},{5,7},{6,4},{7,5},{8,10},{9,11},{10,... | collective-permute-start | bytes 294920 | tf_op jit(solution)/shard_map/ppermute | solution.py:1208
  33.0 14.4 %collective-permute-start.11 = (bf16[4,448,128]{2,1,0:T(8,128)(2,1)S(1)}, bf16[4,448,128]{2,1,0:T(8,128)(2,1)S(1)}, u32[]{:S(2)}, u32[]{:S(2)}) collective-permute-start(bf16[4,448,128]{2,1,0:T(8,128)(2,1)S(1)} %get-tuple-element.84.refs_0_), channel_id=1, source_target_pairs={{0,1},{1,0},{2,3},{3,2},{4,5},{5,4},{6,7},{7,6},{8,9},{9,8},{10,11... | collective-permute-start | bytes 1376264 | tf_op jit(solution)/shard_map/ppermute | solution.py:1208
  33.5 13.9 %collective-permute-start.12 = (bf16[4,448,128]{2,1,0:T(8,128)(2,1)S(1)}, bf16[4,448,128]{2,1,0:T(8,128)(2,1)S(1)}, u32[]{:S(2)}, u32[]{:S(2)}) collective-permute-start(bf16[4,448,128]{2,1,0:T(8,128)(2,1)S(1)} %get-tuple-element.85.refs_1_), channel_id=1, source_target_pairs={{0,1},{1,0},{2,3},{3,2},{4,5},{5,4},{6,7},{7,6},{8,9},{9,8},{10,11... | collective-permute-start | bytes 1376264 | tf_op jit(solution)/shard_map/ppermute | solution.py:1208
  33.6 13.9 %collective-permute-start.13 = (bf16[4,448,128]{2,1,0:T(8,128)(2,1)S(1)}, bf16[4,448,128]{2,1,0:T(8,128)(2,1)S(1)}, u32[]{:S(2)}, u32[]{:S(2)}) collective-permute-start(bf16[4,448,128]{2,1,0:T(8,128)(2,1)S(1)} %get-tuple-element.86.refs_2_), channel_id=1, source_target_pairs={{0,1},{1,0},{2,3},{3,2},{4,5},{5,4},{6,7},{7,6},{8,9},{9,8},{10,11... | collective-permute-start | bytes 1376264 | tf_op jit(solution)/shard_map/ppermute | solution.py:1208
  65.1 3.1 %collective-permute-start.15 = (bf16[3,4,448,128]{3,2,1,0:T(8,128)(2,1)S(1)}, bf16[3,4,448,128]{3,2,1,0:T(8,128)(2,1)S(1)}, u32[]{:S(2)}, u32[]{:S(2)}) collective-permute-start(bf16[3,4,448,128]{3,2,1,0:T(8,128)(2,1)S(1)} %get-tuple-element.115), channel_id=1, source_target_pairs={{0,1},{1,0},{2,3},{3,2},{4,5},{5,4},{6,7},{7,6},{8,9},{9,8},{10,11... | collective-permute-start | bytes 4128776 | tf_op jit(solution)/shard_map/ppermute | solution.py:1208
  68.6 26.4 %collective-permute-start.16 = (bf16[3,1,448,128]{3,2,0,1:T(8,128)(2,1)S(1)}, bf16[3,1,448,128]{3,2,0,1:T(8,128)(2,1)S(1)}, u32[]{:S(2)}, u32[]{:S(2)}) collective-permute-start(bf16[3,1,448,128]{3,2,0,1:T(8,128)(2,1)S(1)} %bitcast.29), channel_id=1, source_target_pairs={{0,4},{1,5},{2,6},{3,7},{4,0},{5,1},{6,2},{7,3},{8,12},{9,13},{10,... | collective-permute-start | bytes 1032200 | tf_op jit(solution)/shard_map/ppermute | solution.py:1208
  70.5 32.4 %collective-permute-start.17 = (bf16[3,1,448,128]{3,2,0,1:T(8,128)(2,1)S(1)}, bf16[3,1,448,128]{3,2,0,1:T(8,128)(2,1)S(1)}, u32[]{:S(2)}, u32[]{:S(2)}) collective-permute-start(bf16[3,1,448,128]{3,2,0,1:T(8,128)(2,1)S(1)} %bitcast.28), channel_id=1, source_target_pairs={{0,6},{1,7},{2,4},{3,5},{4,2},{5,3},{6,0},{7,1},{8,14},{9,15},{10,... | collective-permute-start | bytes 1032200 | tf_op jit(solution)/shard_map/ppermute | solution.py:1208
  72.0 31.0 %collective-permute-start.18 = (bf16[3,1,448,128]{3,2,0,1:T(8,128)(2,1)S(1)}, bf16[3,1,448,128]{3,2,0,1:T(8,128)(2,1)S(1)}, u32[]{:S(2)}, u32[]{:S(2)}) collective-permute-start(bf16[3,1,448,128]{3,2,0,1:T(8,128)(2,1)S(1)} %bitcast.27), channel_id=1, source_target_pairs={{0,2},{1,3},{2,0},{3,1},{4,6},{5,7},{6,4},{7,5},{8,10},{9,11},{10,... | collective-permute-start | bytes 1032200 | tf_op jit(solution)/shard_map/ppermute | solution.py:1208
  87.2 9.1 %collective-permute-start.21 = (bf16[4,160,128]{2,1,0:T(8,128)(2,1)S(1)}, bf16[4,160,128]{2,1,0:T(8,128)(2,1)S(1)}, u32[]{:S(2)}, u32[]{:S(2)}) collective-permute-start(bf16[4,160,128]{2,1,0:T(8,128)(2,1)S(1)} %get-tuple-element.132), channel_id=1, source_target_pairs={{0,1},{1,0},{2,3},{3,2},{4,5},{5,4},{6,7},{7,6},{8,9},{9,8},{10,11... | collective-permute-start | bytes 491528 | tf_op jit(solution)/shard_map/ppermute | solution.py:1208
  87.3 7.7 %collective-permute-start.19 = (bf16[4,144,128]{2,1,0:T(8,128)(2,1)S(1)}, bf16[4,144,128]{2,1,0:T(8,128)(2,1)S(1)}, u32[]{:S(2)}, u32[]{:S(2)}) collective-permute-start(bf16[4,144,128]{2,1,0:T(8,128)(2,1)S(1)} %get-tuple-element.130), channel_id=1, source_target_pairs={{0,1},{1,0},{2,3},{3,2},{4,5},{5,4},{6,7},{7,6},{8,9},{9,8},{10,11... | collective-permute-start | bytes 442376 | tf_op jit(solution)/shard_map/ppermute | solution.py:1208
  97.0 12.7 %collective-permute-start.22 = (bf16[1,448,128]{2,1,0:T(8,128)(2,1)S(1)}, bf16[1,448,128]{2,1,0:T(8,128)(2,1)S(1)}, u32[]{:S(2)}, u32[]{:S(2)}) collective-permute-start(bf16[1,448,128]{2,1,0:T(8,128)(2,1)S(1)} %get-tuple-element.135), channel_id=1, source_target_pairs={{0,4},{1,5},{2,6},{3,7},{4,0},{5,1},{6,2},{7,3},{8,12},{9,13},{10,... | collective-permute-start | bytes 344072 | tf_op jit(solution)/shard_map/ppermute | solution.py:1208
  97.0 12.7 %collective-permute-start.23 = (bf16[1,448,128]{2,1,0:T(8,128)(2,1)S(1)}, bf16[1,448,128]{2,1,0:T(8,128)(2,1)S(1)}, u32[]{:S(2)}, u32[]{:S(2)}) collective-permute-start(bf16[1,448,128]{2,1,0:T(8,128)(2,1)S(1)} %get-tuple-element.136), channel_id=1, source_target_pairs={{0,6},{1,7},{2,4},{3,5},{4,2},{5,3},{6,0},{7,1},{8,14},{9,15},{10,... | collective-permute-start | bytes 344072 | tf_op jit(solution)/shard_map/ppermute | solution.py:1208
  99.3 10.4 %collective-permute-start.24 = (bf16[1,448,128]{2,1,0:T(8,128)(2,1)S(1)}, bf16[1,448,128]{2,1,0:T(8,128)(2,1)S(1)}, u32[]{:S(2)}, u32[]{:S(2)}) collective-permute-start(bf16[1,448,128]{2,1,0:T(8,128)(2,1)S(1)} %get-tuple-element.137), channel_id=1, source_target_pairs={{0,2},{1,3},{2,0},{3,1},{4,6},{5,7},{6,4},{7,5},{8,10},{9,11},{10,... | collective-permute-start | bytes 344072 | tf_op jit(solution)/shard_map/ppermute | solution.py:1208
  109.9 6.9 %collective-permute-start.25 = (bf16[448,128]{1,0:T(8,128)(2,1)S(1)}, bf16[448,128]{1,0:T(8,128)(2,1)S(1)}, u32[]{:S(2)}, u32[]{:S(2)}) collective-permute-start(bf16[448,128]{1,0:T(8,128)(2,1)S(1)} %get-tuple-element.139), channel_id=1, source_target_pairs={{0,24},{8,16},{16,8},{24,0},{1,25},{9,17},{17,9},{25,1},{2,26},{10... | collective-permute-start | bytes 344072 | tf_op jit(solution)/shard_map/ppermute | solution.py:1208
  110.2 7.3 %collective-permute-start.26 = (bf16[448,128]{1,0:T(8,128)(2,1)S(1)}, bf16[448,128]{1,0:T(8,128)(2,1)S(1)}, u32[]{:S(2)}, u32[]{:S(2)}) collective-permute-start(bf16[448,128]{1,0:T(8,128)(2,1)S(1)} %get-tuple-element.140), channel_id=1, source_target_pairs={{0,16},{8,24},{16,0},{24,8},{1,17},{9,25},{17,1},{25,9},{2,18},{10... | collective-permute-start | bytes 344072 | tf_op jit(solution)/shard_map/ppermute | solution.py:1208
  112.9 5.2 %collective-permute-start.27 = (bf16[448,128]{1,0:T(8,128)(2,1)S(1)}, bf16[448,128]{1,0:T(8,128)(2,1)S(1)}, u32[]{:S(2)}, u32[]{:S(2)}) collective-permute-start(bf16[448,128]{1,0:T(8,128)(2,1)S(1)} %get-tuple-element.141), channel_id=1, source_target_pairs={{0,8},{8,0},{16,24},{24,16},{1,9},{9,1},{17,25},{25,17},{2,10},{10... | collective-permute-start | bytes 344072 | tf_op jit(solution)/shard_map/ppermute | solution.py:1208
  120.2 5.4 %collective-permute-start.31 = (f32[8,128]{1,0:T(8,128)S(1)}, f32[8,128]{1,0:T(8,128)S(1)}, u32[]{:S(2)}, u32[]{:S(2)}) collective-permute-start(f32[8,128]{1,0:T(8,128)S(1)} %shard_map.155.refs_0_), channel_id=1, source_target_pairs={{0,6},{1,7},{2,4},{3,5},{4,2},{5,3},{6,0},{7,1},{8,14},{9,15},{10,... | collective-permute-start | bytes 12296 | tf_op jit(solution)/shard_map/ppermute | solution.py:1208
  123.4 4.5 %collective-permute-start.30 = (f32[8,128]{1,0:T(8,128)S(1)}, f32[8,128]{1,0:T(8,128)S(1)}, u32[]{:S(2)}, u32[]{:S(2)}) collective-permute-start(f32[8,128]{1,0:T(8,128)S(1)} %shard_map.155.refs_0_), channel_id=1, source_target_pairs={{0,4},{1,5},{2,6},{3,7},{4,0},{5,1},{6,2},{7,3},{8,12},{9,13},{10,... | collective-permute-start | bytes 12296 | tf_op jit(solution)/shard_map/ppermute | solution.py:1208
  125.0 3.6 %collective-permute-start.29 = (f32[8,128]{1,0:T(8,128)S(1)}, f32[8,128]{1,0:T(8,128)S(1)}, u32[]{:S(2)}, u32[]{:S(2)}) collective-permute-start(f32[8,128]{1,0:T(8,128)S(1)} %shard_map.155.refs_0_), channel_id=1, source_target_pairs={{0,2},{1,3},{2,0},{3,1},{4,6},{5,7},{6,4},{7,5},{8,10},{9,11},{10,... | collective-permute-start | bytes 12296 | tf_op jit(solution)/shard_map/ppermute | solution.py:1208
  128.6 4.5 %collective-permute-start.34 = (f32[8,128]{1,0:T(8,128)S(1)}, f32[8,128]{1,0:T(8,128)S(1)}, u32[]{:S(2)}, u32[]{:S(2)}) collective-permute-start(f32[8,128]{1,0:T(8,128)S(1)} %shard_map.156.refs_0_), channel_id=1, source_target_pairs={{0,24},{8,16},{16,8},{24,0},{1,25},{9,17},{17,9},{25,1},{2,26},{10... | collective-permute-start | bytes 12296 | tf_op jit(solution)/shard_map/ppermute | solution.py:1208
  129.6 3.6 %collective-permute-start.33 = (f32[8,128]{1,0:T(8,128)S(1)}, f32[8,128]{1,0:T(8,128)S(1)}, u32[]{:S(2)}, u32[]{:S(2)}) collective-permute-start(f32[8,128]{1,0:T(8,128)S(1)} %shard_map.156.refs_0_), channel_id=1, source_target_pairs={{0,16},{8,24},{16,0},{24,8},{1,17},{9,25},{17,1},{25,9},{2,18},{10... | collective-permute-start | bytes 12296 | tf_op jit(solution)/shard_map/ppermute | solution.py:1208
  130.6 3.6 %collective-permute-start.32 = (f32[8,128]{1,0:T(8,128)S(1)}, f32[8,128]{1,0:T(8,128)S(1)}, u32[]{:S(2)}, u32[]{:S(2)}) collective-permute-start(f32[8,128]{1,0:T(8,128)S(1)} %shard_map.156.refs_0_), channel_id=1, source_target_pairs={{0,8},{8,0},{16,24},{24,16},{1,9},{9,1},{17,25},{25,17},{2,10},{10... | collective-permute-start | bytes 12296 | tf_op jit(solution)/shard_map/ppermute | solution.py:1208
  (14 other events, 85.0 us)
